TPU v7x, 512 devices: a whole 4x4x16 slice. The times are simulated.
512 devices in a mesh: dp: 4 (over y), seq: 8 (over x, core), vocab: 16 (over z).
Axes of the slice: x: 4, y: 4, z: 16, core: 2. Of those that a mesh axis runs over, the one named last changes fastest.
Arguments:
- teacher_logits: bfloat16 [8, 512, 75776], P('dp', 'seq', 'vocab'), may hold values from -50 to 220
- student_logits: bfloat16 [8, 512, 65536], P('dp', 'seq', 'vocab'), may hold values from -50 to 220
- alignment: int32 [8, 512], P('dp', 'seq'), may hold values from 0 to 511, as said below
- src_block: int32 [512, 2], replicated, may hold values from 0 to 591, as said below
- margin_weight: bfloat16 [512, 2, 128, 128], P('vocab', None, 'dp'), may hold values from 0.0019989014 to 0.029907227
Outputs:
- divergence: float32 [8, 512], P('dp', 'seq')
Inputs may be any that keep to these rules, and one draw needn't show every extreme that they name: alignment[d, j] differs from j by at most 16; every document has a position aligned exactly 16 ahead and one exactly 16 behind. `src_block`: the student blocks of one vocab index name teacher blocks of any one vocab index at most 8 times in all, and this bound is reached in every draw; every teacher block is named; the 2 blocks of a student block differ.
All inputs are finite; a program needn't handle non-finite values.
Results may differ from a plain program's by a relative error of at most 0.0003.
Values may be sent and summed in bfloat16 or wider, within the bound.
No kernel may reach another device: no remote copies, remote signals or barrier semaphores. Data moves between devices by JAX's collectives and lax.ppermute only.
A program may use at most 64 MiB of HBM per device.

v0:
```python
import jax
import jax.numpy as jnp
from jax import lax
from jax.sharding import PartitionSpec as P

BLK = 128
K = 2
W = 16


def with_halo(block, sides, width):
    for axis, dim in sides:
        count = lax.axis_size(axis)
        forward = [(i, i + 1) for i in range(count - 1)]
        backward = [(target, source) for source, target in forward]
        low = lax.ppermute(
            lax.slice_in_dim(block, block.shape[dim] - width, None, axis=dim), axis, forward
        )
        high = lax.ppermute(lax.slice_in_dim(block, 0, width, axis=dim), axis, backward)
        block = jnp.concatenate([low, block, high], axis=dim)
    return block


def shards(teacher_logits, student_logits, alignment, src_block, margin_weight):
    doc_count, pos_count, teacher_cols = teacher_logits.shape
    student_cols = student_logits.shape[2]
    teacher_blocks = teacher_cols // BLK
    student_blocks = student_cols // BLK
    row_count = doc_count * pos_count
    seq_index = lax.axis_index("seq")
    padded = with_halo(teacher_logits, (("seq", 1),), W)
    local_rows = alignment - seq_index * pos_count + W
    aligned = jax.vmap(lambda doc_rows, doc_index: jnp.take(doc_rows, doc_index, axis=0))(
        padded, local_rows
    )
    teacher_float = aligned.reshape(row_count, teacher_cols).astype(jnp.float32)
    student_float = student_logits.reshape(row_count, student_cols).astype(jnp.float32)
    teacher_peak = jnp.max(teacher_float, axis=1)
    student_peak = jnp.max(student_float, axis=1)
    teacher_top, student_top = lax.pmax((teacher_peak, student_peak), "vocab")
    teacher_total, student_total = lax.psum(
        (
            jnp.sum(jnp.exp(teacher_float - teacher_top[:, None]), axis=1),
            jnp.sum(jnp.exp(student_float - student_top[:, None]), axis=1),
        ),
        "vocab",
    )
    teacher_prob = (jnp.exp(teacher_float - teacher_top[:, None]) / teacher_total[:, None]).astype(
        jnp.bfloat16
    )
    student_logprob = student_float - student_top[:, None] - jnp.log(student_total)[:, None]
    vocab_count = lax.axis_size("vocab")
    own_index = lax.axis_index("vocab")
    pair_count = student_blocks * K
    capacity = 2 * K * student_blocks // vocab_count
    pair_blocks = src_block.reshape(vocab_count, pair_count)
    holder = pair_blocks // teacher_blocks
    inside = pair_blocks % teacher_blocks
    same_holder = holder[:, :, None] == holder[:, None, :]
    before = jnp.arange(pair_count)[None, :] < jnp.arange(pair_count)[:, None]
    slot_rank = jnp.sum(same_holder & before[None, :, :], axis=2)
    chosen = (holder == own_index)[:, None, :] & (
        slot_rank[:, None, :] == jnp.arange(capacity)[None, :, None]
    )
    send_index = jnp.sum(jnp.where(chosen, inside[:, None, :], 0), axis=2)
    prob_blocks = teacher_prob.reshape(row_count, teacher_blocks, BLK)
    outgoing = jnp.take(prob_blocks, send_index.reshape(-1), axis=1).reshape(
        row_count, vocab_count, capacity, BLK
    )
    incoming = lax.all_to_all(outgoing, "vocab", split_axis=1, concat_axis=1, tiled=True)
    own_holder = jnp.take(holder, own_index, axis=0)
    own_rank = jnp.take(slot_rank, own_index, axis=0)
    recv_slot = own_holder * capacity + own_rank
    gathered = jnp.take(
        incoming.reshape(row_count, vocab_count * capacity, BLK), recv_slot, axis=1
    ).reshape(row_count, student_blocks, K, BLK)
    mapped = jnp.einsum(
        "rbkc,bkcd->rbd",
        gathered,
        lax.all_gather(margin_weight, "dp", axis=2, tiled=True),
        preferred_element_type=jnp.float32,
    ).reshape(row_count, student_cols)
    total_mass = lax.psum(jnp.sum(mapped, axis=1), "vocab")
    normed = mapped / total_mass[:, None]
    result = lax.psum(
        jnp.sum(jax.scipy.special.xlogy(normed, normed) - normed * student_logprob, axis=1), "vocab"
    )
    return result.reshape(doc_count, pos_count)


def solution(mesh):
    in_specs = (
        P("dp", "seq", "vocab"),
        P("dp", "seq", "vocab"),
        P("dp", "seq"),
        P(),
        P("vocab", None, "dp", None),
    )
    out_specs = P("dp", "seq")
    return jax.shard_map(shards, mesh=mesh, in_specs=in_specs, out_specs=out_specs, check_vma=False)
```

profile of v0, /device:TPU:6, one launch (start us, length us, event | category | flops | bytes accessed | tf_op | source)
XLA Modules:
  0.0 357.6 jit_solution(11614908485376962650)
XLA Ops:
  6.5 1.2 fusion.16
  7.7 1.9 collective-permute-start
  9.7 3.6 %collective-permute-start.1 = (bf16[2,16,4736]{2,1,0:T(8,128)(2,1)S(1)}, bf16[2,16,4736]{2,1,0:T(8,128)(2,1)}, u32[]{:S(2)}, u32[]{:S(2)}) collective-permute-start(bf16[2,16,4736]{2,1,0:T(8,128)(2,1)S(1)} %get-tuple-element.26), channel_id=1, source_target_pairs={{16,0},{32,16},{48,32},{64,48},{80,64},{96,80},{112,96},{17,1},{33... | collective-permute-start | bytes 909320 | tf_op jit(solution)/shard_map/ppermute | solution.py:19
  13.3 0.7 bitcast_or_fusion
  14.0 0.7 compare_and_fusion.1
  14.7 0.7 broadcast_divide_fusion
  15.4 0.7 sign_compare_fusion
  16.2 1.5 reduce_max.35
  18.9 0.5 convert_reduce_fusion
  19.4 0.4 select_reduce_fusion
  19.9 1.1 pad_maximum_fusion
  21.0 4.5 %gather_fusion.2 = bf16[128,4736]{1,0:T(8,128)(2,1)S(1)} fusion(bf16[2,96,4736]{2,1,0:T(8,128)(2,1)S(1)} %pad_maximum_fusion, s32[128]{0:T(128)S(1)} %reshape.270), kind=kCustom, calls=%fused_computation.2 | custom fusion | bytes 2425856 | tf_op jit(solution)/shard_map/vmap(jit(_take))/gather | solution.py:33
  25.5 1.3 copy.16
  26.8 0.4 fusion.7
  27.3 36.5 %all-reduce.1 = (f32[128]{0:T(128)S(1)}, f32[128]{0:T(128)S(1)}) all-reduce(f32[128]{0:T(128)S(1)} %reshape.245, f32[128]{0:T(128)S(1)} %reshape.247), channel_id=1, replica_groups=mesh['dp'=4,'seq'=8,'vocab'=16] {'vocab'}, use_global_device_ids=true, to_apply=%region_3.5 | all-reduce | flops 256 | bytes 2048 | tf_op jit(solution)/shard_map/pmax | solution.py:40
  63.9 0.6 exponential_reduce_fusion
  64.6 27.0 %psum.28 = f32[128]{0:T(128)S(1)} all-reduce(f32[128]{0:T(128)S(1)} %reduce_sum.61), channel_id=1, replica_groups=mesh['dp'=4,'seq'=8,'vocab'=16] {'vocab'}, use_global_device_ids=true, to_apply=%region_5.7 | all-reduce | flops 128 | bytes 1024 | tf_op jit(solution)/shard_map/psum | solution.py:41
  91.6 2.0 copy.17
  93.6 1.9 divide_convert_fusion
  95.5 3.0 gather_fusion
  98.5 4.6 %broadcast_select_fusion = bf16[128,16,8,128]{3,0,2,1:T(8,128)(2,1)} fusion(bf16[128,16,8,128]{3,0,2,1:T(8,128)(2,1)} %bitcast.57, pred[16,8]{1,0:T(8,128)(4,1)S(1)} %compare_and_fusion), kind=kLoop, calls=%fused_computation.3 | loop fusion | flops 2097152 | bytes 8388736 | tf_op jit(solution)/shard_map/jit(_take)/select_n | solution.py:67
  103.1 7.9 %all-to-all-start = ((bf16[128,16,8,128]{3,0,2,1:T(8,128)(2,1)}), bf16[128,16,8,128]{3,0,2,1:T(8,128)(2,1)}, u32[]{:S(2)}, u32[]{:S(2)}) async-start(bf16[128,16,8,128]{3,0,2,1:T(8,128)(2,1)} %broadcast_select_fusion), calls=%async_computation | async-start | bytes 8388608 | tf_op jit(solution)/shard_map/all_to_all | solution.py:70
  111.3 0.5 all-gather.2.cloned.1.call-update
  112.0 1.6 copy.20
  113.6 2.0 copy.18
  115.7 0.5 exponential_reduce_fusion.1
  116.3 162.9 %all-to-all-done = bf16[128,16,8,128]{3,0,2,1:T(8,128)(2,1)} async-done(((bf16[128,16,8,128]{3,0,2,1:T(8,128)(2,1)}), bf16[128,16,8,128]{3,0,2,1:T(8,128)(2,1)}, u32[]{:S(2)}, u32[]{:S(2)}) %all-to-all-start) | async-done | bytes 4194336 | tf_op jit(solution)/shard_map/all_to_all | solution.py:70
  279.1 4.3 %gather_fusion.1 = bf16[64,128,128]{2,1,0:T(8,128)(2,1)} fusion(bf16[128,128,128]{2,0,1:T(8,128)(2,1)} %bitcast.8, s32[1024]{0:T(1024)S(1)} %pad_clamp_fusion), kind=kCustom, calls=%fused_computation.1 | custom fusion | bytes 4194560 | tf_op jit(solution)/shard_map/jit(_take)/gather | solution.py:74
  283.5 4.4 %bitcast_reduce_fusion = (f32[128]{0:T(128)S(1)}, f32[32,128,128,1]{1,2,3,0:T(8,128)}) fusion(bf16[32,2,128,128]{3,2,1,0:T(8,128)(2,1)} %all-gather.2.cloned.1.call-done, bf16[128,32,2,128]{3,0,2,1:T(8,128)(2,1)} %bitcast.60, pred[32,2]{1,0:T(8,128)(4,1)S(1)} %broadcast_in_dim.79), kind=kOutput, calls=%fused_computation.14 | convolution fusion | flops 270008192 | bytes 6292032 | tf_op jit(solution)/shard_map/rbkc,bkcd->rbd/dot_general | solution.py:77
  287.9 30.6 %all-reduce = (f32[128]{0:T(128)S(1)}, f32[128]{0:T(128)S(1)}) all-reduce(f32[128]{0:T(128)S(1)} %reduce_sum.64, f32[128]{0:T(128)S(1)} %get-tuple-element.29), channel_id=1, replica_groups=mesh['dp'=4,'seq'=8,'vocab'=16] {'vocab'}, use_global_device_ids=true, to_apply=%region_11.13 | all-reduce | flops 256 | bytes 2048 | tf_op jit(solution)/shard_map/psum | solution.py:41
  318.5 2.4 fusion.2
  321.1 29.7 %psum.31 = f32[2,64]{1,0:T(2,128)} all-reduce(f32[2,64]{1,0:T(2,128)S(1)} %reshape.207), channel_id=1, replica_groups=mesh['dp'=4,'seq'=8,'vocab'=16] {'vocab'}, use_global_device_ids=true, to_apply=%region_13.15 | all-reduce | flops 128 | bytes 1024 | tf_op jit(solution)/shard_map/psum | solution.py:85
  (34 shorter events, 2.3 us)
Async XLA Ops:
  6.5 13.4 %copy-start.1 = (bf16[2,64,4736]{2,1,0:T(8,128)(2,1)S(1)}, bf16[2,64,4736]{2,1,0:T(8,128)(2,1)}, u32[]{:S(2)}) copy-start(bf16[2,64,4736]{2,1,0:T(8,128)(2,1)} %param.7) | copy-start | bytes 3637252
  7.7 12.2 %collective-permute-start = (bf16[2,16,4736]{2,1,0:T(8,128)(2,1)S(1)}, bf16[2,16,4736]{2,1,0:T(8,128)(2,1)S(1)}, u32[]{:S(2)}, u32[]{:S(2)}) collective-permute-start(bf16[2,16,4736]{2,1,0:T(8,128)(2,1)S(1)} %get-tuple-element.25), channel_id=1, source_target_pairs={{0,16},{16,32},{32,48},{48,64},{64,80},{80,96},{96,112},{1,17},{17... | collective-permute-start | bytes 909320 | tf_op jit(solution)/shard_map/ppermute | solution.py:16
  9.7 10.3 %collective-permute-start.1 = (bf16[2,16,4736]{2,1,0:T(8,128)(2,1)S(1)}, bf16[2,16,4736]{2,1,0:T(8,128)(2,1)}, u32[]{:S(2)}, u32[]{:S(2)}) collective-permute-start(bf16[2,16,4736]{2,1,0:T(8,128)(2,1)S(1)} %get-tuple-element.26), channel_id=1, source_target_pairs={{16,0},{32,16},{48,32},{64,48},{80,64},{96,80},{112,96},{17,1},{33... | collective-permute-start | bytes 909320 | tf_op jit(solution)/shard_map/ppermute | solution.py:19
  103.1 8.8 %copy-start = (bf16[2,64,4096]{2,1,0:T(8,128)(2,1)S(1)}, bf16[2,64,4096]{2,1,0:T(8,128)(2,1)}, u32[]{:S(2)}) copy-start(bf16[2,64,4096]{2,1,0:T(8,128)(2,1)} %param.8) | copy-start | bytes 3145732
  103.1 176.0 %all-to-all-start = ((bf16[128,16,8,128]{3,0,2,1:T(8,128)(2,1)}), bf16[128,16,8,128]{3,0,2,1:T(8,128)(2,1)}, u32[]{:S(2)}, u32[]{:S(2)}) async-start(bf16[128,16,8,128]{3,0,2,1:T(8,128)(2,1)} %broadcast_select_fusion), calls=%async_computation | async-start | bytes 8388608 | tf_op jit(solution)/shard_map/all_to_all | solution.py:70
  111.1 172.4 %all-gather.2.cloned.1.call-start = ((), (), s32[]{:S(2)}) async-start(), calls=%async_computation.1 | async-start | bytes 2621440 | tf_op jit(solution)/shard_map/all_gather | solution.py:80
Sparse Core Ops, SparseCore 0:
  114.0 39.7 all-gather.1
where the time goes:
time: 359 us; the launch traced here: 358 us
  waiting for transfers between devices  163 us (45%)
  blocking collectives  124 us (35%)
  local copies, waits for them, and re-layouts  21.9 us (6%)
  other arithmetic  16.7 us (5%)
  starting transfers between devices  13.7 us (4%)
  between operations  13.6 us (4%)
  matrix products  4.43 us (1%)
    all_to_all x1, waiting for transfers between devices, shards(): lax.all_to_all(outgoing, 'vocab', split_axis=1, concat_axis=1, tiled=True)  163 us
    psum x2, blocking collectives, shards(): lax.psum((jnp.sum(jnp.exp(teacher_float - teacher_top[:, None]), axis=1),...  57.6 us
    pmax x1, blocking collectives, shards(): teacher_top, student_top = lax.pmax((teacher_peak, student_peak), 'vocab')  36.5 us
    psum x1, blocking collectives, shards(): lax.psum(jnp.sum(jax.scipy.special.xlogy(normed, normed) - normed * stude...  29.7 us
    all_to_all x1, starting transfers between devices, shards(): lax.all_to_all(outgoing, 'vocab', split_axis=1, concat_axis=1, tiled=True)  7.93 us
    gather x4, local copies, waits for them, and re-layouts, shards(): jnp.take(doc_rows, doc_index, axis=0)  7.84 us
  transfers between devices with their start and end apart: 4, of which 1 were waited for; matrix products, arithmetic and copies ran while one was open for 4% of the time, Pallas kernels for 0%

commit v1 on v0

v1 whole, which is shorter than its diff:
```python
import functools

import jax
import jax.numpy as jnp
from jax import lax
from jax.experimental import pallas as pl
from jax.experimental.pallas import tpu as pltpu
from jax.sharding import PartitionSpec as P

BLK = 128
K = 2
W = 16
ROWS = 104
PROFILE = (37, 37, 36, 31, 26, 20, 14, 6)
TINY = 1.2e-38


def halo(block, width):
    count = lax.axis_size("seq")
    forward = [(i, i + 1) for i in range(count - 1)]
    backward = [(target, source) for source, target in forward]
    low = lax.ppermute(block[:, block.shape[1] - width :], "seq", forward)
    high = lax.ppermute(block[:, :width], "seq", backward)
    return low, high


def ring_pairs(turn):
    seq_count, vocab_count = lax.axis_size("seq"), lax.axis_size("vocab")
    pairs = []
    for s in range(seq_count):
        step = turn if s % 2 == 0 else -turn
        for v in range(vocab_count):
            pairs.append((s * vocab_count + v, s * vocab_count + (v + step) % vocab_count))
    return pairs


def ways(distance, block, vocab_count):
    half = vocab_count // 2
    even = block % 2 == 0
    ahead = jnp.where(((distance >= 1) & (distance < half)) | ((distance == half) & even), distance, 0)
    behind = jnp.where((distance > half) | ((distance == half) & ~even), vocab_count - distance, 0)
    return ahead, behind


def reaches(need, block, holder, sign, vocab_count):
    targets = jnp.arange(vocab_count)[:, None]
    distance = (sign * (targets - holder[None, :]) + vocab_count) % vocab_count
    ahead, behind = ways(distance, block[None, :], vocab_count)
    return jnp.max(jnp.where(need, ahead, 0), axis=0), jnp.max(jnp.where(need, behind, 0), axis=0)


def ranks(reach):
    size = reach.shape[-1]
    key = reach * size - jnp.arange(size)
    return jnp.sum((key[..., None, :] > key[..., :, None]).astype(jnp.int32), axis=-1)


def pack_kernel(order_ref, own_ref, low_ref, high_ref, pick_ref, ahead_ref, behind_ref, home_ref, cand_ref, logit_ref):
    docs, positions, columns = own_ref.shape
    width = low_ref.shape[1]
    span = positions + 2 * width
    rows = pick_ref.shape[0]
    blocks = columns // BLK
    for doc in range(docs):
        cand_ref[doc * span : doc * span + width, :] = low_ref[doc]
        cand_ref[doc * span + width : doc * span + width + positions, :] = own_ref[doc]
        cand_ref[doc * span + width + positions : (doc + 1) * span, :] = high_ref[doc]
    pick = pick_ref[...]
    peak = jnp.full((rows, BLK), -jnp.inf, jnp.float32)
    for t in range(blocks):
        part = jnp.dot(pick, cand_ref[:, t * BLK : (t + 1) * BLK], preferred_element_type=jnp.float32)
        logit_ref[t] = part.astype(jnp.bfloat16)
        peak = jnp.maximum(peak, part)
    top = jnp.max(peak, axis=1, keepdims=True)
    total = jnp.zeros((rows, BLK), jnp.float32)
    for t in range(blocks):
        power = jnp.exp(logit_ref[t].astype(jnp.float32) - top)
        total = total + power
        home_ref[1 + t] = power.astype(jnp.bfloat16)
    total = jnp.sum(total, axis=1, keepdims=True)
    first = total.astype(jnp.bfloat16).astype(jnp.float32)
    second = (total - first).astype(jnp.bfloat16).astype(jnp.float32)
    third = total - first - second
    lane = lax.broadcasted_iota(jnp.int32, (rows, BLK), 1)
    stats = jnp.where(
        lane == 0, top, jnp.where(lane == 1, first, jnp.where(lane == 2, second, jnp.where(lane == 3, third, 0.0)))
    ).astype(jnp.bfloat16)
    home_ref[0] = stats
    ahead_ref[0] = stats
    behind_ref[0] = stats
    for i in range(ahead_ref.shape[0] - 1):
        ahead_ref[1 + i] = home_ref[1 + order_ref[0, i]]
        behind_ref[1 + i] = home_ref[1 + order_ref[1, i]]


def student_kernel(student_ref, top_ref, total_ref):
    docs, positions, columns = student_ref.shape
    rows = docs * positions
    peak = jnp.full((rows, BLK), -jnp.inf, jnp.float32)
    for b in range(columns // BLK):
        part = student_ref[:, :, b * BLK : (b + 1) * BLK].reshape(rows, BLK).astype(jnp.float32)
        peak = jnp.maximum(peak, part)
    top = jnp.max(peak, axis=1, keepdims=True)
    total = jnp.zeros((rows, BLK), jnp.float32)
    for b in range(columns // BLK):
        part = student_ref[:, :, b * BLK : (b + 1) * BLK].reshape(rows, BLK).astype(jnp.float32)
        total = total + jnp.exp(part - top)
    top_ref[...] = jnp.broadcast_to(top, (rows, BLK))
    total_ref[...] = jnp.broadcast_to(jnp.sum(total, axis=1, keepdims=True), (rows, BLK))


def map_kernel(steps, plan_ref, count_ref, *refs):
    sources = refs[: 2 * steps + 1]
    spread_ref, weight_ref, student_ref, top_ref, total_ref, out_ref, stage_ref, scale_ref = refs[2 * steps + 1 :]
    docs, positions, columns = student_ref.shape
    rows = docs * positions
    blocks = columns // BLK
    spread = spread_ref[...]
    for s, source in enumerate(sources):

        def bring(j, carry, s=s, source=source):
            pair = plan_ref[2, s * 8 + j]
            stage_ref[pair] = source[1 + plan_ref[0, pair]]
            return carry

        lax.fori_loop(0, count_ref[s], bring, 0)
    peaks, sums = [], []
    for source in sources:
        stats = jnp.dot(spread, source[0], preferred_element_type=jnp.float32)
        peaks.append(stats[:, 0:1])
        sums.append(stats[:, 1:2] + stats[:, 2:3] + stats[:, 3:4])
    peak = functools.reduce(jnp.maximum, peaks)
    powers = [jnp.exp(p - peak) for p in peaks]
    norm = sum(p * t for p, t in zip(powers[: 2 * steps], sums[: 2 * steps]))
    for s in range(len(sources)):
        scale_ref[s] = jnp.broadcast_to(powers[s] / norm, (rows, BLK))
    student_top = top_ref[...]
    mass = jnp.zeros((rows, BLK), jnp.float32)
    cross = jnp.zeros((rows, BLK), jnp.float32)
    for b in range(blocks):
        picked = jnp.concatenate([stage_ref[K * b], stage_ref[K * b + 1]], axis=1)
        prob = jnp.dot(spread, picked, preferred_element_type=jnp.float32).astype(jnp.bfloat16)
        mapped = scale_ref[plan_ref[1, K * b]] * jnp.dot(
            prob[:, :BLK], weight_ref[K * b], preferred_element_type=jnp.float32
        ) + scale_ref[plan_ref[1, K * b + 1]] * jnp.dot(
            prob[:, BLK:], weight_ref[K * b + 1], preferred_element_type=jnp.float32
        )
        logit = student_ref[:, :, b * BLK : (b + 1) * BLK].reshape(rows, BLK).astype(jnp.float32) - student_top
        mass = mass + mapped
        cross = cross + mapped * (jnp.log(jnp.maximum(mapped, TINY)) - logit)
    mass = jnp.sum(mass, axis=1, keepdims=True)
    cross = jnp.sum(cross, axis=1, keepdims=True)
    lane = lax.broadcasted_iota(jnp.int32, (rows, BLK), 1)
    table = jnp.where(
        lane == 0, mass, jnp.where(lane == 1, cross, jnp.where(lane == 2, student_top, total_ref[...]))
    )
    out_ref[...] = table.T[:8]


def whole(padded_parts, cand, src_block, weights, student_logits):
    doc_count, pos_count, student_cols = student_logits.shape
    teacher_cols = padded_parts[0].shape[2]
    teacher_blocks = teacher_cols // BLK
    student_blocks = student_cols // BLK
    row_count = doc_count * pos_count
    padded = jnp.concatenate(padded_parts, axis=1).reshape(-1, teacher_cols)
    teacher_float = jnp.take(padded, cand, axis=0).astype(jnp.float32)
    student_float = student_logits.reshape(row_count, student_cols).astype(jnp.float32)
    teacher_peak = jnp.max(teacher_float, axis=1)
    student_peak = jnp.max(student_float, axis=1)
    teacher_top, student_top = lax.pmax((teacher_peak, student_peak), "vocab")
    teacher_total, student_total = lax.psum(
        (
            jnp.sum(jnp.exp(teacher_float - teacher_top[:, None]), axis=1),
            jnp.sum(jnp.exp(student_float - student_top[:, None]), axis=1),
        ),
        "vocab",
    )
    teacher_prob = (jnp.exp(teacher_float - teacher_top[:, None]) / teacher_total[:, None]).astype(jnp.bfloat16)
    student_logprob = student_float - student_top[:, None] - jnp.log(student_total)[:, None]
    vocab_count = lax.axis_size("vocab")
    own_index = lax.axis_index("vocab")
    pair_count = student_blocks * K
    capacity = 2 * K * student_blocks // vocab_count
    pair_blocks = src_block.reshape(vocab_count, pair_count)
    holder = pair_blocks // teacher_blocks
    inside = pair_blocks % teacher_blocks
    same_holder = holder[:, :, None] == holder[:, None, :]
    before = jnp.arange(pair_count)[None, :] < jnp.arange(pair_count)[:, None]
    slot_rank = jnp.sum(same_holder & before[None, :, :], axis=2)
    chosen = (holder == own_index)[:, None, :] & (
        slot_rank[:, None, :] == jnp.arange(capacity)[None, :, None]
    )
    send_index = jnp.sum(jnp.where(chosen, inside[:, None, :], 0), axis=2)
    prob_blocks = teacher_prob.reshape(row_count, teacher_blocks, BLK)
    outgoing = jnp.take(prob_blocks, send_index.reshape(-1), axis=1).reshape(row_count, vocab_count, capacity, BLK)
    incoming = lax.all_to_all(outgoing, "vocab", split_axis=1, concat_axis=1, tiled=True)
    own_holder = jnp.take(holder, own_index, axis=0)
    own_rank = jnp.take(slot_rank, own_index, axis=0)
    recv_slot = own_holder * capacity + own_rank
    gathered = jnp.take(incoming.reshape(row_count, vocab_count * capacity, BLK), recv_slot, axis=1).reshape(
        row_count, student_blocks, K, BLK
    )
    mapped = jnp.einsum("rbkc,bkcd->rbd", gathered, weights, preferred_element_type=jnp.float32).reshape(
        row_count, student_cols
    )
    total_mass = lax.psum(jnp.sum(mapped, axis=1), "vocab")
    normed = mapped / total_mass[:, None]
    return lax.psum(
        jnp.sum(jax.scipy.special.xlogy(normed, normed) - normed * student_logprob, axis=1), "vocab"
    )


def shards(teacher_logits, student_logits, alignment, src_block, margin_weight):
    doc_count, pos_count, teacher_cols = teacher_logits.shape
    student_cols = student_logits.shape[2]
    teacher_blocks = teacher_cols // BLK
    student_blocks = student_cols // BLK
    row_count = doc_count * pos_count
    pair_count = student_blocks * K
    vocab_count = lax.axis_size("vocab")
    steps = vocab_count // 2
    sizes = tuple(min(size, teacher_blocks) for size in PROFILE)
    vocab_index = lax.axis_index("vocab")
    seq_index = lax.axis_index("seq")
    sign = 1 - 2 * (seq_index % 2)
    span = pos_count + 2 * W

    with jax.named_scope("halo"):
        low, high = halo(teacher_logits, W)
    with jax.named_scope("weights"):
        weights = lax.all_gather(margin_weight, "dp", axis=2, tiled=True)

    with jax.named_scope("rows"):
        cand = (alignment - seq_index * pos_count + W + jnp.arange(doc_count)[:, None] * span).reshape(-1)
        cand = jnp.clip(cand, 0, doc_count * span - 1)
        places = jnp.arange(doc_count * span)
        used = jnp.any(cand[:, None] == places[None, :], axis=0)
        place_rank = jnp.sum(used[:, None] & (places[:, None] < places[None, :]), axis=0)
        cand_rank = jnp.sum(used[None, :] & (places[None, :] < cand[:, None]), axis=1)
        row_ids = jnp.arange(ROWS)
        pick = ((row_ids[:, None] == place_rank[None, :]) & used[None, :]).astype(jnp.bfloat16)
        spread = (cand_rank[:, None] == row_ids[None, :]).astype(jnp.bfloat16)
        rows_fit = jnp.sum(used.astype(jnp.int32)) <= ROWS

    with jax.named_scope("send_order"):
        listed = src_block.reshape(vocab_count, pair_count)
        inner = jnp.arange(teacher_blocks)
        own_blocks = vocab_index * teacher_blocks + inner
        own_need = jnp.any(listed[:, :, None] == own_blocks[None, None, :], axis=1)
        own_reach = jnp.stack(
            reaches(own_need, own_blocks, jnp.full((teacher_blocks,), vocab_index), sign, vocab_count)
        )
        own_rank = ranks(own_reach)
        order = jnp.sum(
            jnp.where(own_rank[:, None, :] == inner[None, :, None], inner[None, None, :], 0), axis=2
        ).astype(jnp.int32)

    vmem = pl.BlockSpec(memory_space=pltpu.VMEM)
    smem = pl.BlockSpec(memory_space=pltpu.SMEM)
    big = pltpu.CompilerParams(vmem_limit_bytes=44 * 1024 * 1024)
    buffer = jax.ShapeDtypeStruct((1 + sizes[0], ROWS, BLK), jnp.bfloat16)
    with jax.named_scope("pack"):
        ahead, behind, home = pl.pallas_call(
            pack_kernel,
            out_shape=(buffer, buffer, jax.ShapeDtypeStruct((1 + teacher_blocks, ROWS, BLK), jnp.bfloat16)),
            in_specs=[smem] + [vmem] * 4,
            out_specs=(vmem,) * 3,
            scratch_shapes=[
                pltpu.VMEM((doc_count * span, teacher_cols), jnp.bfloat16),
                pltpu.VMEM((teacher_blocks, ROWS, BLK), jnp.bfloat16),
            ],
            compiler_params=big,
        )(order, teacher_logits, low, high, pick)

    with jax.named_scope("ring"):
        forward, backward = ring_pairs(1), ring_pairs(-1)
        came_ahead, came_behind = [], []
        for size in sizes:
            ahead = lax.ppermute(ahead[: 1 + size], ("seq", "vocab"), forward)
            behind = lax.ppermute(behind[: 1 + size], ("seq", "vocab"), backward)
            came_ahead.append(ahead)
            came_behind.append(behind)

    with jax.named_scope("student"):
        top, total = pl.pallas_call(
            student_kernel,
            out_shape=(jax.ShapeDtypeStruct((row_count, BLK), jnp.float32),) * 2,
            in_specs=[vmem],
            out_specs=(vmem,) * 2,
            compiler_params=big,
        )(student_logits)

    with jax.named_scope("receive_plan"):
        blocks = jnp.arange(vocab_count * teacher_blocks)
        block_holder = blocks // teacher_blocks
        need = jnp.any(listed[:, :, None] == blocks[None, None, :], axis=1)
        reach = jnp.stack(reaches(need, blocks, block_holder, sign, vocab_count)).reshape(
            2, vocab_count, teacher_blocks
        )
        fits = jnp.all(
            jnp.stack([jnp.sum((reach >= k + 1).astype(jnp.int32), axis=2) <= size for k, size in enumerate(sizes)])
        )
        all_rank = ranks(reach).reshape(2, 1, -1)
        mine = lax.dynamic_index_in_dim(listed, vocab_index, 0, keepdims=False)
        at_block = mine[:, None] == blocks[None, :]
        rank_of = jnp.sum(jnp.where(at_block[None], all_rank, 0), axis=2)
        distance = (sign * (vocab_index - mine // teacher_blocks) + vocab_count) % vocab_count
        go_ahead, go_behind = ways(distance, mine, vocab_count)
        source = jnp.where(go_ahead > 0, go_ahead, jnp.where(go_behind > 0, steps + go_behind, 0))
        limits = jnp.array((teacher_blocks,) + sizes + sizes, jnp.int32)
        source_ids = jnp.arange(2 * steps + 1)
        at_source = source[:, None] == source_ids[None, :]
        limit = jnp.sum(jnp.where(at_source, limits[None, :], 0), axis=1)
        place = jnp.where(go_ahead > 0, rank_of[0], jnp.where(go_behind > 0, rank_of[1], mine % teacher_blocks))
        place = jnp.clip(place, 0, limit - 1)
        pairs = jnp.arange(pair_count)
        turn = jnp.sum((source[:, None] == source[None, :]) & (pairs[None, :] < pairs[:, None]), axis=1)
        slots = jnp.arange((2 * steps + 1) * 8)
        pair_list = jnp.sum(jnp.where((source * 8 + turn)[None, :] == slots[:, None], pairs[None, :], 0), axis=1)
        count = jnp.minimum(jnp.sum(at_source.astype(jnp.int32), axis=0), 8).astype(jnp.int32)
        pad = lambda values: jnp.pad(values, (0, 256 - values.shape[0]))
        plan = jnp.stack([pad(place), pad(source), pad(pair_list)]).astype(jnp.int32)

    with jax.named_scope("map"):
        held = pl.pallas_call(
            functools.partial(map_kernel, steps),
            out_shape=jax.ShapeDtypeStruct((8, row_count), jnp.float32),
            in_specs=[smem] * 2 + [vmem] * (2 * steps + 1 + 5),
            out_specs=vmem,
            scratch_shapes=[
                pltpu.VMEM((pair_count, ROWS, BLK), jnp.bfloat16),
                pltpu.VMEM((2 * steps + 1, row_count, BLK), jnp.float32),
            ],
            compiler_params=big,
        )(
            plan,
            count,
            home,
            *came_ahead,
            *came_behind,
            spread,
            weights.reshape(pair_count, BLK, BLK),
            student_logits,
            top,
            total,
        )

    with jax.named_scope("finish"):
        sent = jnp.broadcast_to(held[None, :4], (vocab_count, 4, row_count))
        parts = lax.all_to_all(sent, "vocab", split_axis=0, concat_axis=0, tiled=True)
        mass_part, cross_part, top_part, total_part = (parts[:, i] for i in range(4))
        student_top = jnp.max(top_part, axis=0)
        log_total = student_top + jnp.log(jnp.sum(jnp.exp(top_part - student_top) * total_part, axis=0))
        mass = jnp.sum(mass_part, axis=0)
        result = jnp.sum(cross_part + mass_part * (log_total - top_part), axis=0) / mass - jnp.log(mass)

    result = lax.cond(
        rows_fit & fits,
        lambda *_: result,
        lambda *operands: whole(operands[:3], *operands[3:]),
        low,
        teacher_logits,
        high,
        cand,
        src_block,
        weights,
        student_logits,
    )
    return result.reshape(doc_count, pos_count)


def solution(mesh):
    in_specs = (
        P("dp", "seq", "vocab"),
        P("dp", "seq", "vocab"),
        P("dp", "seq"),
        P(),
        P("vocab", None, "dp", None),
    )
    out_specs = P("dp", "seq")
    return jax.shard_map(shards, mesh=mesh, in_specs=in_specs, out_specs=out_specs, check_vma=False)
```

time: 359 us -> 245 us (0.68)
  blocking collectives: 124 us -> 0 us
  waiting for transfers between devices: 163 us -> 83.1 us
  starting transfers between devices: 13.7 us -> 77.4 us
  Pallas kernels: 0 us -> 10.8 us
  other arithmetic: 16.7 us -> 24.5 us
  between operations: 13.6 us -> 20 us
  local copies, waits for them, and re-layouts: 21.9 us -> 26.6 us
  matrix products: 4.43 us -> 0 us
    all_to_all x1, waiting for transfers between devices: 163 us -> 3.93 us  [shards(): lax.all_to_all(sent, 'vocab', split_axis=0, concat_axis=0, tiled=True)]
    psum x3 -> x0, blocking collectives: 87.4 us -> none  [the longest x2 57.6 us: shards(): lax.psum((jnp.sum(jnp.exp(teacher_float - teacher_top[:, None]), axis=1),...]
    ppermute x2 -> x18, waiting for transfers between devices: 0.01 us -> 79.1 us  [the longest x8 79.1 us: shards(): ahead = lax.ppermute(ahead[:1 + size], ('seq', 'vocab'), forward)]
    ppermute x2 -> x18, starting transfers between devices: 5.56 us -> 69.6 us  [the longest x8 46.7 us: shards(): behind = lax.ppermute(behind[:1 + size], ('seq', 'vocab'), backward)]
    pmax x1 -> x0, blocking collectives: 36.5 us -> none  [shards(): teacher_top, student_top = lax.pmax((teacher_peak, student_peak), 'vocab')]
    gather x6 -> x0, local copies, waits for them, and re-layouts: 15.2 us -> none  [the longest x4 7.84 us: shards(): jnp.take(doc_rows, doc_index, axis=0)]
    pallas_call x0 -> x3, Pallas kernels: none -> 10.8 us  [the longest x1 7.06 us: shards(): pl.pallas_call(functools.partial(map_kernel, steps), out_shape=jax.ShapeD...]
    reduce_and x0 -> x8, other arithmetic: none -> 10.2 us  [shards(): jnp.all(jnp.stack([jnp.sum((reach >= k + 1).astype(jnp.int32), axis=2) <=...]
  transfers between devices with their start and end apart: 4 -> 20, of which waited for: 1 -> 8; matrix products, arithmetic and copies ran while one was open for 4% -> 18% of each run, Pallas kernels for 0% -> 1%
where the time goes in v1:
time: 245 us; the launch traced here: 242 us
  waiting for transfers between devices  83.1 us (34%)
  starting transfers between devices  77.4 us (32%)
  local copies, waits for them, and re-layouts  26.6 us (11%)
  other arithmetic  24.5 us (10%)
  between operations  20 us (8%)
  Pallas kernels  10.8 us (4%)
    ppermute x8, waiting for transfers between devices, shards(): ahead = lax.ppermute(ahead[:1 + size], ('seq', 'vocab'), forward)  79.1 us
    ppermute x8, starting transfers between devices, shards(): behind = lax.ppermute(behind[:1 + size], ('seq', 'vocab'), backward)  46.7 us
    ppermute x8, starting transfers between devices, shards(): ahead = lax.ppermute(ahead[:1 + size], ('seq', 'vocab'), forward)  17.3 us
    reduce_and x8, other arithmetic, shards(): jnp.all(jnp.stack([jnp.sum((reach >= k + 1).astype(jnp.int32), axis=2) <=...  10.2 us
    all_to_all x1, starting transfers between devices, shards(): lax.all_to_all(sent, 'vocab', split_axis=0, concat_axis=0, tiled=True)  7.82 us
    unnamed x71, local copies, waits for them, and re-layouts  7.34 us
    pallas_call x1, Pallas kernels, shards(): pl.pallas_call(functools.partial(map_kernel, steps), out_shape=jax.ShapeD...  7.06 us
    slice x6, local copies, waits for them, and re-layouts, shards(): behind = lax.ppermute(behind[:1 + size], ('seq', 'vocab'), backward)  5.94 us
  transfers between devices with their start and end apart: 20, of which 8 were waited for; matrix products, arithmetic and copies ran while one was open for 18% of the time, Pallas kernels for 1%

profile of v1, /device:TPU:6, one launch (start us, length us, event | category | flops | bytes accessed | tf_op | source)
XLA Modules:
  0.0 242.3 jit_solution(17954035542496036119)
XLA Ops:
  7.7 1.9 collective-permute-start
  9.7 3.6 %collective-permute-start.1 = (bf16[2,16,4736]{2,1,0:T(8,128)(2,1)S(1)}, bf16[2,16,4736]{2,1,0:T(8,128)(2,1)S(1)}, u32[]{:S(2)}, u32[]{:S(2)}) collective-permute-start(bf16[2,16,4736]{2,1,0:T(8,128)(2,1)S(1)} %get-tuple-element.173), channel_id=1, source_target_pairs={{16,0},{32,16},{48,32},{64,48},{80,64},{96,80},{112,96},{17,1},{33... | collective-permute-start | bytes 909320 | tf_op jit(solution)/shard_map/halo/ppermute | solution.py:23
  19.5 1.9 pack.1
  21.5 3.9 %collective-permute-start.2 = (bf16[38,104,128]{2,1,0:T(8,128)(2,1)S(1)}, bf16[38,104,128]{2,1,0:T(8,128)(2,1)S(1)}, u32[]{:S(2)}, u32[]{:S(2)}) collective-permute-start(bf16[38,104,128]{2,1,0:T(8,128)(2,1)S(1)} %get-tuple-element.85), channel_id=1, source_target_pairs={{0,1},{1,2},{2,3},{3,4},{4,5},{5,6},{6,7},{7,8},{8,9},{9,10},{10,1... | collective-permute-start | bytes 3035144 | tf_op jit(solution)/shard_map/ring/ppermute | solution.py:280
  25.4 9.5 %collective-permute-start.10 = (bf16[38,104,128]{2,1,0:T(8,128)(2,1)S(1)}, bf16[38,104,128]{2,1,0:T(8,128)(2,1)S(1)}, u32[]{:S(2)}, u32[]{:S(2)}) collective-permute-start(bf16[38,104,128]{2,1,0:T(8,128)(2,1)S(1)} %get-tuple-element.86), channel_id=1, source_target_pairs={{0,15},{1,0},{2,1},{3,2},{4,3},{5,4},{6,5},{7,6},{8,7},{9,8},{10,9... | collective-permute-start | bytes 3035144 | tf_op jit(solution)/shard_map/ring/ppermute | solution.py:281
  35.0 18.5 %collective-permute-done.2.refs_1_ = bf16[38,104,128]{2,1,0:T(8,128)(2,1)S(1)} collective-permute-done((bf16[38,104,128]{2,1,0:T(8,128)(2,1)S(1)}, bf16[38,104,128]{2,1,0:T(8,128)(2,1)S(1)}, u32[]{:S(2)}, u32[]{:S(2)}) %collective-permute-start.2) | collective-permute-done | bytes 1011744 | tf_op jit(solution)/shard_map/ring/ppermute | solution.py:280
  53.5 1.9 collective-permute-start.3
  56.4 6.3 %collective-permute-start.11 = (bf16[38,104,128]{2,1,0:T(8,128)(2,1)S(1)}, bf16[38,104,128]{2,1,0:T(8,128)(2,1)S(1)}, u32[]{:S(2)}, u32[]{:S(2)}) collective-permute-start(bf16[38,104,128]{2,1,0:T(8,128)(2,1)S(1)} %collective-permute-done.10.refs_9_), channel_id=1, source_target_pairs={{0,15},{1,0},{2,1},{3,2},{4,3},{5,4},{6,5},{7,6},{8,7},{9,8},{10,9... | collective-permute-start | bytes 3035144 | tf_op jit(solution)/shard_map/ring/ppermute | solution.py:281
  62.6 19.9 %collective-permute-done.3.refs_2_ = bf16[38,104,128]{2,1,0:T(8,128)(2,1)S(1)} collective-permute-done((bf16[38,104,128]{2,1,0:T(8,128)(2,1)S(1)}, bf16[38,104,128]{2,1,0:T(8,128)(2,1)S(1)}, u32[]{:S(2)}, u32[]{:S(2)}) %collective-permute-start.3) | collective-permute-done | bytes 1011744 | tf_op jit(solution)/shard_map/ring/ppermute | solution.py:280
  82.6 1.9 collective-permute-start.4
  85.7 5.1 %collective-permute-start.12 = (bf16[37,104,128]{2,1,0:T(8,128)(2,1)}, bf16[37,104,128]{2,1,0:T(8,128)(2,1)S(1)}, u32[]{:S(2)}, u32[]{:S(2)}) collective-permute-start(bf16[37,104,128]{2,1,0:T(8,128)(2,1)} %slice.103), channel_id=1, source_target_pairs={{0,15},{1,0},{2,1},{3,2},{4,3},{5,4},{6,5},{7,6},{8,7},{9,8},{10,9... | collective-permute-start | bytes 2955272 | tf_op jit(solution)/shard_map/ring/ppermute | solution.py:281
  94.0 16.0 %collective-permute-done.4.refs_3_ = bf16[37,104,128]{2,1,0:T(8,128)(2,1)S(1)} collective-permute-done((bf16[37,104,128]{2,1,0:T(8,128)(2,1)S(1)}, bf16[37,104,128]{2,1,0:T(8,128)(2,1)S(1)}, u32[]{:S(2)}, u32[]{:S(2)}) %collective-permute-start.4) | collective-permute-done | bytes 985120 | tf_op jit(solution)/shard_map/ring/ppermute | solution.py:280
  111.0 1.9 collective-permute-start.5
  113.9 5.1 %collective-permute-start.13 = (bf16[32,104,128]{2,1,0:T(8,128)(2,1)}, bf16[32,104,128]{2,1,0:T(8,128)(2,1)}, u32[]{:S(2)}, u32[]{:S(2)}) collective-permute-start(bf16[32,104,128]{2,1,0:T(8,128)(2,1)} %slice.104), channel_id=1, source_target_pairs={{0,15},{1,0},{2,1},{3,2},{4,3},{5,4},{6,5},{7,6},{8,7},{9,8},{10,9... | collective-permute-start | bytes 2555912 | tf_op jit(solution)/shard_map/ring/ppermute | solution.py:281
  119.9 2.1 convert_reduce_fusion.1
  122.7 12.6 %collective-permute-done.5.refs_4_ = bf16[32,104,128]{2,1,0:T(8,128)(2,1)S(1)} collective-permute-done((bf16[32,104,128]{2,1,0:T(8,128)(2,1)}, bf16[32,104,128]{2,1,0:T(8,128)(2,1)S(1)}, u32[]{:S(2)}, u32[]{:S(2)}) %collective-permute-start.5) | collective-permute-done | bytes 852000 | tf_op jit(solution)/shard_map/ring/ppermute | solution.py:280
  136.3 1.9 collective-permute-start.6
  138.2 2.0 slice.105
  140.3 5.1 %collective-permute-start.14 = (bf16[27,104,128]{2,1,0:T(8,128)(2,1)}, bf16[27,104,128]{2,1,0:T(8,128)(2,1)}, u32[]{:S(2)}, u32[]{:S(2)}) collective-permute-start(bf16[27,104,128]{2,1,0:T(8,128)(2,1)} %slice.105), channel_id=1, source_target_pairs={{0,15},{1,0},{2,1},{3,2},{4,3},{5,4},{6,5},{7,6},{8,7},{9,8},{10,9... | collective-permute-start | bytes 2156552 | tf_op jit(solution)/shard_map/ring/ppermute | solution.py:281
  155.9 2.3 collective-permute-done.6.refs_5_
  158.2 1.9 collective-permute-start.7
  161.2 5.1 %collective-permute-start.15 = (bf16[21,104,128]{2,1,0:T(8,128)(2,1)S(1)}, bf16[21,104,128]{2,1,0:T(8,128)(2,1)S(1)}, u32[]{:S(2)}, u32[]{:S(2)}) collective-permute-start(bf16[21,104,128]{2,1,0:T(8,128)(2,1)S(1)} %slice.106), channel_id=1, source_target_pairs={{0,15},{1,0},{2,1},{3,2},{4,3},{5,4},{6,5},{7,6},{8,7},{9,8},{10,9... | collective-permute-start | bytes 1677320 | tf_op jit(solution)/shard_map/ring/ppermute | solution.py:281
  171.9 4.9 %collective-permute-done.7.refs_6_ = bf16[21,104,128]{2,1,0:T(8,128)(2,1)S(1)} collective-permute-done((bf16[21,104,128]{2,1,0:T(8,128)(2,1)S(1)}, bf16[21,104,128]{2,1,0:T(8,128)(2,1)S(1)}, u32[]{:S(2)}, u32[]{:S(2)}) %collective-permute-start.7) | collective-permute-done | bytes 559136 | tf_op jit(solution)/shard_map/ring/ppermute | solution.py:280
  177.6 1.9 collective-permute-start.8
  180.4 5.1 %collective-permute-start.16 = (bf16[15,104,128]{2,1,0:T(8,128)(2,1)S(1)}, bf16[15,104,128]{2,1,0:T(8,128)(2,1)S(1)}, u32[]{:S(2)}, u32[]{:S(2)}) collective-permute-start(bf16[15,104,128]{2,1,0:T(8,128)(2,1)S(1)} %slice.107), channel_id=1, source_target_pairs={{0,15},{1,0},{2,1},{3,2},{4,3},{5,4},{6,5},{7,6},{8,7},{9,8},{10,9... | collective-permute-start | bytes 1198088 | tf_op jit(solution)/shard_map/ring/ppermute | solution.py:281
  187.0 4.8 %collective-permute-done.8.refs_7_ = bf16[15,104,128]{2,1,0:T(8,128)(2,1)S(1)} collective-permute-done((bf16[15,104,128]{2,1,0:T(8,128)(2,1)S(1)}, bf16[15,104,128]{2,1,0:T(8,128)(2,1)S(1)}, u32[]{:S(2)}, u32[]{:S(2)}) %collective-permute-start.8) | collective-permute-done | bytes 399392 | tf_op jit(solution)/shard_map/ring/ppermute | solution.py:280
  193.3 1.9 collective-permute-start.9
  196.7 5.3 %collective-permute-start.17 = (bf16[7,104,128]{2,1,0:T(8,128)(2,1)}, bf16[7,104,128]{2,1,0:T(8,128)(2,1)}, u32[]{:S(2)}, u32[]{:S(2)}) collective-permute-start(bf16[7,104,128]{2,1,0:T(8,128)(2,1)} %slice.108), channel_id=1, source_target_pairs={{0,15},{1,0},{2,1},{3,2},{4,3},{5,4},{6,5},{7,6},{8,7},{9,8},{10,9... | collective-permute-start | bytes 559112 | tf_op jit(solution)/shard_map/ring/ppermute | solution.py:281
  202.1 4.4 %copy.70 = bf16[32,2,128,128]{3,2,1,0:T(8,128)(2,1)} copy(bf16[32,2,128,128]{3,0,1,2:T(8,128)(2,1)} %all-gather.2.cloned.1.call-done) | data formatting | bytes 4194304 | tf_op jit(solution)/shard_map/weights/all_gather | solution.py:232
  206.7 7.1 %map.8 = f32[8,128]{1,0:T(8,128)S(1)} custom-call(s32[3,256]{1,0:T(4,128)S(1)} %pad_add_fusion.plan_ref, s32[17]{0:T(128)S(1)} %broadcast_minimum_fusion.count_ref, bf16[38,104,128]{2,1,0:T(8,128)(2,1)S(1)} %copy-done.5, bf16[38,104,128]{2,1,0:T(8,128)(2,1)S(1)} %copy-done.7, bf16[38,104,128]{2,1,0:T(8,128)(2,1)} %copy-done.20, ...), custom_call_target="tpu_custom_call" | custom-call | tf_op jit(solution)/shard_map/map/pallas_call | solution.py:326
  214.3 7.8 %all-to-all-start.1 = ((f32[16,4,128]{2,1,0:T(4,128)}), f32[16,4,128]{2,1,0:T(4,128)S(1)}, u32[]{:S(2)}, u32[]{:S(2)}) async-start(f32[16,4,128]{2,1,0:T(4,128)} %broadcast_in_dim.212), calls=%async_computation.1 | async-start | bytes 65536 | tf_op jit(solution)/shard_map/finish/all_to_all | solution.py:351
  230.7 3.9 %all-to-all-done.1 = f32[16,4,128]{2,1,0:T(4,128)S(1)} async-done(((f32[16,4,128]{2,1,0:T(4,128)}), f32[16,4,128]{2,1,0:T(4,128)S(1)}, u32[]{:S(2)}, u32[]{:S(2)}) %all-to-all-start.1) | async-done | bytes 32800 | tf_op jit(solution)/shard_map/finish/all_to_all | solution.py:351
  (164 shorter events, 44.5 us)
Async XLA Ops:
  6.5 195.5 %all-gather.2.cloned.1.call-start = ((), (), s32[]{:S(2)}) async-start(), calls=%async_computation.2 | async-start | bytes 2621440 | tf_op jit(solution)/shard_map/weights/all_gather | solution.py:232
  7.7 11.7 %collective-permute-start = (bf16[2,16,4736]{2,1,0:T(8,128)(2,1)S(1)}, bf16[2,16,4736]{2,1,0:T(8,128)(2,1)S(1)}, u32[]{:S(2)}, u32[]{:S(2)}) collective-permute-start(bf16[2,16,4736]{2,1,0:T(8,128)(2,1)S(1)} %get-tuple-element.174), channel_id=1, source_target_pairs={{0,16},{16,32},{32,48},{48,64},{64,80},{80,96},{96,112},{1,17},{17... | collective-permute-start | bytes 909320 | tf_op jit(solution)/shard_map/halo/ppermute | solution.py:22
  9.7 9.8 %collective-permute-start.1 = (bf16[2,16,4736]{2,1,0:T(8,128)(2,1)S(1)}, bf16[2,16,4736]{2,1,0:T(8,128)(2,1)S(1)}, u32[]{:S(2)}, u32[]{:S(2)}) collective-permute-start(bf16[2,16,4736]{2,1,0:T(8,128)(2,1)S(1)} %get-tuple-element.173), channel_id=1, source_target_pairs={{16,0},{32,16},{48,32},{64,48},{80,64},{96,80},{112,96},{17,1},{33... | collective-permute-start | bytes 909320 | tf_op jit(solution)/shard_map/halo/ppermute | solution.py:23
  15.5 47.2 %copy-start.33 = (pred[192]{0:T(512)(128)(4,1)}, pred[192]{0:T(512)(128)(4,1)S(1)}, u32[]{:S(2)}) copy-start(pred[192]{0:T(512)(128)(4,1)S(1)} %fusion.22) | copy-start | bytes 580
  19.5 65.1 %copy-start.22 = (bf16[2,16,4736]{2,1,0:T(8,128)(2,1)}, bf16[2,16,4736]{2,1,0:T(8,128)(2,1)S(1)}, u32[]{:S(2)}) copy-start(bf16[2,16,4736]{2,1,0:T(8,128)(2,1)S(1)} %collective-permute-done.low_ref) | copy-start | bytes 909316
  19.5 65.1 %copy-start.24 = (bf16[2,16,4736]{2,1,0:T(8,128)(2,1)}, bf16[2,16,4736]{2,1,0:T(8,128)(2,1)S(1)}, u32[]{:S(2)}) copy-start(bf16[2,16,4736]{2,1,0:T(8,128)(2,1)S(1)} %collective-permute-done.1.high_ref) | copy-start | bytes 909316
  21.5 63.1 %copy-start.4 = (bf16[38,104,128]{2,1,0:T(8,128)(2,1)}, bf16[38,104,128]{2,1,0:T(8,128)(2,1)S(1)}, u32[]{:S(2)}) copy-start(bf16[38,104,128]{2,1,0:T(8,128)(2,1)S(1)} %get-tuple-element.84.refs_0_) | copy-start | bytes 3035140
  21.5 69.4 %copy-start.26 = (bf16[32,2,32,128]{3,2,1,0:T(8,128)(2,1)S(1)}, bf16[32,2,32,128]{3,2,1,0:T(8,128)(2,1)}, u32[]{:S(2)}) copy-start(bf16[32,2,32,128]{3,2,1,0:T(8,128)(2,1)} %param.14) | copy-start | bytes 1572868
  21.5 32.0 %collective-permute-start.2 = (bf16[38,104,128]{2,1,0:T(8,128)(2,1)S(1)}, bf16[38,104,128]{2,1,0:T(8,128)(2,1)S(1)}, u32[]{:S(2)}, u32[]{:S(2)}) collective-permute-start(bf16[38,104,128]{2,1,0:T(8,128)(2,1)S(1)} %get-tuple-element.85), channel_id=1, source_target_pairs={{0,1},{1,2},{2,3},{3,4},{4,5},{5,6},{6,7},{7,8},{8,9},{9,10},{10,1... | collective-permute-start | bytes 3035144 | tf_op jit(solution)/shard_map/ring/ppermute | solution.py:280
  25.4 30.9 %collective-permute-start.10 = (bf16[38,104,128]{2,1,0:T(8,128)(2,1)S(1)}, bf16[38,104,128]{2,1,0:T(8,128)(2,1)S(1)}, u32[]{:S(2)}, u32[]{:S(2)}) collective-permute-start(bf16[38,104,128]{2,1,0:T(8,128)(2,1)S(1)} %get-tuple-element.86), channel_id=1, source_target_pairs={{0,15},{1,0},{2,1},{3,2},{4,3},{5,4},{6,5},{7,6},{8,7},{9,8},{10,9... | collective-permute-start | bytes 3035144 | tf_op jit(solution)/shard_map/ring/ppermute | solution.py:281
  53.5 29.1 %collective-permute-start.3 = (bf16[38,104,128]{2,1,0:T(8,128)(2,1)S(1)}, bf16[38,104,128]{2,1,0:T(8,128)(2,1)S(1)}, u32[]{:S(2)}, u32[]{:S(2)}) collective-permute-start(bf16[38,104,128]{2,1,0:T(8,128)(2,1)S(1)} %collective-permute-done.2.refs_1_), channel_id=1, source_target_pairs={{0,1},{1,2},{2,3},{3,4},{4,5},{5,6},{6,7},{7,8},{8,9},{9,10},{10,1... | collective-permute-start | bytes 3035144 | tf_op jit(solution)/shard_map/ring/ppermute | solution.py:280
  56.4 34.5 %copy-start.25 = (bf16[38,104,128]{2,1,0:T(8,128)(2,1)}, bf16[38,104,128]{2,1,0:T(8,128)(2,1)S(1)}, u32[]{:S(2)}) copy-start(bf16[38,104,128]{2,1,0:T(8,128)(2,1)S(1)} %collective-permute-done.10.refs_9_) | copy-start | bytes 3035140
  56.4 28.2 %collective-permute-start.11 = (bf16[38,104,128]{2,1,0:T(8,128)(2,1)S(1)}, bf16[38,104,128]{2,1,0:T(8,128)(2,1)S(1)}, u32[]{:S(2)}, u32[]{:S(2)}) collective-permute-start(bf16[38,104,128]{2,1,0:T(8,128)(2,1)S(1)} %collective-permute-done.10.refs_9_), channel_id=1, source_target_pairs={{0,15},{1,0},{2,1},{3,2},{4,3},{5,4},{6,5},{7,6},{8,7},{9,8},{10,9... | collective-permute-start | bytes 3035144 | tf_op jit(solution)/shard_map/ring/ppermute | solution.py:281
  82.6 27.4 %collective-permute-start.4 = (bf16[37,104,128]{2,1,0:T(8,128)(2,1)S(1)}, bf16[37,104,128]{2,1,0:T(8,128)(2,1)S(1)}, u32[]{:S(2)}, u32[]{:S(2)}) collective-permute-start(bf16[37,104,128]{2,1,0:T(8,128)(2,1)S(1)} %slice.97), channel_id=1, source_target_pairs={{0,1},{1,2},{2,3},{3,4},{4,5},{5,6},{6,7},{7,8},{8,9},{9,10},{10,1... | collective-permute-start | bytes 2955272 | tf_op jit(solution)/shard_map/ring/ppermute | solution.py:280
  85.7 27.2 %collective-permute-start.12 = (bf16[37,104,128]{2,1,0:T(8,128)(2,1)}, bf16[37,104,128]{2,1,0:T(8,128)(2,1)S(1)}, u32[]{:S(2)}, u32[]{:S(2)}) collective-permute-start(bf16[37,104,128]{2,1,0:T(8,128)(2,1)} %slice.103), channel_id=1, source_target_pairs={{0,15},{1,0},{2,1},{3,2},{4,3},{5,4},{6,5},{7,6},{8,7},{9,8},{10,9... | collective-permute-start | bytes 2955272 | tf_op jit(solution)/shard_map/ring/ppermute | solution.py:281
  111.0 24.4 %collective-permute-start.5 = (bf16[32,104,128]{2,1,0:T(8,128)(2,1)}, bf16[32,104,128]{2,1,0:T(8,128)(2,1)S(1)}, u32[]{:S(2)}, u32[]{:S(2)}) collective-permute-start(bf16[32,104,128]{2,1,0:T(8,128)(2,1)} %slice.98), channel_id=1, source_target_pairs={{0,1},{1,2},{2,3},{3,4},{4,5},{5,6},{6,7},{7,8},{8,9},{9,10},{10,1... | collective-permute-start | bytes 2555912 | tf_op jit(solution)/shard_map/ring/ppermute | solution.py:280
  113.9 24.3 %collective-permute-start.13 = (bf16[32,104,128]{2,1,0:T(8,128)(2,1)}, bf16[32,104,128]{2,1,0:T(8,128)(2,1)}, u32[]{:S(2)}, u32[]{:S(2)}) collective-permute-start(bf16[32,104,128]{2,1,0:T(8,128)(2,1)} %slice.104), channel_id=1, source_target_pairs={{0,15},{1,0},{2,1},{3,2},{4,3},{5,4},{6,5},{7,6},{8,7},{9,8},{10,9... | collective-permute-start | bytes 2555912 | tf_op jit(solution)/shard_map/ring/ppermute | solution.py:281
  119.7 25.8 %copy-start.27 = (s32[64]{0:T(128)}, s32[64]{0:T(128)S(1)}, u32[]{:S(2)}) copy-start(s32[64]{0:T(128)S(1)} %get-tuple-element.160) | copy-start | bytes 772
  136.3 21.9 %collective-permute-start.6 = (bf16[27,104,128]{2,1,0:T(8,128)(2,1)}, bf16[27,104,128]{2,1,0:T(8,128)(2,1)S(1)}, u32[]{:S(2)}, u32[]{:S(2)}) collective-permute-start(bf16[27,104,128]{2,1,0:T(8,128)(2,1)} %slice.99), channel_id=1, source_target_pairs={{0,1},{1,2},{2,3},{3,4},{4,5},{5,6},{6,7},{7,8},{8,9},{9,10},{10,1... | collective-permute-start | bytes 2156552 | tf_op jit(solution)/shard_map/ring/ppermute | solution.py:280
  140.3 19.9 %collective-permute-start.14 = (bf16[27,104,128]{2,1,0:T(8,128)(2,1)}, bf16[27,104,128]{2,1,0:T(8,128)(2,1)}, u32[]{:S(2)}, u32[]{:S(2)}) collective-permute-start(bf16[27,104,128]{2,1,0:T(8,128)(2,1)} %slice.105), channel_id=1, source_target_pairs={{0,15},{1,0},{2,1},{3,2},{4,3},{5,4},{6,5},{7,6},{8,7},{9,8},{10,9... | collective-permute-start | bytes 2156552 | tf_op jit(solution)/shard_map/ring/ppermute | solution.py:281
  153.2 39.3 %copy-start.13 = (f32[128,128]{1,0:T(8,128)}, f32[128,128]{1,0:T(8,128)S(1)}, u32[]{:S(2)}) copy-start(f32[128,128]{1,0:T(8,128)S(1)} %get-tuple-element.87.refs_20_) | copy-start | bytes 196612
  153.2 39.3 %copy-start.15 = (f32[128,128]{1,0:T(8,128)}, f32[128,128]{1,0:T(8,128)S(1)}, u32[]{:S(2)}) copy-start(f32[128,128]{1,0:T(8,128)S(1)} %get-tuple-element.88.refs_21_) | copy-start | bytes 196612
  153.2 32.3 %copy-start.31 = (s32[2,16]{1,0:T(2,128)S(1)}, s32[2,16]{1,0:T(2,128)}, u32[]{:S(2)}) copy-start(s32[2,16]{1,0:T(2,128)} %get-tuple-element.138) | copy-start | bytes 388
  153.2 33.0 %copy-start.34 = (pred[192]{0:T(512)(128)(4,1)S(1)}, pred[192]{0:T(512)(128)(4,1)}, u32[]{:S(2)}) copy-start(pred[192]{0:T(512)(128)(4,1)} %copy-done.33) | copy-start | bytes 580
  153.2 33.0 %copy-start.36 = (s32[128]{0:T(128)S(1)}, s32[128]{0:T(128)}, u32[]{:S(2)}) copy-start(s32[128]{0:T(128)} %copy-done.35) | copy-start | bytes 1540
  158.2 18.5 %collective-permute-start.7 = (bf16[21,104,128]{2,1,0:T(8,128)(2,1)S(1)}, bf16[21,104,128]{2,1,0:T(8,128)(2,1)S(1)}, u32[]{:S(2)}, u32[]{:S(2)}) collective-permute-start(bf16[21,104,128]{2,1,0:T(8,128)(2,1)S(1)} %slice.100), channel_id=1, source_target_pairs={{0,1},{1,2},{2,3},{3,4},{4,5},{5,6},{6,7},{7,8},{8,9},{9,10},{10,1... | collective-permute-start | bytes 1677320 | tf_op jit(solution)/shard_map/ring/ppermute | solution.py:280
  161.2 18.2 %collective-permute-start.15 = (bf16[21,104,128]{2,1,0:T(8,128)(2,1)S(1)}, bf16[21,104,128]{2,1,0:T(8,128)(2,1)S(1)}, u32[]{:S(2)}, u32[]{:S(2)}) collective-permute-start(bf16[21,104,128]{2,1,0:T(8,128)(2,1)S(1)} %slice.106), channel_id=1, source_target_pairs={{0,15},{1,0},{2,1},{3,2},{4,3},{5,4},{6,5},{7,6},{8,7},{9,8},{10,9... | collective-permute-start | bytes 1677320 | tf_op jit(solution)/shard_map/ring/ppermute | solution.py:281
  177.6 14.2 %collective-permute-start.8 = (bf16[15,104,128]{2,1,0:T(8,128)(2,1)S(1)}, bf16[15,104,128]{2,1,0:T(8,128)(2,1)S(1)}, u32[]{:S(2)}, u32[]{:S(2)}) collective-permute-start(bf16[15,104,128]{2,1,0:T(8,128)(2,1)S(1)} %slice.101), channel_id=1, source_target_pairs={{0,1},{1,2},{2,3},{3,4},{4,5},{5,6},{6,7},{7,8},{8,9},{9,10},{10,1... | collective-permute-start | bytes 1198088 | tf_op jit(solution)/shard_map/ring/ppermute | solution.py:280
  180.4 14.8 %collective-permute-start.16 = (bf16[15,104,128]{2,1,0:T(8,128)(2,1)S(1)}, bf16[15,104,128]{2,1,0:T(8,128)(2,1)S(1)}, u32[]{:S(2)}, u32[]{:S(2)}) collective-permute-start(bf16[15,104,128]{2,1,0:T(8,128)(2,1)S(1)} %slice.107), channel_id=1, source_target_pairs={{0,15},{1,0},{2,1},{3,2},{4,3},{5,4},{6,5},{7,6},{8,7},{9,8},{10,9... | collective-permute-start | bytes 1198088 | tf_op jit(solution)/shard_map/ring/ppermute | solution.py:281
  193.3 13.3 %collective-permute-start.9 = (bf16[7,104,128]{2,1,0:T(8,128)(2,1)}, bf16[7,104,128]{2,1,0:T(8,128)(2,1)}, u32[]{:S(2)}, u32[]{:S(2)}) collective-permute-start(bf16[7,104,128]{2,1,0:T(8,128)(2,1)} %slice.102), channel_id=1, source_target_pairs={{0,1},{1,2},{2,3},{3,4},{4,5},{5,6},{6,7},{7,8},{8,9},{9,10},{10,1... | collective-permute-start | bytes 559112 | tf_op jit(solution)/shard_map/ring/ppermute | solution.py:280
  196.7 9.9 %collective-permute-start.17 = (bf16[7,104,128]{2,1,0:T(8,128)(2,1)}, bf16[7,104,128]{2,1,0:T(8,128)(2,1)}, u32[]{:S(2)}, u32[]{:S(2)}) collective-permute-start(bf16[7,104,128]{2,1,0:T(8,128)(2,1)} %slice.108), channel_id=1, source_target_pairs={{0,15},{1,0},{2,1},{3,2},{4,3},{5,4},{6,5},{7,6},{8,7},{9,8},{10,9... | collective-permute-start | bytes 559112 | tf_op jit(solution)/shard_map/ring/ppermute | solution.py:281
  214.3 20.3 %all-to-all-start.1 = ((f32[16,4,128]{2,1,0:T(4,128)}), f32[16,4,128]{2,1,0:T(4,128)S(1)}, u32[]{:S(2)}, u32[]{:S(2)}) async-start(f32[16,4,128]{2,1,0:T(4,128)} %broadcast_in_dim.212), calls=%async_computation.1 | async-start | bytes 65536 | tf_op jit(solution)/shard_map/finish/all_to_all | solution.py:351
  (22 other events, 130.1 us)
Sparse Core Ops, SparseCore 0:
  92.2 37.5 all-gather.1

commit v2 on v1

--- a/solution.py
+++ b/solution.py
@@ -11,7 +11,7 @@
 K = 2
 W = 16
 ROWS = 104
-PROFILE = (37, 37, 36, 31, 26, 20, 14, 6)
+SLOTS = 21
 TINY = 1.2e-38
 
 
@@ -37,25 +37,183 @@
 def ways(distance, block, vocab_count):
     half = vocab_count // 2
     even = block % 2 == 0
-    ahead = jnp.where(((distance >= 1) & (distance < half)) | ((distance == half) & even), distance, 0)
+    ahead = jnp.where((distance >= 1) & ((distance < half) | ((distance == half) & even)), distance, 0)
     behind = jnp.where((distance > half) | ((distance == half) & ~even), vocab_count - distance, 0)
     return ahead, behind
 
 
-def reaches(need, block, holder, sign, vocab_count):
-    targets = jnp.arange(vocab_count)[:, None]
-    distance = (sign * (targets - holder[None, :]) + vocab_count) % vocab_count
-    ahead, behind = ways(distance, block[None, :], vocab_count)
-    return jnp.max(jnp.where(need, ahead, 0), axis=0), jnp.max(jnp.where(need, behind, 0), axis=0)
-
-
-def ranks(reach):
-    size = reach.shape[-1]
-    key = reach * size - jnp.arange(size)
-    return jnp.sum((key[..., None, :] > key[..., :, None]).astype(jnp.int32), axis=-1)
-
-
-def pack_kernel(order_ref, own_ref, low_ref, high_ref, pick_ref, ahead_ref, behind_ref, home_ref, cand_ref, logit_ref):
+def ones(mask):
+    return jnp.where(mask, 1.0, 0.0).astype(jnp.bfloat16)
+
+
+def plan_kernel(blocks, place_ref, holder_ref, holders_ref, inners_ref, send_ref, item_ref, fit_ref, book_ref):
+    vocab_count, pair_count = holder_ref.shape
+    half = vocab_count // 2
+    steps = half
+    home = blocks + 1
+    me, sign = place_ref[0], place_ref[1]
+    f32, i32 = jnp.float32, jnp.int32
+    shape = (vocab_count, BLK)
+    lane = lax.broadcasted_iota(i32, shape, 1)
+    row = lax.broadcasted_iota(i32, shape, 0)
+
+    reach = [jnp.zeros(shape, i32), jnp.zeros(shape, i32)]
+    pair_lane = lax.broadcasted_iota(i32, (pair_count, BLK), 1)
+    pair_row = lax.broadcasted_iota(i32, (vocab_count, pair_count), 0)
+    for s in range(vocab_count):
+        hits = jnp.dot(
+            ones(pair_row == holder_ref[s : s + 1, :]),
+            ones(pair_lane == inners_ref[:, s : s + 1]),
+            preferred_element_type=f32,
+        )
+        distance = s - row
+        distance = jnp.where(distance < 0, distance + vocab_count, distance)
+        for way, length in enumerate(ways(distance, lane, vocab_count)):
+            reach[way] = jnp.maximum(reach[way], jnp.where(hits > 0, length, 0))
+    reach = [jnp.where(lane == blocks, half - way, reach[way]) for way in range(2)]
+
+    square = (BLK, BLK)
+    up, across = lax.broadcasted_iota(i32, square, 0), lax.broadcasted_iota(i32, square, 1)
+    earlier = ones(up < across)
+    left_up, left_across = (up & 7) + 1 - (up >> 3), (across & 7) + 1 - (across >> 3)
+    goes_first = ones(
+        (left_up > left_across) | ((left_up == left_across) & ((up >> 3) > (across >> 3)))
+    )
+    index, waiting, moved = [], [], [jnp.zeros(shape, f32)] * 2
+    for way in range(2):
+        masks = jnp.concatenate([ones(reach[way] == r) for r in range(1, half + 1)], axis=0)
+        before = jnp.dot(masks, earlier, preferred_element_type=f32)
+        place = jnp.zeros(shape, f32)
+        count = jnp.zeros(shape, f32)
+        for r in range(1, half + 1):
+            same = reach[way] == r
+            place = jnp.where(same, before[(r - 1) * vocab_count : r * vocab_count], place)
+            total = jnp.sum(jnp.where(same, 1.0, 0.0), axis=1, keepdims=True)
+            count = jnp.where(lane == r - 1, total, count)
+        index.append(place)
+        waiting.append(count)
+    travels = (lane >= 8) & (lane < 8 * half) & ((lane & 7) + 1 > (lane >> 3))
+    for f in range(steps):
+        ahead_of = jnp.dot(
+            jnp.concatenate(waiting, axis=0).astype(jnp.bfloat16), goes_first, preferred_element_type=f32
+        )
+        for way in range(2):
+            first = ahead_of[way * vocab_count : (way + 1) * vocab_count]
+            go = jnp.clip(SLOTS - first, 0.0, waiting[way])
+            book_ref[(f * 2 + way) * 3] = moved[way]
+            moved[way] = moved[way] + go
+            book_ref[(f * 2 + way) * 3 + 1] = moved[way]
+            book_ref[(f * 2 + way) * 3 + 2] = jnp.minimum(first, float(SLOTS))
+            come = pltpu.roll(pltpu.roll(go, 8, 1), 1 if way == 0 else vocab_count - 1, 0)
+            waiting[way] = waiting[way] - go + jnp.where(travels, come, 0.0)
+    left = jnp.sum(waiting[0] + waiting[1], axis=1, keepdims=True)
+    left = jnp.sum(jnp.broadcast_to(left, shape), axis=0, keepdims=True)
+    fit_ref[...] = jnp.broadcast_to(left, fit_ref.shape).astype(i32)
+
+    small = (vocab_count, vocab_count)
+    target = lax.broadcasted_iota(i32, (BLK, 2 * BLK), 1).astype(f32)
+    pointer, sends = [], []
+    for way in range(2):
+        step = 1 if way == 0 else -1
+        back = me - step * lax.broadcasted_iota(i32, small, 0)
+        back = jnp.where(back < 0, back + vocab_count, jnp.where(back >= vocab_count, back - vocab_count, back))
+        pick = ones(back == lax.broadcasted_iota(i32, small, 1))
+        far = jnp.dot(pick, reach[way].astype(f32).astype(jnp.bfloat16), preferred_element_type=f32).astype(i32)
+        order = jnp.dot(pick, index[way].astype(jnp.bfloat16), preferred_element_type=f32)
+        giver = me - step
+        giver = jnp.where(giver < 0, giver + vocab_count, jnp.where(giver >= vocab_count, giver - vocab_count, giver))
+
+        def slot(at, hops, valid):
+            column = jnp.clip(hops * 8 + far - 1, 0, BLK - 1)
+            where = jnp.full(shape, -1.0, f32)
+            for f in range(steps):
+                start, end, first = (
+                    jnp.take_along_axis(
+                        jnp.broadcast_to(book_ref[(f * 2 + way) * 3 + kind, pl.ds(at, 1), :], shape),
+                        column,
+                        axis=1,
+                        mode="promise_in_bounds",
+                    )
+                    for kind in range(3)
+                )
+                now = valid & (start <= order) & (order < end)
+                where = jnp.where(now, f * SLOTS + first + order - start, where)
+            return where
+
+        leave = slot(me, row, (far > row) & (row < half))
+        arrive = slot(giver, row - 1, (far >= row) & (row >= 1) & (row <= half))
+        point = jnp.where(row == 0, lane.astype(f32), jnp.maximum(home + arrive, 0.0))
+        pointer.append(point)
+        leave_turned = jnp.concatenate([leave, jnp.full((BLK - vocab_count, BLK), -1.0, f32)], axis=0).T
+        chosen = jnp.zeros((1, 2 * BLK), f32)
+        for h in range(half):
+            chosen = chosen + jnp.dot(
+                point[h : h + 1].astype(jnp.bfloat16),
+                ones(leave_turned[:, h : h + 1] == target),
+                preferred_element_type=f32,
+            )
+        sends.append(chosen.astype(i32))
+    straight = sign > 0
+    send_ref[0:1, :] = jnp.where(straight, sends[0], sends[1])
+    send_ref[1:2, :] = jnp.where(straight, sends[1], sends[0])
+    send_ref[2:8, :] = jnp.zeros((6, 2 * BLK), i32)
+
+    mine_lane = lax.broadcasted_iota(i32, (pair_count, vocab_count), 1)
+    holder = jnp.sum(jnp.where(mine_lane == me, holders_ref[...], 0), axis=1, keepdims=True)
+    inner = jnp.sum(jnp.where(mine_lane == me, inners_ref[...], 0), axis=1, keepdims=True)
+    distance = me - holder
+    distance = jnp.where(distance < 0, distance + vocab_count, distance)
+    hops = ways(distance, inner, vocab_count)
+    scale = jnp.where(distance <= half, distance, 2 * vocab_count - distance)
+    points = jnp.zeros((pair_count, 1), f32)
+    for way in range(2):
+        found = lax.dot_general(
+            ones(pair_lane == inner),
+            pointer[way].astype(jnp.bfloat16),
+            (((1,), (1,)), ((), ())),
+            preferred_element_type=f32,
+        )
+        points = points + jnp.sum(
+            jnp.where((mine_lane == hops[way]) & (hops[way] > 0), found, 0.0), axis=1, keepdims=True
+        )
+    points = jnp.where(distance == 0, inner.astype(f32), points)
+    by_stats = [jnp.sum(jnp.where(lane == blocks, p, 0.0), axis=1, keepdims=True) for p in pointer]
+    hop = lax.broadcasted_iota(i32, (vocab_count, 1), 0)
+    stat_ok = [hop <= half, (hop >= 1) & (hop < half)]
+    points = jnp.concatenate(
+        [points] + [jnp.where(ok, p, 0.0) for ok, p in zip(stat_ok, by_stats)], axis=0
+    ).astype(i32)
+    other = jnp.concatenate(
+        [(hops[1] > 0).astype(i32), jnp.zeros((vocab_count, 1), i32), jnp.ones((vocab_count, 1), i32)], axis=0
+    )
+    other = jnp.where(straight, other, 1 - other)
+    scale = jnp.concatenate([scale, jnp.zeros((2 * vocab_count, 1), i32)], axis=0)
+    frame = jnp.zeros(points.shape, i32)
+    for f in range(1, steps):
+        frame = frame + (points >= home + f * SLOTS).astype(i32)
+    away = points >= home
+    source = jnp.where(away, 1 + frame + steps * other, 0)
+    spot = jnp.where(away, points - home - frame * SLOTS, points)
+    spot = jnp.clip(spot, 0, jnp.where(away, SLOTS - 1, home - 1))
+    items = points.shape[0]
+    item_lane = lax.broadcasted_iota(i32, (items, BLK), 1)
+    table = jnp.where(
+        item_lane == 0, spot, jnp.where(item_lane == 1, scale, jnp.where(item_lane == 2, source, 0))
+    ).astype(f32)
+    turned = jnp.concatenate([table, jnp.zeros((BLK - items, BLK), f32)], axis=0).T
+    source_row = turned[2:3].astype(i32)
+    item_up = lax.broadcasted_iota(i32, (items, BLK), 0)
+    is_item = item_lane < items
+    sooner = is_item & ((source_row < source) | ((source_row == source) & (item_lane < item_up)))
+    rank = jnp.sum(sooner.astype(i32), axis=1, keepdims=True)
+    item_ref[0:1, :] = turned[0:1].astype(i32)
+    item_ref[1:2, :] = turned[1:2].astype(i32)
+    item_ref[2:3, :] = jnp.sum(jnp.where(rank == item_lane, item_up, 0), axis=0, keepdims=True)
+    item_ref[3:4, :] = jnp.sum((source < item_lane).astype(i32), axis=0, keepdims=True)
+    item_ref[4:8, :] = jnp.zeros((4, BLK), i32)
+
+
+def pack_kernel(send_ref, own_ref, low_ref, high_ref, pick_ref, home_ref, first_ref, second_ref, cand_ref, logit_ref):
     docs, positions, columns = own_ref.shape
     width = low_ref.shape[1]
     span = positions + 2 * width
@@ -76,21 +234,41 @@
     for t in range(blocks):
         power = jnp.exp(logit_ref[t].astype(jnp.float32) - top)
         total = total + power
-        home_ref[1 + t] = power.astype(jnp.bfloat16)
+        home_ref[t] = power.astype(jnp.bfloat16)
     total = jnp.sum(total, axis=1, keepdims=True)
     first = total.astype(jnp.bfloat16).astype(jnp.float32)
     second = (total - first).astype(jnp.bfloat16).astype(jnp.float32)
     third = total - first - second
     lane = lax.broadcasted_iota(jnp.int32, (rows, BLK), 1)
-    stats = jnp.where(
+    home_ref[blocks] = jnp.where(
         lane == 0, top, jnp.where(lane == 1, first, jnp.where(lane == 2, second, jnp.where(lane == 3, third, 0.0)))
     ).astype(jnp.bfloat16)
-    home_ref[0] = stats
-    ahead_ref[0] = stats
-    behind_ref[0] = stats
-    for i in range(ahead_ref.shape[0] - 1):
-        ahead_ref[1 + i] = home_ref[1 + order_ref[0, i]]
-        behind_ref[1 + i] = home_ref[1 + order_ref[1, i]]
+    for j in range(SLOTS):
+        first_ref[j] = home_ref[send_ref[0, j]]
+        second_ref[j] = home_ref[send_ref[1, j]]
+
+
+def pass_kernel(chain, step, send_ref, home_ref, *refs):
+    frames, out_ref = refs[:-1], refs[-1]
+    home = home_ref.shape[0]
+
+    def choose(j, carry):
+        at = send_ref[chain, step * SLOTS + j]
+
+        @pl.when(at < home)
+        def _():
+            out_ref[j] = home_ref[at]
+
+        for f, frame in enumerate(frames):
+            start = home + f * SLOTS
+
+            @pl.when((at >= start) & (at < start + SLOTS))
+            def _(frame=frame, start=start):
+                out_ref[j] = frame[at - start]
+
+        return carry
+
+    lax.fori_loop(0, SLOTS, choose, 0)
 
 
 def student_kernel(student_ref, top_ref, total_ref):
@@ -109,7 +287,7 @@
     total_ref[...] = jnp.broadcast_to(jnp.sum(total, axis=1, keepdims=True), (rows, BLK))
 
 
-def map_kernel(steps, plan_ref, count_ref, *refs):
+def map_kernel(steps, item_ref, *refs):
     sources = refs[: 2 * steps + 1]
     spread_ref, weight_ref, student_ref, top_ref, total_ref, out_ref, stage_ref, scale_ref = refs[2 * steps + 1 :]
     docs, positions, columns = student_ref.shape
@@ -118,32 +296,33 @@
     spread = spread_ref[...]
     for s, source in enumerate(sources):
 
-        def bring(j, carry, s=s, source=source):
-            pair = plan_ref[2, s * 8 + j]
-            stage_ref[pair] = source[1 + plan_ref[0, pair]]
+        def bring(q, carry, source=source):
+            item = item_ref[2, q]
+            stage_ref[item] = source[item_ref[0, item]]
             return carry
 
-        lax.fori_loop(0, count_ref[s], bring, 0)
+        lax.fori_loop(item_ref[3, s], item_ref[3, s + 1], bring, 0)
+    holders = [h for h in range(steps + 1)] + [2 * steps + h for h in range(1, steps)]
     peaks, sums = [], []
-    for source in sources:
-        stats = jnp.dot(spread, source[0], preferred_element_type=jnp.float32)
+    for h in holders:
+        stats = jnp.dot(spread, stage_ref[K * blocks + h], preferred_element_type=jnp.float32)
         peaks.append(stats[:, 0:1])
         sums.append(stats[:, 1:2] + stats[:, 2:3] + stats[:, 3:4])
     peak = functools.reduce(jnp.maximum, peaks)
     powers = [jnp.exp(p - peak) for p in peaks]
-    norm = sum(p * t for p, t in zip(powers[: 2 * steps], sums[: 2 * steps]))
-    for s in range(len(sources)):
-        scale_ref[s] = jnp.broadcast_to(powers[s] / norm, (rows, BLK))
+    norm = sum(p * t for p, t in zip(powers, sums))
+    for h, power in zip(holders, powers):
+        scale_ref[h] = jnp.broadcast_to(power / norm, (rows, BLK))
     student_top = top_ref[...]
     mass = jnp.zeros((rows, BLK), jnp.float32)
     cross = jnp.zeros((rows, BLK), jnp.float32)
     for b in range(blocks):
         picked = jnp.concatenate([stage_ref[K * b], stage_ref[K * b + 1]], axis=1)
         prob = jnp.dot(spread, picked, preferred_element_type=jnp.float32).astype(jnp.bfloat16)
-        mapped = scale_ref[plan_ref[1, K * b]] * jnp.dot(
-            prob[:, :BLK], weight_ref[K * b], preferred_element_type=jnp.float32
-        ) + scale_ref[plan_ref[1, K * b + 1]] * jnp.dot(
-            prob[:, BLK:], weight_ref[K * b + 1], preferred_element_type=jnp.float32
+        mapped = scale_ref[item_ref[1, K * b]] * jnp.dot(
+            prob[:, :BLK], weight_ref[:, K * b].reshape(BLK, BLK), preferred_element_type=jnp.float32
+        ) + scale_ref[item_ref[1, K * b + 1]] * jnp.dot(
+            prob[:, BLK:], weight_ref[:, K * b + 1].reshape(BLK, BLK), preferred_element_type=jnp.float32
         )
         logit = student_ref[:, :, b * BLK : (b + 1) * BLK].reshape(rows, BLK).astype(jnp.float32) - student_top
         mass = mass + mapped
@@ -201,6 +380,7 @@
     gathered = jnp.take(incoming.reshape(row_count, vocab_count * capacity, BLK), recv_slot, axis=1).reshape(
         row_count, student_blocks, K, BLK
     )
+    weights = weights.swapaxes(0, 1).reshape(student_blocks, K, BLK, BLK)
     mapped = jnp.einsum("rbkc,bkcd->rbd", gathered, weights, preferred_element_type=jnp.float32).reshape(
         row_count, student_cols
     )
@@ -220,7 +400,7 @@
     pair_count = student_blocks * K
     vocab_count = lax.axis_size("vocab")
     steps = vocab_count // 2
-    sizes = tuple(min(size, teacher_blocks) for size in PROFILE)
+    home = teacher_blocks + 1
     vocab_index = lax.axis_index("vocab")
     seq_index = lax.axis_index("seq")
     sign = 1 - 2 * (seq_index % 2)
@@ -229,7 +409,9 @@
     with jax.named_scope("halo"):
         low, high = halo(teacher_logits, W)
     with jax.named_scope("weights"):
-        weights = lax.all_gather(margin_weight, "dp", axis=2, tiled=True)
+        weights = lax.all_gather(
+            margin_weight.reshape(pair_count, -1, BLK), "dp", axis=0, tiled=False
+        )
 
     with jax.named_scope("rows"):
         cand = (alignment - seq_index * pos_count + W + jnp.arange(doc_count)[:, None] * span).reshape(-1)
@@ -243,44 +425,59 @@
         spread = (cand_rank[:, None] == row_ids[None, :]).astype(jnp.bfloat16)
         rows_fit = jnp.sum(used.astype(jnp.int32)) <= ROWS
 
-    with jax.named_scope("send_order"):
-        listed = src_block.reshape(vocab_count, pair_count)
-        inner = jnp.arange(teacher_blocks)
-        own_blocks = vocab_index * teacher_blocks + inner
-        own_need = jnp.any(listed[:, :, None] == own_blocks[None, None, :], axis=1)
-        own_reach = jnp.stack(
-            reaches(own_need, own_blocks, jnp.full((teacher_blocks,), vocab_index), sign, vocab_count)
-        )
-        own_rank = ranks(own_reach)
-        order = jnp.sum(
-            jnp.where(own_rank[:, None, :] == inner[None, :, None], inner[None, None, :], 0), axis=2
-        ).astype(jnp.int32)
-
     vmem = pl.BlockSpec(memory_space=pltpu.VMEM)
     smem = pl.BlockSpec(memory_space=pltpu.SMEM)
-    big = pltpu.CompilerParams(vmem_limit_bytes=44 * 1024 * 1024)
-    buffer = jax.ShapeDtypeStruct((1 + sizes[0], ROWS, BLK), jnp.bfloat16)
+    def room(mib):
+        return pltpu.CompilerParams(vmem_limit_bytes=mib * 1024 * 1024)
+
+    with jax.named_scope("plan"):
+        listed = src_block.reshape(vocab_count, pair_count)
+        holder, inner = listed // teacher_blocks, listed % teacher_blocks
+        table = jax.ShapeDtypeStruct((8, BLK), jnp.int32)
+        send, items, left = pl.pallas_call(
+            functools.partial(plan_kernel, teacher_blocks),
+            out_shape=(jax.ShapeDtypeStruct((8, 2 * BLK), jnp.int32), table, table),
+            in_specs=[smem] + [vmem] * 3,
+            out_specs=(vmem,) * 3,
+            scratch_shapes=[pltpu.VMEM((6 * steps, vocab_count, BLK), jnp.float32)],
+            compiler_params=room(16),
+        )(jnp.stack([vocab_index, sign]).astype(jnp.int32), holder, holder.T, inner.T)
+
+    def planes(count):
+        return jax.ShapeDtypeStruct((count, ROWS, BLK), jnp.bfloat16)
+
     with jax.named_scope("pack"):
-        ahead, behind, home = pl.pallas_call(
+        own, ahead, behind = pl.pallas_call(
             pack_kernel,
-            out_shape=(buffer, buffer, jax.ShapeDtypeStruct((1 + teacher_blocks, ROWS, BLK), jnp.bfloat16)),
+            out_shape=(planes(home), planes(SLOTS), planes(SLOTS)),
             in_specs=[smem] + [vmem] * 4,
             out_specs=(vmem,) * 3,
             scratch_shapes=[
                 pltpu.VMEM((doc_count * span, teacher_cols), jnp.bfloat16),
                 pltpu.VMEM((teacher_blocks, ROWS, BLK), jnp.bfloat16),
             ],
-            compiler_params=big,
-        )(order, teacher_logits, low, high, pick)
+            compiler_params=room(24),
+        )(send, teacher_logits, low, high, pick)
+
+    def chosen(chain, step, frames):
+        return pl.pallas_call(
+            functools.partial(pass_kernel, chain, step),
+            out_shape=planes(SLOTS),
+            in_specs=[smem] + [vmem] * (1 + len(frames)),
+            out_specs=vmem,
+            compiler_params=room(16),
+        )(send, own, *frames)
 
     with jax.named_scope("ring"):
         forward, backward = ring_pairs(1), ring_pairs(-1)
         came_ahead, came_behind = [], []
-        for size in sizes:
-            ahead = lax.ppermute(ahead[: 1 + size], ("seq", "vocab"), forward)
-            behind = lax.ppermute(behind[: 1 + size], ("seq", "vocab"), backward)
-            came_ahead.append(ahead)
-            came_behind.append(behind)
+        for step in range(steps):
+            if step:
+                ahead = chosen(0, step, came_ahead)
+            came_ahead.append(lax.ppermute(ahead, ("seq", "vocab"), forward))
+            if step:
+                behind = chosen(1, step, came_behind)
+            came_behind.append(lax.ppermute(behind, ("seq", "vocab"), backward))
 
     with jax.named_scope("student"):
         top, total = pl.pallas_call(
@@ -288,63 +485,21 @@
             out_shape=(jax.ShapeDtypeStruct((row_count, BLK), jnp.float32),) * 2,
             in_specs=[vmem],
             out_specs=(vmem,) * 2,
-            compiler_params=big,
+            compiler_params=room(16),
         )(student_logits)
-
-    with jax.named_scope("receive_plan"):
-        blocks = jnp.arange(vocab_count * teacher_blocks)
-        block_holder = blocks // teacher_blocks
-        need = jnp.any(listed[:, :, None] == blocks[None, None, :], axis=1)
-        reach = jnp.stack(reaches(need, blocks, block_holder, sign, vocab_count)).reshape(
-            2, vocab_count, teacher_blocks
-        )
-        fits = jnp.all(
-            jnp.stack([jnp.sum((reach >= k + 1).astype(jnp.int32), axis=2) <= size for k, size in enumerate(sizes)])
-        )
-        all_rank = ranks(reach).reshape(2, 1, -1)
-        mine = lax.dynamic_index_in_dim(listed, vocab_index, 0, keepdims=False)
-        at_block = mine[:, None] == blocks[None, :]
-        rank_of = jnp.sum(jnp.where(at_block[None], all_rank, 0), axis=2)
-        distance = (sign * (vocab_index - mine // teacher_blocks) + vocab_count) % vocab_count
-        go_ahead, go_behind = ways(distance, mine, vocab_count)
-        source = jnp.where(go_ahead > 0, go_ahead, jnp.where(go_behind > 0, steps + go_behind, 0))
-        limits = jnp.array((teacher_blocks,) + sizes + sizes, jnp.int32)
-        source_ids = jnp.arange(2 * steps + 1)
-        at_source = source[:, None] == source_ids[None, :]
-        limit = jnp.sum(jnp.where(at_source, limits[None, :], 0), axis=1)
-        place = jnp.where(go_ahead > 0, rank_of[0], jnp.where(go_behind > 0, rank_of[1], mine % teacher_blocks))
-        place = jnp.clip(place, 0, limit - 1)
-        pairs = jnp.arange(pair_count)
-        turn = jnp.sum((source[:, None] == source[None, :]) & (pairs[None, :] < pairs[:, None]), axis=1)
-        slots = jnp.arange((2 * steps + 1) * 8)
-        pair_list = jnp.sum(jnp.where((source * 8 + turn)[None, :] == slots[:, None], pairs[None, :], 0), axis=1)
-        count = jnp.minimum(jnp.sum(at_source.astype(jnp.int32), axis=0), 8).astype(jnp.int32)
-        pad = lambda values: jnp.pad(values, (0, 256 - values.shape[0]))
-        plan = jnp.stack([pad(place), pad(source), pad(pair_list)]).astype(jnp.int32)
 
     with jax.named_scope("map"):
         held = pl.pallas_call(
             functools.partial(map_kernel, steps),
             out_shape=jax.ShapeDtypeStruct((8, row_count), jnp.float32),
-            in_specs=[smem] * 2 + [vmem] * (2 * steps + 1 + 5),
+            in_specs=[smem] + [vmem] * (2 * steps + 1 + 5),
             out_specs=vmem,
             scratch_shapes=[
-                pltpu.VMEM((pair_count, ROWS, BLK), jnp.bfloat16),
-                pltpu.VMEM((2 * steps + 1, row_count, BLK), jnp.float32),
+                pltpu.VMEM((pair_count + 2 * vocab_count, ROWS, BLK), jnp.bfloat16),
+                pltpu.VMEM((3 * steps, row_count, BLK), jnp.float32),
             ],
-            compiler_params=big,
-        )(
-            plan,
-            count,
-            home,
-            *came_ahead,
-            *came_behind,
-            spread,
-            weights.reshape(pair_count, BLK, BLK),
-            student_logits,
-            top,
-            total,
-        )
+            compiler_params=room(32),
+        )(items, own, *came_ahead, *came_behind, spread, weights, student_logits, top, total)
 
     with jax.named_scope("finish"):
         sent = jnp.broadcast_to(held[None, :4], (vocab_count, 4, row_count))
@@ -356,7 +511,7 @@
         result = jnp.sum(cross_part + mass_part * (log_total - top_part), axis=0) / mass - jnp.log(mass)
 
     result = lax.cond(
-        rows_fit & fits,
+        rows_fit & (left[0, 0] == 0),
         lambda *_: result,
         lambda *operands: whole(operands[:3], *operands[3:]),
         low,

time: 245 us -> 229 us (0.935)
  the two profiles are of different devices: /device:TPU:6 before, /device:TPU:26 now
where the time goes in v2:
time: 229 us; the launch traced here: 228 us
  starting transfers between devices  82.7 us (36%)
  waiting for transfers between devices  71.1 us (31%)
  Pallas kernels  43.1 us (19%)
  between operations  15.2 us (7%)
  local copies, waits for them, and re-layouts  13 us (6%)
  other arithmetic  2.77 us (1%)
    ppermute x8, waiting for transfers between devices, shards(): came_behind.append(lax.ppermute(behind, ('seq', 'vocab'), backward))  52.3 us
    ppermute x8, starting transfers between devices, shards(): came_behind.append(lax.ppermute(behind, ('seq', 'vocab'), backward))  50.7 us
    pallas_call x14, Pallas kernels, chosen(): pl.pallas_call(functools.partial(pass_kernel, chain, step), out_shape=pla...  30 us
    ppermute x8, starting transfers between devices, shards(): came_ahead.append(lax.ppermute(ahead, ('seq', 'vocab'), forward))  15.3 us
    all_to_all x1, starting transfers between devices, shards(): lax.all_to_all(sent, 'vocab', split_axis=0, concat_axis=0, tiled=True)  11.1 us
    all_to_all x1, waiting for transfers between devices, shards(): lax.all_to_all(sent, 'vocab', split_axis=0, concat_axis=0, tiled=True)  10.1 us
    unnamed x46, local copies, waits for them, and re-layouts  9.05 us
    ppermute x8, waiting for transfers between devices, shards(): came_ahead.append(lax.ppermute(ahead, ('seq', 'vocab'), forward))  8.67 us
  transfers between devices with their start and end apart: 20, of which 10 were waited for; matrix products, arithmetic and copies ran while one was open for 2% of the time, Pallas kernels for 15%

profile of v2, /device:TPU:26, one launch (start us, length us, event | category | flops | bytes accessed | tf_op | source)
XLA Modules:
  0.0 227.9 jit_solution(3374097911524799938)
XLA Ops:
  9.7 3.6 %collective-permute-start.1 = (bf16[2,16,4736]{2,1,0:T(8,128)(2,1)S(1)}, bf16[2,16,4736]{2,1,0:T(8,128)(2,1)S(1)}, u32[]{:S(2)}, u32[]{:S(2)}) collective-permute-start(bf16[2,16,4736]{2,1,0:T(8,128)(2,1)S(1)} %get-tuple-element.153), channel_id=1, source_target_pairs={{16,0},{32,16},{48,32},{64,48},{80,64},{96,80},{112,96},{17,1},{33... | collective-permute-start | bytes 909320 | tf_op jit(solution)/shard_map/halo/ppermute | solution.py:23
  16.5 3.7 %plan.1 = (s32[8,256]{1,0:T(8,128)S(1)}, s32[8,128]{1,0:T(8,128)S(1)}, s32[8,128]{1,0:T(8,128)S(1)}) custom-call(s32[2]{0:T(128)S(1)} %pad_add_fusion.place_ref, s32[16,64]{1,0:T(8,128)S(1)} %copy.72.holder_ref, s32[64,16]{1,0:T(8,128)S(1)} %bitcast.73, s32[64,16]{1,0:T(8,128)S(1)} %get-tuple-element.155.inners_ref), custom_call_target="tpu_custom_call" | custom-call | tf_op jit(solution)/shard_map/plan/pallas_call | solution.py:437
  20.5 2.0 pack.1
  22.5 11.4 %collective-permute-start.10 = (bf16[21,104,128]{2,1,0:T(8,128)(2,1)S(1)}, bf16[21,104,128]{2,1,0:T(8,128)(2,1)S(1)}, u32[]{:S(2)}, u32[]{:S(2)}) collective-permute-start(bf16[21,104,128]{2,1,0:T(8,128)(2,1)S(1)} %get-tuple-element.92), channel_id=1, source_target_pairs={{0,15},{1,0},{2,1},{3,2},{4,3},{5,4},{6,5},{7,6},{8,7},{9,8},{10,9... | collective-permute-start | bytes 1677320 | tf_op jit(solution)/shard_map/ring/ppermute | solution.py:480
  35.8 10.3 %collective-permute-done.10.refs_0_.refs_9_ = bf16[21,104,128]{2,1,0:T(8,128)(2,1)S(1)} collective-permute-done((bf16[21,104,128]{2,1,0:T(8,128)(2,1)S(1)}, bf16[21,104,128]{2,1,0:T(8,128)(2,1)S(1)}, u32[]{:S(2)}, u32[]{:S(2)}) %collective-permute-start.10) | collective-permute-done | bytes 559136 | tf_op jit(solution)/shard_map/ring/ppermute | solution.py:480
  47.3 5.6 %collective-permute-start.11 = (bf16[21,104,128]{2,1,0:T(8,128)(2,1)S(1)}, bf16[21,104,128]{2,1,0:T(8,128)(2,1)S(1)}, u32[]{:S(2)}, u32[]{:S(2)}) collective-permute-start(bf16[21,104,128]{2,1,0:T(8,128)(2,1)S(1)} %ring.21), channel_id=1, source_target_pairs={{0,15},{1,0},{2,1},{3,2},{4,3},{5,4},{6,5},{7,6},{8,7},{9,8},{10,9... | collective-permute-start | bytes 1677320 | tf_op jit(solution)/shard_map/ring/ppermute | solution.py:480
  56.0 9.6 %collective-permute-done.11.refs_1_.refs_10_ = bf16[21,104,128]{2,1,0:T(8,128)(2,1)S(1)} collective-permute-done((bf16[21,104,128]{2,1,0:T(8,128)(2,1)S(1)}, bf16[21,104,128]{2,1,0:T(8,128)(2,1)S(1)}, u32[]{:S(2)}, u32[]{:S(2)}) %collective-permute-start.11) | collective-permute-done | bytes 559136 | tf_op jit(solution)/shard_map/ring/ppermute | solution.py:480
  65.6 2.1 ring.22
  67.7 5.6 %collective-permute-start.12 = (bf16[21,104,128]{2,1,0:T(8,128)(2,1)}, bf16[21,104,128]{2,1,0:T(8,128)(2,1)}, u32[]{:S(2)}, u32[]{:S(2)}) collective-permute-start(bf16[21,104,128]{2,1,0:T(8,128)(2,1)} %ring.22), channel_id=1, source_target_pairs={{0,15},{1,0},{2,1},{3,2},{4,3},{5,4},{6,5},{7,6},{8,7},{9,8},{10,9... | collective-permute-start | bytes 1677320 | tf_op jit(solution)/shard_map/ring/ppermute | solution.py:480
  73.3 2.1 ring.15
  77.4 8.2 %collective-permute-done.12.refs_2_.refs_11_ = bf16[21,104,128]{2,1,0:T(8,128)(2,1)} collective-permute-done((bf16[21,104,128]{2,1,0:T(8,128)(2,1)}, bf16[21,104,128]{2,1,0:T(8,128)(2,1)}, u32[]{:S(2)}, u32[]{:S(2)}) %collective-permute-start.12) | collective-permute-done | bytes 559136 | tf_op jit(solution)/shard_map/ring/ppermute | solution.py:480
  87.3 5.6 %collective-permute-start.13 = (bf16[21,104,128]{2,1,0:T(8,128)(2,1)S(1)}, bf16[21,104,128]{2,1,0:T(8,128)(2,1)S(1)}, u32[]{:S(2)}, u32[]{:S(2)}) collective-permute-start(bf16[21,104,128]{2,1,0:T(8,128)(2,1)S(1)} %ring.23), channel_id=1, source_target_pairs={{0,15},{1,0},{2,1},{3,2},{4,3},{5,4},{6,5},{7,6},{8,7},{9,8},{10,9... | collective-permute-start | bytes 1677320 | tf_op jit(solution)/shard_map/ring/ppermute | solution.py:480
  96.7 7.3 %collective-permute-done.13.refs_3_.refs_12_ = bf16[21,104,128]{2,1,0:T(8,128)(2,1)S(1)} collective-permute-done((bf16[21,104,128]{2,1,0:T(8,128)(2,1)S(1)}, bf16[21,104,128]{2,1,0:T(8,128)(2,1)S(1)}, u32[]{:S(2)}, u32[]{:S(2)}) %collective-permute-start.13) | collective-permute-done | bytes 559136 | tf_op jit(solution)/shard_map/ring/ppermute | solution.py:480
  104.0 2.1 ring.24
  106.1 5.6 %collective-permute-start.14 = (bf16[21,104,128]{2,1,0:T(8,128)(2,1)S(1)}, bf16[21,104,128]{2,1,0:T(8,128)(2,1)S(1)}, u32[]{:S(2)}, u32[]{:S(2)}) collective-permute-start(bf16[21,104,128]{2,1,0:T(8,128)(2,1)S(1)} %ring.24), channel_id=1, source_target_pairs={{0,15},{1,0},{2,1},{3,2},{4,3},{5,4},{6,5},{7,6},{8,7},{9,8},{10,9... | collective-permute-start | bytes 1677320 | tf_op jit(solution)/shard_map/ring/ppermute | solution.py:480
  111.7 2.1 ring.17
  115.8 6.2 %collective-permute-done.14.refs_4_.refs_13_ = bf16[21,104,128]{2,1,0:T(8,128)(2,1)S(1)} collective-permute-done((bf16[21,104,128]{2,1,0:T(8,128)(2,1)S(1)}, bf16[21,104,128]{2,1,0:T(8,128)(2,1)S(1)}, u32[]{:S(2)}, u32[]{:S(2)}) %collective-permute-start.14) | collective-permute-done | bytes 559136 | tf_op jit(solution)/shard_map/ring/ppermute | solution.py:480
  121.9 2.2 ring.25
  124.2 5.6 %collective-permute-start.15 = (bf16[21,104,128]{2,1,0:T(8,128)(2,1)S(1)}, bf16[21,104,128]{2,1,0:T(8,128)(2,1)S(1)}, u32[]{:S(2)}, u32[]{:S(2)}) collective-permute-start(bf16[21,104,128]{2,1,0:T(8,128)(2,1)S(1)} %ring.25), channel_id=1, source_target_pairs={{0,15},{1,0},{2,1},{3,2},{4,3},{5,4},{6,5},{7,6},{8,7},{9,8},{10,9... | collective-permute-start | bytes 1677320 | tf_op jit(solution)/shard_map/ring/ppermute | solution.py:480
  129.8 2.2 ring.18
  134.0 5.1 %collective-permute-done.15.refs_5_.refs_14_ = bf16[21,104,128]{2,1,0:T(8,128)(2,1)S(1)} collective-permute-done((bf16[21,104,128]{2,1,0:T(8,128)(2,1)S(1)}, bf16[21,104,128]{2,1,0:T(8,128)(2,1)S(1)}, u32[]{:S(2)}, u32[]{:S(2)}) %collective-permute-start.15) | collective-permute-done | bytes 559136 | tf_op jit(solution)/shard_map/ring/ppermute | solution.py:480
  139.1 2.3 %ring.26 = bf16[21,104,128]{2,1,0:T(8,128)(2,1)S(1)} custom-call(s32[8,256]{1,0:T(8,128)S(1)} %get-tuple-element.89.send_ref, bf16[38,104,128]{2,1,0:T(8,128)(2,1)S(1)} %get-tuple-element.90.home_ref.refs_0_, bf16[21,104,128]{2,1,0:T(8,128)(2,1)S(1)} %collective-permute-done.10.refs_0_.refs_9_, ...), custom_call_target="tpu_custom_call" | custom-call | tf_op jit(solution)/shard_map/ring/pallas_call | solution.py:463
  141.4 5.6 %collective-permute-start.16 = (bf16[21,104,128]{2,1,0:T(8,128)(2,1)S(1)}, bf16[21,104,128]{2,1,0:T(8,128)(2,1)S(1)}, u32[]{:S(2)}, u32[]{:S(2)}) collective-permute-start(bf16[21,104,128]{2,1,0:T(8,128)(2,1)S(1)} %ring.26), channel_id=1, source_target_pairs={{0,15},{1,0},{2,1},{3,2},{4,3},{5,4},{6,5},{7,6},{8,7},{9,8},{10,9... | collective-permute-start | bytes 1677320 | tf_op jit(solution)/shard_map/ring/ppermute | solution.py:480
  147.1 2.3 %ring.19 = bf16[21,104,128]{2,1,0:T(8,128)(2,1)S(1)} custom-call(s32[8,256]{1,0:T(8,128)S(1)} %get-tuple-element.89.send_ref, bf16[38,104,128]{2,1,0:T(8,128)(2,1)S(1)} %get-tuple-element.90.home_ref.refs_0_, bf16[21,104,128]{2,1,0:T(8,128)(2,1)S(1)} %collective-permute-done.2.refs_0_.refs_1_, ...), custom_call_target="tpu_custom_call" | custom-call | tf_op jit(solution)/shard_map/ring/pallas_call | solution.py:463
  151.4 4.1 %collective-permute-done.16.refs_6_.refs_15_ = bf16[21,104,128]{2,1,0:T(8,128)(2,1)S(1)} collective-permute-done((bf16[21,104,128]{2,1,0:T(8,128)(2,1)S(1)}, bf16[21,104,128]{2,1,0:T(8,128)(2,1)S(1)}, u32[]{:S(2)}, u32[]{:S(2)}) %collective-permute-start.16) | collective-permute-done | bytes 559136 | tf_op jit(solution)/shard_map/ring/ppermute | solution.py:480
  155.4 3.3 %ring.27 = bf16[21,104,128]{2,1,0:T(8,128)(2,1)} custom-call(s32[8,256]{1,0:T(8,128)S(1)} %get-tuple-element.89.send_ref, bf16[38,104,128]{2,1,0:T(8,128)(2,1)S(1)} %get-tuple-element.90.home_ref.refs_0_, bf16[21,104,128]{2,1,0:T(8,128)(2,1)S(1)} %collective-permute-done.10.refs_0_.refs_9_, ...), custom_call_target="tpu_custom_call" | custom-call | tf_op jit(solution)/shard_map/ring/pallas_call | solution.py:463
  158.7 5.7 %collective-permute-start.17 = (bf16[21,104,128]{2,1,0:T(8,128)(2,1)}, bf16[21,104,128]{2,1,0:T(8,128)(2,1)}, u32[]{:S(2)}, u32[]{:S(2)}) collective-permute-start(bf16[21,104,128]{2,1,0:T(8,128)(2,1)} %ring.27), channel_id=1, source_target_pairs={{0,15},{1,0},{2,1},{3,2},{4,3},{5,4},{6,5},{7,6},{8,7},{9,8},{10,9... | collective-permute-start | bytes 1677320 | tf_op jit(solution)/shard_map/ring/ppermute | solution.py:480
  164.5 3.3 %ring.20 = bf16[21,104,128]{2,1,0:T(8,128)(2,1)} custom-call(s32[8,256]{1,0:T(8,128)S(1)} %get-tuple-element.89.send_ref, bf16[38,104,128]{2,1,0:T(8,128)(2,1)S(1)} %get-tuple-element.90.home_ref.refs_0_, bf16[21,104,128]{2,1,0:T(8,128)(2,1)S(1)} %collective-permute-done.2.refs_0_.refs_1_, bf16[21,104,128]{2,1,0:T(8,128)(2,1)S(1)} %collective-permute-done.3.refs_1_.refs_2_, ...), custom_call_target="tpu_custom_call" | custom-call | tf_op jit(solution)/shard_map/ring/pallas_call | solution.py:463
  172.1 8.7 %collective-permute-done.9.refs_8_ = bf16[21,104,128]{2,1,0:T(8,128)(2,1)} collective-permute-done((bf16[21,104,128]{2,1,0:T(8,128)(2,1)}, bf16[21,104,128]{2,1,0:T(8,128)(2,1)}, u32[]{:S(2)}, u32[]{:S(2)}) %collective-permute-start.9) | collective-permute-done | bytes 559136 | tf_op jit(solution)/shard_map/ring/ppermute | solution.py:477
  189.2 6.8 %map.1 = f32[8,128]{1,0:T(8,128)S(1)} custom-call(s32[8,128]{1,0:T(8,128)S(1)} %get-tuple-element.88.item_ref, bf16[38,104,128]{2,1,0:T(8,128)(2,1)S(1)} %get-tuple-element.90.home_ref.refs_0_, bf16[21,104,128]{2,1,0:T(8,128)(2,1)S(1)} %collective-permute-done.2.refs_0_.refs_1_, bf16[21,104,128]{2,1,0:T(8,128)(2,1)S(1)} %collective-permute-done.3.refs_1_.refs_2_, ...), custom_call_target="tpu_custom_call" | custom-call | tf_op jit(solution)/shard_map/map/pallas_call | solution.py:492
  196.6 11.1 %all-to-all-start.1 = ((f32[16,4,128]{2,1,0:T(4,128)}), f32[16,4,128]{2,1,0:T(4,128)S(1)}, u32[]{:S(2)}, u32[]{:S(2)}) async-start(f32[16,4,128]{2,1,0:T(4,128)} %broadcast_in_dim.55), calls=%async_computation.1 | async-start | bytes 65536 | tf_op jit(solution)/shard_map/finish/all_to_all | solution.py:506
  210.2 10.1 %all-to-all-done.1 = f32[16,4,128]{2,1,0:T(4,128)S(1)} async-done(((f32[16,4,128]{2,1,0:T(4,128)}), f32[16,4,128]{2,1,0:T(4,128)S(1)}, u32[]{:S(2)}, u32[]{:S(2)}) %all-to-all-start.1) | async-done | bytes 32800 | tf_op jit(solution)/shard_map/finish/all_to_all | solution.py:506
  (109 shorter events, 41.3 us)
Async XLA Ops:
  6.5 13.9 %copy-start.19 = (bf16[2,64,4736]{2,1,0:T(8,128)(2,1)S(1)}, bf16[2,64,4736]{2,1,0:T(8,128)(2,1)}, u32[]{:S(2)}) copy-start(bf16[2,64,4736]{2,1,0:T(8,128)(2,1)} %own_ref.1) | copy-start | bytes 3637252
  6.5 9.6 %copy-start.26 = (s32[2,64]{1,0:T(2,128)S(1)}, s32[2,64]{1,0:T(2,128)}, u32[]{:S(2)}) copy-start(s32[2,64]{1,0:T(2,128)} %param.11) | copy-start | bytes 1540
  6.5 164.0 %all-gather.2.cloned.1.call-start = ((), (), s32[]{:S(2)}) async-start(), calls=%async_computation.2 | async-start | bytes 2621440 | tf_op jit(solution)/shard_map/weights/all_gather | solution.py:412
  7.8 12.7 %collective-permute-start = (bf16[2,16,4736]{2,1,0:T(8,128)(2,1)S(1)}, bf16[2,16,4736]{2,1,0:T(8,128)(2,1)S(1)}, u32[]{:S(2)}, u32[]{:S(2)}) collective-permute-start(bf16[2,16,4736]{2,1,0:T(8,128)(2,1)S(1)} %get-tuple-element.154), channel_id=1, source_target_pairs={{0,16},{16,32},{32,48},{48,64},{64,80},{80,96},{96,112},{1,17},{17... | collective-permute-start | bytes 909320 | tf_op jit(solution)/shard_map/halo/ppermute | solution.py:22
  9.7 10.8 %collective-permute-start.1 = (bf16[2,16,4736]{2,1,0:T(8,128)(2,1)S(1)}, bf16[2,16,4736]{2,1,0:T(8,128)(2,1)S(1)}, u32[]{:S(2)}, u32[]{:S(2)}) collective-permute-start(bf16[2,16,4736]{2,1,0:T(8,128)(2,1)S(1)} %get-tuple-element.153), channel_id=1, source_target_pairs={{16,0},{32,16},{48,32},{64,48},{80,64},{96,80},{112,96},{17,1},{33... | collective-permute-start | bytes 909320 | tf_op jit(solution)/shard_map/halo/ppermute | solution.py:23
  22.5 23.7 %collective-permute-start.10 = (bf16[21,104,128]{2,1,0:T(8,128)(2,1)S(1)}, bf16[21,104,128]{2,1,0:T(8,128)(2,1)S(1)}, u32[]{:S(2)}, u32[]{:S(2)}) collective-permute-start(bf16[21,104,128]{2,1,0:T(8,128)(2,1)S(1)} %get-tuple-element.92), channel_id=1, source_target_pairs={{0,15},{1,0},{2,1},{3,2},{4,3},{5,4},{6,5},{7,6},{8,7},{9,8},{10,9... | collective-permute-start | bytes 1677320 | tf_op jit(solution)/shard_map/ring/ppermute | solution.py:480
  33.9 19.0 %collective-permute-start.2 = (bf16[21,104,128]{2,1,0:T(8,128)(2,1)S(1)}, bf16[21,104,128]{2,1,0:T(8,128)(2,1)S(1)}, u32[]{:S(2)}, u32[]{:S(2)}) collective-permute-start(bf16[21,104,128]{2,1,0:T(8,128)(2,1)S(1)} %get-tuple-element.91), channel_id=1, source_target_pairs={{0,1},{1,2},{2,3},{3,4},{4,5},{5,6},{6,7},{7,8},{8,9},{9,10},{10,1... | collective-permute-start | bytes 1677320 | tf_op jit(solution)/shard_map/ring/ppermute | solution.py:477
  47.3 18.3 %collective-permute-start.11 = (bf16[21,104,128]{2,1,0:T(8,128)(2,1)S(1)}, bf16[21,104,128]{2,1,0:T(8,128)(2,1)S(1)}, u32[]{:S(2)}, u32[]{:S(2)}) collective-permute-start(bf16[21,104,128]{2,1,0:T(8,128)(2,1)S(1)} %ring.21), channel_id=1, source_target_pairs={{0,15},{1,0},{2,1},{3,2},{4,3},{5,4},{6,5},{7,6},{8,7},{9,8},{10,9... | collective-permute-start | bytes 1677320 | tf_op jit(solution)/shard_map/ring/ppermute | solution.py:480
  54.1 19.2 %collective-permute-start.3 = (bf16[21,104,128]{2,1,0:T(8,128)(2,1)S(1)}, bf16[21,104,128]{2,1,0:T(8,128)(2,1)S(1)}, u32[]{:S(2)}, u32[]{:S(2)}) collective-permute-start(bf16[21,104,128]{2,1,0:T(8,128)(2,1)S(1)} %ring.14), channel_id=1, source_target_pairs={{0,1},{1,2},{2,3},{3,4},{4,5},{5,6},{6,7},{7,8},{8,9},{9,10},{10,1... | collective-permute-start | bytes 1677320 | tf_op jit(solution)/shard_map/ring/ppermute | solution.py:477
  67.7 17.8 %collective-permute-start.12 = (bf16[21,104,128]{2,1,0:T(8,128)(2,1)}, bf16[21,104,128]{2,1,0:T(8,128)(2,1)}, u32[]{:S(2)}, u32[]{:S(2)}) collective-permute-start(bf16[21,104,128]{2,1,0:T(8,128)(2,1)} %ring.22), channel_id=1, source_target_pairs={{0,15},{1,0},{2,1},{3,2},{4,3},{5,4},{6,5},{7,6},{8,7},{9,8},{10,9... | collective-permute-start | bytes 1677320 | tf_op jit(solution)/shard_map/ring/ppermute | solution.py:480
  75.4 17.5 %collective-permute-start.4 = (bf16[21,104,128]{2,1,0:T(8,128)(2,1)}, bf16[21,104,128]{2,1,0:T(8,128)(2,1)}, u32[]{:S(2)}, u32[]{:S(2)}) collective-permute-start(bf16[21,104,128]{2,1,0:T(8,128)(2,1)} %ring.15), channel_id=1, source_target_pairs={{0,1},{1,2},{2,3},{3,4},{4,5},{5,6},{6,7},{7,8},{8,9},{9,10},{10,1... | collective-permute-start | bytes 1677320 | tf_op jit(solution)/shard_map/ring/ppermute | solution.py:477
  87.3 16.7 %collective-permute-start.13 = (bf16[21,104,128]{2,1,0:T(8,128)(2,1)S(1)}, bf16[21,104,128]{2,1,0:T(8,128)(2,1)S(1)}, u32[]{:S(2)}, u32[]{:S(2)}) collective-permute-start(bf16[21,104,128]{2,1,0:T(8,128)(2,1)S(1)} %ring.23), channel_id=1, source_target_pairs={{0,15},{1,0},{2,1},{3,2},{4,3},{5,4},{6,5},{7,6},{8,7},{9,8},{10,9... | collective-permute-start | bytes 1677320 | tf_op jit(solution)/shard_map/ring/ppermute | solution.py:480
  94.7 17.0 %collective-permute-start.5 = (bf16[21,104,128]{2,1,0:T(8,128)(2,1)S(1)}, bf16[21,104,128]{2,1,0:T(8,128)(2,1)S(1)}, u32[]{:S(2)}, u32[]{:S(2)}) collective-permute-start(bf16[21,104,128]{2,1,0:T(8,128)(2,1)S(1)} %ring.16), channel_id=1, source_target_pairs={{0,1},{1,2},{2,3},{3,4},{4,5},{5,6},{6,7},{7,8},{8,9},{9,10},{10,1... | collective-permute-start | bytes 1677320 | tf_op jit(solution)/shard_map/ring/ppermute | solution.py:477
  104.0 51.5 %copy-start = (bf16[21,104,128]{2,1,0:T(8,128)(2,1)}, bf16[21,104,128]{2,1,0:T(8,128)(2,1)S(1)}, u32[]{:S(2)}) copy-start(bf16[21,104,128]{2,1,0:T(8,128)(2,1)S(1)} %collective-permute-done.13.refs_3_.refs_12_) | copy-start | bytes 1677316
  106.1 15.8 %collective-permute-start.14 = (bf16[21,104,128]{2,1,0:T(8,128)(2,1)S(1)}, bf16[21,104,128]{2,1,0:T(8,128)(2,1)S(1)}, u32[]{:S(2)}, u32[]{:S(2)}) collective-permute-start(bf16[21,104,128]{2,1,0:T(8,128)(2,1)S(1)} %ring.24), channel_id=1, source_target_pairs={{0,15},{1,0},{2,1},{3,2},{4,3},{5,4},{6,5},{7,6},{8,7},{9,8},{10,9... | collective-permute-start | bytes 1677320 | tf_op jit(solution)/shard_map/ring/ppermute | solution.py:480
  111.7 52.8 %copy-start.2 = (bf16[21,104,128]{2,1,0:T(8,128)(2,1)}, bf16[21,104,128]{2,1,0:T(8,128)(2,1)S(1)}, u32[]{:S(2)}) copy-start(bf16[21,104,128]{2,1,0:T(8,128)(2,1)S(1)} %collective-permute-done.5.refs_3_.refs_4_) | copy-start | bytes 1677316
  113.8 15.9 %collective-permute-start.6 = (bf16[21,104,128]{2,1,0:T(8,128)(2,1)S(1)}, bf16[21,104,128]{2,1,0:T(8,128)(2,1)S(1)}, u32[]{:S(2)}, u32[]{:S(2)}) collective-permute-start(bf16[21,104,128]{2,1,0:T(8,128)(2,1)S(1)} %ring.17), channel_id=1, source_target_pairs={{0,1},{1,2},{2,3},{3,4},{4,5},{5,6},{6,7},{7,8},{8,9},{9,10},{10,1... | collective-permute-start | bytes 1677320 | tf_op jit(solution)/shard_map/ring/ppermute | solution.py:477
  121.9 33.5 %copy-start.4 = (bf16[21,104,128]{2,1,0:T(8,128)(2,1)}, bf16[21,104,128]{2,1,0:T(8,128)(2,1)S(1)}, u32[]{:S(2)}) copy-start(bf16[21,104,128]{2,1,0:T(8,128)(2,1)S(1)} %collective-permute-done.14.refs_4_.refs_13_) | copy-start | bytes 1677316
  124.2 14.9 %collective-permute-start.15 = (bf16[21,104,128]{2,1,0:T(8,128)(2,1)S(1)}, bf16[21,104,128]{2,1,0:T(8,128)(2,1)S(1)}, u32[]{:S(2)}, u32[]{:S(2)}) collective-permute-start(bf16[21,104,128]{2,1,0:T(8,128)(2,1)S(1)} %ring.25), channel_id=1, source_target_pairs={{0,15},{1,0},{2,1},{3,2},{4,3},{5,4},{6,5},{7,6},{8,7},{9,8},{10,9... | collective-permute-start | bytes 1677320 | tf_op jit(solution)/shard_map/ring/ppermute | solution.py:480
  129.8 34.7 %copy-start.6 = (bf16[21,104,128]{2,1,0:T(8,128)(2,1)}, bf16[21,104,128]{2,1,0:T(8,128)(2,1)S(1)}, u32[]{:S(2)}) copy-start(bf16[21,104,128]{2,1,0:T(8,128)(2,1)S(1)} %collective-permute-done.6.refs_4_.refs_5_) | copy-start | bytes 1677316
  132.0 15.0 %collective-permute-start.7 = (bf16[21,104,128]{2,1,0:T(8,128)(2,1)S(1)}, bf16[21,104,128]{2,1,0:T(8,128)(2,1)S(1)}, u32[]{:S(2)}, u32[]{:S(2)}) collective-permute-start(bf16[21,104,128]{2,1,0:T(8,128)(2,1)S(1)} %ring.18), channel_id=1, source_target_pairs={{0,1},{1,2},{2,3},{3,4},{4,5},{5,6},{6,7},{7,8},{8,9},{9,10},{10,1... | collective-permute-start | bytes 1677320 | tf_op jit(solution)/shard_map/ring/ppermute | solution.py:477
  139.1 16.4 %copy-start.8 = (bf16[21,104,128]{2,1,0:T(8,128)(2,1)}, bf16[21,104,128]{2,1,0:T(8,128)(2,1)S(1)}, u32[]{:S(2)}) copy-start(bf16[21,104,128]{2,1,0:T(8,128)(2,1)S(1)} %collective-permute-done.15.refs_5_.refs_14_) | copy-start | bytes 1677316
  141.4 14.0 %collective-permute-start.16 = (bf16[21,104,128]{2,1,0:T(8,128)(2,1)S(1)}, bf16[21,104,128]{2,1,0:T(8,128)(2,1)S(1)}, u32[]{:S(2)}, u32[]{:S(2)}) collective-permute-start(bf16[21,104,128]{2,1,0:T(8,128)(2,1)S(1)} %ring.26), channel_id=1, source_target_pairs={{0,15},{1,0},{2,1},{3,2},{4,3},{5,4},{6,5},{7,6},{8,7},{9,8},{10,9... | collective-permute-start | bytes 1677320 | tf_op jit(solution)/shard_map/ring/ppermute | solution.py:480
  147.1 17.4 %copy-start.10 = (bf16[21,104,128]{2,1,0:T(8,128)(2,1)}, bf16[21,104,128]{2,1,0:T(8,128)(2,1)S(1)}, u32[]{:S(2)}) copy-start(bf16[21,104,128]{2,1,0:T(8,128)(2,1)S(1)} %collective-permute-done.7.refs_5_.refs_6_) | copy-start | bytes 1677316
  149.4 15.0 %collective-permute-start.8 = (bf16[21,104,128]{2,1,0:T(8,128)(2,1)S(1)}, bf16[21,104,128]{2,1,0:T(8,128)(2,1)S(1)}, u32[]{:S(2)}, u32[]{:S(2)}) collective-permute-start(bf16[21,104,128]{2,1,0:T(8,128)(2,1)S(1)} %ring.19), channel_id=1, source_target_pairs={{0,1},{1,2},{2,3},{3,4},{4,5},{5,6},{6,7},{7,8},{8,9},{9,10},{10,1... | collective-permute-start | bytes 1677320 | tf_op jit(solution)/shard_map/ring/ppermute | solution.py:477
  155.4 3.3 %copy-start.12 = (bf16[21,104,128]{2,1,0:T(8,128)(2,1)}, bf16[21,104,128]{2,1,0:T(8,128)(2,1)S(1)}, u32[]{:S(2)}) copy-start(bf16[21,104,128]{2,1,0:T(8,128)(2,1)S(1)} %collective-permute-done.16.refs_6_.refs_15_) | copy-start | bytes 1677316
  158.7 11.0 %copy-start.16 = (bf16[2,64,4096]{2,1,0:T(8,128)(2,1)S(1)}, bf16[2,64,4096]{2,1,0:T(8,128)(2,1)}, u32[]{:S(2)}) copy-start(bf16[2,64,4096]{2,1,0:T(8,128)(2,1)} %refs_19_.1) | copy-start | bytes 3145732
  158.7 13.4 %collective-permute-start.17 = (bf16[21,104,128]{2,1,0:T(8,128)(2,1)}, bf16[21,104,128]{2,1,0:T(8,128)(2,1)}, u32[]{:S(2)}, u32[]{:S(2)}) collective-permute-start(bf16[21,104,128]{2,1,0:T(8,128)(2,1)} %ring.27), channel_id=1, source_target_pairs={{0,15},{1,0},{2,1},{3,2},{4,3},{5,4},{6,5},{7,6},{8,7},{9,8},{10,9... | collective-permute-start | bytes 1677320 | tf_op jit(solution)/shard_map/ring/ppermute | solution.py:480
  164.5 3.3 %copy-start.14 = (bf16[21,104,128]{2,1,0:T(8,128)(2,1)}, bf16[21,104,128]{2,1,0:T(8,128)(2,1)S(1)}, u32[]{:S(2)}) copy-start(bf16[21,104,128]{2,1,0:T(8,128)(2,1)S(1)} %collective-permute-done.8.refs_6_.refs_7_) | copy-start | bytes 1677316
  167.8 13.0 %collective-permute-start.9 = (bf16[21,104,128]{2,1,0:T(8,128)(2,1)}, bf16[21,104,128]{2,1,0:T(8,128)(2,1)}, u32[]{:S(2)}, u32[]{:S(2)}) collective-permute-start(bf16[21,104,128]{2,1,0:T(8,128)(2,1)} %ring.20), channel_id=1, source_target_pairs={{0,1},{1,2},{2,3},{3,4},{4,5},{5,6},{6,7},{7,8},{8,9},{9,10},{10,1... | collective-permute-start | bytes 1677320 | tf_op jit(solution)/shard_map/ring/ppermute | solution.py:477
  189.2 21.0 %copy-start.24 = (s32[512,2]{0,1:T(2,128)S(1)}, s32[512,2]{0,1:T(2,128)}, u32[]{:S(2)}) copy-start(s32[512,2]{0,1:T(2,128)} %param.12) | copy-start | bytes 12292
  196.6 23.7 %all-to-all-start.1 = ((f32[16,4,128]{2,1,0:T(4,128)}), f32[16,4,128]{2,1,0:T(4,128)S(1)}, u32[]{:S(2)}, u32[]{:S(2)}) async-start(f32[16,4,128]{2,1,0:T(4,128)} %broadcast_in_dim.55), calls=%async_computation.1 | async-start | bytes 65536 | tf_op jit(solution)/shard_map/finish/all_to_all | solution.py:506
  (11 other events, 13.1 us)
Sparse Core Ops, SparseCore 0:
  77.5 32.9 all-gather.1

commit v3 on v2

--- a/solution.py
+++ b/solution.py
@@ -46,14 +46,24 @@
     return jnp.where(mask, 1.0, 0.0).astype(jnp.bfloat16)
 
 
-def plan_kernel(blocks, place_ref, holder_ref, holders_ref, inners_ref, send_ref, item_ref, fit_ref, book_ref):
-    vocab_count, pair_count = holder_ref.shape
+def plan_kernel(blocks, place_ref, listed_ref, send_ref, item_ref, fit_ref, book_ref):
+    vocab_count, pair_count = listed_ref.shape
     half = vocab_count // 2
     steps = half
     home = blocks + 1
     me, sign = place_ref[0], place_ref[1]
     f32, i32 = jnp.float32, jnp.int32
     shape = (vocab_count, BLK)
+
+    def split(listed):
+        holder = sum((listed >= h * blocks).astype(i32) for h in range(1, vocab_count))
+        return holder, listed - holder * blocks
+
+    listed = listed_ref[...]
+    wide = jnp.concatenate([listed, jnp.zeros((vocab_count, BLK - pair_count), i32)], axis=1)
+    tall = jnp.concatenate([wide, jnp.zeros((BLK - vocab_count, BLK), i32)], axis=0).astype(f32).T.astype(i32)
+    row_holder, _ = split(listed)
+    holders, inners = split(tall[:pair_count])
     lane = lax.broadcasted_iota(i32, shape, 1)
     row = lax.broadcasted_iota(i32, shape, 0)
 
@@ -62,8 +72,8 @@
     pair_row = lax.broadcasted_iota(i32, (vocab_count, pair_count), 0)
     for s in range(vocab_count):
         hits = jnp.dot(
-            ones(pair_row == holder_ref[s : s + 1, :]),
-            ones(pair_lane == inners_ref[:, s : s + 1]),
+            ones(pair_row == row_holder[s : s + 1, :]),
+            ones(pair_lane == inners[:, s : s + 1]),
             preferred_element_type=f32,
         )
         distance = s - row
@@ -159,8 +169,8 @@
     send_ref[2:8, :] = jnp.zeros((6, 2 * BLK), i32)
 
     mine_lane = lax.broadcasted_iota(i32, (pair_count, vocab_count), 1)
-    holder = jnp.sum(jnp.where(mine_lane == me, holders_ref[...], 0), axis=1, keepdims=True)
-    inner = jnp.sum(jnp.where(mine_lane == me, inners_ref[...], 0), axis=1, keepdims=True)
+    holder = jnp.sum(jnp.where(pair_lane == me, holders, 0), axis=1, keepdims=True)
+    inner = jnp.sum(jnp.where(pair_lane == me, inners, 0), axis=1, keepdims=True)
     distance = me - holder
     distance = jnp.where(distance < 0, distance + vocab_count, distance)
     hops = ways(distance, inner, vocab_count)
@@ -248,27 +258,42 @@
         second_ref[j] = home_ref[send_ref[1, j]]
 
 
-def pass_kernel(chain, step, send_ref, home_ref, *refs):
+def ready_kernel(chain, step, send_ref, home_ref, *refs):
     frames, out_ref = refs[:-1], refs[-1]
     home = home_ref.shape[0]
 
     def choose(j, carry):
         at = send_ref[chain, step * SLOTS + j]
 
-        @pl.when(at < home)
-        def _():
-            out_ref[j] = home_ref[at]
-
-        for f, frame in enumerate(frames):
-            start = home + f * SLOTS
-
-            @pl.when((at >= start) & (at < start + SLOTS))
-            def _(frame=frame, start=start):
-                out_ref[j] = frame[at - start]
-
+        def copy(low, high):
+            if high - low == 1:
+                if low == 0:
+                    out_ref[j] = home_ref[at]
+                elif low <= len(frames):
+                    out_ref[j] = frames[low - 1][at - home - (low - 1) * SLOTS]
+                return
+            mid = (low + high) // 2
+            split = home + (mid - 1) * SLOTS
+            pl.when(at < split)(lambda: copy(low, mid))
+            pl.when(at >= split)(lambda: copy(mid, high))
+
+        copy(0, len(frames) + 2)
         return carry
 
     lax.fori_loop(0, SLOTS, choose, 0)
+
+
+def pass_kernel(chain, step, home, send_ref, part_ref, newest_ref, out_ref):
+    for j in range(SLOTS):
+        at = send_ref[chain, step * SLOTS + j] - (home + (step - 1) * SLOTS)
+
+        @pl.when(at >= 0)
+        def _(j=j, at=at):
+            out_ref[j] = newest_ref[at]
+
+        @pl.when(at < 0)
+        def _(j=j):
+            out_ref[j] = part_ref[j]
 
 
 def student_kernel(student_ref, top_ref, total_ref):
@@ -432,16 +457,15 @@
 
     with jax.named_scope("plan"):
         listed = src_block.reshape(vocab_count, pair_count)
-        holder, inner = listed // teacher_blocks, listed % teacher_blocks
         table = jax.ShapeDtypeStruct((8, BLK), jnp.int32)
         send, items, left = pl.pallas_call(
             functools.partial(plan_kernel, teacher_blocks),
             out_shape=(jax.ShapeDtypeStruct((8, 2 * BLK), jnp.int32), table, table),
-            in_specs=[smem] + [vmem] * 3,
+            in_specs=[smem, vmem],
             out_specs=(vmem,) * 3,
             scratch_shapes=[pltpu.VMEM((6 * steps, vocab_count, BLK), jnp.float32)],
             compiler_params=room(16),
-        )(jnp.stack([vocab_index, sign]).astype(jnp.int32), holder, holder.T, inner.T)
+        )(jnp.stack([vocab_index, sign]).astype(jnp.int32), listed)
 
     def planes(count):
         return jax.ShapeDtypeStruct((count, ROWS, BLK), jnp.bfloat16)
@@ -460,13 +484,20 @@
         )(send, teacher_logits, low, high, pick)
 
     def chosen(chain, step, frames):
+        part = pl.pallas_call(
+            functools.partial(ready_kernel, chain, step),
+            out_shape=planes(SLOTS),
+            in_specs=[smem] + [vmem] * len(frames),
+            out_specs=vmem,
+            compiler_params=room(12),
+        )(send, own, *frames[:-1])
         return pl.pallas_call(
-            functools.partial(pass_kernel, chain, step),
+            functools.partial(pass_kernel, chain, step, home),
             out_shape=planes(SLOTS),
-            in_specs=[smem] + [vmem] * (1 + len(frames)),
+            in_specs=[smem] + [vmem] * 2,
             out_specs=vmem,
-            compiler_params=room(16),
-        )(send, own, *frames)
+            compiler_params=room(8),
+        )(send, part, frames[-1])
 
     with jax.named_scope("ring"):
         forward, backward = ring_pairs(1), ring_pairs(-1)
@@ -498,7 +529,7 @@
                 pltpu.VMEM((pair_count + 2 * vocab_count, ROWS, BLK), jnp.bfloat16),
                 pltpu.VMEM((3 * steps, row_count, BLK), jnp.float32),
             ],
-            compiler_params=room(32),
+            compiler_params=room(20),
         )(items, own, *came_ahead, *came_behind, spread, weights, student_logits, top, total)
 
     with jax.named_scope("finish"):

time: 229 us -> 226 us (0.987)
  the two profiles are of different devices: /device:TPU:26 before, /device:TPU:6 now
where the time goes in v3:
time: 226 us; the launch traced here: 224 us
  starting transfers between devices  84 us (37%)
  waiting for transfers between devices  59.2 us (26%)
  Pallas kernels  50.9 us (23%)
  between operations  15.3 us (7%)
  local copies, waits for them, and re-layouts  12.6 us (6%)
    ppermute x8, starting transfers between devices, shards(): came_behind.append(lax.ppermute(behind, ('seq', 'vocab'), backward))  49.3 us
    ppermute x8, waiting for transfers between devices, shards(): came_ahead.append(lax.ppermute(ahead, ('seq', 'vocab'), forward))  26.3 us
    ppermute x8, waiting for transfers between devices, shards(): came_behind.append(lax.ppermute(behind, ('seq', 'vocab'), backward))  22.8 us
    pallas_call x14, Pallas kernels, chosen(): pl.pallas_call(functools.partial(ready_kernel, chain, step), out_shape=pl...  20.1 us
    pallas_call x14, Pallas kernels, chosen(): pl.pallas_call(functools.partial(pass_kernel, chain, step, home), out_sha...  17.4 us
    ppermute x8, starting transfers between devices, shards(): came_ahead.append(lax.ppermute(ahead, ('seq', 'vocab'), forward))  15.3 us
    all_to_all x1, starting transfers between devices, shards(): lax.all_to_all(sent, 'vocab', split_axis=0, concat_axis=0, tiled=True)  13.8 us
    all_to_all x1, waiting for transfers between devices, shards(): lax.all_to_all(sent, 'vocab', split_axis=0, concat_axis=0, tiled=True)  10.1 us
  transfers between devices with their start and end apart: 20, of which 12 were waited for; matrix products, arithmetic and copies ran while one was open for 2% of the time, Pallas kernels for 19%

profile of v3, /device:TPU:6, one launch (start us, length us, event | category | flops | bytes accessed | tf_op | source)
XLA Modules:
  0.0 223.9 jit_solution(6511873214263205663)
XLA Ops:
  7.7 1.9 collective-permute-start
  9.7 3.6 %collective-permute-start.1 = (bf16[2,16,4736]{2,1,0:T(8,128)(2,1)S(1)}, bf16[2,16,4736]{2,1,0:T(8,128)(2,1)S(1)}, u32[]{:S(2)}, u32[]{:S(2)}) collective-permute-start(bf16[2,16,4736]{2,1,0:T(8,128)(2,1)S(1)} %get-tuple-element.153), channel_id=1, source_target_pairs={{16,0},{32,16},{48,32},{64,48},{80,64},{96,80},{112,96},{17,1},{33... | collective-permute-start | bytes 909320 | tf_op jit(solution)/shard_map/halo/ppermute | solution.py:23
  15.4 3.9 %plan.1 = (s32[8,256]{1,0:T(8,128)S(1)}, s32[8,128]{1,0:T(8,128)S(1)}, s32[8,128]{1,0:T(8,128)S(1)}) custom-call(s32[2]{0:T(128)S(1)} %pad_add_fusion.place_ref, s32[16,64]{1,0:T(8,128)S(1)} %reshape.251.listed_ref), custom_call_target="tpu_custom_call" | custom-call | tf_op jit(solution)/shard_map/plan/pallas_call | solution.py:461
  19.4 2.0 pack.1
  21.5 11.4 %collective-permute-start.10 = (bf16[21,104,128]{2,1,0:T(8,128)(2,1)S(1)}, bf16[21,104,128]{2,1,0:T(8,128)(2,1)S(1)}, u32[]{:S(2)}, u32[]{:S(2)}) collective-permute-start(bf16[21,104,128]{2,1,0:T(8,128)(2,1)S(1)} %get-tuple-element.92), channel_id=1, source_target_pairs={{0,15},{1,0},{2,1},{3,2},{4,3},{5,4},{6,5},{7,6},{8,7},{9,8},{10,9... | collective-permute-start | bytes 1677320 | tf_op jit(solution)/shard_map/ring/ppermute | solution.py:511
  32.9 1.9 collective-permute-start.2
  36.8 8.9 %collective-permute-done.10.newest_ref.refs_0_.refs_9_ = bf16[21,104,128]{2,1,0:T(8,128)(2,1)S(1)} collective-permute-done((bf16[21,104,128]{2,1,0:T(8,128)(2,1)S(1)}, bf16[21,104,128]{2,1,0:T(8,128)(2,1)S(1)}, u32[]{:S(2)}, u32[]{:S(2)}) %collective-permute-start.10) | collective-permute-done | bytes 559136 | tf_op jit(solution)/shard_map/ring/ppermute | solution.py:511
  46.6 5.6 %collective-permute-start.11 = (bf16[21,104,128]{2,1,0:T(8,128)(2,1)S(1)}, bf16[21,104,128]{2,1,0:T(8,128)(2,1)S(1)}, u32[]{:S(2)}, u32[]{:S(2)}) collective-permute-start(bf16[21,104,128]{2,1,0:T(8,128)(2,1)S(1)} %ring.43), channel_id=1, source_target_pairs={{0,15},{1,0},{2,1},{3,2},{4,3},{5,4},{6,5},{7,6},{8,7},{9,8},{10,9... | collective-permute-start | bytes 1677320 | tf_op jit(solution)/shard_map/ring/ppermute | solution.py:511
  53.2 1.9 collective-permute-start.3
  57.4 6.8 %collective-permute-done.11.newest_ref.refs_1_.refs_10_ = bf16[21,104,128]{2,1,0:T(8,128)(2,1)S(1)} collective-permute-done((bf16[21,104,128]{2,1,0:T(8,128)(2,1)S(1)}, bf16[21,104,128]{2,1,0:T(8,128)(2,1)S(1)}, u32[]{:S(2)}, u32[]{:S(2)}) %collective-permute-start.11) | collective-permute-done | bytes 559136 | tf_op jit(solution)/shard_map/ring/ppermute | solution.py:511
  66.0 5.6 %collective-permute-start.12 = (bf16[21,104,128]{2,1,0:T(8,128)(2,1)}, bf16[21,104,128]{2,1,0:T(8,128)(2,1)}, u32[]{:S(2)}, u32[]{:S(2)}) collective-permute-start(bf16[21,104,128]{2,1,0:T(8,128)(2,1)} %ring.45), channel_id=1, source_target_pairs={{0,15},{1,0},{2,1},{3,2},{4,3},{5,4},{6,5},{7,6},{8,7},{9,8},{10,9... | collective-permute-start | bytes 1677320 | tf_op jit(solution)/shard_map/ring/ppermute | solution.py:511
  73.4 1.9 collective-permute-start.4
  77.6 5.3 %collective-permute-done.12.newest_ref.refs_2_.refs_11_ = bf16[21,104,128]{2,1,0:T(8,128)(2,1)} collective-permute-done((bf16[21,104,128]{2,1,0:T(8,128)(2,1)}, bf16[21,104,128]{2,1,0:T(8,128)(2,1)}, u32[]{:S(2)}, u32[]{:S(2)}) %collective-permute-start.12) | collective-permute-done | bytes 559136 | tf_op jit(solution)/shard_map/ring/ppermute | solution.py:511
  84.3 5.6 %collective-permute-start.13 = (bf16[21,104,128]{2,1,0:T(8,128)(2,1)S(1)}, bf16[21,104,128]{2,1,0:T(8,128)(2,1)S(1)}, u32[]{:S(2)}, u32[]{:S(2)}) collective-permute-start(bf16[21,104,128]{2,1,0:T(8,128)(2,1)S(1)} %ring.47), channel_id=1, source_target_pairs={{0,15},{1,0},{2,1},{3,2},{4,3},{5,4},{6,5},{7,6},{8,7},{9,8},{10,9... | collective-permute-start | bytes 1677320 | tf_op jit(solution)/shard_map/ring/ppermute | solution.py:511
  89.9 1.8 collective-permute-done.4.newest_ref.refs_2_.refs_3_
  93.1 1.9 collective-permute-start.5
  101.0 5.6 %collective-permute-start.14 = (bf16[21,104,128]{2,1,0:T(8,128)(2,1)S(1)}, bf16[21,104,128]{2,1,0:T(8,128)(2,1)S(1)}, u32[]{:S(2)}, u32[]{:S(2)}) collective-permute-start(bf16[21,104,128]{2,1,0:T(8,128)(2,1)S(1)} %ring.49), channel_id=1, source_target_pairs={{0,15},{1,0},{2,1},{3,2},{4,3},{5,4},{6,5},{7,6},{8,7},{9,8},{10,9... | collective-permute-start | bytes 1677320 | tf_op jit(solution)/shard_map/ring/ppermute | solution.py:511
  106.6 3.4 %collective-permute-done.5.newest_ref.refs_3_.refs_4_ = bf16[21,104,128]{2,1,0:T(8,128)(2,1)S(1)} collective-permute-done((bf16[21,104,128]{2,1,0:T(8,128)(2,1)S(1)}, bf16[21,104,128]{2,1,0:T(8,128)(2,1)S(1)}, u32[]{:S(2)}, u32[]{:S(2)}) %collective-permute-start.5) | collective-permute-done | bytes 559136 | tf_op jit(solution)/shard_map/ring/ppermute | solution.py:508
  111.0 1.9 collective-permute-start.6
  117.2 5.3 %collective-permute-start.15 = (bf16[21,104,128]{2,1,0:T(8,128)(2,1)S(1)}, bf16[21,104,128]{2,1,0:T(8,128)(2,1)S(1)}, u32[]{:S(2)}, u32[]{:S(2)}) collective-permute-start(bf16[21,104,128]{2,1,0:T(8,128)(2,1)S(1)} %ring.51), channel_id=1, source_target_pairs={{0,15},{1,0},{2,1},{3,2},{4,3},{5,4},{6,5},{7,6},{8,7},{9,8},{10,9... | collective-permute-start | bytes 1677320 | tf_op jit(solution)/shard_map/ring/ppermute | solution.py:511
  122.5 4.5 %collective-permute-done.6.newest_ref.refs_4_.refs_5_ = bf16[21,104,128]{2,1,0:T(8,128)(2,1)S(1)} collective-permute-done((bf16[21,104,128]{2,1,0:T(8,128)(2,1)S(1)}, bf16[21,104,128]{2,1,0:T(8,128)(2,1)S(1)}, u32[]{:S(2)}, u32[]{:S(2)}) %collective-permute-start.6) | collective-permute-done | bytes 559136 | tf_op jit(solution)/shard_map/ring/ppermute | solution.py:508
  128.0 1.9 collective-permute-start.7
  134.2 5.1 %collective-permute-start.16 = (bf16[21,104,128]{2,1,0:T(8,128)(2,1)S(1)}, bf16[21,104,128]{2,1,0:T(8,128)(2,1)S(1)}, u32[]{:S(2)}, u32[]{:S(2)}) collective-permute-start(bf16[21,104,128]{2,1,0:T(8,128)(2,1)S(1)} %ring.53), channel_id=1, source_target_pairs={{0,15},{1,0},{2,1},{3,2},{4,3},{5,4},{6,5},{7,6},{8,7},{9,8},{10,9... | collective-permute-start | bytes 1677320 | tf_op jit(solution)/shard_map/ring/ppermute | solution.py:511
  139.4 3.8 %collective-permute-done.7.newest_ref.refs_5_.refs_6_ = bf16[21,104,128]{2,1,0:T(8,128)(2,1)S(1)} collective-permute-done((bf16[21,104,128]{2,1,0:T(8,128)(2,1)S(1)}, bf16[21,104,128]{2,1,0:T(8,128)(2,1)S(1)}, u32[]{:S(2)}, u32[]{:S(2)}) %collective-permute-start.7) | collective-permute-done | bytes 559136 | tf_op jit(solution)/shard_map/ring/ppermute | solution.py:508
  144.1 1.9 collective-permute-start.8
  151.4 5.1 %collective-permute-start.17 = (bf16[21,104,128]{2,1,0:T(8,128)(2,1)}, bf16[21,104,128]{2,1,0:T(8,128)(2,1)}, u32[]{:S(2)}, u32[]{:S(2)}) collective-permute-start(bf16[21,104,128]{2,1,0:T(8,128)(2,1)} %ring.55), channel_id=1, source_target_pairs={{0,15},{1,0},{2,1},{3,2},{4,3},{5,4},{6,5},{7,6},{8,7},{9,8},{10,9... | collective-permute-start | bytes 1677320 | tf_op jit(solution)/shard_map/ring/ppermute | solution.py:511
  156.5 2.7 %collective-permute-done.8.newest_ref.refs_7_ = bf16[21,104,128]{2,1,0:T(8,128)(2,1)S(1)} collective-permute-done((bf16[21,104,128]{2,1,0:T(8,128)(2,1)S(1)}, bf16[21,104,128]{2,1,0:T(8,128)(2,1)S(1)}, u32[]{:S(2)}, u32[]{:S(2)}) %collective-permute-start.8) | collective-permute-done | bytes 559136 | tf_op jit(solution)/shard_map/ring/ppermute | solution.py:508
  161.0 1.9 collective-permute-start.9
  163.9 10.1 %collective-permute-done.9.refs_8_ = bf16[21,104,128]{2,1,0:T(8,128)(2,1)} collective-permute-done((bf16[21,104,128]{2,1,0:T(8,128)(2,1)}, bf16[21,104,128]{2,1,0:T(8,128)(2,1)}, u32[]{:S(2)}, u32[]{:S(2)}) %collective-permute-start.9) | collective-permute-done | bytes 559136 | tf_op jit(solution)/shard_map/ring/ppermute | solution.py:508
  182.4 7.0 %map.1 = f32[8,128]{1,0:T(8,128)S(1)} custom-call(s32[8,128]{1,0:T(8,128)S(1)} %get-tuple-element.88.item_ref, bf16[38,104,128]{2,1,0:T(8,128)(2,1)S(1)} %get-tuple-element.90.home_ref.refs_0_, bf16[21,104,128]{2,1,0:T(8,128)(2,1)S(1)} %collective-permute-done.2.newest_ref.refs_0_.refs_1_, ...), custom_call_target="tpu_custom_call" | custom-call | tf_op jit(solution)/shard_map/map/pallas_call | solution.py:523
  190.0 13.8 %all-to-all-start.1 = ((f32[16,4,128]{2,1,0:T(4,128)}), f32[16,4,128]{2,1,0:T(4,128)S(1)}, u32[]{:S(2)}, u32[]{:S(2)}) async-start(f32[16,4,128]{2,1,0:T(4,128)} %broadcast_in_dim.55), calls=%async_computation.1 | async-start | bytes 65536 | tf_op jit(solution)/shard_map/finish/all_to_all | solution.py:537
  206.2 10.1 %all-to-all-done.1 = f32[16,4,128]{2,1,0:T(4,128)S(1)} async-done(((f32[16,4,128]{2,1,0:T(4,128)}), f32[16,4,128]{2,1,0:T(4,128)S(1)}, u32[]{:S(2)}, u32[]{:S(2)}) %all-to-all-start.1) | async-done | bytes 32800 | tf_op jit(solution)/shard_map/finish/all_to_all | solution.py:537
  (110 shorter events, 54.7 us)
Async XLA Ops:
  6.5 12.9 %copy-start.19 = (bf16[2,64,4736]{2,1,0:T(8,128)(2,1)S(1)}, bf16[2,64,4736]{2,1,0:T(8,128)(2,1)}, u32[]{:S(2)}) copy-start(bf16[2,64,4736]{2,1,0:T(8,128)(2,1)} %own_ref.1) | copy-start | bytes 3637252
  6.5 157.2 %all-gather.2.cloned.1.call-start = ((), (), s32[]{:S(2)}) async-start(), calls=%async_computation.2 | async-start | bytes 2621440 | tf_op jit(solution)/shard_map/weights/all_gather | solution.py:437
  7.7 11.7 %collective-permute-start = (bf16[2,16,4736]{2,1,0:T(8,128)(2,1)S(1)}, bf16[2,16,4736]{2,1,0:T(8,128)(2,1)S(1)}, u32[]{:S(2)}, u32[]{:S(2)}) collective-permute-start(bf16[2,16,4736]{2,1,0:T(8,128)(2,1)S(1)} %get-tuple-element.154), channel_id=1, source_target_pairs={{0,16},{16,32},{32,48},{48,64},{64,80},{80,96},{96,112},{1,17},{17... | collective-permute-start | bytes 909320 | tf_op jit(solution)/shard_map/halo/ppermute | solution.py:22
  9.7 9.7 %collective-permute-start.1 = (bf16[2,16,4736]{2,1,0:T(8,128)(2,1)S(1)}, bf16[2,16,4736]{2,1,0:T(8,128)(2,1)S(1)}, u32[]{:S(2)}, u32[]{:S(2)}) collective-permute-start(bf16[2,16,4736]{2,1,0:T(8,128)(2,1)S(1)} %get-tuple-element.153), channel_id=1, source_target_pairs={{16,0},{32,16},{48,32},{64,48},{80,64},{96,80},{112,96},{17,1},{33... | collective-permute-start | bytes 909320 | tf_op jit(solution)/shard_map/halo/ppermute | solution.py:23
  19.4 2.1 copy-start.21
  21.5 24.2 %collective-permute-start.10 = (bf16[21,104,128]{2,1,0:T(8,128)(2,1)S(1)}, bf16[21,104,128]{2,1,0:T(8,128)(2,1)S(1)}, u32[]{:S(2)}, u32[]{:S(2)}) collective-permute-start(bf16[21,104,128]{2,1,0:T(8,128)(2,1)S(1)} %get-tuple-element.92), channel_id=1, source_target_pairs={{0,15},{1,0},{2,1},{3,2},{4,3},{5,4},{6,5},{7,6},{8,7},{9,8},{10,9... | collective-permute-start | bytes 1677320 | tf_op jit(solution)/shard_map/ring/ppermute | solution.py:511
  32.9 19.4 %collective-permute-start.2 = (bf16[21,104,128]{2,1,0:T(8,128)(2,1)S(1)}, bf16[21,104,128]{2,1,0:T(8,128)(2,1)S(1)}, u32[]{:S(2)}, u32[]{:S(2)}) collective-permute-start(bf16[21,104,128]{2,1,0:T(8,128)(2,1)S(1)} %get-tuple-element.91), channel_id=1, source_target_pairs={{0,1},{1,2},{2,3},{3,4},{4,5},{5,6},{6,7},{7,8},{8,9},{9,10},{10,1... | collective-permute-start | bytes 1677320 | tf_op jit(solution)/shard_map/ring/ppermute | solution.py:508
  46.6 17.6 %collective-permute-start.11 = (bf16[21,104,128]{2,1,0:T(8,128)(2,1)S(1)}, bf16[21,104,128]{2,1,0:T(8,128)(2,1)S(1)}, u32[]{:S(2)}, u32[]{:S(2)}) collective-permute-start(bf16[21,104,128]{2,1,0:T(8,128)(2,1)S(1)} %ring.43), channel_id=1, source_target_pairs={{0,15},{1,0},{2,1},{3,2},{4,3},{5,4},{6,5},{7,6},{8,7},{9,8},{10,9... | collective-permute-start | bytes 1677320 | tf_op jit(solution)/shard_map/ring/ppermute | solution.py:511
  53.2 18.4 %collective-permute-start.3 = (bf16[21,104,128]{2,1,0:T(8,128)(2,1)S(1)}, bf16[21,104,128]{2,1,0:T(8,128)(2,1)S(1)}, u32[]{:S(2)}, u32[]{:S(2)}) collective-permute-start(bf16[21,104,128]{2,1,0:T(8,128)(2,1)S(1)} %ring.29), channel_id=1, source_target_pairs={{0,1},{1,2},{2,3},{3,4},{4,5},{5,6},{6,7},{7,8},{8,9},{9,10},{10,1... | collective-permute-start | bytes 1677320 | tf_op jit(solution)/shard_map/ring/ppermute | solution.py:508
  66.0 17.0 %collective-permute-start.12 = (bf16[21,104,128]{2,1,0:T(8,128)(2,1)}, bf16[21,104,128]{2,1,0:T(8,128)(2,1)}, u32[]{:S(2)}, u32[]{:S(2)}) collective-permute-start(bf16[21,104,128]{2,1,0:T(8,128)(2,1)} %ring.45), channel_id=1, source_target_pairs={{0,15},{1,0},{2,1},{3,2},{4,3},{5,4},{6,5},{7,6},{8,7},{9,8},{10,9... | collective-permute-start | bytes 1677320 | tf_op jit(solution)/shard_map/ring/ppermute | solution.py:511
  73.4 18.4 %collective-permute-start.4 = (bf16[21,104,128]{2,1,0:T(8,128)(2,1)}, bf16[21,104,128]{2,1,0:T(8,128)(2,1)}, u32[]{:S(2)}, u32[]{:S(2)}) collective-permute-start(bf16[21,104,128]{2,1,0:T(8,128)(2,1)} %ring.31), channel_id=1, source_target_pairs={{0,1},{1,2},{2,3},{3,4},{4,5},{5,6},{6,7},{7,8},{8,9},{9,10},{10,1... | collective-permute-start | bytes 1677320 | tf_op jit(solution)/shard_map/ring/ppermute | solution.py:508
  84.3 15.7 %collective-permute-start.13 = (bf16[21,104,128]{2,1,0:T(8,128)(2,1)S(1)}, bf16[21,104,128]{2,1,0:T(8,128)(2,1)S(1)}, u32[]{:S(2)}, u32[]{:S(2)}) collective-permute-start(bf16[21,104,128]{2,1,0:T(8,128)(2,1)S(1)} %ring.47), channel_id=1, source_target_pairs={{0,15},{1,0},{2,1},{3,2},{4,3},{5,4},{6,5},{7,6},{8,7},{9,8},{10,9... | collective-permute-start | bytes 1677320 | tf_op jit(solution)/shard_map/ring/ppermute | solution.py:511
  93.1 16.9 %collective-permute-start.5 = (bf16[21,104,128]{2,1,0:T(8,128)(2,1)S(1)}, bf16[21,104,128]{2,1,0:T(8,128)(2,1)S(1)}, u32[]{:S(2)}, u32[]{:S(2)}) collective-permute-start(bf16[21,104,128]{2,1,0:T(8,128)(2,1)S(1)} %ring.33), channel_id=1, source_target_pairs={{0,1},{1,2},{2,3},{3,4},{4,5},{5,6},{6,7},{7,8},{8,9},{9,10},{10,1... | collective-permute-start | bytes 1677320 | tf_op jit(solution)/shard_map/ring/ppermute | solution.py:508
  100.1 45.9 %copy-start = (bf16[21,104,128]{2,1,0:T(8,128)(2,1)}, bf16[21,104,128]{2,1,0:T(8,128)(2,1)S(1)}, u32[]{:S(2)}) copy-start(bf16[21,104,128]{2,1,0:T(8,128)(2,1)S(1)} %collective-permute-done.13.newest_ref.refs_3_.refs_12_) | copy-start | bytes 1677316
  101.0 15.2 %collective-permute-start.14 = (bf16[21,104,128]{2,1,0:T(8,128)(2,1)S(1)}, bf16[21,104,128]{2,1,0:T(8,128)(2,1)S(1)}, u32[]{:S(2)}, u32[]{:S(2)}) collective-permute-start(bf16[21,104,128]{2,1,0:T(8,128)(2,1)S(1)} %ring.49), channel_id=1, source_target_pairs={{0,15},{1,0},{2,1},{3,2},{4,3},{5,4},{6,5},{7,6},{8,7},{9,8},{10,9... | collective-permute-start | bytes 1677320 | tf_op jit(solution)/shard_map/ring/ppermute | solution.py:511
  110.0 37.8 %copy-start.2 = (bf16[21,104,128]{2,1,0:T(8,128)(2,1)}, bf16[21,104,128]{2,1,0:T(8,128)(2,1)S(1)}, u32[]{:S(2)}) copy-start(bf16[21,104,128]{2,1,0:T(8,128)(2,1)S(1)} %collective-permute-done.5.newest_ref.refs_3_.refs_4_) | copy-start | bytes 1677316
  111.0 16.1 %collective-permute-start.6 = (bf16[21,104,128]{2,1,0:T(8,128)(2,1)S(1)}, bf16[21,104,128]{2,1,0:T(8,128)(2,1)S(1)}, u32[]{:S(2)}, u32[]{:S(2)}) collective-permute-start(bf16[21,104,128]{2,1,0:T(8,128)(2,1)S(1)} %ring.35), channel_id=1, source_target_pairs={{0,1},{1,2},{2,3},{3,4},{4,5},{5,6},{6,7},{7,8},{8,9},{9,10},{10,1... | collective-permute-start | bytes 1677320 | tf_op jit(solution)/shard_map/ring/ppermute | solution.py:508
  116.3 29.8 %copy-start.4 = (bf16[21,104,128]{2,1,0:T(8,128)(2,1)}, bf16[21,104,128]{2,1,0:T(8,128)(2,1)S(1)}, u32[]{:S(2)}) copy-start(bf16[21,104,128]{2,1,0:T(8,128)(2,1)S(1)} %collective-permute-done.14.newest_ref.refs_4_.refs_13_) | copy-start | bytes 1677316
  117.2 16.0 %collective-permute-start.15 = (bf16[21,104,128]{2,1,0:T(8,128)(2,1)S(1)}, bf16[21,104,128]{2,1,0:T(8,128)(2,1)S(1)}, u32[]{:S(2)}, u32[]{:S(2)}) collective-permute-start(bf16[21,104,128]{2,1,0:T(8,128)(2,1)S(1)} %ring.51), channel_id=1, source_target_pairs={{0,15},{1,0},{2,1},{3,2},{4,3},{5,4},{6,5},{7,6},{8,7},{9,8},{10,9... | collective-permute-start | bytes 1677320 | tf_op jit(solution)/shard_map/ring/ppermute | solution.py:511
  127.0 20.8 %copy-start.6 = (bf16[21,104,128]{2,1,0:T(8,128)(2,1)}, bf16[21,104,128]{2,1,0:T(8,128)(2,1)S(1)}, u32[]{:S(2)}) copy-start(bf16[21,104,128]{2,1,0:T(8,128)(2,1)S(1)} %collective-permute-done.6.newest_ref.refs_4_.refs_5_) | copy-start | bytes 1677316
  128.0 15.1 %collective-permute-start.7 = (bf16[21,104,128]{2,1,0:T(8,128)(2,1)S(1)}, bf16[21,104,128]{2,1,0:T(8,128)(2,1)S(1)}, u32[]{:S(2)}, u32[]{:S(2)}) collective-permute-start(bf16[21,104,128]{2,1,0:T(8,128)(2,1)S(1)} %ring.37), channel_id=1, source_target_pairs={{0,1},{1,2},{2,3},{3,4},{4,5},{5,6},{6,7},{7,8},{8,9},{9,10},{10,1... | collective-permute-start | bytes 1677320 | tf_op jit(solution)/shard_map/ring/ppermute | solution.py:508
  133.3 14.6 %copy-start.8 = (bf16[21,104,128]{2,1,0:T(8,128)(2,1)}, bf16[21,104,128]{2,1,0:T(8,128)(2,1)S(1)}, u32[]{:S(2)}) copy-start(bf16[21,104,128]{2,1,0:T(8,128)(2,1)S(1)} %collective-permute-done.15.newest_ref.refs_5_.refs_14_) | copy-start | bytes 1677316
  134.2 15.4 %collective-permute-start.16 = (bf16[21,104,128]{2,1,0:T(8,128)(2,1)S(1)}, bf16[21,104,128]{2,1,0:T(8,128)(2,1)S(1)}, u32[]{:S(2)}, u32[]{:S(2)}) collective-permute-start(bf16[21,104,128]{2,1,0:T(8,128)(2,1)S(1)} %ring.53), channel_id=1, source_target_pairs={{0,15},{1,0},{2,1},{3,2},{4,3},{5,4},{6,5},{7,6},{8,7},{9,8},{10,9... | collective-permute-start | bytes 1677320 | tf_op jit(solution)/shard_map/ring/ppermute | solution.py:511
  143.1 4.7 %copy-start.10 = (bf16[21,104,128]{2,1,0:T(8,128)(2,1)}, bf16[21,104,128]{2,1,0:T(8,128)(2,1)S(1)}, u32[]{:S(2)}) copy-start(bf16[21,104,128]{2,1,0:T(8,128)(2,1)S(1)} %collective-permute-done.7.newest_ref.refs_5_.refs_6_) | copy-start | bytes 1677316
  144.1 15.2 %collective-permute-start.8 = (bf16[21,104,128]{2,1,0:T(8,128)(2,1)S(1)}, bf16[21,104,128]{2,1,0:T(8,128)(2,1)S(1)}, u32[]{:S(2)}, u32[]{:S(2)}) collective-permute-start(bf16[21,104,128]{2,1,0:T(8,128)(2,1)S(1)} %ring.39), channel_id=1, source_target_pairs={{0,1},{1,2},{2,3},{3,4},{4,5},{5,6},{6,7},{7,8},{8,9},{9,10},{10,1... | collective-permute-start | bytes 1677320 | tf_op jit(solution)/shard_map/ring/ppermute | solution.py:508
  149.6 13.3 %copy-start.16 = (bf16[2,64,4096]{2,1,0:T(8,128)(2,1)S(1)}, bf16[2,64,4096]{2,1,0:T(8,128)(2,1)}, u32[]{:S(2)}) copy-start(bf16[2,64,4096]{2,1,0:T(8,128)(2,1)} %refs_19_.1) | copy-start | bytes 3145732
  149.6 11.4 %copy-start.12 = (bf16[21,104,128]{2,1,0:T(8,128)(2,1)}, bf16[21,104,128]{2,1,0:T(8,128)(2,1)S(1)}, u32[]{:S(2)}) copy-start(bf16[21,104,128]{2,1,0:T(8,128)(2,1)S(1)} %collective-permute-done.16.newest_ref.refs_15_) | copy-start | bytes 1677316
  151.4 12.5 %collective-permute-start.17 = (bf16[21,104,128]{2,1,0:T(8,128)(2,1)}, bf16[21,104,128]{2,1,0:T(8,128)(2,1)}, u32[]{:S(2)}, u32[]{:S(2)}) collective-permute-start(bf16[21,104,128]{2,1,0:T(8,128)(2,1)} %ring.55), channel_id=1, source_target_pairs={{0,15},{1,0},{2,1},{3,2},{4,3},{5,4},{6,5},{7,6},{8,7},{9,8},{10,9... | collective-permute-start | bytes 1677320 | tf_op jit(solution)/shard_map/ring/ppermute | solution.py:511
  159.3 3.7 %copy-start.14 = (bf16[21,104,128]{2,1,0:T(8,128)(2,1)}, bf16[21,104,128]{2,1,0:T(8,128)(2,1)S(1)}, u32[]{:S(2)}) copy-start(bf16[21,104,128]{2,1,0:T(8,128)(2,1)S(1)} %collective-permute-done.8.newest_ref.refs_7_) | copy-start | bytes 1677316
  161.0 13.0 %collective-permute-start.9 = (bf16[21,104,128]{2,1,0:T(8,128)(2,1)}, bf16[21,104,128]{2,1,0:T(8,128)(2,1)}, u32[]{:S(2)}, u32[]{:S(2)}) collective-permute-start(bf16[21,104,128]{2,1,0:T(8,128)(2,1)} %ring.41), channel_id=1, source_target_pairs={{0,1},{1,2},{2,3},{3,4},{4,5},{5,6},{6,7},{7,8},{8,9},{9,10},{10,1... | collective-permute-start | bytes 1677320 | tf_op jit(solution)/shard_map/ring/ppermute | solution.py:508
  182.4 23.8 %copy-start.24 = (s32[512,2]{0,1:T(2,128)S(1)}, s32[512,2]{0,1:T(2,128)}, u32[]{:S(2)}) copy-start(s32[512,2]{0,1:T(2,128)} %param.12) | copy-start | bytes 12292
  190.0 26.3 %all-to-all-start.1 = ((f32[16,4,128]{2,1,0:T(4,128)}), f32[16,4,128]{2,1,0:T(4,128)S(1)}, u32[]{:S(2)}, u32[]{:S(2)}) async-start(f32[16,4,128]{2,1,0:T(4,128)} %broadcast_in_dim.55), calls=%async_computation.1 | async-start | bytes 65536 | tf_op jit(solution)/shard_map/finish/all_to_all | solution.py:537
  (10 other events, 11.0 us)
Sparse Core Ops, SparseCore 0:
  75.4 35.2 all-gather.1

commit v4 on v3

--- a/solution.py
+++ b/solution.py
@@ -34,11 +34,11 @@
     return pairs
 
 
-def ways(distance, block, vocab_count):
+def ways(distance, block, share, vocab_count):
     half = vocab_count // 2
-    even = block % 2 == 0
-    ahead = jnp.where((distance >= 1) & ((distance < half) | ((distance == half) & even)), distance, 0)
-    behind = jnp.where((distance > half) | ((distance == half) & ~even), vocab_count - distance, 0)
+    first = (block * 5) % 8 < share
+    ahead = jnp.where((distance >= 1) & ((distance < half) | ((distance == half) & first)), distance, 0)
+    behind = jnp.where((distance > half) | ((distance == half) & ~first), vocab_count - distance, 0)
     return ahead, behind
 
 
@@ -68,6 +68,7 @@
     row = lax.broadcasted_iota(i32, shape, 0)
 
     reach = [jnp.zeros(shape, i32), jnp.zeros(shape, i32)]
+    across = jnp.zeros(shape, i32)
     pair_lane = lax.broadcasted_iota(i32, (pair_count, BLK), 1)
     pair_row = lax.broadcasted_iota(i32, (vocab_count, pair_count), 0)
     for s in range(vocab_count):
@@ -78,17 +79,27 @@
         )
         distance = s - row
         distance = jnp.where(distance < 0, distance + vocab_count, distance)
-        for way, length in enumerate(ways(distance, lane, vocab_count)):
-            reach[way] = jnp.maximum(reach[way], jnp.where(hits > 0, length, 0))
+        needed = hits > 0
+        reach[0] = jnp.maximum(reach[0], jnp.where(needed & (distance < half), distance, 0))
+        reach[1] = jnp.maximum(reach[1], jnp.where(needed & (distance > half), vocab_count - distance, 0))
+        across = jnp.maximum(across, jnp.where(needed & (distance == half), 1, 0))
+    order_key = (lane * 5) % 8
+    share = jnp.zeros((1, 1), i32)
+    for part in range(1, 9):
+        first = (across > 0) & (order_key < part)
+        more = jnp.where(first, half, reach[0]) - jnp.where((across > 0) & ~first, half, reach[1])
+        more = jnp.sum(jnp.sum(more, axis=1, keepdims=True), axis=0, keepdims=True)
+        share = share + (more <= 0).astype(i32)
+    first = order_key < share
+    reach[0] = jnp.where((across > 0) & first, half, reach[0])
+    reach[1] = jnp.where((across > 0) & ~first, half, reach[1])
     reach = [jnp.where(lane == blocks, half - way, reach[way]) for way in range(2)]
 
     square = (BLK, BLK)
-    up, across = lax.broadcasted_iota(i32, square, 0), lax.broadcasted_iota(i32, square, 1)
-    earlier = ones(up < across)
-    left_up, left_across = (up & 7) + 1 - (up >> 3), (across & 7) + 1 - (across >> 3)
-    goes_first = ones(
-        (left_up > left_across) | ((left_up == left_across) & ((up >> 3) > (across >> 3)))
-    )
+    up, over = lax.broadcasted_iota(i32, square, 0), lax.broadcasted_iota(i32, square, 1)
+    earlier = ones(up < over)
+    left_up, left_over = (up & 7) + 1 - (up >> 3), (over & 7) + 1 - (over >> 3)
+    goes_first = ones((left_up > left_over) | ((left_up == left_over) & ((up >> 3) > (over >> 3))))
     index, waiting, moved = [], [], [jnp.zeros(shape, f32)] * 2
     for way in range(2):
         masks = jnp.concatenate([ones(reach[way] == r) for r in range(1, half + 1)], axis=0)
@@ -173,7 +184,7 @@
     inner = jnp.sum(jnp.where(pair_lane == me, inners, 0), axis=1, keepdims=True)
     distance = me - holder
     distance = jnp.where(distance < 0, distance + vocab_count, distance)
-    hops = ways(distance, inner, vocab_count)
+    hops = ways(distance, inner, share, vocab_count)
     scale = jnp.where(distance <= half, distance, 2 * vocab_count - distance)
     points = jnp.zeros((pair_count, 1), f32)
     for way in range(2):
@@ -221,6 +232,11 @@
     item_ref[2:3, :] = jnp.sum(jnp.where(rank == item_lane, item_up, 0), axis=0, keepdims=True)
     item_ref[3:4, :] = jnp.sum((source < item_lane).astype(i32), axis=0, keepdims=True)
     item_ref[4:8, :] = jnp.zeros((4, BLK), i32)
+
+
+def scalars(table_ref, row, start, count):
+    values = table_ref[row : row + 1, :]
+    return [values[0, start + j] for j in range(count)]
 
 
 def pack_kernel(send_ref, own_ref, low_ref, high_ref, pick_ref, home_ref, first_ref, second_ref, cand_ref, logit_ref):
@@ -253,19 +269,17 @@
     home_ref[blocks] = jnp.where(
         lane == 0, top, jnp.where(lane == 1, first, jnp.where(lane == 2, second, jnp.where(lane == 3, third, 0.0)))
     ).astype(jnp.bfloat16)
-    for j in range(SLOTS):
-        first_ref[j] = home_ref[send_ref[0, j]]
-        second_ref[j] = home_ref[send_ref[1, j]]
+    for chain, out_ref in enumerate((first_ref, second_ref)):
+        for j, at in enumerate(scalars(send_ref, chain, 0, SLOTS)):
+            out_ref[j] = home_ref[at]
 
 
 def ready_kernel(chain, step, send_ref, home_ref, *refs):
     frames, out_ref = refs[:-1], refs[-1]
     home = home_ref.shape[0]
-
-    def choose(j, carry):
-        at = send_ref[chain, step * SLOTS + j]
-
-        def copy(low, high):
+    for j, at in enumerate(scalars(send_ref, chain, step * SLOTS, SLOTS)):
+
+        def copy(low, high, j=j, at=at):
             if high - low == 1:
                 if low == 0:
                     out_ref[j] = home_ref[at]
@@ -278,22 +292,28 @@
             pl.when(at >= split)(lambda: copy(mid, high))
 
         copy(0, len(frames) + 2)
+
+
+def pass_kernel(chain, step, home, send_ref, part_ref, newest_ref, out_ref):
+    start = home + (step - 1) * SLOTS
+    for j, at in enumerate(scalars(send_ref, chain, step * SLOTS, SLOTS)):
+        newest = newest_ref[jnp.maximum(at - start, 0)]
+        out_ref[j] = jnp.where(at >= start, newest, part_ref[j])
+
+
+def stage_kernel(steps, item_ref, *refs):
+    sources, stage_ref = refs[:-1], refs[-1]
+    for s, source in zip([s for s in range(2 * steps + 1) if s not in (steps, 2 * steps)], sources):
+        bring(item_ref, s, source, stage_ref)
+
+
+def bring(item_ref, s, source_ref, stage_ref):
+    def one(q, carry):
+        item = item_ref[2, q]
+        stage_ref[item] = source_ref[item_ref[0, item]]
         return carry
 
-    lax.fori_loop(0, SLOTS, choose, 0)
-
-
-def pass_kernel(chain, step, home, send_ref, part_ref, newest_ref, out_ref):
-    for j in range(SLOTS):
-        at = send_ref[chain, step * SLOTS + j] - (home + (step - 1) * SLOTS)
-
-        @pl.when(at >= 0)
-        def _(j=j, at=at):
-            out_ref[j] = newest_ref[at]
-
-        @pl.when(at < 0)
-        def _(j=j):
-            out_ref[j] = part_ref[j]
+    lax.fori_loop(item_ref[3, s], item_ref[3, s + 1], one, 0)
 
 
 def student_kernel(student_ref, top_ref, total_ref):
@@ -312,21 +332,29 @@
     total_ref[...] = jnp.broadcast_to(jnp.sum(total, axis=1, keepdims=True), (rows, BLK))
 
 
-def map_kernel(steps, item_ref, *refs):
-    sources = refs[: 2 * steps + 1]
-    spread_ref, weight_ref, student_ref, top_ref, total_ref, out_ref, stage_ref, scale_ref = refs[2 * steps + 1 :]
+def map_kernel(
+    steps,
+    item_ref,
+    held_ref,
+    ahead_ref,
+    behind_ref,
+    spread_ref,
+    weight_ref,
+    student_ref,
+    top_ref,
+    total_ref,
+    out_ref,
+    stage_ref,
+    scale_ref,
+):
     docs, positions, columns = student_ref.shape
     rows = docs * positions
     blocks = columns // BLK
     spread = spread_ref[...]
-    for s, source in enumerate(sources):
-
-        def bring(q, carry, source=source):
-            item = item_ref[2, q]
-            stage_ref[item] = source[item_ref[0, item]]
-            return carry
-
-        lax.fori_loop(item_ref[3, s], item_ref[3, s + 1], bring, 0)
+    for i in range(stage_ref.shape[0]):
+        stage_ref[i] = held_ref[i]
+    bring(item_ref, steps, ahead_ref, stage_ref)
+    bring(item_ref, 2 * steps, behind_ref, stage_ref)
     holders = [h for h in range(steps + 1)] + [2 * steps + h for h in range(1, steps)]
     peaks, sums = [], []
     for h in holders:
@@ -474,7 +502,7 @@
         own, ahead, behind = pl.pallas_call(
             pack_kernel,
             out_shape=(planes(home), planes(SLOTS), planes(SLOTS)),
-            in_specs=[smem] + [vmem] * 4,
+            in_specs=[vmem] * 5,
             out_specs=(vmem,) * 3,
             scratch_shapes=[
                 pltpu.VMEM((doc_count * span, teacher_cols), jnp.bfloat16),
@@ -487,14 +515,14 @@
         part = pl.pallas_call(
             functools.partial(ready_kernel, chain, step),
             out_shape=planes(SLOTS),
-            in_specs=[smem] + [vmem] * len(frames),
+            in_specs=[vmem] * (1 + len(frames)),
             out_specs=vmem,
             compiler_params=room(12),
         )(send, own, *frames[:-1])
         return pl.pallas_call(
             functools.partial(pass_kernel, chain, step, home),
             out_shape=planes(SLOTS),
-            in_specs=[smem] + [vmem] * 2,
+            in_specs=[vmem] * 3,
             out_specs=vmem,
             compiler_params=room(8),
         )(send, part, frames[-1])
@@ -519,21 +547,31 @@
             compiler_params=room(16),
         )(student_logits)
 
+    with jax.named_scope("stage"):
+        early = (own, *came_ahead[:-1], *came_behind[:-1])
+        held = pl.pallas_call(
+            functools.partial(stage_kernel, steps),
+            out_shape=planes(pair_count + 2 * vocab_count),
+            in_specs=[smem] + [vmem] * len(early),
+            out_specs=vmem,
+            compiler_params=room(20),
+        )(items, *early)
+
     with jax.named_scope("map"):
-        held = pl.pallas_call(
+        sums = pl.pallas_call(
             functools.partial(map_kernel, steps),
             out_shape=jax.ShapeDtypeStruct((8, row_count), jnp.float32),
-            in_specs=[smem] + [vmem] * (2 * steps + 1 + 5),
+            in_specs=[smem] + [vmem] * 8,
             out_specs=vmem,
             scratch_shapes=[
                 pltpu.VMEM((pair_count + 2 * vocab_count, ROWS, BLK), jnp.bfloat16),
                 pltpu.VMEM((3 * steps, row_count, BLK), jnp.float32),
             ],
-            compiler_params=room(20),
-        )(items, own, *came_ahead, *came_behind, spread, weights, student_logits, top, total)
+            compiler_params=room(16),
+        )(items, held, came_ahead[-1], came_behind[-1], spread, weights, student_logits, top, total)
 
     with jax.named_scope("finish"):
-        sent = jnp.broadcast_to(held[None, :4], (vocab_count, 4, row_count))
+        sent = jnp.broadcast_to(sums[None, :4], (vocab_count, 4, row_count))
         parts = lax.all_to_all(sent, "vocab", split_axis=0, concat_axis=0, tiled=True)
         mass_part, cross_part, top_part, total_part = (parts[:, i] for i in range(4))
         student_top = jnp.max(top_part, axis=0)

time: 226 us -> 211 us (0.934)
  Pallas kernels: 50.9 us -> 38.7 us
  local copies, waits for them, and re-layouts: 12.6 us -> 7.29 us
  waiting for transfers between devices: 59.2 us -> 61.6 us
    pallas_call x14, Pallas kernels: 17.4 us -> 9.1 us  [chosen(): pl.pallas_call(functools.partial(pass_kernel, chain, step, home), out_sha...]
    ppermute x8, waiting for transfers between devices: 22.8 us -> 29.8 us  [shards(): came_behind.append(lax.ppermute(behind, ('seq', 'vocab'), backward))]
    unnamed x45 -> x17, local copies, waits for them, and re-layouts: 9.88 us -> 4.6 us
    ppermute x8, waiting for transfers between devices: 26.3 us -> 21.8 us  [shards(): came_ahead.append(lax.ppermute(ahead, ('seq', 'vocab'), forward))]
    pallas_call x14, Pallas kernels: 20.1 us -> 15.9 us  [chosen(): pl.pallas_call(functools.partial(ready_kernel, chain, step), out_shape=pl...]
    pallas_call x0 -> x1, Pallas kernels: none -> 2.47 us  [shards(): pl.pallas_call(functools.partial(stage_kernel, steps), out_shape=planes(p...]
  transfers between devices with their start and end apart: 20 -> 20, of which waited for: 12 -> 12; matrix products, arithmetic and copies ran while one was open for 2% -> 2% of each run, Pallas kernels for 19% -> 15%
where the time goes in v4:
time: 211 us; the launch traced here: 210 us
  starting transfers between devices  84.7 us (40%)
  waiting for transfers between devices  61.6 us (29%)
  Pallas kernels  38.7 us (18%)
  between operations  15.2 us (7%)
  local copies, waits for them, and re-layouts  7.29 us (3%)
    ppermute x8, starting transfers between devices, shards(): came_behind.append(lax.ppermute(behind, ('seq', 'vocab'), backward))  49.7 us
    ppermute x8, waiting for transfers between devices, shards(): came_behind.append(lax.ppermute(behind, ('seq', 'vocab'), backward))  29.8 us
    ppermute x8, waiting for transfers between devices, shards(): came_ahead.append(lax.ppermute(ahead, ('seq', 'vocab'), forward))  21.8 us
    pallas_call x14, Pallas kernels, chosen(): pl.pallas_call(functools.partial(ready_kernel, chain, step), out_shape=pl...  15.9 us
    ppermute x8, starting transfers between devices, shards(): came_ahead.append(lax.ppermute(ahead, ('seq', 'vocab'), forward))  15.3 us
    all_to_all x1, starting transfers between devices, shards(): lax.all_to_all(sent, 'vocab', split_axis=0, concat_axis=0, tiled=True)  14.2 us
    all_to_all x1, waiting for transfers between devices, shards(): lax.all_to_all(sent, 'vocab', split_axis=0, concat_axis=0, tiled=True)  10 us
    pallas_call x14, Pallas kernels, chosen(): pl.pallas_call(functools.partial(pass_kernel, chain, step, home), out_sha...  9.1 us
  transfers between devices with their start and end apart: 20, of which 12 were waited for; matrix products, arithmetic and copies ran while one was open for 2% of the time, Pallas kernels for 15%

profile of v4, /device:TPU:6, one launch (start us, length us, event | category | flops | bytes accessed | tf_op | source)
XLA Modules:
  0.0 209.6 jit_solution(5375462231555888744)
XLA Ops:
  7.7 1.9 collective-permute-start
  9.7 3.6 %collective-permute-start.1 = (bf16[2,16,4736]{2,1,0:T(8,128)(2,1)S(1)}, bf16[2,16,4736]{2,1,0:T(8,128)(2,1)S(1)}, u32[]{:S(2)}, u32[]{:S(2)}) collective-permute-start(bf16[2,16,4736]{2,1,0:T(8,128)(2,1)S(1)} %get-tuple-element.153), channel_id=1, source_target_pairs={{16,0},{32,16},{48,32},{64,48},{80,64},{96,80},{112,96},{17,1},{33... | collective-permute-start | bytes 909320 | tf_op jit(solution)/shard_map/halo/ppermute | solution.py:23
  15.4 4.0 %plan.1 = (s32[8,256]{1,0:T(8,128)S(1)}, s32[8,128]{1,0:T(8,128)S(1)}, s32[8,128]{1,0:T(8,128)S(1)}) custom-call(s32[2]{0:T(128)S(1)} %pad_add_fusion.place_ref, s32[16,64]{1,0:T(8,128)S(1)} %reshape.251.listed_ref), custom_call_target="tpu_custom_call" | custom-call | tf_op jit(solution)/shard_map/plan/pallas_call | solution.py:489
  20.9 11.4 %collective-permute-start.9 = (bf16[21,104,128]{2,1,0:T(8,128)(2,1)S(1)}, bf16[21,104,128]{2,1,0:T(8,128)(2,1)S(1)}, u32[]{:S(2)}, u32[]{:S(2)}) collective-permute-start(bf16[21,104,128]{2,1,0:T(8,128)(2,1)S(1)} %get-tuple-element.92), channel_id=1, source_target_pairs={{0,15},{1,0},{2,1},{3,2},{4,3},{5,4},{6,5},{7,6},{8,7},{9,8},{10,9... | collective-permute-start | bytes 1677320 | tf_op jit(solution)/shard_map/ring/ppermute | solution.py:539
  32.3 1.9 collective-permute-start.2
  34.8 10.3 %collective-permute-done.9.newest_ref.refs_0_.refs_8_ = bf16[21,104,128]{2,1,0:T(8,128)(2,1)S(1)} collective-permute-done((bf16[21,104,128]{2,1,0:T(8,128)(2,1)S(1)}, bf16[21,104,128]{2,1,0:T(8,128)(2,1)S(1)}, u32[]{:S(2)}, u32[]{:S(2)}) %collective-permute-start.9) | collective-permute-done | bytes 559136 | tf_op jit(solution)/shard_map/ring/ppermute | solution.py:539
  45.4 5.6 %collective-permute-start.10 = (bf16[21,104,128]{2,1,0:T(8,128)(2,1)S(1)}, bf16[21,104,128]{2,1,0:T(8,128)(2,1)S(1)}, u32[]{:S(2)}, u32[]{:S(2)}) collective-permute-start(bf16[21,104,128]{2,1,0:T(8,128)(2,1)S(1)} %ring.41), channel_id=1, source_target_pairs={{0,15},{1,0},{2,1},{3,2},{4,3},{5,4},{6,5},{7,6},{8,7},{9,8},{10,9... | collective-permute-start | bytes 1677320 | tf_op jit(solution)/shard_map/ring/ppermute | solution.py:539
  51.3 1.9 collective-permute-start.3
  54.0 8.9 %collective-permute-done.10.newest_ref.refs_1_.refs_9_ = bf16[21,104,128]{2,1,0:T(8,128)(2,1)S(1)} collective-permute-done((bf16[21,104,128]{2,1,0:T(8,128)(2,1)S(1)}, bf16[21,104,128]{2,1,0:T(8,128)(2,1)S(1)}, u32[]{:S(2)}, u32[]{:S(2)}) %collective-permute-start.10) | collective-permute-done | bytes 559136 | tf_op jit(solution)/shard_map/ring/ppermute | solution.py:539
  64.0 5.6 %collective-permute-start.11 = (bf16[21,104,128]{2,1,0:T(8,128)(2,1)}, bf16[21,104,128]{2,1,0:T(8,128)(2,1)}, u32[]{:S(2)}, u32[]{:S(2)}) collective-permute-start(bf16[21,104,128]{2,1,0:T(8,128)(2,1)} %ring.43), channel_id=1, source_target_pairs={{0,15},{1,0},{2,1},{3,2},{4,3},{5,4},{6,5},{7,6},{8,7},{9,8},{10,9... | collective-permute-start | bytes 1677320 | tf_op jit(solution)/shard_map/ring/ppermute | solution.py:539
  70.7 1.9 collective-permute-start.4
  73.5 7.4 %collective-permute-done.11.newest_ref.refs_2_.refs_10_ = bf16[21,104,128]{2,1,0:T(8,128)(2,1)} collective-permute-done((bf16[21,104,128]{2,1,0:T(8,128)(2,1)}, bf16[21,104,128]{2,1,0:T(8,128)(2,1)}, u32[]{:S(2)}, u32[]{:S(2)}) %collective-permute-start.11) | collective-permute-done | bytes 559136 | tf_op jit(solution)/shard_map/ring/ppermute | solution.py:539
  82.3 5.6 %collective-permute-start.12 = (bf16[21,104,128]{2,1,0:T(8,128)(2,1)S(1)}, bf16[21,104,128]{2,1,0:T(8,128)(2,1)S(1)}, u32[]{:S(2)}, u32[]{:S(2)}) collective-permute-start(bf16[21,104,128]{2,1,0:T(8,128)(2,1)S(1)} %ring.45), channel_id=1, source_target_pairs={{0,15},{1,0},{2,1},{3,2},{4,3},{5,4},{6,5},{7,6},{8,7},{9,8},{10,9... | collective-permute-start | bytes 1677320 | tf_op jit(solution)/shard_map/ring/ppermute | solution.py:539
  90.3 1.9 collective-permute-start.5
  95.5 2.5 %collective-permute-done.12.newest_ref.refs_3_.refs_11_ = bf16[21,104,128]{2,1,0:T(8,128)(2,1)S(1)} collective-permute-done((bf16[21,104,128]{2,1,0:T(8,128)(2,1)S(1)}, bf16[21,104,128]{2,1,0:T(8,128)(2,1)S(1)}, u32[]{:S(2)}, u32[]{:S(2)}) %collective-permute-start.12) | collective-permute-done | bytes 559136 | tf_op jit(solution)/shard_map/ring/ppermute | solution.py:539
  98.3 5.6 %collective-permute-start.13 = (bf16[21,104,128]{2,1,0:T(8,128)(2,1)S(1)}, bf16[21,104,128]{2,1,0:T(8,128)(2,1)S(1)}, u32[]{:S(2)}, u32[]{:S(2)}) collective-permute-start(bf16[21,104,128]{2,1,0:T(8,128)(2,1)S(1)} %ring.47), channel_id=1, source_target_pairs={{0,15},{1,0},{2,1},{3,2},{4,3},{5,4},{6,5},{7,6},{8,7},{9,8},{10,9... | collective-permute-start | bytes 1677320 | tf_op jit(solution)/shard_map/ring/ppermute | solution.py:539
  103.9 3.0 %collective-permute-done.5.newest_ref.refs_3_.refs_4_ = bf16[21,104,128]{2,1,0:T(8,128)(2,1)S(1)} collective-permute-done((bf16[21,104,128]{2,1,0:T(8,128)(2,1)S(1)}, bf16[21,104,128]{2,1,0:T(8,128)(2,1)S(1)}, u32[]{:S(2)}, u32[]{:S(2)}) %collective-permute-start.5) | collective-permute-done | bytes 559136 | tf_op jit(solution)/shard_map/ring/ppermute | solution.py:536
  107.2 1.9 collective-permute-start.6
  113.5 5.6 %collective-permute-start.14 = (bf16[21,104,128]{2,1,0:T(8,128)(2,1)S(1)}, bf16[21,104,128]{2,1,0:T(8,128)(2,1)S(1)}, u32[]{:S(2)}, u32[]{:S(2)}) collective-permute-start(bf16[21,104,128]{2,1,0:T(8,128)(2,1)S(1)} %ring.49), channel_id=1, source_target_pairs={{0,15},{1,0},{2,1},{3,2},{4,3},{5,4},{6,5},{7,6},{8,7},{9,8},{10,9... | collective-permute-start | bytes 1677320 | tf_op jit(solution)/shard_map/ring/ppermute | solution.py:539
  119.1 4.0 %collective-permute-done.6.newest_ref.refs_4_.refs_5_ = bf16[21,104,128]{2,1,0:T(8,128)(2,1)S(1)} collective-permute-done((bf16[21,104,128]{2,1,0:T(8,128)(2,1)S(1)}, bf16[21,104,128]{2,1,0:T(8,128)(2,1)S(1)}, u32[]{:S(2)}, u32[]{:S(2)}) %collective-permute-start.6) | collective-permute-done | bytes 559136 | tf_op jit(solution)/shard_map/ring/ppermute | solution.py:536
  123.4 1.9 collective-permute-start.7
  128.9 5.1 %collective-permute-start.15 = (bf16[21,104,128]{2,1,0:T(8,128)(2,1)S(1)}, bf16[21,104,128]{2,1,0:T(8,128)(2,1)S(1)}, u32[]{:S(2)}, u32[]{:S(2)}) collective-permute-start(bf16[21,104,128]{2,1,0:T(8,128)(2,1)S(1)} %ring.51), channel_id=1, source_target_pairs={{0,15},{1,0},{2,1},{3,2},{4,3},{5,4},{6,5},{7,6},{8,7},{9,8},{10,9... | collective-permute-start | bytes 1677320 | tf_op jit(solution)/shard_map/ring/ppermute | solution.py:539
  134.0 4.3 %collective-permute-done.7.newest_ref.refs_6_.refs_5_ = bf16[21,104,128]{2,1,0:T(8,128)(2,1)S(1)} collective-permute-done((bf16[21,104,128]{2,1,0:T(8,128)(2,1)S(1)}, bf16[21,104,128]{2,1,0:T(8,128)(2,1)S(1)}, u32[]{:S(2)}, u32[]{:S(2)}) %collective-permute-start.7) | collective-permute-done | bytes 559136 | tf_op jit(solution)/shard_map/ring/ppermute | solution.py:536
  138.6 1.9 collective-permute-start.8
  145.3 5.1 %collective-permute-start.17 = (bf16[21,104,128]{2,1,0:T(8,128)(2,1)}, bf16[21,104,128]{2,1,0:T(8,128)(2,1)}, u32[]{:S(2)}, u32[]{:S(2)}) collective-permute-start(bf16[21,104,128]{2,1,0:T(8,128)(2,1)} %ring.55), channel_id=1, source_target_pairs={{0,15},{1,0},{2,1},{3,2},{4,3},{5,4},{6,5},{7,6},{8,7},{9,8},{10,9... | collective-permute-start | bytes 1677320 | tf_op jit(solution)/shard_map/ring/ppermute | solution.py:539
  150.4 3.2 %collective-permute-done.8.refs_7_.newest_ref = bf16[21,104,128]{2,1,0:T(8,128)(2,1)S(1)} collective-permute-done((bf16[21,104,128]{2,1,0:T(8,128)(2,1)S(1)}, bf16[21,104,128]{2,1,0:T(8,128)(2,1)S(1)}, u32[]{:S(2)}, u32[]{:S(2)}) %collective-permute-start.8) | collective-permute-done | bytes 559136 | tf_op jit(solution)/shard_map/ring/ppermute | solution.py:536
  154.7 1.9 collective-permute-start.16
  157.4 2.5 %stage.1.held_ref = bf16[96,104,128]{2,1,0:T(8,128)(2,1)S(1)} custom-call(s32[8,128]{1,0:T(8,128)S(1)} %get-tuple-element.88.item_ref, bf16[38,104,128]{2,1,0:T(8,128)(2,1)S(1)} %get-tuple-element.90.home_ref.refs_0_, bf16[21,104,128]{2,1,0:T(8,128)(2,1)S(1)} %collective-permute-done.2.newest_ref.refs_0_.refs_1_, ...), custom_call_target="tpu_custom_call" | custom-call | tf_op jit(solution)/shard_map/stage/pallas_call | solution.py:552
  161.3 6.3 %collective-permute-done.16.ahead_ref = bf16[21,104,128]{2,1,0:T(8,128)(2,1)} collective-permute-done((bf16[21,104,128]{2,1,0:T(8,128)(2,1)}, bf16[21,104,128]{2,1,0:T(8,128)(2,1)}, u32[]{:S(2)}, u32[]{:S(2)}) %collective-permute-start.16) | collective-permute-done | bytes 559136 | tf_op jit(solution)/shard_map/ring/ppermute | solution.py:536
  169.3 5.3 %map.1 = f32[8,128]{1,0:T(8,128)S(1)} custom-call(s32[8,128]{1,0:T(8,128)S(1)} %get-tuple-element.88.item_ref, bf16[96,104,128]{2,1,0:T(8,128)(2,1)S(1)} %copy-done.1, bf16[21,104,128]{2,1,0:T(8,128)(2,1)} %collective-permute-done.16.ahead_ref, bf16[21,104,128]{2,1,0:T(8,128)(2,1)} %collective-permute-done.17.behind_ref, ...), custom_call_target="tpu_custom_call" | custom-call | tf_op jit(solution)/shard_map/map/pallas_call | solution.py:561
  175.3 14.2 %all-to-all-start.1 = ((f32[16,4,128]{2,1,0:T(4,128)}), f32[16,4,128]{2,1,0:T(4,128)S(1)}, u32[]{:S(2)}, u32[]{:S(2)}) async-start(f32[16,4,128]{2,1,0:T(4,128)} %broadcast_in_dim.55), calls=%async_computation.1 | async-start | bytes 65536 | tf_op jit(solution)/shard_map/finish/all_to_all | solution.py:575
  191.9 10.0 %all-to-all-done.1 = f32[16,4,128]{2,1,0:T(4,128)S(1)} async-done(((f32[16,4,128]{2,1,0:T(4,128)}), f32[16,4,128]{2,1,0:T(4,128)S(1)}, u32[]{:S(2)}, u32[]{:S(2)}) %all-to-all-start.1) | async-done | bytes 32800 | tf_op jit(solution)/shard_map/finish/all_to_all | solution.py:575
  (83 shorter events, 38.1 us)
Async XLA Ops:
  6.5 13.0 %copy-start.5 = (bf16[2,64,4736]{2,1,0:T(8,128)(2,1)S(1)}, bf16[2,64,4736]{2,1,0:T(8,128)(2,1)}, u32[]{:S(2)}) copy-start(bf16[2,64,4736]{2,1,0:T(8,128)(2,1)} %own_ref.1) | copy-start | bytes 3637252
  6.5 154.8 %all-gather.2.cloned.1.call-start = ((), (), s32[]{:S(2)}) async-start(), calls=%async_computation.2 | async-start | bytes 2621440 | tf_op jit(solution)/shard_map/weights/all_gather | solution.py:465
  7.7 11.8 %collective-permute-start = (bf16[2,16,4736]{2,1,0:T(8,128)(2,1)S(1)}, bf16[2,16,4736]{2,1,0:T(8,128)(2,1)S(1)}, u32[]{:S(2)}, u32[]{:S(2)}) collective-permute-start(bf16[2,16,4736]{2,1,0:T(8,128)(2,1)S(1)} %get-tuple-element.154), channel_id=1, source_target_pairs={{0,16},{16,32},{32,48},{48,64},{64,80},{80,96},{96,112},{1,17},{17... | collective-permute-start | bytes 909320 | tf_op jit(solution)/shard_map/halo/ppermute | solution.py:22
  9.7 9.9 %collective-permute-start.1 = (bf16[2,16,4736]{2,1,0:T(8,128)(2,1)S(1)}, bf16[2,16,4736]{2,1,0:T(8,128)(2,1)S(1)}, u32[]{:S(2)}, u32[]{:S(2)}) collective-permute-start(bf16[2,16,4736]{2,1,0:T(8,128)(2,1)S(1)} %get-tuple-element.153), channel_id=1, source_target_pairs={{16,0},{32,16},{48,32},{64,48},{80,64},{96,80},{112,96},{17,1},{33... | collective-permute-start | bytes 909320 | tf_op jit(solution)/shard_map/halo/ppermute | solution.py:23
  19.5 15.2 %copy-start.7 = (bf16[2,16,4736]{2,1,0:T(8,128)(2,1)}, bf16[2,16,4736]{2,1,0:T(8,128)(2,1)S(1)}, u32[]{:S(2)}) copy-start(bf16[2,16,4736]{2,1,0:T(8,128)(2,1)S(1)} %collective-permute-done.low_ref) | copy-start | bytes 909316
  19.5 15.2 %copy-start.9 = (bf16[2,16,4736]{2,1,0:T(8,128)(2,1)}, bf16[2,16,4736]{2,1,0:T(8,128)(2,1)S(1)}, u32[]{:S(2)}) copy-start(bf16[2,16,4736]{2,1,0:T(8,128)(2,1)S(1)} %collective-permute-done.1.high_ref) | copy-start | bytes 909316
  20.9 24.2 %collective-permute-start.9 = (bf16[21,104,128]{2,1,0:T(8,128)(2,1)S(1)}, bf16[21,104,128]{2,1,0:T(8,128)(2,1)S(1)}, u32[]{:S(2)}, u32[]{:S(2)}) collective-permute-start(bf16[21,104,128]{2,1,0:T(8,128)(2,1)S(1)} %get-tuple-element.92), channel_id=1, source_target_pairs={{0,15},{1,0},{2,1},{3,2},{4,3},{5,4},{6,5},{7,6},{8,7},{9,8},{10,9... | collective-permute-start | bytes 1677320 | tf_op jit(solution)/shard_map/ring/ppermute | solution.py:539
  32.3 18.7 %collective-permute-start.2 = (bf16[21,104,128]{2,1,0:T(8,128)(2,1)S(1)}, bf16[21,104,128]{2,1,0:T(8,128)(2,1)S(1)}, u32[]{:S(2)}, u32[]{:S(2)}) collective-permute-start(bf16[21,104,128]{2,1,0:T(8,128)(2,1)S(1)} %get-tuple-element.91), channel_id=1, source_target_pairs={{0,1},{1,2},{2,3},{3,4},{4,5},{5,6},{6,7},{7,8},{8,9},{9,10},{10,1... | collective-permute-start | bytes 1677320 | tf_op jit(solution)/shard_map/ring/ppermute | solution.py:536
  45.4 17.5 %collective-permute-start.10 = (bf16[21,104,128]{2,1,0:T(8,128)(2,1)S(1)}, bf16[21,104,128]{2,1,0:T(8,128)(2,1)S(1)}, u32[]{:S(2)}, u32[]{:S(2)}) collective-permute-start(bf16[21,104,128]{2,1,0:T(8,128)(2,1)S(1)} %ring.41), channel_id=1, source_target_pairs={{0,15},{1,0},{2,1},{3,2},{4,3},{5,4},{6,5},{7,6},{8,7},{9,8},{10,9... | collective-permute-start | bytes 1677320 | tf_op jit(solution)/shard_map/ring/ppermute | solution.py:539
  51.3 18.3 %collective-permute-start.3 = (bf16[21,104,128]{2,1,0:T(8,128)(2,1)S(1)}, bf16[21,104,128]{2,1,0:T(8,128)(2,1)S(1)}, u32[]{:S(2)}, u32[]{:S(2)}) collective-permute-start(bf16[21,104,128]{2,1,0:T(8,128)(2,1)S(1)} %ring.29), channel_id=1, source_target_pairs={{0,1},{1,2},{2,3},{3,4},{4,5},{5,6},{6,7},{7,8},{8,9},{9,10},{10,1... | collective-permute-start | bytes 1677320 | tf_op jit(solution)/shard_map/ring/ppermute | solution.py:536
  64.0 17.0 %collective-permute-start.11 = (bf16[21,104,128]{2,1,0:T(8,128)(2,1)}, bf16[21,104,128]{2,1,0:T(8,128)(2,1)}, u32[]{:S(2)}, u32[]{:S(2)}) collective-permute-start(bf16[21,104,128]{2,1,0:T(8,128)(2,1)} %ring.43), channel_id=1, source_target_pairs={{0,15},{1,0},{2,1},{3,2},{4,3},{5,4},{6,5},{7,6},{8,7},{9,8},{10,9... | collective-permute-start | bytes 1677320 | tf_op jit(solution)/shard_map/ring/ppermute | solution.py:539
  70.7 18.3 %collective-permute-start.4 = (bf16[21,104,128]{2,1,0:T(8,128)(2,1)}, bf16[21,104,128]{2,1,0:T(8,128)(2,1)}, u32[]{:S(2)}, u32[]{:S(2)}) collective-permute-start(bf16[21,104,128]{2,1,0:T(8,128)(2,1)} %ring.31), channel_id=1, source_target_pairs={{0,1},{1,2},{2,3},{3,4},{4,5},{5,6},{6,7},{7,8},{8,9},{9,10},{10,1... | collective-permute-start | bytes 1677320 | tf_op jit(solution)/shard_map/ring/ppermute | solution.py:536
  82.3 15.7 %collective-permute-start.12 = (bf16[21,104,128]{2,1,0:T(8,128)(2,1)S(1)}, bf16[21,104,128]{2,1,0:T(8,128)(2,1)S(1)}, u32[]{:S(2)}, u32[]{:S(2)}) collective-permute-start(bf16[21,104,128]{2,1,0:T(8,128)(2,1)S(1)} %ring.45), channel_id=1, source_target_pairs={{0,15},{1,0},{2,1},{3,2},{4,3},{5,4},{6,5},{7,6},{8,7},{9,8},{10,9... | collective-permute-start | bytes 1677320 | tf_op jit(solution)/shard_map/ring/ppermute | solution.py:539
  90.3 16.7 %collective-permute-start.5 = (bf16[21,104,128]{2,1,0:T(8,128)(2,1)S(1)}, bf16[21,104,128]{2,1,0:T(8,128)(2,1)S(1)}, u32[]{:S(2)}, u32[]{:S(2)}) collective-permute-start(bf16[21,104,128]{2,1,0:T(8,128)(2,1)S(1)} %ring.33), channel_id=1, source_target_pairs={{0,1},{1,2},{2,3},{3,4},{4,5},{5,6},{6,7},{7,8},{8,9},{9,10},{10,1... | collective-permute-start | bytes 1677320 | tf_op jit(solution)/shard_map/ring/ppermute | solution.py:536
  98.3 14.9 %collective-permute-start.13 = (bf16[21,104,128]{2,1,0:T(8,128)(2,1)S(1)}, bf16[21,104,128]{2,1,0:T(8,128)(2,1)S(1)}, u32[]{:S(2)}, u32[]{:S(2)}) collective-permute-start(bf16[21,104,128]{2,1,0:T(8,128)(2,1)S(1)} %ring.47), channel_id=1, source_target_pairs={{0,15},{1,0},{2,1},{3,2},{4,3},{5,4},{6,5},{7,6},{8,7},{9,8},{10,9... | collective-permute-start | bytes 1677320 | tf_op jit(solution)/shard_map/ring/ppermute | solution.py:539
  107.2 15.9 %collective-permute-start.6 = (bf16[21,104,128]{2,1,0:T(8,128)(2,1)S(1)}, bf16[21,104,128]{2,1,0:T(8,128)(2,1)S(1)}, u32[]{:S(2)}, u32[]{:S(2)}) collective-permute-start(bf16[21,104,128]{2,1,0:T(8,128)(2,1)S(1)} %ring.35), channel_id=1, source_target_pairs={{0,1},{1,2},{2,3},{3,4},{4,5},{5,6},{6,7},{7,8},{8,9},{9,10},{10,1... | collective-permute-start | bytes 1677320 | tf_op jit(solution)/shard_map/ring/ppermute | solution.py:536
  113.5 15.1 %collective-permute-start.14 = (bf16[21,104,128]{2,1,0:T(8,128)(2,1)S(1)}, bf16[21,104,128]{2,1,0:T(8,128)(2,1)S(1)}, u32[]{:S(2)}, u32[]{:S(2)}) collective-permute-start(bf16[21,104,128]{2,1,0:T(8,128)(2,1)S(1)} %ring.49), channel_id=1, source_target_pairs={{0,15},{1,0},{2,1},{3,2},{4,3},{5,4},{6,5},{7,6},{8,7},{9,8},{10,9... | collective-permute-start | bytes 1677320 | tf_op jit(solution)/shard_map/ring/ppermute | solution.py:539
  123.4 14.9 %collective-permute-start.7 = (bf16[21,104,128]{2,1,0:T(8,128)(2,1)S(1)}, bf16[21,104,128]{2,1,0:T(8,128)(2,1)S(1)}, u32[]{:S(2)}, u32[]{:S(2)}) collective-permute-start(bf16[21,104,128]{2,1,0:T(8,128)(2,1)S(1)} %ring.37), channel_id=1, source_target_pairs={{0,1},{1,2},{2,3},{3,4},{4,5},{5,6},{6,7},{7,8},{8,9},{9,10},{10,1... | collective-permute-start | bytes 1677320 | tf_op jit(solution)/shard_map/ring/ppermute | solution.py:536
  128.9 15.3 %collective-permute-start.15 = (bf16[21,104,128]{2,1,0:T(8,128)(2,1)S(1)}, bf16[21,104,128]{2,1,0:T(8,128)(2,1)S(1)}, u32[]{:S(2)}, u32[]{:S(2)}) collective-permute-start(bf16[21,104,128]{2,1,0:T(8,128)(2,1)S(1)} %ring.51), channel_id=1, source_target_pairs={{0,15},{1,0},{2,1},{3,2},{4,3},{5,4},{6,5},{7,6},{8,7},{9,8},{10,9... | collective-permute-start | bytes 1677320 | tf_op jit(solution)/shard_map/ring/ppermute | solution.py:539
  138.6 15.0 %collective-permute-start.8 = (bf16[21,104,128]{2,1,0:T(8,128)(2,1)S(1)}, bf16[21,104,128]{2,1,0:T(8,128)(2,1)S(1)}, u32[]{:S(2)}, u32[]{:S(2)}) collective-permute-start(bf16[21,104,128]{2,1,0:T(8,128)(2,1)S(1)} %ring.39), channel_id=1, source_target_pairs={{0,1},{1,2},{2,3},{3,4},{4,5},{5,6},{6,7},{7,8},{8,9},{9,10},{10,1... | collective-permute-start | bytes 1677320 | tf_op jit(solution)/shard_map/ring/ppermute | solution.py:536
  144.2 12.4 %copy-start.2 = (bf16[2,64,4096]{2,1,0:T(8,128)(2,1)S(1)}, bf16[2,64,4096]{2,1,0:T(8,128)(2,1)}, u32[]{:S(2)}) copy-start(bf16[2,64,4096]{2,1,0:T(8,128)(2,1)} %student_ref.3) | copy-start | bytes 3145732
  145.3 16.1 %collective-permute-start.17 = (bf16[21,104,128]{2,1,0:T(8,128)(2,1)}, bf16[21,104,128]{2,1,0:T(8,128)(2,1)}, u32[]{:S(2)}, u32[]{:S(2)}) collective-permute-start(bf16[21,104,128]{2,1,0:T(8,128)(2,1)} %ring.55), channel_id=1, source_target_pairs={{0,15},{1,0},{2,1},{3,2},{4,3},{5,4},{6,5},{7,6},{8,7},{9,8},{10,9... | collective-permute-start | bytes 1677320 | tf_op jit(solution)/shard_map/ring/ppermute | solution.py:539
  154.7 13.0 %collective-permute-start.16 = (bf16[21,104,128]{2,1,0:T(8,128)(2,1)}, bf16[21,104,128]{2,1,0:T(8,128)(2,1)}, u32[]{:S(2)}, u32[]{:S(2)}) collective-permute-start(bf16[21,104,128]{2,1,0:T(8,128)(2,1)} %ring.53), channel_id=1, source_target_pairs={{0,1},{1,2},{2,3},{3,4},{4,5},{5,6},{6,7},{7,8},{8,9},{9,10},{10,1... | collective-permute-start | bytes 1677320 | tf_op jit(solution)/shard_map/ring/ppermute | solution.py:536
  159.9 1.5 copy-start
  167.6 1.7 copy-start.1
  169.3 22.6 %copy-start.10 = (s32[512,2]{0,1:T(2,128)S(1)}, s32[512,2]{0,1:T(2,128)}, u32[]{:S(2)}) copy-start(s32[512,2]{0,1:T(2,128)} %param.12) | copy-start | bytes 12292
  175.3 26.7 %all-to-all-start.1 = ((f32[16,4,128]{2,1,0:T(4,128)}), f32[16,4,128]{2,1,0:T(4,128)S(1)}, u32[]{:S(2)}, u32[]{:S(2)}) async-start(f32[16,4,128]{2,1,0:T(4,128)} %broadcast_in_dim.55), calls=%async_computation.1 | async-start | bytes 65536 | tf_op jit(solution)/shard_map/finish/all_to_all | solution.py:575
  202.2 0.6 copy-start.11
Sparse Core Ops, SparseCore 0:
  72.8 35.3 all-gather.1

commit v5 on v4

--- a/solution.py
+++ b/solution.py
@@ -492,7 +492,7 @@
             in_specs=[smem, vmem],
             out_specs=(vmem,) * 3,
             scratch_shapes=[pltpu.VMEM((6 * steps, vocab_count, BLK), jnp.float32)],
-            compiler_params=room(16),
+            compiler_params=room(8),
         )(jnp.stack([vocab_index, sign]).astype(jnp.int32), listed)
 
     def planes(count):
@@ -508,7 +508,7 @@
                 pltpu.VMEM((doc_count * span, teacher_cols), jnp.bfloat16),
                 pltpu.VMEM((teacher_blocks, ROWS, BLK), jnp.bfloat16),
             ],
-            compiler_params=room(24),
+            compiler_params=room(16),
         )(send, teacher_logits, low, high, pick)
 
     def chosen(chain, step, frames):
@@ -517,14 +517,14 @@
             out_shape=planes(SLOTS),
             in_specs=[vmem] * (1 + len(frames)),
             out_specs=vmem,
-            compiler_params=room(12),
+            compiler_params=room(8),
         )(send, own, *frames[:-1])
         return pl.pallas_call(
             functools.partial(pass_kernel, chain, step, home),
             out_shape=planes(SLOTS),
             in_specs=[vmem] * 3,
             out_specs=vmem,
-            compiler_params=room(8),
+            compiler_params=room(4),
         )(send, part, frames[-1])
 
     with jax.named_scope("ring"):
@@ -544,7 +544,7 @@
             out_shape=(jax.ShapeDtypeStruct((row_count, BLK), jnp.float32),) * 2,
             in_specs=[vmem],
             out_specs=(vmem,) * 2,
-            compiler_params=room(16),
+            compiler_params=room(8),
         )(student_logits)
 
     with jax.named_scope("stage"):
@@ -554,7 +554,7 @@
             out_shape=planes(pair_count + 2 * vocab_count),
             in_specs=[smem] + [vmem] * len(early),
             out_specs=vmem,
-            compiler_params=room(20),
+            compiler_params=room(16),
         )(items, *early)
 
     with jax.named_scope("map"):
@@ -567,7 +567,7 @@
                 pltpu.VMEM((pair_count + 2 * vocab_count, ROWS, BLK), jnp.bfloat16),
                 pltpu.VMEM((3 * steps, row_count, BLK), jnp.float32),
             ],
-            compiler_params=room(16),
+            compiler_params=room(20),
         )(items, held, came_ahead[-1], came_behind[-1], spread, weights, student_logits, top, total)
 
     with jax.named_scope("finish"):

time: 211 us -> 211 us (level)
  no operation moved by 1% of the time
where the time goes in v5:
time: 211 us; the launch traced here: 210 us
  starting transfers between devices  84.8 us (40%)
  waiting for transfers between devices  61.6 us (29%)
  Pallas kernels  38.7 us (18%)
  between operations  15.2 us (7%)
  local copies, waits for them, and re-layouts  7.29 us (3%)
    ppermute x8, starting transfers between devices, shards(): came_behind.append(lax.ppermute(behind, ('seq', 'vocab'), backward))  49.7 us
    ppermute x8, waiting for transfers between devices, shards(): came_behind.append(lax.ppermute(behind, ('seq', 'vocab'), backward))  29.8 us
    ppermute x8, waiting for transfers between devices, shards(): came_ahead.append(lax.ppermute(ahead, ('seq', 'vocab'), forward))  21.7 us
    pallas_call x14, Pallas kernels, chosen(): pl.pallas_call(functools.partial(ready_kernel, chain, step), out_shape=pl...  15.8 us
    ppermute x8, starting transfers between devices, shards(): came_ahead.append(lax.ppermute(ahead, ('seq', 'vocab'), forward))  15.3 us
    all_to_all x1, starting transfers between devices, shards(): lax.all_to_all(sent, 'vocab', split_axis=0, concat_axis=0, tiled=True)  14.2 us
    all_to_all x1, waiting for transfers between devices, shards(): lax.all_to_all(sent, 'vocab', split_axis=0, concat_axis=0, tiled=True)  10 us
    pallas_call x14, Pallas kernels, chosen(): pl.pallas_call(functools.partial(pass_kernel, chain, step, home), out_sha...  9.1 us
  transfers between devices with their start and end apart: 20, of which 12 were waited for; matrix products, arithmetic and copies ran while one was open for 2% of the time, Pallas kernels for 15%

profile of v5, /device:TPU:6, one launch (start us, length us, event | category | flops | bytes accessed | tf_op | source)
XLA Modules:
  0.0 209.6 jit_solution(11386892889603674737)
XLA Ops:
  7.7 1.9 collective-permute-start
  9.7 3.6 %collective-permute-start.1 = (bf16[2,16,4736]{2,1,0:T(8,128)(2,1)S(1)}, bf16[2,16,4736]{2,1,0:T(8,128)(2,1)S(1)}, u32[]{:S(2)}, u32[]{:S(2)}) collective-permute-start(bf16[2,16,4736]{2,1,0:T(8,128)(2,1)S(1)} %get-tuple-element.153), channel_id=1, source_target_pairs={{16,0},{32,16},{48,32},{64,48},{80,64},{96,80},{112,96},{17,1},{33... | collective-permute-start | bytes 909320 | tf_op jit(solution)/shard_map/halo/ppermute | solution.py:23
  15.4 4.0 %plan.1 = (s32[8,256]{1,0:T(8,128)S(1)}, s32[8,128]{1,0:T(8,128)S(1)}, s32[8,128]{1,0:T(8,128)S(1)}) custom-call(s32[2]{0:T(128)S(1)} %pad_add_fusion.place_ref, s32[16,64]{1,0:T(8,128)S(1)} %reshape.251.listed_ref), custom_call_target="tpu_custom_call" | custom-call | tf_op jit(solution)/shard_map/plan/pallas_call | solution.py:489
  20.9 11.4 %collective-permute-start.9 = (bf16[21,104,128]{2,1,0:T(8,128)(2,1)S(1)}, bf16[21,104,128]{2,1,0:T(8,128)(2,1)S(1)}, u32[]{:S(2)}, u32[]{:S(2)}) collective-permute-start(bf16[21,104,128]{2,1,0:T(8,128)(2,1)S(1)} %get-tuple-element.92), channel_id=1, source_target_pairs={{0,15},{1,0},{2,1},{3,2},{4,3},{5,4},{6,5},{7,6},{8,7},{9,8},{10,9... | collective-permute-start | bytes 1677320 | tf_op jit(solution)/shard_map/ring/ppermute | solution.py:539
  32.3 1.9 collective-permute-start.2
  34.8 10.3 %collective-permute-done.9.newest_ref.refs_0_.refs_8_ = bf16[21,104,128]{2,1,0:T(8,128)(2,1)S(1)} collective-permute-done((bf16[21,104,128]{2,1,0:T(8,128)(2,1)S(1)}, bf16[21,104,128]{2,1,0:T(8,128)(2,1)S(1)}, u32[]{:S(2)}, u32[]{:S(2)}) %collective-permute-start.9) | collective-permute-done | bytes 559136 | tf_op jit(solution)/shard_map/ring/ppermute | solution.py:539
  45.4 5.6 %collective-permute-start.10 = (bf16[21,104,128]{2,1,0:T(8,128)(2,1)S(1)}, bf16[21,104,128]{2,1,0:T(8,128)(2,1)S(1)}, u32[]{:S(2)}, u32[]{:S(2)}) collective-permute-start(bf16[21,104,128]{2,1,0:T(8,128)(2,1)S(1)} %ring.41), channel_id=1, source_target_pairs={{0,15},{1,0},{2,1},{3,2},{4,3},{5,4},{6,5},{7,6},{8,7},{9,8},{10,9... | collective-permute-start | bytes 1677320 | tf_op jit(solution)/shard_map/ring/ppermute | solution.py:539
  51.3 1.9 collective-permute-start.3
  54.0 8.9 %collective-permute-done.10.newest_ref.refs_1_.refs_9_ = bf16[21,104,128]{2,1,0:T(8,128)(2,1)S(1)} collective-permute-done((bf16[21,104,128]{2,1,0:T(8,128)(2,1)S(1)}, bf16[21,104,128]{2,1,0:T(8,128)(2,1)S(1)}, u32[]{:S(2)}, u32[]{:S(2)}) %collective-permute-start.10) | collective-permute-done | bytes 559136 | tf_op jit(solution)/shard_map/ring/ppermute | solution.py:539
  64.0 5.6 %collective-permute-start.11 = (bf16[21,104,128]{2,1,0:T(8,128)(2,1)}, bf16[21,104,128]{2,1,0:T(8,128)(2,1)}, u32[]{:S(2)}, u32[]{:S(2)}) collective-permute-start(bf16[21,104,128]{2,1,0:T(8,128)(2,1)} %ring.43), channel_id=1, source_target_pairs={{0,15},{1,0},{2,1},{3,2},{4,3},{5,4},{6,5},{7,6},{8,7},{9,8},{10,9... | collective-permute-start | bytes 1677320 | tf_op jit(solution)/shard_map/ring/ppermute | solution.py:539
  70.7 1.9 collective-permute-start.4
  73.5 7.4 %collective-permute-done.11.newest_ref.refs_2_.refs_10_ = bf16[21,104,128]{2,1,0:T(8,128)(2,1)} collective-permute-done((bf16[21,104,128]{2,1,0:T(8,128)(2,1)}, bf16[21,104,128]{2,1,0:T(8,128)(2,1)}, u32[]{:S(2)}, u32[]{:S(2)}) %collective-permute-start.11) | collective-permute-done | bytes 559136 | tf_op jit(solution)/shard_map/ring/ppermute | solution.py:539
  82.3 5.6 %collective-permute-start.12 = (bf16[21,104,128]{2,1,0:T(8,128)(2,1)S(1)}, bf16[21,104,128]{2,1,0:T(8,128)(2,1)S(1)}, u32[]{:S(2)}, u32[]{:S(2)}) collective-permute-start(bf16[21,104,128]{2,1,0:T(8,128)(2,1)S(1)} %ring.45), channel_id=1, source_target_pairs={{0,15},{1,0},{2,1},{3,2},{4,3},{5,4},{6,5},{7,6},{8,7},{9,8},{10,9... | collective-permute-start | bytes 1677320 | tf_op jit(solution)/shard_map/ring/ppermute | solution.py:539
  90.3 1.9 collective-permute-start.5
  95.5 2.6 %collective-permute-done.12.newest_ref.refs_3_.refs_11_ = bf16[21,104,128]{2,1,0:T(8,128)(2,1)S(1)} collective-permute-done((bf16[21,104,128]{2,1,0:T(8,128)(2,1)S(1)}, bf16[21,104,128]{2,1,0:T(8,128)(2,1)S(1)}, u32[]{:S(2)}, u32[]{:S(2)}) %collective-permute-start.12) | collective-permute-done | bytes 559136 | tf_op jit(solution)/shard_map/ring/ppermute | solution.py:539
  98.3 5.6 %collective-permute-start.13 = (bf16[21,104,128]{2,1,0:T(8,128)(2,1)S(1)}, bf16[21,104,128]{2,1,0:T(8,128)(2,1)S(1)}, u32[]{:S(2)}, u32[]{:S(2)}) collective-permute-start(bf16[21,104,128]{2,1,0:T(8,128)(2,1)S(1)} %ring.47), channel_id=1, source_target_pairs={{0,15},{1,0},{2,1},{3,2},{4,3},{5,4},{6,5},{7,6},{8,7},{9,8},{10,9... | collective-permute-start | bytes 1677320 | tf_op jit(solution)/shard_map/ring/ppermute | solution.py:539
  103.9 3.0 %collective-permute-done.5.newest_ref.refs_3_.refs_4_ = bf16[21,104,128]{2,1,0:T(8,128)(2,1)S(1)} collective-permute-done((bf16[21,104,128]{2,1,0:T(8,128)(2,1)S(1)}, bf16[21,104,128]{2,1,0:T(8,128)(2,1)S(1)}, u32[]{:S(2)}, u32[]{:S(2)}) %collective-permute-start.5) | collective-permute-done | bytes 559136 | tf_op jit(solution)/shard_map/ring/ppermute | solution.py:536
  107.2 1.9 collective-permute-start.6
  113.5 5.6 %collective-permute-start.14 = (bf16[21,104,128]{2,1,0:T(8,128)(2,1)S(1)}, bf16[21,104,128]{2,1,0:T(8,128)(2,1)S(1)}, u32[]{:S(2)}, u32[]{:S(2)}) collective-permute-start(bf16[21,104,128]{2,1,0:T(8,128)(2,1)S(1)} %ring.49), channel_id=1, source_target_pairs={{0,15},{1,0},{2,1},{3,2},{4,3},{5,4},{6,5},{7,6},{8,7},{9,8},{10,9... | collective-permute-start | bytes 1677320 | tf_op jit(solution)/shard_map/ring/ppermute | solution.py:539
  119.1 4.0 %collective-permute-done.6.newest_ref.refs_4_.refs_5_ = bf16[21,104,128]{2,1,0:T(8,128)(2,1)S(1)} collective-permute-done((bf16[21,104,128]{2,1,0:T(8,128)(2,1)S(1)}, bf16[21,104,128]{2,1,0:T(8,128)(2,1)S(1)}, u32[]{:S(2)}, u32[]{:S(2)}) %collective-permute-start.6) | collective-permute-done | bytes 559136 | tf_op jit(solution)/shard_map/ring/ppermute | solution.py:536
  123.3 1.9 collective-permute-start.7
  128.9 5.1 %collective-permute-start.15 = (bf16[21,104,128]{2,1,0:T(8,128)(2,1)S(1)}, bf16[21,104,128]{2,1,0:T(8,128)(2,1)S(1)}, u32[]{:S(2)}, u32[]{:S(2)}) collective-permute-start(bf16[21,104,128]{2,1,0:T(8,128)(2,1)S(1)} %ring.51), channel_id=1, source_target_pairs={{0,15},{1,0},{2,1},{3,2},{4,3},{5,4},{6,5},{7,6},{8,7},{9,8},{10,9... | collective-permute-start | bytes 1677320 | tf_op jit(solution)/shard_map/ring/ppermute | solution.py:539
  134.0 4.2 %collective-permute-done.7.newest_ref.refs_6_.refs_5_ = bf16[21,104,128]{2,1,0:T(8,128)(2,1)S(1)} collective-permute-done((bf16[21,104,128]{2,1,0:T(8,128)(2,1)S(1)}, bf16[21,104,128]{2,1,0:T(8,128)(2,1)S(1)}, u32[]{:S(2)}, u32[]{:S(2)}) %collective-permute-start.7) | collective-permute-done | bytes 559136 | tf_op jit(solution)/shard_map/ring/ppermute | solution.py:536
  138.5 1.9 collective-permute-start.8
  145.2 5.1 %collective-permute-start.17 = (bf16[21,104,128]{2,1,0:T(8,128)(2,1)}, bf16[21,104,128]{2,1,0:T(8,128)(2,1)}, u32[]{:S(2)}, u32[]{:S(2)}) collective-permute-start(bf16[21,104,128]{2,1,0:T(8,128)(2,1)} %ring.55), channel_id=1, source_target_pairs={{0,15},{1,0},{2,1},{3,2},{4,3},{5,4},{6,5},{7,6},{8,7},{9,8},{10,9... | collective-permute-start | bytes 1677320 | tf_op jit(solution)/shard_map/ring/ppermute | solution.py:539
  150.4 3.1 %collective-permute-done.8.refs_7_.newest_ref = bf16[21,104,128]{2,1,0:T(8,128)(2,1)S(1)} collective-permute-done((bf16[21,104,128]{2,1,0:T(8,128)(2,1)S(1)}, bf16[21,104,128]{2,1,0:T(8,128)(2,1)S(1)}, u32[]{:S(2)}, u32[]{:S(2)}) %collective-permute-start.8) | collective-permute-done | bytes 559136 | tf_op jit(solution)/shard_map/ring/ppermute | solution.py:536
  154.6 1.9 collective-permute-start.16
  157.3 2.5 %stage.1.held_ref = bf16[96,104,128]{2,1,0:T(8,128)(2,1)S(1)} custom-call(s32[8,128]{1,0:T(8,128)S(1)} %get-tuple-element.88.item_ref, bf16[38,104,128]{2,1,0:T(8,128)(2,1)S(1)} %get-tuple-element.90.home_ref.refs_0_, bf16[21,104,128]{2,1,0:T(8,128)(2,1)S(1)} %collective-permute-done.2.newest_ref.refs_0_.refs_1_, ...), custom_call_target="tpu_custom_call" | custom-call | tf_op jit(solution)/shard_map/stage/pallas_call | solution.py:552
  161.3 6.3 %collective-permute-done.16.ahead_ref = bf16[21,104,128]{2,1,0:T(8,128)(2,1)} collective-permute-done((bf16[21,104,128]{2,1,0:T(8,128)(2,1)}, bf16[21,104,128]{2,1,0:T(8,128)(2,1)}, u32[]{:S(2)}, u32[]{:S(2)}) %collective-permute-start.16) | collective-permute-done | bytes 559136 | tf_op jit(solution)/shard_map/ring/ppermute | solution.py:536
  169.3 5.3 %map.1 = f32[8,128]{1,0:T(8,128)S(1)} custom-call(s32[8,128]{1,0:T(8,128)S(1)} %get-tuple-element.88.item_ref, bf16[96,104,128]{2,1,0:T(8,128)(2,1)S(1)} %copy-done.1, bf16[21,104,128]{2,1,0:T(8,128)(2,1)} %collective-permute-done.16.ahead_ref, bf16[21,104,128]{2,1,0:T(8,128)(2,1)} %collective-permute-done.17.behind_ref, ...), custom_call_target="tpu_custom_call" | custom-call | tf_op jit(solution)/shard_map/map/pallas_call | solution.py:561
  175.2 14.2 %all-to-all-start.1 = ((f32[16,4,128]{2,1,0:T(4,128)}), f32[16,4,128]{2,1,0:T(4,128)S(1)}, u32[]{:S(2)}, u32[]{:S(2)}) async-start(f32[16,4,128]{2,1,0:T(4,128)} %broadcast_in_dim.55), calls=%async_computation.1 | async-start | bytes 65536 | tf_op jit(solution)/shard_map/finish/all_to_all | solution.py:575
  191.9 10.0 %all-to-all-done.1 = f32[16,4,128]{2,1,0:T(4,128)S(1)} async-done(((f32[16,4,128]{2,1,0:T(4,128)}), f32[16,4,128]{2,1,0:T(4,128)S(1)}, u32[]{:S(2)}, u32[]{:S(2)}) %all-to-all-start.1) | async-done | bytes 32800 | tf_op jit(solution)/shard_map/finish/all_to_all | solution.py:575
  (83 shorter events, 38.1 us)
Async XLA Ops:
  6.5 13.0 %copy-start.5 = (bf16[2,64,4736]{2,1,0:T(8,128)(2,1)S(1)}, bf16[2,64,4736]{2,1,0:T(8,128)(2,1)}, u32[]{:S(2)}) copy-start(bf16[2,64,4736]{2,1,0:T(8,128)(2,1)} %own_ref.1) | copy-start | bytes 3637252
  6.5 154.8 %all-gather.2.cloned.1.call-start = ((), (), s32[]{:S(2)}) async-start(), calls=%async_computation.2 | async-start | bytes 2621440 | tf_op jit(solution)/shard_map/weights/all_gather | solution.py:465
  7.7 11.8 %collective-permute-start = (bf16[2,16,4736]{2,1,0:T(8,128)(2,1)S(1)}, bf16[2,16,4736]{2,1,0:T(8,128)(2,1)S(1)}, u32[]{:S(2)}, u32[]{:S(2)}) collective-permute-start(bf16[2,16,4736]{2,1,0:T(8,128)(2,1)S(1)} %get-tuple-element.154), channel_id=1, source_target_pairs={{0,16},{16,32},{32,48},{48,64},{64,80},{80,96},{96,112},{1,17},{17... | collective-permute-start | bytes 909320 | tf_op jit(solution)/shard_map/halo/ppermute | solution.py:22
  9.7 9.9 %collective-permute-start.1 = (bf16[2,16,4736]{2,1,0:T(8,128)(2,1)S(1)}, bf16[2,16,4736]{2,1,0:T(8,128)(2,1)S(1)}, u32[]{:S(2)}, u32[]{:S(2)}) collective-permute-start(bf16[2,16,4736]{2,1,0:T(8,128)(2,1)S(1)} %get-tuple-element.153), channel_id=1, source_target_pairs={{16,0},{32,16},{48,32},{64,48},{80,64},{96,80},{112,96},{17,1},{33... | collective-permute-start | bytes 909320 | tf_op jit(solution)/shard_map/halo/ppermute | solution.py:23
  19.5 15.3 %copy-start.7 = (bf16[2,16,4736]{2,1,0:T(8,128)(2,1)}, bf16[2,16,4736]{2,1,0:T(8,128)(2,1)S(1)}, u32[]{:S(2)}) copy-start(bf16[2,16,4736]{2,1,0:T(8,128)(2,1)S(1)} %collective-permute-done.low_ref) | copy-start | bytes 909316
  19.5 15.2 %copy-start.9 = (bf16[2,16,4736]{2,1,0:T(8,128)(2,1)}, bf16[2,16,4736]{2,1,0:T(8,128)(2,1)S(1)}, u32[]{:S(2)}) copy-start(bf16[2,16,4736]{2,1,0:T(8,128)(2,1)S(1)} %collective-permute-done.1.high_ref) | copy-start | bytes 909316
  20.9 24.2 %collective-permute-start.9 = (bf16[21,104,128]{2,1,0:T(8,128)(2,1)S(1)}, bf16[21,104,128]{2,1,0:T(8,128)(2,1)S(1)}, u32[]{:S(2)}, u32[]{:S(2)}) collective-permute-start(bf16[21,104,128]{2,1,0:T(8,128)(2,1)S(1)} %get-tuple-element.92), channel_id=1, source_target_pairs={{0,15},{1,0},{2,1},{3,2},{4,3},{5,4},{6,5},{7,6},{8,7},{9,8},{10,9... | collective-permute-start | bytes 1677320 | tf_op jit(solution)/shard_map/ring/ppermute | solution.py:539
  32.3 18.7 %collective-permute-start.2 = (bf16[21,104,128]{2,1,0:T(8,128)(2,1)S(1)}, bf16[21,104,128]{2,1,0:T(8,128)(2,1)S(1)}, u32[]{:S(2)}, u32[]{:S(2)}) collective-permute-start(bf16[21,104,128]{2,1,0:T(8,128)(2,1)S(1)} %get-tuple-element.91), channel_id=1, source_target_pairs={{0,1},{1,2},{2,3},{3,4},{4,5},{5,6},{6,7},{7,8},{8,9},{9,10},{10,1... | collective-permute-start | bytes 1677320 | tf_op jit(solution)/shard_map/ring/ppermute | solution.py:536
  45.4 17.5 %collective-permute-start.10 = (bf16[21,104,128]{2,1,0:T(8,128)(2,1)S(1)}, bf16[21,104,128]{2,1,0:T(8,128)(2,1)S(1)}, u32[]{:S(2)}, u32[]{:S(2)}) collective-permute-start(bf16[21,104,128]{2,1,0:T(8,128)(2,1)S(1)} %ring.41), channel_id=1, source_target_pairs={{0,15},{1,0},{2,1},{3,2},{4,3},{5,4},{6,5},{7,6},{8,7},{9,8},{10,9... | collective-permute-start | bytes 1677320 | tf_op jit(solution)/shard_map/ring/ppermute | solution.py:539
  51.3 18.3 %collective-permute-start.3 = (bf16[21,104,128]{2,1,0:T(8,128)(2,1)S(1)}, bf16[21,104,128]{2,1,0:T(8,128)(2,1)S(1)}, u32[]{:S(2)}, u32[]{:S(2)}) collective-permute-start(bf16[21,104,128]{2,1,0:T(8,128)(2,1)S(1)} %ring.29), channel_id=1, source_target_pairs={{0,1},{1,2},{2,3},{3,4},{4,5},{5,6},{6,7},{7,8},{8,9},{9,10},{10,1... | collective-permute-start | bytes 1677320 | tf_op jit(solution)/shard_map/ring/ppermute | solution.py:536
  64.0 17.0 %collective-permute-start.11 = (bf16[21,104,128]{2,1,0:T(8,128)(2,1)}, bf16[21,104,128]{2,1,0:T(8,128)(2,1)}, u32[]{:S(2)}, u32[]{:S(2)}) collective-permute-start(bf16[21,104,128]{2,1,0:T(8,128)(2,1)} %ring.43), channel_id=1, source_target_pairs={{0,15},{1,0},{2,1},{3,2},{4,3},{5,4},{6,5},{7,6},{8,7},{9,8},{10,9... | collective-permute-start | bytes 1677320 | tf_op jit(solution)/shard_map/ring/ppermute | solution.py:539
  70.7 18.3 %collective-permute-start.4 = (bf16[21,104,128]{2,1,0:T(8,128)(2,1)}, bf16[21,104,128]{2,1,0:T(8,128)(2,1)}, u32[]{:S(2)}, u32[]{:S(2)}) collective-permute-start(bf16[21,104,128]{2,1,0:T(8,128)(2,1)} %ring.31), channel_id=1, source_target_pairs={{0,1},{1,2},{2,3},{3,4},{4,5},{5,6},{6,7},{7,8},{8,9},{9,10},{10,1... | collective-permute-start | bytes 1677320 | tf_op jit(solution)/shard_map/ring/ppermute | solution.py:536
  82.3 15.7 %collective-permute-start.12 = (bf16[21,104,128]{2,1,0:T(8,128)(2,1)S(1)}, bf16[21,104,128]{2,1,0:T(8,128)(2,1)S(1)}, u32[]{:S(2)}, u32[]{:S(2)}) collective-permute-start(bf16[21,104,128]{2,1,0:T(8,128)(2,1)S(1)} %ring.45), channel_id=1, source_target_pairs={{0,15},{1,0},{2,1},{3,2},{4,3},{5,4},{6,5},{7,6},{8,7},{9,8},{10,9... | collective-permute-start | bytes 1677320 | tf_op jit(solution)/shard_map/ring/ppermute | solution.py:539
  90.3 16.7 %collective-permute-start.5 = (bf16[21,104,128]{2,1,0:T(8,128)(2,1)S(1)}, bf16[21,104,128]{2,1,0:T(8,128)(2,1)S(1)}, u32[]{:S(2)}, u32[]{:S(2)}) collective-permute-start(bf16[21,104,128]{2,1,0:T(8,128)(2,1)S(1)} %ring.33), channel_id=1, source_target_pairs={{0,1},{1,2},{2,3},{3,4},{4,5},{5,6},{6,7},{7,8},{8,9},{9,10},{10,1... | collective-permute-start | bytes 1677320 | tf_op jit(solution)/shard_map/ring/ppermute | solution.py:536
  98.3 14.9 %collective-permute-start.13 = (bf16[21,104,128]{2,1,0:T(8,128)(2,1)S(1)}, bf16[21,104,128]{2,1,0:T(8,128)(2,1)S(1)}, u32[]{:S(2)}, u32[]{:S(2)}) collective-permute-start(bf16[21,104,128]{2,1,0:T(8,128)(2,1)S(1)} %ring.47), channel_id=1, source_target_pairs={{0,15},{1,0},{2,1},{3,2},{4,3},{5,4},{6,5},{7,6},{8,7},{9,8},{10,9... | collective-permute-start | bytes 1677320 | tf_op jit(solution)/shard_map/ring/ppermute | solution.py:539
  107.2 15.8 %collective-permute-start.6 = (bf16[21,104,128]{2,1,0:T(8,128)(2,1)S(1)}, bf16[21,104,128]{2,1,0:T(8,128)(2,1)S(1)}, u32[]{:S(2)}, u32[]{:S(2)}) collective-permute-start(bf16[21,104,128]{2,1,0:T(8,128)(2,1)S(1)} %ring.35), channel_id=1, source_target_pairs={{0,1},{1,2},{2,3},{3,4},{4,5},{5,6},{6,7},{7,8},{8,9},{9,10},{10,1... | collective-permute-start | bytes 1677320 | tf_op jit(solution)/shard_map/ring/ppermute | solution.py:536
  113.5 15.1 %collective-permute-start.14 = (bf16[21,104,128]{2,1,0:T(8,128)(2,1)S(1)}, bf16[21,104,128]{2,1,0:T(8,128)(2,1)S(1)}, u32[]{:S(2)}, u32[]{:S(2)}) collective-permute-start(bf16[21,104,128]{2,1,0:T(8,128)(2,1)S(1)} %ring.49), channel_id=1, source_target_pairs={{0,15},{1,0},{2,1},{3,2},{4,3},{5,4},{6,5},{7,6},{8,7},{9,8},{10,9... | collective-permute-start | bytes 1677320 | tf_op jit(solution)/shard_map/ring/ppermute | solution.py:539
  123.3 14.9 %collective-permute-start.7 = (bf16[21,104,128]{2,1,0:T(8,128)(2,1)S(1)}, bf16[21,104,128]{2,1,0:T(8,128)(2,1)S(1)}, u32[]{:S(2)}, u32[]{:S(2)}) collective-permute-start(bf16[21,104,128]{2,1,0:T(8,128)(2,1)S(1)} %ring.37), channel_id=1, source_target_pairs={{0,1},{1,2},{2,3},{3,4},{4,5},{5,6},{6,7},{7,8},{8,9},{9,10},{10,1... | collective-permute-start | bytes 1677320 | tf_op jit(solution)/shard_map/ring/ppermute | solution.py:536
  128.9 15.3 %collective-permute-start.15 = (bf16[21,104,128]{2,1,0:T(8,128)(2,1)S(1)}, bf16[21,104,128]{2,1,0:T(8,128)(2,1)S(1)}, u32[]{:S(2)}, u32[]{:S(2)}) collective-permute-start(bf16[21,104,128]{2,1,0:T(8,128)(2,1)S(1)} %ring.51), channel_id=1, source_target_pairs={{0,15},{1,0},{2,1},{3,2},{4,3},{5,4},{6,5},{7,6},{8,7},{9,8},{10,9... | collective-permute-start | bytes 1677320 | tf_op jit(solution)/shard_map/ring/ppermute | solution.py:539
  138.5 15.0 %collective-permute-start.8 = (bf16[21,104,128]{2,1,0:T(8,128)(2,1)S(1)}, bf16[21,104,128]{2,1,0:T(8,128)(2,1)S(1)}, u32[]{:S(2)}, u32[]{:S(2)}) collective-permute-start(bf16[21,104,128]{2,1,0:T(8,128)(2,1)S(1)} %ring.39), channel_id=1, source_target_pairs={{0,1},{1,2},{2,3},{3,4},{4,5},{5,6},{6,7},{7,8},{8,9},{9,10},{10,1... | collective-permute-start | bytes 1677320 | tf_op jit(solution)/shard_map/ring/ppermute | solution.py:536
  144.1 12.4 %copy-start.2 = (bf16[2,64,4096]{2,1,0:T(8,128)(2,1)S(1)}, bf16[2,64,4096]{2,1,0:T(8,128)(2,1)}, u32[]{:S(2)}) copy-start(bf16[2,64,4096]{2,1,0:T(8,128)(2,1)} %student_ref.3) | copy-start | bytes 3145732
  145.2 16.1 %collective-permute-start.17 = (bf16[21,104,128]{2,1,0:T(8,128)(2,1)}, bf16[21,104,128]{2,1,0:T(8,128)(2,1)}, u32[]{:S(2)}, u32[]{:S(2)}) collective-permute-start(bf16[21,104,128]{2,1,0:T(8,128)(2,1)} %ring.55), channel_id=1, source_target_pairs={{0,15},{1,0},{2,1},{3,2},{4,3},{5,4},{6,5},{7,6},{8,7},{9,8},{10,9... | collective-permute-start | bytes 1677320 | tf_op jit(solution)/shard_map/ring/ppermute | solution.py:539
  154.6 13.0 %collective-permute-start.16 = (bf16[21,104,128]{2,1,0:T(8,128)(2,1)}, bf16[21,104,128]{2,1,0:T(8,128)(2,1)}, u32[]{:S(2)}, u32[]{:S(2)}) collective-permute-start(bf16[21,104,128]{2,1,0:T(8,128)(2,1)} %ring.53), channel_id=1, source_target_pairs={{0,1},{1,2},{2,3},{3,4},{4,5},{5,6},{6,7},{7,8},{8,9},{9,10},{10,1... | collective-permute-start | bytes 1677320 | tf_op jit(solution)/shard_map/ring/ppermute | solution.py:536
  159.8 1.5 copy-start
  167.6 1.7 copy-start.1
  169.3 22.6 %copy-start.10 = (s32[512,2]{0,1:T(2,128)S(1)}, s32[512,2]{0,1:T(2,128)}, u32[]{:S(2)}) copy-start(s32[512,2]{0,1:T(2,128)} %param.12) | copy-start | bytes 12292
  175.2 26.7 %all-to-all-start.1 = ((f32[16,4,128]{2,1,0:T(4,128)}), f32[16,4,128]{2,1,0:T(4,128)S(1)}, u32[]{:S(2)}, u32[]{:S(2)}) async-start(f32[16,4,128]{2,1,0:T(4,128)} %broadcast_in_dim.55), calls=%async_computation.1 | async-start | bytes 65536 | tf_op jit(solution)/shard_map/finish/all_to_all | solution.py:575
  202.2 0.6 copy-start.11
Sparse Core Ops, SparseCore 0:
  72.8 35.3 all-gather.1

commit v6 on v5

--- a/solution.py
+++ b/solution.py
@@ -11,7 +11,8 @@
 K = 2
 W = 16
 ROWS = 104
-SLOTS = 21
+SLOTS = 22
+DIRECT = 9
 TINY = 1.2e-38
 
 
@@ -34,41 +35,51 @@
     return pairs
 
 
-def ways(distance, block, share, vocab_count):
-    half = vocab_count // 2
-    first = (block * 5) % 8 < share
-    ahead = jnp.where((distance >= 1) & ((distance < half) | ((distance == half) & first)), distance, 0)
-    behind = jnp.where((distance > half) | ((distance == half) & ~first), vocab_count - distance, 0)
-    return ahead, behind
-
-
 def ones(mask):
     return jnp.where(mask, 1.0, 0.0).astype(jnp.bfloat16)
 
 
-def plan_kernel(blocks, place_ref, listed_ref, send_ref, item_ref, fit_ref, book_ref):
+def split(listed, blocks, vocab_count):
+    holder = sum((listed >= h * blocks).astype(jnp.int32) for h in range(1, vocab_count))
+    return holder, listed - holder * blocks
+
+
+def turn(table):
+    rows, columns = table.shape
+    table = table.astype(jnp.float32)
+    if columns < BLK:
+        table = jnp.concatenate([table, jnp.zeros((rows, BLK - columns), jnp.float32)], axis=1)
+    if rows < BLK:
+        table = jnp.concatenate([table, jnp.zeros((BLK - rows, BLK), jnp.float32)], axis=0)
+    return table.T.astype(jnp.int32)
+
+
+def earlier_lanes():
+    square = (BLK, BLK)
+    return ones(lax.broadcasted_iota(jnp.int32, square, 0) < lax.broadcasted_iota(jnp.int32, square, 1))
+
+
+def plan_kernel(blocks, place_ref, listed_ref, after_ref, send_ref, item_ref, fit_ref, book_ref):
     vocab_count, pair_count = listed_ref.shape
     half = vocab_count // 2
-    steps = half
+    steps = half - 1
     home = blocks + 1
+    beyond = home + steps * SLOTS
     me, sign = place_ref[0], place_ref[1]
     f32, i32 = jnp.float32, jnp.int32
     shape = (vocab_count, BLK)
 
-    def split(listed):
-        holder = sum((listed >= h * blocks).astype(i32) for h in range(1, vocab_count))
-        return holder, listed - holder * blocks
-
+    del after_ref
     listed = listed_ref[...]
-    wide = jnp.concatenate([listed, jnp.zeros((vocab_count, BLK - pair_count), i32)], axis=1)
-    tall = jnp.concatenate([wide, jnp.zeros((BLK - vocab_count, BLK), i32)], axis=0).astype(f32).T.astype(i32)
-    row_holder, _ = split(listed)
-    holders, inners = split(tall[:pair_count])
+    row_holder, _ = split(listed, blocks, vocab_count)
+    holders, inners = split(turn(listed)[:pair_count], blocks, vocab_count)
+    facing = me + half
+    facing = jnp.where(facing >= vocab_count, facing - vocab_count, facing)
     lane = lax.broadcasted_iota(i32, shape, 1)
     row = lax.broadcasted_iota(i32, shape, 0)
 
     reach = [jnp.zeros(shape, i32), jnp.zeros(shape, i32)]
-    across = jnp.zeros(shape, i32)
+    across = jnp.zeros((1, BLK), i32)
     pair_lane = lax.broadcasted_iota(i32, (pair_count, BLK), 1)
     pair_row = lax.broadcasted_iota(i32, (vocab_count, pair_count), 0)
     for s in range(vocab_count):
@@ -82,38 +93,29 @@
         needed = hits > 0
         reach[0] = jnp.maximum(reach[0], jnp.where(needed & (distance < half), distance, 0))
         reach[1] = jnp.maximum(reach[1], jnp.where(needed & (distance > half), vocab_count - distance, 0))
-        across = jnp.maximum(across, jnp.where(needed & (distance == half), 1, 0))
-    order_key = (lane * 5) % 8
-    share = jnp.zeros((1, 1), i32)
-    for part in range(1, 9):
-        first = (across > 0) & (order_key < part)
-        more = jnp.where(first, half, reach[0]) - jnp.where((across > 0) & ~first, half, reach[1])
-        more = jnp.sum(jnp.sum(more, axis=1, keepdims=True), axis=0, keepdims=True)
-        share = share + (more <= 0).astype(i32)
-    first = order_key < share
-    reach[0] = jnp.where((across > 0) & first, half, reach[0])
-    reach[1] = jnp.where((across > 0) & ~first, half, reach[1])
-    reach = [jnp.where(lane == blocks, half - way, reach[way]) for way in range(2)]
+        seen = jnp.max(jnp.where(needed & (row == facing), 1, 0), axis=0, keepdims=True)
+        across = jnp.maximum(across, jnp.where(me == s, seen, 0))
+    reach = [jnp.where(lane == blocks, steps, r) for r in reach]
 
     square = (BLK, BLK)
     up, over = lax.broadcasted_iota(i32, square, 0), lax.broadcasted_iota(i32, square, 1)
-    earlier = ones(up < over)
+    earlier = earlier_lanes()
     left_up, left_over = (up & 7) + 1 - (up >> 3), (over & 7) + 1 - (over >> 3)
     goes_first = ones((left_up > left_over) | ((left_up == left_over) & ((up >> 3) > (over >> 3))))
     index, waiting, moved = [], [], [jnp.zeros(shape, f32)] * 2
     for way in range(2):
-        masks = jnp.concatenate([ones(reach[way] == r) for r in range(1, half + 1)], axis=0)
+        masks = jnp.concatenate([ones(reach[way] == r) for r in range(1, steps + 1)], axis=0)
         before = jnp.dot(masks, earlier, preferred_element_type=f32)
         place = jnp.zeros(shape, f32)
         count = jnp.zeros(shape, f32)
-        for r in range(1, half + 1):
+        for r in range(1, steps + 1):
             same = reach[way] == r
             place = jnp.where(same, before[(r - 1) * vocab_count : r * vocab_count], place)
             total = jnp.sum(jnp.where(same, 1.0, 0.0), axis=1, keepdims=True)
             count = jnp.where(lane == r - 1, total, count)
         index.append(place)
         waiting.append(count)
-    travels = (lane >= 8) & (lane < 8 * half) & ((lane & 7) + 1 > (lane >> 3))
+    travels = (lane >= 8) & (lane < 8 * steps) & ((lane & 7) + 1 > (lane >> 3))
     for f in range(steps):
         ahead_of = jnp.dot(
             jnp.concatenate(waiting, axis=0).astype(jnp.bfloat16), goes_first, preferred_element_type=f32
@@ -161,13 +163,13 @@
                 where = jnp.where(now, f * SLOTS + first + order - start, where)
             return where
 
-        leave = slot(me, row, (far > row) & (row < half))
-        arrive = slot(giver, row - 1, (far >= row) & (row >= 1) & (row <= half))
+        leave = slot(me, row, (far > row) & (row < steps))
+        arrive = slot(giver, row - 1, (far >= row) & (row >= 1) & (row <= steps))
         point = jnp.where(row == 0, lane.astype(f32), jnp.maximum(home + arrive, 0.0))
         pointer.append(point)
         leave_turned = jnp.concatenate([leave, jnp.full((BLK - vocab_count, BLK), -1.0, f32)], axis=0).T
         chosen = jnp.zeros((1, 2 * BLK), f32)
-        for h in range(half):
+        for h in range(steps):
             chosen = chosen + jnp.dot(
                 point[h : h + 1].astype(jnp.bfloat16),
                 ones(leave_turned[:, h : h + 1] == target),
@@ -184,8 +186,16 @@
     inner = jnp.sum(jnp.where(pair_lane == me, inners, 0), axis=1, keepdims=True)
     distance = me - holder
     distance = jnp.where(distance < 0, distance + vocab_count, distance)
-    hops = ways(distance, inner, share, vocab_count)
-    scale = jnp.where(distance <= half, distance, 2 * vocab_count - distance)
+    hops = [
+        jnp.where(distance < half, distance, 0),
+        jnp.where(distance > half, vocab_count - distance, 0),
+    ]
+    scale = jnp.where(distance < half, distance, 2 * vocab_count - distance)
+    lanes = lax.broadcasted_iota(i32, (1, BLK), 1)
+    across = jnp.where(lanes == blocks, 1, across)
+    met = beyond + jnp.dot(
+        jnp.broadcast_to(ones(across > 0), (8, BLK)), earlier, preferred_element_type=f32
+    )[:1]
     points = jnp.zeros((pair_count, 1), f32)
     for way in range(2):
         found = lax.dot_general(
@@ -197,13 +207,15 @@
         points = points + jnp.sum(
             jnp.where((mine_lane == hops[way]) & (hops[way] > 0), found, 0.0), axis=1, keepdims=True
         )
+    faced = jnp.sum(jnp.where(pair_lane == inner, met, 0.0), axis=1, keepdims=True)
+    points = jnp.where(distance == half, faced, points)
     points = jnp.where(distance == 0, inner.astype(f32), points)
     by_stats = [jnp.sum(jnp.where(lane == blocks, p, 0.0), axis=1, keepdims=True) for p in pointer]
     hop = lax.broadcasted_iota(i32, (vocab_count, 1), 0)
-    stat_ok = [hop <= half, (hop >= 1) & (hop < half)]
-    points = jnp.concatenate(
-        [points] + [jnp.where(ok, p, 0.0) for ok, p in zip(stat_ok, by_stats)], axis=0
-    ).astype(i32)
+    met_stats = jnp.sum(jnp.where(lanes == blocks, met, 0.0), axis=1, keepdims=True)
+    by_stats[0] = jnp.where(hop < half, by_stats[0], 0.0)
+    by_stats[1] = jnp.where((hop >= 1) & (hop < half), by_stats[1], jnp.where(hop == half, met_stats, 0.0))
+    points = jnp.concatenate([points] + by_stats, axis=0).astype(i32)
     other = jnp.concatenate(
         [(hops[1] > 0).astype(i32), jnp.zeros((vocab_count, 1), i32), jnp.ones((vocab_count, 1), i32)], axis=0
     )
@@ -213,9 +225,10 @@
     for f in range(1, steps):
         frame = frame + (points >= home + f * SLOTS).astype(i32)
     away = points >= home
-    source = jnp.where(away, 1 + frame + steps * other, 0)
-    spot = jnp.where(away, points - home - frame * SLOTS, points)
-    spot = jnp.clip(spot, 0, jnp.where(away, SLOTS - 1, home - 1))
+    direct = points >= beyond
+    source = jnp.where(direct, 2 * steps + 1, jnp.where(away, 1 + frame + steps * other, 0))
+    spot = jnp.where(direct, points - beyond, jnp.where(away, points - home - frame * SLOTS, points))
+    spot = jnp.clip(spot, 0, jnp.where(direct, DIRECT - 1, jnp.where(away, SLOTS - 1, home - 1)))
     items = points.shape[0]
     item_lane = lax.broadcasted_iota(i32, (items, BLK), 1)
     table = jnp.where(
@@ -239,7 +252,60 @@
     return [values[0, start + j] for j in range(count)]
 
 
-def pack_kernel(send_ref, own_ref, low_ref, high_ref, pick_ref, home_ref, first_ref, second_ref, cand_ref, logit_ref):
+def in_order(place, valid, count):
+    square = (BLK, BLK)
+    up, over = lax.broadcasted_iota(jnp.int32, square, 0), lax.broadcasted_iota(jnp.int32, square, 1)
+    lanes = jnp.sum(jnp.where((place == up) & valid, over, 0), axis=1, keepdims=True)
+    row = turn(jnp.broadcast_to(lanes, square))[:1]
+    return [row[0, j] for j in range(count)]
+
+
+def first_choice(blocks, place_ref, listed_ref):
+    vocab_count, pair_count = listed_ref.shape
+    half = vocab_count // 2
+    i32 = jnp.int32
+    me, sign = place_ref[0:1, :], place_ref[1:2, :]
+    holders, inners = split(turn(listed_ref[...])[:pair_count], blocks, vocab_count)
+    pair_lane = lax.broadcasted_iota(i32, (pair_count, BLK), 1)
+    lane = lax.broadcasted_iota(i32, (1, BLK), 1)
+    reach = [jnp.zeros((1, BLK), i32), jnp.zeros((1, BLK), i32)]
+    facing = jnp.where(lane == blocks, 1, 0)
+    for s in range(vocab_count):
+        hits = (pair_lane == inners[:, s : s + 1]) & (jnp.broadcast_to(holders[:, s : s + 1], pair_lane.shape) == me)
+        seen = jnp.max(jnp.where(hits, 1, 0), axis=0, keepdims=True)
+        distance = (s - me) * sign
+        distance = jnp.where(distance < 0, distance + vocab_count, distance)
+        reach[0] = jnp.maximum(reach[0], jnp.where(distance < half, distance * seen, 0))
+        reach[1] = jnp.maximum(reach[1], jnp.where(distance > half, (vocab_count - distance) * seen, 0))
+        facing = jnp.maximum(facing, jnp.where(distance == half, seen, 0))
+    choices = []
+    for far in reach:
+        far = jnp.where(lane == blocks, half - 1, far)
+        key = jnp.broadcast_to(far * BLK + (BLK - 1 - lane), (BLK, BLK))
+        place = jnp.sum((turn(key) > key).astype(i32), axis=0, keepdims=True)
+        choices.append(in_order(place, far > 0, SLOTS))
+    place = jnp.dot(
+        jnp.broadcast_to(ones(facing > 0), (8, BLK)), earlier_lanes(), preferred_element_type=jnp.float32
+    )[:1].astype(i32)
+    choices.append(in_order(place, facing > 0, DIRECT))
+    return choices
+
+
+def pack_kernel(
+    place_ref,
+    listed_ref,
+    own_ref,
+    low_ref,
+    high_ref,
+    pick_ref,
+    home_ref,
+    first_ref,
+    second_ref,
+    direct_ref,
+    done_ref,
+    cand_ref,
+    logit_ref,
+):
     docs, positions, columns = own_ref.shape
     width = low_ref.shape[1]
     span = positions + 2 * width
@@ -269,9 +335,10 @@
     home_ref[blocks] = jnp.where(
         lane == 0, top, jnp.where(lane == 1, first, jnp.where(lane == 2, second, jnp.where(lane == 3, third, 0.0)))
     ).astype(jnp.bfloat16)
-    for chain, out_ref in enumerate((first_ref, second_ref)):
-        for j, at in enumerate(scalars(send_ref, chain, 0, SLOTS)):
+    for out_ref, choice in zip((first_ref, second_ref, direct_ref), first_choice(blocks, place_ref, listed_ref)):
+        for j, at in enumerate(choice):
             out_ref[j] = home_ref[at]
+    done_ref[...] = jnp.zeros(done_ref.shape, jnp.int32)
 
 
 def ready_kernel(chain, step, send_ref, home_ref, *refs):
@@ -303,7 +370,7 @@
 
 def stage_kernel(steps, item_ref, *refs):
     sources, stage_ref = refs[:-1], refs[-1]
-    for s, source in zip([s for s in range(2 * steps + 1) if s not in (steps, 2 * steps)], sources):
+    for s, source in zip([s for s in range(2 * steps + 2) if s not in (steps, 2 * steps)], sources):
         bring(item_ref, s, source, stage_ref)
 
 
@@ -355,7 +422,8 @@
         stage_ref[i] = held_ref[i]
     bring(item_ref, steps, ahead_ref, stage_ref)
     bring(item_ref, 2 * steps, behind_ref, stage_ref)
-    holders = [h for h in range(steps + 1)] + [2 * steps + h for h in range(1, steps)]
+    facing = steps + 1
+    holders = [h for h in range(facing)] + [2 * facing + h for h in range(1, facing + 1)]
     peaks, sums = [], []
     for h in holders:
         stats = jnp.dot(spread, stage_ref[K * blocks + h], preferred_element_type=jnp.float32)
@@ -452,7 +520,7 @@
     row_count = doc_count * pos_count
     pair_count = student_blocks * K
     vocab_count = lax.axis_size("vocab")
-    steps = vocab_count // 2
+    steps = vocab_count // 2 - 1
     home = teacher_blocks + 1
     vocab_index = lax.axis_index("vocab")
     seq_index = lax.axis_index("seq")
@@ -483,33 +551,40 @@
     def room(mib):
         return pltpu.CompilerParams(vmem_limit_bytes=mib * 1024 * 1024)
 
-    with jax.named_scope("plan"):
-        listed = src_block.reshape(vocab_count, pair_count)
-        table = jax.ShapeDtypeStruct((8, BLK), jnp.int32)
-        send, items, left = pl.pallas_call(
-            functools.partial(plan_kernel, teacher_blocks),
-            out_shape=(jax.ShapeDtypeStruct((8, 2 * BLK), jnp.int32), table, table),
-            in_specs=[smem, vmem],
-            out_specs=(vmem,) * 3,
-            scratch_shapes=[pltpu.VMEM((6 * steps, vocab_count, BLK), jnp.float32)],
-            compiler_params=room(8),
-        )(jnp.stack([vocab_index, sign]).astype(jnp.int32), listed)
-
     def planes(count):
         return jax.ShapeDtypeStruct((count, ROWS, BLK), jnp.bfloat16)
 
     with jax.named_scope("pack"):
-        own, ahead, behind = pl.pallas_call(
+        listed = src_block.reshape(vocab_count, pair_count)
+        place = jnp.stack([vocab_index, sign]).astype(jnp.int32)
+        own, ahead, behind, direct, packed = pl.pallas_call(
             pack_kernel,
-            out_shape=(planes(home), planes(SLOTS), planes(SLOTS)),
-            in_specs=[vmem] * 5,
-            out_specs=(vmem,) * 3,
+            out_shape=(
+                planes(home),
+                planes(SLOTS),
+                planes(SLOTS),
+                planes(DIRECT),
+                jax.ShapeDtypeStruct((8, BLK), jnp.int32),
+            ),
+            in_specs=[vmem] * 6,
+            out_specs=(vmem,) * 5,
             scratch_shapes=[
                 pltpu.VMEM((doc_count * span, teacher_cols), jnp.bfloat16),
                 pltpu.VMEM((teacher_blocks, ROWS, BLK), jnp.bfloat16),
             ],
             compiler_params=room(16),
-        )(send, teacher_logits, low, high, pick)
+        )(jnp.broadcast_to(place[:, None], (2, BLK)), listed, teacher_logits, low, high, pick)
+
+    with jax.named_scope("plan"):
+        table = jax.ShapeDtypeStruct((8, BLK), jnp.int32)
+        send, items, left = pl.pallas_call(
+            functools.partial(plan_kernel, teacher_blocks),
+            out_shape=(jax.ShapeDtypeStruct((8, 2 * BLK), jnp.int32), table, table),
+            in_specs=[smem, vmem, vmem],
+            out_specs=(vmem,) * 3,
+            scratch_shapes=[pltpu.VMEM((6 * steps, vocab_count, BLK), jnp.float32)],
+            compiler_params=room(8),
+        )(place, listed, packed)
 
     def chosen(chain, step, frames):
         part = pl.pallas_call(
@@ -537,6 +612,8 @@
             if step:
                 behind = chosen(1, step, came_behind)
             came_behind.append(lax.ppermute(behind, ("seq", "vocab"), backward))
+        across = [(v, (v + vocab_count // 2) % vocab_count) for v in range(vocab_count)]
+        came_direct = lax.ppermute(direct, "vocab", across)
 
     with jax.named_scope("student"):
         top, total = pl.pallas_call(
@@ -548,7 +625,7 @@
         )(student_logits)
 
     with jax.named_scope("stage"):
-        early = (own, *came_ahead[:-1], *came_behind[:-1])
+        early = (own, *came_ahead[:-1], *came_behind[:-1], came_direct)
         held = pl.pallas_call(
             functools.partial(stage_kernel, steps),
             out_shape=planes(pair_count + 2 * vocab_count),
@@ -565,7 +642,7 @@
             out_specs=vmem,
             scratch_shapes=[
                 pltpu.VMEM((pair_count + 2 * vocab_count, ROWS, BLK), jnp.bfloat16),
-                pltpu.VMEM((3 * steps, row_count, BLK), jnp.float32),
+                pltpu.VMEM((2 * vocab_count, row_count, BLK), jnp.float32),
             ],
             compiler_params=room(20),
         )(items, held, came_ahead[-1], came_behind[-1], spread, weights, student_logits, top, total)

time: 211 us -> 218 us (1.033)
  the two profiles are of different devices: /device:TPU:6 before, /device:TPU:28 now
where the time goes in v6:
time: 218 us; the launch traced here: 217 us
  waiting for transfers between devices  90.8 us (42%)
  starting transfers between devices  74.9 us (34%)
  Pallas kernels  26.1 us (12%)
  between operations  15.2 us (7%)
  local copies, waits for them, and re-layouts  8.07 us (4%)
    ppermute x7, waiting for transfers between devices, shards(): came_behind.append(lax.ppermute(behind, ('seq', 'vocab'), backward))  48.8 us
    ppermute x7, starting transfers between devices, shards(): came_behind.append(lax.ppermute(behind, ('seq', 'vocab'), backward))  44.9 us
    ppermute x1, waiting for transfers between devices, shards(): came_direct = lax.ppermute(direct, 'vocab', across)  18.5 us
    ppermute x7, starting transfers between devices, shards(): came_ahead.append(lax.ppermute(ahead, ('seq', 'vocab'), forward))  13.4 us
    ppermute x7, waiting for transfers between devices, shards(): came_ahead.append(lax.ppermute(ahead, ('seq', 'vocab'), forward))  11.3 us
    all_to_all x1, waiting for transfers between devices, shards(): lax.all_to_all(sent, 'vocab', split_axis=0, concat_axis=0, tiled=True)  10.1 us
    all_to_all x1, starting transfers between devices, shards(): lax.all_to_all(sent, 'vocab', split_axis=0, concat_axis=0, tiled=True)  9.14 us
    pallas_call x12, Pallas kernels, chosen(): pl.pallas_call(functools.partial(pass_kernel, chain, step, home), out_sha...  6.55 us
  transfers between devices with their start and end apart: 19, of which 12 were waited for; matrix products, arithmetic and copies ran while one was open for 2% of the time, Pallas kernels for 9%

profile of v6, /device:TPU:28, one launch (start us, length us, event | category | flops | bytes accessed | tf_op | source)
XLA Modules:
  0.0 217.2 jit_solution(16266486776994741494)
XLA Ops:
  7.7 1.9 collective-permute-start
  9.7 3.6 %collective-permute-start.1 = (bf16[2,16,4736]{2,1,0:T(8,128)(2,1)S(1)}, bf16[2,16,4736]{2,1,0:T(8,128)(2,1)S(1)}, u32[]{:S(2)}, u32[]{:S(2)}) collective-permute-start(bf16[2,16,4736]{2,1,0:T(8,128)(2,1)S(1)} %get-tuple-element.157), channel_id=1, source_target_pairs={{16,0},{32,16},{48,32},{64,48},{80,64},{96,80},{112,96},{17,1},{33... | collective-permute-start | bytes 909320 | tf_op jit(solution)/shard_map/halo/ppermute | solution.py:24
  15.9 1.8 collective-permute-done.1.high_ref
  17.7 1.8 pack.1
  20.2 11.4 %collective-permute-start.8 = (bf16[22,104,128]{2,1,0:T(8,128)(2,1)S(1)}, bf16[22,104,128]{2,1,0:T(8,128)(2,1)S(1)}, u32[]{:S(2)}, u32[]{:S(2)}) collective-permute-start(bf16[22,104,128]{2,1,0:T(8,128)(2,1)S(1)} %get-tuple-element.95), channel_id=1, source_target_pairs={{0,15},{1,0},{2,1},{3,2},{4,3},{5,4},{6,5},{7,6},{8,7},{9,8},{10,9... | collective-permute-start | bytes 1757192 | tf_op jit(solution)/shard_map/ring/ppermute | solution.py:614
  31.6 1.9 collective-permute-start.2
  33.5 3.7 %plan.1 = (s32[8,256]{1,0:T(8,128)S(1)}, s32[8,128]{1,0:T(8,128)S(1)}, s32[8,128]{1,0:T(8,128)S(1)}) custom-call(s32[2]{0:T(128)S(1)} %pad_add_fusion.place_ref, s32[16,64]{1,0:T(8,128)S(1)} %reshape.252.listed_ref, s32[8,128]{1,0:T(8,128)S(1)} %get-tuple-element.89.after_ref), custom_call_target="tpu_custom_call" | custom-call | tf_op jit(solution)/shard_map/plan/pallas_call | solution.py:580
  37.7 4.9 %collective-permute-done.8.newest_ref.refs_0_.refs_7_ = bf16[22,104,128]{2,1,0:T(8,128)(2,1)S(1)} collective-permute-done((bf16[22,104,128]{2,1,0:T(8,128)(2,1)S(1)}, bf16[22,104,128]{2,1,0:T(8,128)(2,1)S(1)}, u32[]{:S(2)}, u32[]{:S(2)}) %collective-permute-start.8) | collective-permute-done | bytes 585760 | tf_op jit(solution)/shard_map/ring/ppermute | solution.py:614
  43.8 5.6 %collective-permute-start.9 = (bf16[22,104,128]{2,1,0:T(8,128)(2,1)}, bf16[22,104,128]{2,1,0:T(8,128)(2,1)S(1)}, u32[]{:S(2)}, u32[]{:S(2)}) collective-permute-start(bf16[22,104,128]{2,1,0:T(8,128)(2,1)} %ring.35), channel_id=1, source_target_pairs={{0,15},{1,0},{2,1},{3,2},{4,3},{5,4},{6,5},{7,6},{8,7},{9,8},{10,9... | collective-permute-start | bytes 1757192 | tf_op jit(solution)/shard_map/ring/ppermute | solution.py:614
  50.4 1.9 collective-permute-start.3
  53.2 8.5 %collective-permute-done.9.newest_ref.refs_1_.refs_8_ = bf16[22,104,128]{2,1,0:T(8,128)(2,1)S(1)} collective-permute-done((bf16[22,104,128]{2,1,0:T(8,128)(2,1)}, bf16[22,104,128]{2,1,0:T(8,128)(2,1)S(1)}, u32[]{:S(2)}, u32[]{:S(2)}) %collective-permute-start.9) | collective-permute-done | bytes 585760 | tf_op jit(solution)/shard_map/ring/ppermute | solution.py:614
  62.0 5.5 %collective-permute-start.10 = (bf16[22,104,128]{2,1,0:T(8,128)(2,1)S(1)}, bf16[22,104,128]{2,1,0:T(8,128)(2,1)S(1)}, u32[]{:S(2)}, u32[]{:S(2)}) collective-permute-start(bf16[22,104,128]{2,1,0:T(8,128)(2,1)S(1)} %ring.37), channel_id=1, source_target_pairs={{0,15},{1,0},{2,1},{3,2},{4,3},{5,4},{6,5},{7,6},{8,7},{9,8},{10,9... | collective-permute-start | bytes 1757192 | tf_op jit(solution)/shard_map/ring/ppermute | solution.py:614
  67.8 1.9 collective-permute-start.4
  70.7 10.1 %collective-permute-done.10.newest_ref.refs_2_.refs_9_ = bf16[22,104,128]{2,1,0:T(8,128)(2,1)S(1)} collective-permute-done((bf16[22,104,128]{2,1,0:T(8,128)(2,1)S(1)}, bf16[22,104,128]{2,1,0:T(8,128)(2,1)S(1)}, u32[]{:S(2)}, u32[]{:S(2)}) %collective-permute-start.10) | collective-permute-done | bytes 585760 | tf_op jit(solution)/shard_map/ring/ppermute | solution.py:614
  81.1 5.6 %collective-permute-start.11 = (bf16[22,104,128]{2,1,0:T(8,128)(2,1)S(1)}, bf16[22,104,128]{2,1,0:T(8,128)(2,1)S(1)}, u32[]{:S(2)}, u32[]{:S(2)}) collective-permute-start(bf16[22,104,128]{2,1,0:T(8,128)(2,1)S(1)} %ring.39), channel_id=1, source_target_pairs={{0,15},{1,0},{2,1},{3,2},{4,3},{5,4},{6,5},{7,6},{8,7},{9,8},{10,9... | collective-permute-start | bytes 1757192 | tf_op jit(solution)/shard_map/ring/ppermute | solution.py:614
  87.0 1.9 collective-permute-start.5
  90.2 9.7 %collective-permute-done.11.newest_ref.refs_3_.refs_10_ = bf16[22,104,128]{2,1,0:T(8,128)(2,1)S(1)} collective-permute-done((bf16[22,104,128]{2,1,0:T(8,128)(2,1)S(1)}, bf16[22,104,128]{2,1,0:T(8,128)(2,1)S(1)}, u32[]{:S(2)}, u32[]{:S(2)}) %collective-permute-start.11) | collective-permute-done | bytes 585760 | tf_op jit(solution)/shard_map/ring/ppermute | solution.py:614
  100.2 5.6 %collective-permute-start.12 = (bf16[22,104,128]{2,1,0:T(8,128)(2,1)S(1)}, bf16[22,104,128]{2,1,0:T(8,128)(2,1)S(1)}, u32[]{:S(2)}, u32[]{:S(2)}) collective-permute-start(bf16[22,104,128]{2,1,0:T(8,128)(2,1)S(1)} %ring.41), channel_id=1, source_target_pairs={{0,15},{1,0},{2,1},{3,2},{4,3},{5,4},{6,5},{7,6},{8,7},{9,8},{10,9... | collective-permute-start | bytes 1757192 | tf_op jit(solution)/shard_map/ring/ppermute | solution.py:614
  106.1 1.9 collective-permute-start.6
  109.5 8.7 %collective-permute-done.12.newest_ref.refs_11_.refs_4_ = bf16[22,104,128]{2,1,0:T(8,128)(2,1)S(1)} collective-permute-done((bf16[22,104,128]{2,1,0:T(8,128)(2,1)S(1)}, bf16[22,104,128]{2,1,0:T(8,128)(2,1)S(1)}, u32[]{:S(2)}, u32[]{:S(2)}) %collective-permute-start.12) | collective-permute-done | bytes 585760 | tf_op jit(solution)/shard_map/ring/ppermute | solution.py:614
  118.4 5.6 %collective-permute-start.13 = (bf16[22,104,128]{2,1,0:T(8,128)(2,1)S(1)}, bf16[22,104,128]{2,1,0:T(8,128)(2,1)S(1)}, u32[]{:S(2)}, u32[]{:S(2)}) collective-permute-start(bf16[22,104,128]{2,1,0:T(8,128)(2,1)S(1)} %ring.43), channel_id=1, source_target_pairs={{0,15},{1,0},{2,1},{3,2},{4,3},{5,4},{6,5},{7,6},{8,7},{9,8},{10,9... | collective-permute-start | bytes 1757192 | tf_op jit(solution)/shard_map/ring/ppermute | solution.py:614
  125.5 1.9 collective-permute-start.7
  128.8 6.8 %collective-permute-done.13.refs_12_.newest_ref = bf16[22,104,128]{2,1,0:T(8,128)(2,1)S(1)} collective-permute-done((bf16[22,104,128]{2,1,0:T(8,128)(2,1)S(1)}, bf16[22,104,128]{2,1,0:T(8,128)(2,1)S(1)}, u32[]{:S(2)}, u32[]{:S(2)}) %collective-permute-start.13) | collective-permute-done | bytes 585760 | tf_op jit(solution)/shard_map/ring/ppermute | solution.py:614
  136.6 5.6 %collective-permute-start.16 = (bf16[22,104,128]{2,1,0:T(8,128)(2,1)}, bf16[22,104,128]{2,1,0:T(8,128)(2,1)}, u32[]{:S(2)}, u32[]{:S(2)}) collective-permute-start(bf16[22,104,128]{2,1,0:T(8,128)(2,1)} %ring.47), channel_id=1, source_target_pairs={{0,15},{1,0},{2,1},{3,2},{4,3},{5,4},{6,5},{7,6},{8,7},{9,8},{10,9... | collective-permute-start | bytes 1757192 | tf_op jit(solution)/shard_map/ring/ppermute | solution.py:614
  142.2 10.1 %collective-permute-done.7.refs_6_.newest_ref = bf16[22,104,128]{2,1,0:T(8,128)(2,1)S(1)} collective-permute-done((bf16[22,104,128]{2,1,0:T(8,128)(2,1)S(1)}, bf16[22,104,128]{2,1,0:T(8,128)(2,1)S(1)}, u32[]{:S(2)}, u32[]{:S(2)}) %collective-permute-start.7) | collective-permute-done | bytes 585760 | tf_op jit(solution)/shard_map/ring/ppermute | solution.py:611
  153.5 1.9 collective-permute-start.15
  155.4 1.9 collective-permute-start.14
  158.1 18.5 %collective-permute-done.14.refs_13_ = bf16[9,104,128]{2,1,0:T(8,128)(2,1)S(1)} collective-permute-done((bf16[9,104,128]{2,1,0:T(8,128)(2,1)S(1)}, bf16[9,104,128]{2,1,0:T(8,128)(2,1)S(1)}, u32[]{:S(2)}, u32[]{:S(2)}) %collective-permute-start.14) | collective-permute-done | bytes 239648 | tf_op jit(solution)/shard_map/ring/ppermute | solution.py:616
  176.6 1.8 stage.1.held_ref
  181.6 5.5 %map.1 = f32[8,128]{1,0:T(8,128)S(1)} custom-call(s32[8,128]{1,0:T(8,128)S(1)} %get-tuple-element.91.item_ref, bf16[96,104,128]{2,1,0:T(8,128)(2,1)S(1)} %copy-done.1, bf16[22,104,128]{2,1,0:T(8,128)(2,1)} %collective-permute-done.15.ahead_ref, bf16[22,104,128]{2,1,0:T(8,128)(2,1)} %collective-permute-done.16.behind_ref, ...), custom_call_target="tpu_custom_call" | custom-call | tf_op jit(solution)/shard_map/map/pallas_call | solution.py:638
  187.7 9.1 %all-to-all-start.1 = ((f32[16,4,128]{2,1,0:T(4,128)}), f32[16,4,128]{2,1,0:T(4,128)S(1)}, u32[]{:S(2)}, u32[]{:S(2)}) async-start(f32[16,4,128]{2,1,0:T(4,128)} %broadcast_in_dim.55), calls=%async_computation.1 | async-start | bytes 65536 | tf_op jit(solution)/shard_map/finish/all_to_all | solution.py:652
  199.4 10.1 %all-to-all-done.1 = f32[16,4,128]{2,1,0:T(4,128)S(1)} async-done(((f32[16,4,128]{2,1,0:T(4,128)}), f32[16,4,128]{2,1,0:T(4,128)S(1)}, u32[]{:S(2)}, u32[]{:S(2)}) %all-to-all-start.1) | async-done | bytes 32800 | tf_op jit(solution)/shard_map/finish/all_to_all | solution.py:652
  (86 shorter events, 25.3 us)
Async XLA Ops:
  6.5 11.2 %copy-start.7 = (bf16[2,64,4736]{2,1,0:T(8,128)(2,1)S(1)}, bf16[2,64,4736]{2,1,0:T(8,128)(2,1)}, u32[]{:S(2)}) copy-start(bf16[2,64,4736]{2,1,0:T(8,128)(2,1)} %own_ref.1) | copy-start | bytes 3637252
  6.5 173.3 %all-gather.2.cloned.1.call-start = ((), (), s32[]{:S(2)}) async-start(), calls=%async_computation.2 | async-start | bytes 2621440 | tf_op jit(solution)/shard_map/weights/all_gather | solution.py:533
  7.7 8.1 %collective-permute-start = (bf16[2,16,4736]{2,1,0:T(8,128)(2,1)S(1)}, bf16[2,16,4736]{2,1,0:T(8,128)(2,1)S(1)}, u32[]{:S(2)}, u32[]{:S(2)}) collective-permute-start(bf16[2,16,4736]{2,1,0:T(8,128)(2,1)S(1)} %get-tuple-element.158), channel_id=1, source_target_pairs={{0,16},{16,32},{32,48},{48,64},{64,80},{80,96},{96,112},{1,17},{17... | collective-permute-start | bytes 909320 | tf_op jit(solution)/shard_map/halo/ppermute | solution.py:23
  9.7 8.0 %collective-permute-start.1 = (bf16[2,16,4736]{2,1,0:T(8,128)(2,1)S(1)}, bf16[2,16,4736]{2,1,0:T(8,128)(2,1)S(1)}, u32[]{:S(2)}, u32[]{:S(2)}) collective-permute-start(bf16[2,16,4736]{2,1,0:T(8,128)(2,1)S(1)} %get-tuple-element.157), channel_id=1, source_target_pairs={{16,0},{32,16},{48,32},{64,48},{80,64},{96,80},{112,96},{17,1},{33... | collective-permute-start | bytes 909320 | tf_op jit(solution)/shard_map/halo/ppermute | solution.py:24
  15.9 3.6 %copy-start.8 = (bf16[2,16,4736]{2,1,0:T(8,128)(2,1)}, bf16[2,16,4736]{2,1,0:T(8,128)(2,1)S(1)}, u32[]{:S(2)}) copy-start(bf16[2,16,4736]{2,1,0:T(8,128)(2,1)S(1)} %collective-permute-done.low_ref) | copy-start | bytes 909316
  17.6 13.9 %copy-start.10 = (bf16[2,16,4736]{2,1,0:T(8,128)(2,1)}, bf16[2,16,4736]{2,1,0:T(8,128)(2,1)S(1)}, u32[]{:S(2)}) copy-start(bf16[2,16,4736]{2,1,0:T(8,128)(2,1)S(1)} %collective-permute-done.1.high_ref) | copy-start | bytes 909316
  19.5 0.7 copy-start.2
  20.2 22.5 %collective-permute-start.8 = (bf16[22,104,128]{2,1,0:T(8,128)(2,1)S(1)}, bf16[22,104,128]{2,1,0:T(8,128)(2,1)S(1)}, u32[]{:S(2)}, u32[]{:S(2)}) collective-permute-start(bf16[22,104,128]{2,1,0:T(8,128)(2,1)S(1)} %get-tuple-element.95), channel_id=1, source_target_pairs={{0,15},{1,0},{2,1},{3,2},{4,3},{5,4},{6,5},{7,6},{8,7},{9,8},{10,9... | collective-permute-start | bytes 1757192 | tf_op jit(solution)/shard_map/ring/ppermute | solution.py:614
  31.6 17.8 %collective-permute-start.2 = (bf16[22,104,128]{2,1,0:T(8,128)(2,1)S(1)}, bf16[22,104,128]{2,1,0:T(8,128)(2,1)S(1)}, u32[]{:S(2)}, u32[]{:S(2)}) collective-permute-start(bf16[22,104,128]{2,1,0:T(8,128)(2,1)S(1)} %get-tuple-element.93), channel_id=1, source_target_pairs={{0,1},{1,2},{2,3},{3,4},{4,5},{5,6},{6,7},{7,8},{8,9},{9,10},{10,1... | collective-permute-start | bytes 1757192 | tf_op jit(solution)/shard_map/ring/ppermute | solution.py:611
  43.8 18.0 %collective-permute-start.9 = (bf16[22,104,128]{2,1,0:T(8,128)(2,1)}, bf16[22,104,128]{2,1,0:T(8,128)(2,1)S(1)}, u32[]{:S(2)}, u32[]{:S(2)}) collective-permute-start(bf16[22,104,128]{2,1,0:T(8,128)(2,1)} %ring.35), channel_id=1, source_target_pairs={{0,15},{1,0},{2,1},{3,2},{4,3},{5,4},{6,5},{7,6},{8,7},{9,8},{10,9... | collective-permute-start | bytes 1757192 | tf_op jit(solution)/shard_map/ring/ppermute | solution.py:614
  50.4 17.1 %collective-permute-start.3 = (bf16[22,104,128]{2,1,0:T(8,128)(2,1)}, bf16[22,104,128]{2,1,0:T(8,128)(2,1)S(1)}, u32[]{:S(2)}, u32[]{:S(2)}) collective-permute-start(bf16[22,104,128]{2,1,0:T(8,128)(2,1)} %ring.25), channel_id=1, source_target_pairs={{0,1},{1,2},{2,3},{3,4},{4,5},{5,6},{6,7},{7,8},{8,9},{9,10},{10,1... | collective-permute-start | bytes 1757192 | tf_op jit(solution)/shard_map/ring/ppermute | solution.py:611
  62.0 18.8 %collective-permute-start.10 = (bf16[22,104,128]{2,1,0:T(8,128)(2,1)S(1)}, bf16[22,104,128]{2,1,0:T(8,128)(2,1)S(1)}, u32[]{:S(2)}, u32[]{:S(2)}) collective-permute-start(bf16[22,104,128]{2,1,0:T(8,128)(2,1)S(1)} %ring.37), channel_id=1, source_target_pairs={{0,15},{1,0},{2,1},{3,2},{4,3},{5,4},{6,5},{7,6},{8,7},{9,8},{10,9... | collective-permute-start | bytes 1757192 | tf_op jit(solution)/shard_map/ring/ppermute | solution.py:614
  67.8 18.9 %collective-permute-start.4 = (bf16[22,104,128]{2,1,0:T(8,128)(2,1)S(1)}, bf16[22,104,128]{2,1,0:T(8,128)(2,1)S(1)}, u32[]{:S(2)}, u32[]{:S(2)}) collective-permute-start(bf16[22,104,128]{2,1,0:T(8,128)(2,1)S(1)} %ring.27), channel_id=1, source_target_pairs={{0,1},{1,2},{2,3},{3,4},{4,5},{5,6},{6,7},{7,8},{8,9},{9,10},{10,1... | collective-permute-start | bytes 1757192 | tf_op jit(solution)/shard_map/ring/ppermute | solution.py:611
  81.1 18.8 %collective-permute-start.11 = (bf16[22,104,128]{2,1,0:T(8,128)(2,1)S(1)}, bf16[22,104,128]{2,1,0:T(8,128)(2,1)S(1)}, u32[]{:S(2)}, u32[]{:S(2)}) collective-permute-start(bf16[22,104,128]{2,1,0:T(8,128)(2,1)S(1)} %ring.39), channel_id=1, source_target_pairs={{0,15},{1,0},{2,1},{3,2},{4,3},{5,4},{6,5},{7,6},{8,7},{9,8},{10,9... | collective-permute-start | bytes 1757192 | tf_op jit(solution)/shard_map/ring/ppermute | solution.py:614
  87.0 18.8 %collective-permute-start.5 = (bf16[22,104,128]{2,1,0:T(8,128)(2,1)S(1)}, bf16[22,104,128]{2,1,0:T(8,128)(2,1)S(1)}, u32[]{:S(2)}, u32[]{:S(2)}) collective-permute-start(bf16[22,104,128]{2,1,0:T(8,128)(2,1)S(1)} %ring.29), channel_id=1, source_target_pairs={{0,1},{1,2},{2,3},{3,4},{4,5},{5,6},{6,7},{7,8},{8,9},{9,10},{10,1... | collective-permute-start | bytes 1757192 | tf_op jit(solution)/shard_map/ring/ppermute | solution.py:611
  100.2 18.0 %collective-permute-start.12 = (bf16[22,104,128]{2,1,0:T(8,128)(2,1)S(1)}, bf16[22,104,128]{2,1,0:T(8,128)(2,1)S(1)}, u32[]{:S(2)}, u32[]{:S(2)}) collective-permute-start(bf16[22,104,128]{2,1,0:T(8,128)(2,1)S(1)} %ring.41), channel_id=1, source_target_pairs={{0,15},{1,0},{2,1},{3,2},{4,3},{5,4},{6,5},{7,6},{8,7},{9,8},{10,9... | collective-permute-start | bytes 1757192 | tf_op jit(solution)/shard_map/ring/ppermute | solution.py:614
  106.1 19.2 %collective-permute-start.6 = (bf16[22,104,128]{2,1,0:T(8,128)(2,1)S(1)}, bf16[22,104,128]{2,1,0:T(8,128)(2,1)S(1)}, u32[]{:S(2)}, u32[]{:S(2)}) collective-permute-start(bf16[22,104,128]{2,1,0:T(8,128)(2,1)S(1)} %ring.31), channel_id=1, source_target_pairs={{0,1},{1,2},{2,3},{3,4},{4,5},{5,6},{6,7},{7,8},{8,9},{9,10},{10,1... | collective-permute-start | bytes 1757192 | tf_op jit(solution)/shard_map/ring/ppermute | solution.py:611
  118.4 17.1 %collective-permute-start.13 = (bf16[22,104,128]{2,1,0:T(8,128)(2,1)S(1)}, bf16[22,104,128]{2,1,0:T(8,128)(2,1)S(1)}, u32[]{:S(2)}, u32[]{:S(2)}) collective-permute-start(bf16[22,104,128]{2,1,0:T(8,128)(2,1)S(1)} %ring.43), channel_id=1, source_target_pairs={{0,15},{1,0},{2,1},{3,2},{4,3},{5,4},{6,5},{7,6},{8,7},{9,8},{10,9... | collective-permute-start | bytes 1757192 | tf_op jit(solution)/shard_map/ring/ppermute | solution.py:614
  125.5 26.8 %collective-permute-start.7 = (bf16[22,104,128]{2,1,0:T(8,128)(2,1)S(1)}, bf16[22,104,128]{2,1,0:T(8,128)(2,1)S(1)}, u32[]{:S(2)}, u32[]{:S(2)}) collective-permute-start(bf16[22,104,128]{2,1,0:T(8,128)(2,1)S(1)} %ring.33), channel_id=1, source_target_pairs={{0,1},{1,2},{2,3},{3,4},{4,5},{5,6},{6,7},{7,8},{8,9},{9,10},{10,1... | collective-permute-start | bytes 1757192 | tf_op jit(solution)/shard_map/ring/ppermute | solution.py:611
  128.8 26.6 %copy-start.3 = (bf16[9,104,128]{2,1,0:T(8,128)(2,1)S(1)}, bf16[9,104,128]{2,1,0:T(8,128)(2,1)}, u32[]{:S(2)}) copy-start(bf16[9,104,128]{2,1,0:T(8,128)(2,1)} %copy-done.2) | copy-start | bytes 718852
  128.8 28.6 %copy-start.4 = (bf16[2,64,4096]{2,1,0:T(8,128)(2,1)S(1)}, bf16[2,64,4096]{2,1,0:T(8,128)(2,1)}, u32[]{:S(2)}) copy-start(bf16[2,64,4096]{2,1,0:T(8,128)(2,1)} %student_ref.3) | copy-start | bytes 3145732
  136.6 43.2 %collective-permute-start.16 = (bf16[22,104,128]{2,1,0:T(8,128)(2,1)}, bf16[22,104,128]{2,1,0:T(8,128)(2,1)}, u32[]{:S(2)}, u32[]{:S(2)}) collective-permute-start(bf16[22,104,128]{2,1,0:T(8,128)(2,1)} %ring.47), channel_id=1, source_target_pairs={{0,15},{1,0},{2,1},{3,2},{4,3},{5,4},{6,5},{7,6},{8,7},{9,8},{10,9... | collective-permute-start | bytes 1757192 | tf_op jit(solution)/shard_map/ring/ppermute | solution.py:614
  153.5 26.4 %collective-permute-start.15 = (bf16[22,104,128]{2,1,0:T(8,128)(2,1)}, bf16[22,104,128]{2,1,0:T(8,128)(2,1)}, u32[]{:S(2)}, u32[]{:S(2)}) collective-permute-start(bf16[22,104,128]{2,1,0:T(8,128)(2,1)} %ring.45), channel_id=1, source_target_pairs={{0,1},{1,2},{2,3},{3,4},{4,5},{5,6},{6,7},{7,8},{8,9},{9,10},{10,1... | collective-permute-start | bytes 1757192 | tf_op jit(solution)/shard_map/ring/ppermute | solution.py:611
  155.4 21.2 %collective-permute-start.14 = (bf16[9,104,128]{2,1,0:T(8,128)(2,1)S(1)}, bf16[9,104,128]{2,1,0:T(8,128)(2,1)S(1)}, u32[]{:S(2)}, u32[]{:S(2)}) collective-permute-start(bf16[9,104,128]{2,1,0:T(8,128)(2,1)S(1)} %copy-done.3), channel_id=1, source_target_pairs={{0,8},{1,9},{2,10},{3,11},{4,12},{5,13},{6,14},{7,15},{8,0},{9,1},... | collective-permute-start | bytes 718856 | tf_op jit(solution)/shard_map/ring/ppermute | solution.py:616
  178.4 1.5 copy-start
  179.9 1.7 copy-start.1
  181.6 17.7 %copy-start.5 = (bf16[2,64,4096]{2,1,0:T(8,128)(2,1)S(1)}, bf16[2,64,4096]{2,1,0:T(8,128)(2,1)}, u32[]{:S(2)}) copy-start(bf16[2,64,4096]{2,1,0:T(8,128)(2,1)} %student_ref.3) | copy-start | bytes 3145732
  181.6 17.7 %copy-start.9 = (bf16[2,16,4736]{2,1,0:T(8,128)(2,1)S(1)}, bf16[2,16,4736]{2,1,0:T(8,128)(2,1)}, u32[]{:S(2)}) copy-start(bf16[2,16,4736]{2,1,0:T(8,128)(2,1)} %copy-done.8) | copy-start | bytes 909316
  181.6 17.8 %copy-start.12 = (s32[512,2]{0,1:T(2,128)S(1)}, s32[512,2]{0,1:T(2,128)}, u32[]{:S(2)}) copy-start(s32[512,2]{0,1:T(2,128)} %param.12) | copy-start | bytes 12292
  187.7 21.8 %all-to-all-start.1 = ((f32[16,4,128]{2,1,0:T(4,128)}), f32[16,4,128]{2,1,0:T(4,128)S(1)}, u32[]{:S(2)}, u32[]{:S(2)}) async-start(f32[16,4,128]{2,1,0:T(4,128)} %broadcast_in_dim.55), calls=%async_computation.1 | async-start | bytes 65536 | tf_op jit(solution)/shard_map/finish/all_to_all | solution.py:652
  209.7 0.6 copy-start.13
Sparse Core Ops, SparseCore 0:
  52.5 35.1 all-gather.1

commit v7 on v6

--- a/solution.py
+++ b/solution.py
@@ -11,8 +11,7 @@
 K = 2
 W = 16
 ROWS = 104
-SLOTS = 22
-DIRECT = 9
+SLOTS = 21
 TINY = 1.2e-38
 
 
@@ -35,8 +34,36 @@
     return pairs
 
 
+def tie_key(block):
+    return (block * 5) & 7
+
+
+def ways(distance, block, share, vocab_count):
+    half = vocab_count // 2
+    first = tie_key(block) < share
+    ahead = jnp.where((distance >= 1) & ((distance < half) | ((distance == half) & first)), distance, 0)
+    behind = jnp.where((distance > half) | ((distance == half) & ~first), vocab_count - distance, 0)
+    return ahead, behind
+
+
 def ones(mask):
     return jnp.where(mask, 1.0, 0.0).astype(jnp.bfloat16)
+
+
+def tie_share(reach, facing, lane, half):
+    share = jnp.zeros((reach[0].shape[0], 1), jnp.int32)
+    for part in range(1, 9):
+        first = tie_key(lane) < part
+        more = jnp.where(facing & first, half, reach[0]) - jnp.where(facing & ~first, half, reach[1])
+        share = share + (jnp.sum(more, axis=1, keepdims=True) <= 0).astype(jnp.int32)
+    return share
+
+
+def full_reach(reach, facing, lane, share, blocks, half):
+    first = tie_key(lane) < share
+    ahead = jnp.where(facing & first, half, reach[0])
+    behind = jnp.where(facing & ~first, half, reach[1])
+    return [jnp.where(lane == blocks, half, ahead), jnp.where(lane == blocks, half - 1, behind)]
 
 
 def split(listed, blocks, vocab_count):
@@ -62,9 +89,8 @@
 def plan_kernel(blocks, place_ref, listed_ref, after_ref, send_ref, item_ref, fit_ref, book_ref):
     vocab_count, pair_count = listed_ref.shape
     half = vocab_count // 2
-    steps = half - 1
+    steps = half
     home = blocks + 1
-    beyond = home + steps * SLOTS
     me, sign = place_ref[0], place_ref[1]
     f32, i32 = jnp.float32, jnp.int32
     shape = (vocab_count, BLK)
@@ -73,13 +99,11 @@
     listed = listed_ref[...]
     row_holder, _ = split(listed, blocks, vocab_count)
     holders, inners = split(turn(listed)[:pair_count], blocks, vocab_count)
-    facing = me + half
-    facing = jnp.where(facing >= vocab_count, facing - vocab_count, facing)
     lane = lax.broadcasted_iota(i32, shape, 1)
     row = lax.broadcasted_iota(i32, shape, 0)
 
     reach = [jnp.zeros(shape, i32), jnp.zeros(shape, i32)]
-    across = jnp.zeros((1, BLK), i32)
+    across = jnp.zeros(shape, i32)
     pair_lane = lax.broadcasted_iota(i32, (pair_count, BLK), 1)
     pair_row = lax.broadcasted_iota(i32, (vocab_count, pair_count), 0)
     for s in range(vocab_count):
@@ -93,9 +117,9 @@
         needed = hits > 0
         reach[0] = jnp.maximum(reach[0], jnp.where(needed & (distance < half), distance, 0))
         reach[1] = jnp.maximum(reach[1], jnp.where(needed & (distance > half), vocab_count - distance, 0))
-        seen = jnp.max(jnp.where(needed & (row == facing), 1, 0), axis=0, keepdims=True)
-        across = jnp.maximum(across, jnp.where(me == s, seen, 0))
-    reach = [jnp.where(lane == blocks, steps, r) for r in reach]
+        across = jnp.maximum(across, jnp.where(needed & (distance == half), 1, 0))
+    share = tie_share(reach, across > 0, lane, half)
+    reach = full_reach(reach, across > 0, lane, share, blocks, half)
 
     square = (BLK, BLK)
     up, over = lax.broadcasted_iota(i32, square, 0), lax.broadcasted_iota(i32, square, 1)
@@ -104,18 +128,18 @@
     goes_first = ones((left_up > left_over) | ((left_up == left_over) & ((up >> 3) > (over >> 3))))
     index, waiting, moved = [], [], [jnp.zeros(shape, f32)] * 2
     for way in range(2):
-        masks = jnp.concatenate([ones(reach[way] == r) for r in range(1, steps + 1)], axis=0)
+        masks = jnp.concatenate([ones(reach[way] == r) for r in range(1, half + 1)], axis=0)
         before = jnp.dot(masks, earlier, preferred_element_type=f32)
         place = jnp.zeros(shape, f32)
         count = jnp.zeros(shape, f32)
-        for r in range(1, steps + 1):
+        for r in range(1, half + 1):
             same = reach[way] == r
             place = jnp.where(same, before[(r - 1) * vocab_count : r * vocab_count], place)
             total = jnp.sum(jnp.where(same, 1.0, 0.0), axis=1, keepdims=True)
             count = jnp.where(lane == r - 1, total, count)
         index.append(place)
         waiting.append(count)
-    travels = (lane >= 8) & (lane < 8 * steps) & ((lane & 7) + 1 > (lane >> 3))
+    travels = (lane >= 8) & (lane < 8 * half) & ((lane & 7) + 1 > (lane >> 3))
     for f in range(steps):
         ahead_of = jnp.dot(
             jnp.concatenate(waiting, axis=0).astype(jnp.bfloat16), goes_first, preferred_element_type=f32
@@ -163,13 +187,13 @@
                 where = jnp.where(now, f * SLOTS + first + order - start, where)
             return where
 
-        leave = slot(me, row, (far > row) & (row < steps))
-        arrive = slot(giver, row - 1, (far >= row) & (row >= 1) & (row <= steps))
+        leave = slot(me, row, (far > row) & (row < half))
+        arrive = slot(giver, row - 1, (far >= row) & (row >= 1) & (row <= half))
         point = jnp.where(row == 0, lane.astype(f32), jnp.maximum(home + arrive, 0.0))
         pointer.append(point)
         leave_turned = jnp.concatenate([leave, jnp.full((BLK - vocab_count, BLK), -1.0, f32)], axis=0).T
         chosen = jnp.zeros((1, 2 * BLK), f32)
-        for h in range(steps):
+        for h in range(half):
             chosen = chosen + jnp.dot(
                 point[h : h + 1].astype(jnp.bfloat16),
                 ones(leave_turned[:, h : h + 1] == target),
@@ -186,16 +210,10 @@
     inner = jnp.sum(jnp.where(pair_lane == me, inners, 0), axis=1, keepdims=True)
     distance = me - holder
     distance = jnp.where(distance < 0, distance + vocab_count, distance)
-    hops = [
-        jnp.where(distance < half, distance, 0),
-        jnp.where(distance > half, vocab_count - distance, 0),
-    ]
-    scale = jnp.where(distance < half, distance, 2 * vocab_count - distance)
-    lanes = lax.broadcasted_iota(i32, (1, BLK), 1)
-    across = jnp.where(lanes == blocks, 1, across)
-    met = beyond + jnp.dot(
-        jnp.broadcast_to(ones(across > 0), (8, BLK)), earlier, preferred_element_type=f32
-    )[:1]
+    share = turn(jnp.broadcast_to(share, shape))[:1]
+    share = jnp.sum(jnp.where(pair_lane == holder, share, 0), axis=1, keepdims=True)
+    hops = ways(distance, inner, share, vocab_count)
+    scale = jnp.where(distance <= half, distance, 2 * vocab_count - distance)
     points = jnp.zeros((pair_count, 1), f32)
     for way in range(2):
         found = lax.dot_general(
@@ -207,15 +225,13 @@
         points = points + jnp.sum(
             jnp.where((mine_lane == hops[way]) & (hops[way] > 0), found, 0.0), axis=1, keepdims=True
         )
-    faced = jnp.sum(jnp.where(pair_lane == inner, met, 0.0), axis=1, keepdims=True)
-    points = jnp.where(distance == half, faced, points)
     points = jnp.where(distance == 0, inner.astype(f32), points)
     by_stats = [jnp.sum(jnp.where(lane == blocks, p, 0.0), axis=1, keepdims=True) for p in pointer]
     hop = lax.broadcasted_iota(i32, (vocab_count, 1), 0)
-    met_stats = jnp.sum(jnp.where(lanes == blocks, met, 0.0), axis=1, keepdims=True)
-    by_stats[0] = jnp.where(hop < half, by_stats[0], 0.0)
-    by_stats[1] = jnp.where((hop >= 1) & (hop < half), by_stats[1], jnp.where(hop == half, met_stats, 0.0))
-    points = jnp.concatenate([points] + by_stats, axis=0).astype(i32)
+    stat_ok = [hop <= half, (hop >= 1) & (hop < half)]
+    points = jnp.concatenate(
+        [points] + [jnp.where(ok, p, 0.0) for ok, p in zip(stat_ok, by_stats)], axis=0
+    ).astype(i32)
     other = jnp.concatenate(
         [(hops[1] > 0).astype(i32), jnp.zeros((vocab_count, 1), i32), jnp.ones((vocab_count, 1), i32)], axis=0
     )
@@ -225,10 +241,9 @@
     for f in range(1, steps):
         frame = frame + (points >= home + f * SLOTS).astype(i32)
     away = points >= home
-    direct = points >= beyond
-    source = jnp.where(direct, 2 * steps + 1, jnp.where(away, 1 + frame + steps * other, 0))
-    spot = jnp.where(direct, points - beyond, jnp.where(away, points - home - frame * SLOTS, points))
-    spot = jnp.clip(spot, 0, jnp.where(direct, DIRECT - 1, jnp.where(away, SLOTS - 1, home - 1)))
+    source = jnp.where(away, 1 + frame + steps * other, 0)
+    spot = jnp.where(away, points - home - frame * SLOTS, points)
+    spot = jnp.clip(spot, 0, jnp.where(away, SLOTS - 1, home - 1))
     items = points.shape[0]
     item_lane = lax.broadcasted_iota(i32, (items, BLK), 1)
     table = jnp.where(
@@ -269,25 +284,23 @@
     pair_lane = lax.broadcasted_iota(i32, (pair_count, BLK), 1)
     lane = lax.broadcasted_iota(i32, (1, BLK), 1)
     reach = [jnp.zeros((1, BLK), i32), jnp.zeros((1, BLK), i32)]
-    facing = jnp.where(lane == blocks, 1, 0)
+    facing = jnp.zeros((1, BLK), i32)
     for s in range(vocab_count):
         hits = (pair_lane == inners[:, s : s + 1]) & (jnp.broadcast_to(holders[:, s : s + 1], pair_lane.shape) == me)
         seen = jnp.max(jnp.where(hits, 1, 0), axis=0, keepdims=True)
-        distance = (s - me) * sign
+        distance = s - me
         distance = jnp.where(distance < 0, distance + vocab_count, distance)
         reach[0] = jnp.maximum(reach[0], jnp.where(distance < half, distance * seen, 0))
         reach[1] = jnp.maximum(reach[1], jnp.where(distance > half, (vocab_count - distance) * seen, 0))
         facing = jnp.maximum(facing, jnp.where(distance == half, seen, 0))
+    share = tie_share(reach, facing > 0, lane, half)
+    reach = full_reach(reach, facing > 0, lane, share, blocks, half)
     choices = []
-    for far in reach:
-        far = jnp.where(lane == blocks, half - 1, far)
+    for one, other in (reach, reach[::-1]):
+        far = jnp.where(sign > 0, one, other)
         key = jnp.broadcast_to(far * BLK + (BLK - 1 - lane), (BLK, BLK))
         place = jnp.sum((turn(key) > key).astype(i32), axis=0, keepdims=True)
         choices.append(in_order(place, far > 0, SLOTS))
-    place = jnp.dot(
-        jnp.broadcast_to(ones(facing > 0), (8, BLK)), earlier_lanes(), preferred_element_type=jnp.float32
-    )[:1].astype(i32)
-    choices.append(in_order(place, facing > 0, DIRECT))
     return choices
 
 
@@ -301,7 +314,6 @@
     home_ref,
     first_ref,
     second_ref,
-    direct_ref,
     done_ref,
     cand_ref,
     logit_ref,
@@ -335,7 +347,7 @@
     home_ref[blocks] = jnp.where(
         lane == 0, top, jnp.where(lane == 1, first, jnp.where(lane == 2, second, jnp.where(lane == 3, third, 0.0)))
     ).astype(jnp.bfloat16)
-    for out_ref, choice in zip((first_ref, second_ref, direct_ref), first_choice(blocks, place_ref, listed_ref)):
+    for out_ref, choice in zip((first_ref, second_ref), first_choice(blocks, place_ref, listed_ref)):
         for j, at in enumerate(choice):
             out_ref[j] = home_ref[at]
     done_ref[...] = jnp.zeros(done_ref.shape, jnp.int32)
@@ -370,7 +382,7 @@
 
 def stage_kernel(steps, item_ref, *refs):
     sources, stage_ref = refs[:-1], refs[-1]
-    for s, source in zip([s for s in range(2 * steps + 2) if s not in (steps, 2 * steps)], sources):
+    for s, source in zip([s for s in range(2 * steps + 1) if s not in (steps, 2 * steps)], sources):
         bring(item_ref, s, source, stage_ref)
 
 
@@ -422,8 +434,7 @@
         stage_ref[i] = held_ref[i]
     bring(item_ref, steps, ahead_ref, stage_ref)
     bring(item_ref, 2 * steps, behind_ref, stage_ref)
-    facing = steps + 1
-    holders = [h for h in range(facing)] + [2 * facing + h for h in range(1, facing + 1)]
+    holders = [h for h in range(steps + 1)] + [2 * steps + h for h in range(1, steps)]
     peaks, sums = [], []
     for h in holders:
         stats = jnp.dot(spread, stage_ref[K * blocks + h], preferred_element_type=jnp.float32)
@@ -520,7 +531,7 @@
     row_count = doc_count * pos_count
     pair_count = student_blocks * K
     vocab_count = lax.axis_size("vocab")
-    steps = vocab_count // 2 - 1
+    steps = vocab_count // 2
     home = teacher_blocks + 1
     vocab_index = lax.axis_index("vocab")
     seq_index = lax.axis_index("seq")
@@ -557,17 +568,11 @@
     with jax.named_scope("pack"):
         listed = src_block.reshape(vocab_count, pair_count)
         place = jnp.stack([vocab_index, sign]).astype(jnp.int32)
-        own, ahead, behind, direct, packed = pl.pallas_call(
+        own, ahead, behind, packed = pl.pallas_call(
             pack_kernel,
-            out_shape=(
-                planes(home),
-                planes(SLOTS),
-                planes(SLOTS),
-                planes(DIRECT),
-                jax.ShapeDtypeStruct((8, BLK), jnp.int32),
-            ),
+            out_shape=(planes(home), planes(SLOTS), planes(SLOTS), jax.ShapeDtypeStruct((8, BLK), jnp.int32)),
             in_specs=[vmem] * 6,
-            out_specs=(vmem,) * 5,
+            out_specs=(vmem,) * 4,
             scratch_shapes=[
                 pltpu.VMEM((doc_count * span, teacher_cols), jnp.bfloat16),
                 pltpu.VMEM((teacher_blocks, ROWS, BLK), jnp.bfloat16),
@@ -612,8 +617,6 @@
             if step:
                 behind = chosen(1, step, came_behind)
             came_behind.append(lax.ppermute(behind, ("seq", "vocab"), backward))
-        across = [(v, (v + vocab_count // 2) % vocab_count) for v in range(vocab_count)]
-        came_direct = lax.ppermute(direct, "vocab", across)
 
     with jax.named_scope("student"):
         top, total = pl.pallas_call(
@@ -625,7 +628,7 @@
         )(student_logits)
 
     with jax.named_scope("stage"):
-        early = (own, *came_ahead[:-1], *came_behind[:-1], came_direct)
+        early = (own, *came_ahead[:-1], *came_behind[:-1])
         held = pl.pallas_call(
             functools.partial(stage_kernel, steps),
             out_shape=planes(pair_count + 2 * vocab_count),
@@ -642,7 +645,7 @@
             out_specs=vmem,
             scratch_shapes=[
                 pltpu.VMEM((pair_count + 2 * vocab_count, ROWS, BLK), jnp.bfloat16),
-                pltpu.VMEM((2 * vocab_count, row_count, BLK), jnp.float32),
+                pltpu.VMEM((3 * steps, row_count, BLK), jnp.float32),
             ],
             compiler_params=room(20),
         )(items, held, came_ahead[-1], came_behind[-1], spread, weights, student_logits, top, total)

time: 218 us -> 207 us (0.950)
  the two profiles are of different devices: /device:TPU:28 before, /device:TPU:6 now
where the time goes in v7:
time: 207 us; the launch traced here: 205 us
  starting transfers between devices  81.5 us (39%)
  waiting for transfers between devices  59.3 us (29%)
  Pallas kernels  39.1 us (19%)
  between operations  15.2 us (7%)
  local copies, waits for them, and re-layouts  7.38 us (4%)
    ppermute x8, starting transfers between devices, shards(): came_behind.append(lax.ppermute(behind, ('seq', 'vocab'), backward))  48.7 us
    ppermute x8, waiting for transfers between devices, shards(): came_ahead.append(lax.ppermute(ahead, ('seq', 'vocab'), forward))  31.1 us
    ppermute x8, waiting for transfers between devices, shards(): came_behind.append(lax.ppermute(behind, ('seq', 'vocab'), backward))  15.9 us
    pallas_call x14, Pallas kernels, chosen(): pl.pallas_call(functools.partial(ready_kernel, chain, step), out_shape=pl...  15.9 us
    ppermute x8, starting transfers between devices, shards(): came_ahead.append(lax.ppermute(ahead, ('seq', 'vocab'), forward))  15.3 us
    all_to_all x1, starting transfers between devices, shards(): lax.all_to_all(sent, 'vocab', split_axis=0, concat_axis=0, tiled=True)  11.9 us
    all_to_all x1, waiting for transfers between devices, shards(): lax.all_to_all(sent, 'vocab', split_axis=0, concat_axis=0, tiled=True)  10.1 us
    pallas_call x14, Pallas kernels, chosen(): pl.pallas_call(functools.partial(pass_kernel, chain, step, home), out_sha...  9.18 us
  transfers between devices with their start and end apart: 20, of which 13 were waited for; matrix products, arithmetic and copies ran while one was open for 2% of the time, Pallas kernels for 16%

profile of v7, /device:TPU:6, one launch (start us, length us, event | category | flops | bytes accessed | tf_op | source)
XLA Modules:
  0.0 204.5 jit_solution(15892253208759990540)
XLA Ops:
  7.7 1.9 collective-permute-start
  9.7 3.6 %collective-permute-start.1 = (bf16[2,16,4736]{2,1,0:T(8,128)(2,1)S(1)}, bf16[2,16,4736]{2,1,0:T(8,128)(2,1)S(1)}, u32[]{:S(2)}, u32[]{:S(2)}) collective-permute-start(bf16[2,16,4736]{2,1,0:T(8,128)(2,1)S(1)} %get-tuple-element.155), channel_id=1, source_target_pairs={{16,0},{32,16},{48,32},{64,48},{80,64},{96,80},{112,96},{17,1},{33... | collective-permute-start | bytes 909320 | tf_op jit(solution)/shard_map/halo/ppermute | solution.py:23
  19.3 11.4 %collective-permute-start.9 = (bf16[21,104,128]{2,1,0:T(8,128)(2,1)S(1)}, bf16[21,104,128]{2,1,0:T(8,128)(2,1)S(1)}, u32[]{:S(2)}, u32[]{:S(2)}) collective-permute-start(bf16[21,104,128]{2,1,0:T(8,128)(2,1)S(1)} %get-tuple-element.94), channel_id=1, source_target_pairs={{0,15},{1,0},{2,1},{3,2},{4,3},{5,4},{6,5},{7,6},{8,7},{9,8},{10,9... | collective-permute-start | bytes 1677320 | tf_op jit(solution)/shard_map/ring/ppermute | solution.py:619
  30.8 1.9 collective-permute-start.2
  32.7 4.0 %plan.1 = (s32[8,256]{1,0:T(8,128)S(1)}, s32[8,128]{1,0:T(8,128)S(1)}, s32[8,128]{1,0:T(8,128)S(1)}) custom-call(s32[2]{0:T(128)S(1)} %pad_add_fusion.place_ref, s32[16,64]{1,0:T(8,128)S(1)} %reshape.252.listed_ref, s32[8,128]{1,0:T(8,128)S(1)} %get-tuple-element.88.after_ref), custom_call_target="tpu_custom_call" | custom-call | tf_op jit(solution)/shard_map/plan/pallas_call | solution.py:585
  37.2 4.3 %collective-permute-done.9.newest_ref.refs_0_.refs_8_ = bf16[21,104,128]{2,1,0:T(8,128)(2,1)S(1)} collective-permute-done((bf16[21,104,128]{2,1,0:T(8,128)(2,1)S(1)}, bf16[21,104,128]{2,1,0:T(8,128)(2,1)S(1)}, u32[]{:S(2)}, u32[]{:S(2)}) %collective-permute-start.9) | collective-permute-done | bytes 559136 | tf_op jit(solution)/shard_map/ring/ppermute | solution.py:619
  41.8 5.6 %collective-permute-start.10 = (bf16[21,104,128]{2,1,0:T(8,128)(2,1)S(1)}, bf16[21,104,128]{2,1,0:T(8,128)(2,1)S(1)}, u32[]{:S(2)}, u32[]{:S(2)}) collective-permute-start(bf16[21,104,128]{2,1,0:T(8,128)(2,1)S(1)} %ring.41), channel_id=1, source_target_pairs={{0,15},{1,0},{2,1},{3,2},{4,3},{5,4},{6,5},{7,6},{8,7},{9,8},{10,9... | collective-permute-start | bytes 1677320 | tf_op jit(solution)/shard_map/ring/ppermute | solution.py:619
  47.7 1.9 collective-permute-start.3
  50.4 6.8 %collective-permute-done.10.newest_ref.refs_1_.refs_9_ = bf16[21,104,128]{2,1,0:T(8,128)(2,1)S(1)} collective-permute-done((bf16[21,104,128]{2,1,0:T(8,128)(2,1)S(1)}, bf16[21,104,128]{2,1,0:T(8,128)(2,1)S(1)}, u32[]{:S(2)}, u32[]{:S(2)}) %collective-permute-start.10) | collective-permute-done | bytes 559136 | tf_op jit(solution)/shard_map/ring/ppermute | solution.py:619
  58.3 5.6 %collective-permute-start.11 = (bf16[21,104,128]{2,1,0:T(8,128)(2,1)}, bf16[21,104,128]{2,1,0:T(8,128)(2,1)}, u32[]{:S(2)}, u32[]{:S(2)}) collective-permute-start(bf16[21,104,128]{2,1,0:T(8,128)(2,1)} %ring.43), channel_id=1, source_target_pairs={{0,15},{1,0},{2,1},{3,2},{4,3},{5,4},{6,5},{7,6},{8,7},{9,8},{10,9... | collective-permute-start | bytes 1677320 | tf_op jit(solution)/shard_map/ring/ppermute | solution.py:619
  65.4 1.9 collective-permute-start.4
  68.3 4.8 %collective-permute-done.11.newest_ref.refs_2_.refs_10_ = bf16[21,104,128]{2,1,0:T(8,128)(2,1)} collective-permute-done((bf16[21,104,128]{2,1,0:T(8,128)(2,1)}, bf16[21,104,128]{2,1,0:T(8,128)(2,1)}, u32[]{:S(2)}, u32[]{:S(2)}) %collective-permute-start.11) | collective-permute-done | bytes 559136 | tf_op jit(solution)/shard_map/ring/ppermute | solution.py:619
  74.4 5.6 %collective-permute-start.12 = (bf16[21,104,128]{2,1,0:T(8,128)(2,1)S(1)}, bf16[21,104,128]{2,1,0:T(8,128)(2,1)S(1)}, u32[]{:S(2)}, u32[]{:S(2)}) collective-permute-start(bf16[21,104,128]{2,1,0:T(8,128)(2,1)S(1)} %ring.45), channel_id=1, source_target_pairs={{0,15},{1,0},{2,1},{3,2},{4,3},{5,4},{6,5},{7,6},{8,7},{9,8},{10,9... | collective-permute-start | bytes 1677320 | tf_op jit(solution)/shard_map/ring/ppermute | solution.py:619
  80.0 3.5 %collective-permute-done.4.newest_ref.refs_2_.refs_3_ = bf16[21,104,128]{2,1,0:T(8,128)(2,1)} collective-permute-done((bf16[21,104,128]{2,1,0:T(8,128)(2,1)}, bf16[21,104,128]{2,1,0:T(8,128)(2,1)}, u32[]{:S(2)}, u32[]{:S(2)}) %collective-permute-start.4) | collective-permute-done | bytes 559136 | tf_op jit(solution)/shard_map/ring/ppermute | solution.py:616
  84.8 1.9 collective-permute-start.5
  90.3 5.1 %collective-permute-start.13 = (bf16[21,104,128]{2,1,0:T(8,128)(2,1)S(1)}, bf16[21,104,128]{2,1,0:T(8,128)(2,1)S(1)}, u32[]{:S(2)}, u32[]{:S(2)}) collective-permute-start(bf16[21,104,128]{2,1,0:T(8,128)(2,1)S(1)} %ring.47), channel_id=1, source_target_pairs={{0,15},{1,0},{2,1},{3,2},{4,3},{5,4},{6,5},{7,6},{8,7},{9,8},{10,9... | collective-permute-start | bytes 1677320 | tf_op jit(solution)/shard_map/ring/ppermute | solution.py:619
  95.5 6.6 %collective-permute-done.5.newest_ref.refs_3_.refs_4_ = bf16[21,104,128]{2,1,0:T(8,128)(2,1)S(1)} collective-permute-done((bf16[21,104,128]{2,1,0:T(8,128)(2,1)S(1)}, bf16[21,104,128]{2,1,0:T(8,128)(2,1)S(1)}, u32[]{:S(2)}, u32[]{:S(2)}) %collective-permute-start.5) | collective-permute-done | bytes 559136 | tf_op jit(solution)/shard_map/ring/ppermute | solution.py:616
  102.3 1.9 collective-permute-start.6
  108.0 5.1 %collective-permute-start.14 = (bf16[21,104,128]{2,1,0:T(8,128)(2,1)S(1)}, bf16[21,104,128]{2,1,0:T(8,128)(2,1)S(1)}, u32[]{:S(2)}, u32[]{:S(2)}) collective-permute-start(bf16[21,104,128]{2,1,0:T(8,128)(2,1)S(1)} %ring.49), channel_id=1, source_target_pairs={{0,15},{1,0},{2,1},{3,2},{4,3},{5,4},{6,5},{7,6},{8,7},{9,8},{10,9... | collective-permute-start | bytes 1677320 | tf_op jit(solution)/shard_map/ring/ppermute | solution.py:619
  113.2 5.6 %collective-permute-done.6.newest_ref.refs_4_.refs_5_ = bf16[21,104,128]{2,1,0:T(8,128)(2,1)S(1)} collective-permute-done((bf16[21,104,128]{2,1,0:T(8,128)(2,1)S(1)}, bf16[21,104,128]{2,1,0:T(8,128)(2,1)S(1)}, u32[]{:S(2)}, u32[]{:S(2)}) %collective-permute-start.6) | collective-permute-done | bytes 559136 | tf_op jit(solution)/shard_map/ring/ppermute | solution.py:616
  119.1 1.9 collective-permute-start.7
  124.6 5.1 %collective-permute-start.15 = (bf16[21,104,128]{2,1,0:T(8,128)(2,1)S(1)}, bf16[21,104,128]{2,1,0:T(8,128)(2,1)S(1)}, u32[]{:S(2)}, u32[]{:S(2)}) collective-permute-start(bf16[21,104,128]{2,1,0:T(8,128)(2,1)S(1)} %ring.51), channel_id=1, source_target_pairs={{0,15},{1,0},{2,1},{3,2},{4,3},{5,4},{6,5},{7,6},{8,7},{9,8},{10,9... | collective-permute-start | bytes 1677320 | tf_op jit(solution)/shard_map/ring/ppermute | solution.py:619
  129.7 4.8 %collective-permute-done.7.newest_ref.refs_6_.refs_5_ = bf16[21,104,128]{2,1,0:T(8,128)(2,1)S(1)} collective-permute-done((bf16[21,104,128]{2,1,0:T(8,128)(2,1)S(1)}, bf16[21,104,128]{2,1,0:T(8,128)(2,1)S(1)}, u32[]{:S(2)}, u32[]{:S(2)}) %collective-permute-start.7) | collective-permute-done | bytes 559136 | tf_op jit(solution)/shard_map/ring/ppermute | solution.py:616
  134.8 1.9 collective-permute-start.8
  141.5 5.1 %collective-permute-start.17 = (bf16[21,104,128]{2,1,0:T(8,128)(2,1)}, bf16[21,104,128]{2,1,0:T(8,128)(2,1)}, u32[]{:S(2)}, u32[]{:S(2)}) collective-permute-start(bf16[21,104,128]{2,1,0:T(8,128)(2,1)} %ring.55), channel_id=1, source_target_pairs={{0,15},{1,0},{2,1},{3,2},{4,3},{5,4},{6,5},{7,6},{8,7},{9,8},{10,9... | collective-permute-start | bytes 1677320 | tf_op jit(solution)/shard_map/ring/ppermute | solution.py:619
  146.7 3.8 %collective-permute-done.8.refs_7_.newest_ref = bf16[21,104,128]{2,1,0:T(8,128)(2,1)S(1)} collective-permute-done((bf16[21,104,128]{2,1,0:T(8,128)(2,1)S(1)}, bf16[21,104,128]{2,1,0:T(8,128)(2,1)S(1)}, u32[]{:S(2)}, u32[]{:S(2)}) %collective-permute-start.8) | collective-permute-done | bytes 559136 | tf_op jit(solution)/shard_map/ring/ppermute | solution.py:616
  151.5 1.9 collective-permute-start.16
  154.2 2.4 %stage.1.held_ref = bf16[96,104,128]{2,1,0:T(8,128)(2,1)S(1)} custom-call(s32[8,128]{1,0:T(8,128)S(1)} %get-tuple-element.90.item_ref, bf16[38,104,128]{2,1,0:T(8,128)(2,1)S(1)} %get-tuple-element.91.home_ref.refs_0_, bf16[21,104,128]{2,1,0:T(8,128)(2,1)S(1)} %collective-permute-done.2.newest_ref.refs_0_.refs_1_, ...), custom_call_target="tpu_custom_call" | custom-call | tf_op jit(solution)/shard_map/stage/pallas_call | solution.py:632
  158.1 6.3 %collective-permute-done.16.ahead_ref = bf16[21,104,128]{2,1,0:T(8,128)(2,1)} collective-permute-done((bf16[21,104,128]{2,1,0:T(8,128)(2,1)}, bf16[21,104,128]{2,1,0:T(8,128)(2,1)}, u32[]{:S(2)}, u32[]{:S(2)}) %collective-permute-start.16) | collective-permute-done | bytes 559136 | tf_op jit(solution)/shard_map/ring/ppermute | solution.py:616
  166.2 5.5 %map.1 = f32[8,128]{1,0:T(8,128)S(1)} custom-call(s32[8,128]{1,0:T(8,128)S(1)} %get-tuple-element.90.item_ref, bf16[96,104,128]{2,1,0:T(8,128)(2,1)S(1)} %copy-done.1, bf16[21,104,128]{2,1,0:T(8,128)(2,1)} %collective-permute-done.16.ahead_ref, bf16[21,104,128]{2,1,0:T(8,128)(2,1)} %collective-permute-done.17.behind_ref, ...), custom_call_target="tpu_custom_call" | custom-call | tf_op jit(solution)/shard_map/map/pallas_call | solution.py:641
  172.3 11.9 %all-to-all-start.1 = ((f32[16,4,128]{2,1,0:T(4,128)}), f32[16,4,128]{2,1,0:T(4,128)S(1)}, u32[]{:S(2)}, u32[]{:S(2)}) async-start(f32[16,4,128]{2,1,0:T(4,128)} %broadcast_in_dim.55), calls=%async_computation.1 | async-start | bytes 65536 | tf_op jit(solution)/shard_map/finish/all_to_all | solution.py:655
  186.7 10.1 %all-to-all-done.1 = f32[16,4,128]{2,1,0:T(4,128)S(1)} async-done(((f32[16,4,128]{2,1,0:T(4,128)}), f32[16,4,128]{2,1,0:T(4,128)S(1)}, u32[]{:S(2)}, u32[]{:S(2)}) %all-to-all-start.1) | async-done | bytes 32800 | tf_op jit(solution)/shard_map/finish/all_to_all | solution.py:655
  (88 shorter events, 39.5 us)
Async XLA Ops:
  6.5 11.2 %copy-start.6 = (bf16[2,64,4736]{2,1,0:T(8,128)(2,1)S(1)}, bf16[2,64,4736]{2,1,0:T(8,128)(2,1)}, u32[]{:S(2)}) copy-start(bf16[2,64,4736]{2,1,0:T(8,128)(2,1)} %own_ref.1) | copy-start | bytes 3637252
  6.5 151.6 %all-gather.2.cloned.1.call-start = ((), (), s32[]{:S(2)}) async-start(), calls=%async_computation.2 | async-start | bytes 2621440 | tf_op jit(solution)/shard_map/weights/all_gather | solution.py:544
  7.7 8.1 %collective-permute-start = (bf16[2,16,4736]{2,1,0:T(8,128)(2,1)S(1)}, bf16[2,16,4736]{2,1,0:T(8,128)(2,1)S(1)}, u32[]{:S(2)}, u32[]{:S(2)}) collective-permute-start(bf16[2,16,4736]{2,1,0:T(8,128)(2,1)S(1)} %get-tuple-element.156), channel_id=1, source_target_pairs={{0,16},{16,32},{32,48},{48,64},{64,80},{80,96},{96,112},{1,17},{17... | collective-permute-start | bytes 909320 | tf_op jit(solution)/shard_map/halo/ppermute | solution.py:22
  9.7 8.0 %collective-permute-start.1 = (bf16[2,16,4736]{2,1,0:T(8,128)(2,1)S(1)}, bf16[2,16,4736]{2,1,0:T(8,128)(2,1)S(1)}, u32[]{:S(2)}, u32[]{:S(2)}) collective-permute-start(bf16[2,16,4736]{2,1,0:T(8,128)(2,1)S(1)} %get-tuple-element.155), channel_id=1, source_target_pairs={{16,0},{32,16},{48,32},{64,48},{80,64},{96,80},{112,96},{17,1},{33... | collective-permute-start | bytes 909320 | tf_op jit(solution)/shard_map/halo/ppermute | solution.py:23
  15.9 21.3 %copy-start.7 = (bf16[2,16,4736]{2,1,0:T(8,128)(2,1)}, bf16[2,16,4736]{2,1,0:T(8,128)(2,1)S(1)}, u32[]{:S(2)}) copy-start(bf16[2,16,4736]{2,1,0:T(8,128)(2,1)S(1)} %collective-permute-done.low_ref) | copy-start | bytes 909316
  17.6 19.5 %copy-start.9 = (bf16[2,16,4736]{2,1,0:T(8,128)(2,1)}, bf16[2,16,4736]{2,1,0:T(8,128)(2,1)S(1)}, u32[]{:S(2)}) copy-start(bf16[2,16,4736]{2,1,0:T(8,128)(2,1)S(1)} %collective-permute-done.1.high_ref) | copy-start | bytes 909316
  19.3 22.1 %collective-permute-start.9 = (bf16[21,104,128]{2,1,0:T(8,128)(2,1)S(1)}, bf16[21,104,128]{2,1,0:T(8,128)(2,1)S(1)}, u32[]{:S(2)}, u32[]{:S(2)}) collective-permute-start(bf16[21,104,128]{2,1,0:T(8,128)(2,1)S(1)} %get-tuple-element.94), channel_id=1, source_target_pairs={{0,15},{1,0},{2,1},{3,2},{4,3},{5,4},{6,5},{7,6},{8,7},{9,8},{10,9... | collective-permute-start | bytes 1677320 | tf_op jit(solution)/shard_map/ring/ppermute | solution.py:619
  30.8 16.6 %collective-permute-start.2 = (bf16[21,104,128]{2,1,0:T(8,128)(2,1)S(1)}, bf16[21,104,128]{2,1,0:T(8,128)(2,1)S(1)}, u32[]{:S(2)}, u32[]{:S(2)}) collective-permute-start(bf16[21,104,128]{2,1,0:T(8,128)(2,1)S(1)} %get-tuple-element.92), channel_id=1, source_target_pairs={{0,1},{1,2},{2,3},{3,4},{4,5},{5,6},{6,7},{7,8},{8,9},{9,10},{10,1... | collective-permute-start | bytes 1677320 | tf_op jit(solution)/shard_map/ring/ppermute | solution.py:616
  41.8 15.4 %collective-permute-start.10 = (bf16[21,104,128]{2,1,0:T(8,128)(2,1)S(1)}, bf16[21,104,128]{2,1,0:T(8,128)(2,1)S(1)}, u32[]{:S(2)}, u32[]{:S(2)}) collective-permute-start(bf16[21,104,128]{2,1,0:T(8,128)(2,1)S(1)} %ring.41), channel_id=1, source_target_pairs={{0,15},{1,0},{2,1},{3,2},{4,3},{5,4},{6,5},{7,6},{8,7},{9,8},{10,9... | collective-permute-start | bytes 1677320 | tf_op jit(solution)/shard_map/ring/ppermute | solution.py:619
  47.7 16.7 %collective-permute-start.3 = (bf16[21,104,128]{2,1,0:T(8,128)(2,1)S(1)}, bf16[21,104,128]{2,1,0:T(8,128)(2,1)S(1)}, u32[]{:S(2)}, u32[]{:S(2)}) collective-permute-start(bf16[21,104,128]{2,1,0:T(8,128)(2,1)S(1)} %ring.29), channel_id=1, source_target_pairs={{0,1},{1,2},{2,3},{3,4},{4,5},{5,6},{6,7},{7,8},{8,9},{9,10},{10,1... | collective-permute-start | bytes 1677320 | tf_op jit(solution)/shard_map/ring/ppermute | solution.py:616
  58.3 14.8 %collective-permute-start.11 = (bf16[21,104,128]{2,1,0:T(8,128)(2,1)}, bf16[21,104,128]{2,1,0:T(8,128)(2,1)}, u32[]{:S(2)}, u32[]{:S(2)}) collective-permute-start(bf16[21,104,128]{2,1,0:T(8,128)(2,1)} %ring.43), channel_id=1, source_target_pairs={{0,15},{1,0},{2,1},{3,2},{4,3},{5,4},{6,5},{7,6},{8,7},{9,8},{10,9... | collective-permute-start | bytes 1677320 | tf_op jit(solution)/shard_map/ring/ppermute | solution.py:619
  65.4 18.0 %collective-permute-start.4 = (bf16[21,104,128]{2,1,0:T(8,128)(2,1)}, bf16[21,104,128]{2,1,0:T(8,128)(2,1)}, u32[]{:S(2)}, u32[]{:S(2)}) collective-permute-start(bf16[21,104,128]{2,1,0:T(8,128)(2,1)} %ring.31), channel_id=1, source_target_pairs={{0,1},{1,2},{2,3},{3,4},{4,5},{5,6},{6,7},{7,8},{8,9},{9,10},{10,1... | collective-permute-start | bytes 1677320 | tf_op jit(solution)/shard_map/ring/ppermute | solution.py:616
  74.4 15.7 %collective-permute-start.12 = (bf16[21,104,128]{2,1,0:T(8,128)(2,1)S(1)}, bf16[21,104,128]{2,1,0:T(8,128)(2,1)S(1)}, u32[]{:S(2)}, u32[]{:S(2)}) collective-permute-start(bf16[21,104,128]{2,1,0:T(8,128)(2,1)S(1)} %ring.45), channel_id=1, source_target_pairs={{0,15},{1,0},{2,1},{3,2},{4,3},{5,4},{6,5},{7,6},{8,7},{9,8},{10,9... | collective-permute-start | bytes 1677320 | tf_op jit(solution)/shard_map/ring/ppermute | solution.py:619
  84.8 17.2 %collective-permute-start.5 = (bf16[21,104,128]{2,1,0:T(8,128)(2,1)S(1)}, bf16[21,104,128]{2,1,0:T(8,128)(2,1)S(1)}, u32[]{:S(2)}, u32[]{:S(2)}) collective-permute-start(bf16[21,104,128]{2,1,0:T(8,128)(2,1)S(1)} %ring.33), channel_id=1, source_target_pairs={{0,1},{1,2},{2,3},{3,4},{4,5},{5,6},{6,7},{7,8},{8,9},{9,10},{10,1... | collective-permute-start | bytes 1677320 | tf_op jit(solution)/shard_map/ring/ppermute | solution.py:616
  90.3 17.4 %collective-permute-start.13 = (bf16[21,104,128]{2,1,0:T(8,128)(2,1)S(1)}, bf16[21,104,128]{2,1,0:T(8,128)(2,1)S(1)}, u32[]{:S(2)}, u32[]{:S(2)}) collective-permute-start(bf16[21,104,128]{2,1,0:T(8,128)(2,1)S(1)} %ring.47), channel_id=1, source_target_pairs={{0,15},{1,0},{2,1},{3,2},{4,3},{5,4},{6,5},{7,6},{8,7},{9,8},{10,9... | collective-permute-start | bytes 1677320 | tf_op jit(solution)/shard_map/ring/ppermute | solution.py:619
  102.3 16.4 %collective-permute-start.6 = (bf16[21,104,128]{2,1,0:T(8,128)(2,1)S(1)}, bf16[21,104,128]{2,1,0:T(8,128)(2,1)S(1)}, u32[]{:S(2)}, u32[]{:S(2)}) collective-permute-start(bf16[21,104,128]{2,1,0:T(8,128)(2,1)S(1)} %ring.35), channel_id=1, source_target_pairs={{0,1},{1,2},{2,3},{3,4},{4,5},{5,6},{6,7},{7,8},{8,9},{9,10},{10,1... | collective-permute-start | bytes 1677320 | tf_op jit(solution)/shard_map/ring/ppermute | solution.py:616
  108.0 16.3 %collective-permute-start.14 = (bf16[21,104,128]{2,1,0:T(8,128)(2,1)S(1)}, bf16[21,104,128]{2,1,0:T(8,128)(2,1)S(1)}, u32[]{:S(2)}, u32[]{:S(2)}) collective-permute-start(bf16[21,104,128]{2,1,0:T(8,128)(2,1)S(1)} %ring.49), channel_id=1, source_target_pairs={{0,15},{1,0},{2,1},{3,2},{4,3},{5,4},{6,5},{7,6},{8,7},{9,8},{10,9... | collective-permute-start | bytes 1677320 | tf_op jit(solution)/shard_map/ring/ppermute | solution.py:619
  119.1 15.5 %collective-permute-start.7 = (bf16[21,104,128]{2,1,0:T(8,128)(2,1)S(1)}, bf16[21,104,128]{2,1,0:T(8,128)(2,1)S(1)}, u32[]{:S(2)}, u32[]{:S(2)}) collective-permute-start(bf16[21,104,128]{2,1,0:T(8,128)(2,1)S(1)} %ring.37), channel_id=1, source_target_pairs={{0,1},{1,2},{2,3},{3,4},{4,5},{5,6},{6,7},{7,8},{8,9},{9,10},{10,1... | collective-permute-start | bytes 1677320 | tf_op jit(solution)/shard_map/ring/ppermute | solution.py:616
  124.6 15.9 %collective-permute-start.15 = (bf16[21,104,128]{2,1,0:T(8,128)(2,1)S(1)}, bf16[21,104,128]{2,1,0:T(8,128)(2,1)S(1)}, u32[]{:S(2)}, u32[]{:S(2)}) collective-permute-start(bf16[21,104,128]{2,1,0:T(8,128)(2,1)S(1)} %ring.51), channel_id=1, source_target_pairs={{0,15},{1,0},{2,1},{3,2},{4,3},{5,4},{6,5},{7,6},{8,7},{9,8},{10,9... | collective-permute-start | bytes 1677320 | tf_op jit(solution)/shard_map/ring/ppermute | solution.py:619
  134.8 15.6 %collective-permute-start.8 = (bf16[21,104,128]{2,1,0:T(8,128)(2,1)S(1)}, bf16[21,104,128]{2,1,0:T(8,128)(2,1)S(1)}, u32[]{:S(2)}, u32[]{:S(2)}) collective-permute-start(bf16[21,104,128]{2,1,0:T(8,128)(2,1)S(1)} %ring.39), channel_id=1, source_target_pairs={{0,1},{1,2},{2,3},{3,4},{4,5},{5,6},{6,7},{7,8},{8,9},{9,10},{10,1... | collective-permute-start | bytes 1677320 | tf_op jit(solution)/shard_map/ring/ppermute | solution.py:616
  140.4 13.0 %copy-start.2 = (bf16[2,64,4096]{2,1,0:T(8,128)(2,1)S(1)}, bf16[2,64,4096]{2,1,0:T(8,128)(2,1)}, u32[]{:S(2)}) copy-start(bf16[2,64,4096]{2,1,0:T(8,128)(2,1)} %student_ref.3) | copy-start | bytes 3145732
  141.5 16.6 %collective-permute-start.17 = (bf16[21,104,128]{2,1,0:T(8,128)(2,1)}, bf16[21,104,128]{2,1,0:T(8,128)(2,1)}, u32[]{:S(2)}, u32[]{:S(2)}) collective-permute-start(bf16[21,104,128]{2,1,0:T(8,128)(2,1)} %ring.55), channel_id=1, source_target_pairs={{0,15},{1,0},{2,1},{3,2},{4,3},{5,4},{6,5},{7,6},{8,7},{9,8},{10,9... | collective-permute-start | bytes 1677320 | tf_op jit(solution)/shard_map/ring/ppermute | solution.py:619
  151.5 13.0 %collective-permute-start.16 = (bf16[21,104,128]{2,1,0:T(8,128)(2,1)}, bf16[21,104,128]{2,1,0:T(8,128)(2,1)}, u32[]{:S(2)}, u32[]{:S(2)}) collective-permute-start(bf16[21,104,128]{2,1,0:T(8,128)(2,1)} %ring.53), channel_id=1, source_target_pairs={{0,1},{1,2},{2,3},{3,4},{4,5},{5,6},{6,7},{7,8},{8,9},{9,10},{10,1... | collective-permute-start | bytes 1677320 | tf_op jit(solution)/shard_map/ring/ppermute | solution.py:616
  156.7 1.5 copy-start
  164.5 1.7 copy-start.1
  166.2 20.5 %copy-start.3 = (bf16[2,64,4096]{2,1,0:T(8,128)(2,1)S(1)}, bf16[2,64,4096]{2,1,0:T(8,128)(2,1)}, u32[]{:S(2)}) copy-start(bf16[2,64,4096]{2,1,0:T(8,128)(2,1)} %student_ref.3) | copy-start | bytes 3145732
  166.2 20.5 %copy-start.8 = (bf16[2,16,4736]{2,1,0:T(8,128)(2,1)S(1)}, bf16[2,16,4736]{2,1,0:T(8,128)(2,1)}, u32[]{:S(2)}) copy-start(bf16[2,16,4736]{2,1,0:T(8,128)(2,1)} %copy-done.7) | copy-start | bytes 909316
  166.2 20.5 %copy-start.11 = (s32[512,2]{0,1:T(2,128)S(1)}, s32[512,2]{0,1:T(2,128)}, u32[]{:S(2)}) copy-start(s32[512,2]{0,1:T(2,128)} %param.12) | copy-start | bytes 12292
  172.3 24.5 %all-to-all-start.1 = ((f32[16,4,128]{2,1,0:T(4,128)}), f32[16,4,128]{2,1,0:T(4,128)S(1)}, u32[]{:S(2)}, u32[]{:S(2)}) async-start(f32[16,4,128]{2,1,0:T(4,128)} %broadcast_in_dim.55), calls=%async_computation.1 | async-start | bytes 65536 | tf_op jit(solution)/shard_map/finish/all_to_all | solution.py:655
  197.1 0.6 copy-start.12
Sparse Core Ops, SparseCore 0:
  67.5 37.7 all-gather.1

commit v8 on v7

--- a/solution.py
+++ b/solution.py
@@ -11,7 +11,8 @@
 K = 2
 W = 16
 ROWS = 104
-SLOTS = 21
+SIZES = ((21,) * 8, (12, 23, 23, 23, 22, 22, 22, 22))
+STARTS = tuple(tuple(sum(sizes[:f]) for f in range(len(sizes))) for sizes in SIZES)
 TINY = 1.2e-38
 
 
@@ -94,6 +95,11 @@
     me, sign = place_ref[0], place_ref[1]
     f32, i32 = jnp.float32, jnp.int32
     shape = (vocab_count, BLK)
+    straight = sign > 0
+
+    def of_chain(table, way, f):
+        return jnp.where(straight, float(table[way][f]), float(table[1 - way][f]))
+
 
     del after_ref
     listed = listed_ref[...]
@@ -146,11 +152,12 @@
         )
         for way in range(2):
             first = ahead_of[way * vocab_count : (way + 1) * vocab_count]
-            go = jnp.clip(SLOTS - first, 0.0, waiting[way])
+            size = of_chain(SIZES, way, f)
+            go = jnp.clip(size - first, 0.0, waiting[way])
             book_ref[(f * 2 + way) * 3] = moved[way]
             moved[way] = moved[way] + go
             book_ref[(f * 2 + way) * 3 + 1] = moved[way]
-            book_ref[(f * 2 + way) * 3 + 2] = jnp.minimum(first, float(SLOTS))
+            book_ref[(f * 2 + way) * 3 + 2] = jnp.minimum(first, size)
             come = pltpu.roll(pltpu.roll(go, 8, 1), 1 if way == 0 else vocab_count - 1, 0)
             waiting[way] = waiting[way] - go + jnp.where(travels, come, 0.0)
     left = jnp.sum(waiting[0] + waiting[1], axis=1, keepdims=True)
@@ -184,7 +191,7 @@
                     for kind in range(3)
                 )
                 now = valid & (start <= order) & (order < end)
-                where = jnp.where(now, f * SLOTS + first + order - start, where)
+                where = jnp.where(now, of_chain(STARTS, way, f) + first + order - start, where)
             return where
 
         leave = slot(me, row, (far > row) & (row < half))
@@ -200,7 +207,6 @@
                 preferred_element_type=f32,
             )
         sends.append(chosen.astype(i32))
-    straight = sign > 0
     send_ref[0:1, :] = jnp.where(straight, sends[0], sends[1])
     send_ref[1:2, :] = jnp.where(straight, sends[1], sends[0])
     send_ref[2:8, :] = jnp.zeros((6, 2 * BLK), i32)
@@ -238,12 +244,17 @@
     other = jnp.where(straight, other, 1 - other)
     scale = jnp.concatenate([scale, jnp.zeros((2 * vocab_count, 1), i32)], axis=0)
     frame = jnp.zeros(points.shape, i32)
+    base = jnp.full(points.shape, home, i32)
+    limit = jnp.where(other == 1, SIZES[1][0], SIZES[0][0])
     for f in range(1, steps):
-        frame = frame + (points >= home + f * SLOTS).astype(i32)
+        reached = points >= home + jnp.where(other == 1, STARTS[1][f], STARTS[0][f])
+        frame = frame + reached.astype(i32)
+        base = jnp.where(reached, home + jnp.where(other == 1, STARTS[1][f], STARTS[0][f]), base)
+        limit = jnp.where(reached, jnp.where(other == 1, SIZES[1][f], SIZES[0][f]), limit)
     away = points >= home
     source = jnp.where(away, 1 + frame + steps * other, 0)
-    spot = jnp.where(away, points - home - frame * SLOTS, points)
-    spot = jnp.clip(spot, 0, jnp.where(away, SLOTS - 1, home - 1))
+    spot = jnp.where(away, points - base, points)
+    spot = jnp.clip(spot, 0, jnp.where(away, limit, home) - 1)
     items = points.shape[0]
     item_lane = lax.broadcasted_iota(i32, (items, BLK), 1)
     table = jnp.where(
@@ -296,11 +307,11 @@
     share = tie_share(reach, facing > 0, lane, half)
     reach = full_reach(reach, facing > 0, lane, share, blocks, half)
     choices = []
-    for one, other in (reach, reach[::-1]):
+    for sizes, one, other in zip(SIZES, reach, reach[::-1]):
         far = jnp.where(sign > 0, one, other)
         key = jnp.broadcast_to(far * BLK + (BLK - 1 - lane), (BLK, BLK))
         place = jnp.sum((turn(key) > key).astype(i32), axis=0, keepdims=True)
-        choices.append(in_order(place, far > 0, SLOTS))
+        choices.append(in_order(place, far > 0, sizes[0]))
     return choices
 
 
@@ -353,20 +364,21 @@
     done_ref[...] = jnp.zeros(done_ref.shape, jnp.int32)
 
 
-def ready_kernel(chain, step, send_ref, home_ref, *refs):
+def ready_kernel(chain, step, after_ref, send_ref, home_ref, *refs):
+    del after_ref
     frames, out_ref = refs[:-1], refs[-1]
     home = home_ref.shape[0]
-    for j, at in enumerate(scalars(send_ref, chain, step * SLOTS, SLOTS)):
+    for j, at in enumerate(scalars(send_ref, chain, STARTS[chain][step], SIZES[chain][step])):
 
         def copy(low, high, j=j, at=at):
             if high - low == 1:
                 if low == 0:
                     out_ref[j] = home_ref[at]
                 elif low <= len(frames):
-                    out_ref[j] = frames[low - 1][at - home - (low - 1) * SLOTS]
+                    out_ref[j] = frames[low - 1][at - home - STARTS[chain][low - 1]]
                 return
             mid = (low + high) // 2
-            split = home + (mid - 1) * SLOTS
+            split = home + STARTS[chain][mid - 1]
             pl.when(at < split)(lambda: copy(low, mid))
             pl.when(at >= split)(lambda: copy(mid, high))
 
@@ -374,8 +386,8 @@
 
 
 def pass_kernel(chain, step, home, send_ref, part_ref, newest_ref, out_ref):
-    start = home + (step - 1) * SLOTS
-    for j, at in enumerate(scalars(send_ref, chain, step * SLOTS, SLOTS)):
+    start = home + STARTS[chain][step - 1]
+    for j, at in enumerate(scalars(send_ref, chain, STARTS[chain][step], SIZES[chain][step])):
         newest = newest_ref[jnp.maximum(at - start, 0)]
         out_ref[j] = jnp.where(at >= start, newest, part_ref[j])
 
@@ -559,6 +571,7 @@
 
     vmem = pl.BlockSpec(memory_space=pltpu.VMEM)
     smem = pl.BlockSpec(memory_space=pltpu.SMEM)
+    anywhere = pl.BlockSpec(memory_space=pl.ANY)
     def room(mib):
         return pltpu.CompilerParams(vmem_limit_bytes=mib * 1024 * 1024)
 
@@ -570,7 +583,7 @@
         place = jnp.stack([vocab_index, sign]).astype(jnp.int32)
         own, ahead, behind, packed = pl.pallas_call(
             pack_kernel,
-            out_shape=(planes(home), planes(SLOTS), planes(SLOTS), jax.ShapeDtypeStruct((8, BLK), jnp.int32)),
+            out_shape=(planes(home), planes(SIZES[0][0]), planes(SIZES[1][0]), jax.ShapeDtypeStruct((8, BLK), jnp.int32)),
             in_specs=[vmem] * 6,
             out_specs=(vmem,) * 4,
             scratch_shapes=[
@@ -591,32 +604,35 @@
             compiler_params=room(8),
         )(place, listed, packed)
 
-    def chosen(chain, step, frames):
-        part = pl.pallas_call(
+    def ready(chain, step, after, frames):
+        return pl.pallas_call(
             functools.partial(ready_kernel, chain, step),
-            out_shape=planes(SLOTS),
-            in_specs=[vmem] * (1 + len(frames)),
+            out_shape=planes(SIZES[chain][step]),
+            in_specs=[anywhere] + [vmem] * (2 + len(frames)),
             out_specs=vmem,
             compiler_params=room(8),
-        )(send, own, *frames[:-1])
+        )(after, send, own, *frames)
+
+    def passed(chain, step, part, newest):
         return pl.pallas_call(
             functools.partial(pass_kernel, chain, step, home),
-            out_shape=planes(SLOTS),
+            out_shape=planes(SIZES[chain][step]),
             in_specs=[vmem] * 3,
             out_specs=vmem,
             compiler_params=room(4),
-        )(send, part, frames[-1])
+        )(send, part, newest)
 
     with jax.named_scope("ring"):
         forward, backward = ring_pairs(1), ring_pairs(-1)
-        came_ahead, came_behind = [], []
-        for step in range(steps):
-            if step:
-                ahead = chosen(0, step, came_ahead)
+        came_behind = [lax.ppermute(behind, ("seq", "vocab"), backward)]
+        came_ahead = [lax.ppermute(ahead, ("seq", "vocab"), forward)]
+        for step in range(1, steps):
+            part = ready(1, step, ahead, came_behind[:-1])
+            behind = passed(1, step, part, came_behind[-1])
+            came_behind.append(lax.ppermute(behind, ("seq", "vocab"), backward))
+            part = ready(0, step, behind, came_ahead[:-1])
+            ahead = passed(0, step, part, came_ahead[-1])
             came_ahead.append(lax.ppermute(ahead, ("seq", "vocab"), forward))
-            if step:
-                behind = chosen(1, step, came_behind)
-            came_behind.append(lax.ppermute(behind, ("seq", "vocab"), backward))
 
     with jax.named_scope("student"):
         top, total = pl.pallas_call(

time: 207 us -> 204 us (0.986)
  waiting for transfers between devices: 59.3 us -> 64.6 us
  Pallas kernels: 39.1 us -> 34.3 us
  starting transfers between devices: 81.5 us -> 78 us
    ppermute x0 -> x2, starting transfers between devices: none -> 13.3 us  [the longest x1 11.4 us: shards(): came_behind = [lax.ppermute(behind, ('seq', 'vocab'), backward)]]
    ppermute x8 -> x7, starting transfers between devices: 48.7 us -> 39.1 us  [shards(): came_behind.append(lax.ppermute(behind, ('seq', 'vocab'), backward))]
    all_to_all x1, starting transfers between devices: 11.9 us -> 6.58 us  [shards(): lax.all_to_all(sent, 'vocab', split_axis=0, concat_axis=0, tiled=True)]
    pallas_call x29, Pallas kernels: 26.7 us -> 21.7 us  [the longest x14 12 us: ready(): pl.pallas_call(functools.partial(ready_kernel, chain, step), out_shape=pl...]
    ppermute x0 -> x2, waiting for transfers between devices: none -> 4.21 us  [the longest x1 2.46 us: shards(): came_ahead = [lax.ppermute(ahead, ('seq', 'vocab'), forward)]]
    ppermute x8 -> x7, waiting for transfers between devices: 15.9 us -> 19.8 us  [shards(): came_behind.append(lax.ppermute(behind, ('seq', 'vocab'), backward))]
    ppermute x8 -> x7, waiting for transfers between devices: 31.1 us -> 28.3 us  [shards(): came_ahead.append(lax.ppermute(ahead, ('seq', 'vocab'), forward))]
    ppermute x8 -> x7, starting transfers between devices: 15.3 us -> 13.4 us  [shards(): came_ahead.append(lax.ppermute(ahead, ('seq', 'vocab'), forward))]
  transfers between devices with their start and end apart: 20 -> 20, of which waited for: 13 -> 17; matrix products, arithmetic and copies ran while one was open for 2% -> 2% of each run, Pallas kernels for 16% -> 13%
where the time goes in v8:
time: 204 us; the launch traced here: 202 us
  starting transfers between devices  78 us (38%)
  waiting for transfers between devices  64.6 us (32%)
  Pallas kernels  34.3 us (17%)
  between operations  15.2 us (7%)
  local copies, waits for them, and re-layouts  8.35 us (4%)
    ppermute x7, starting transfers between devices, shards(): came_behind.append(lax.ppermute(behind, ('seq', 'vocab'), backward))  39.1 us
    ppermute x7, waiting for transfers between devices, shards(): came_ahead.append(lax.ppermute(ahead, ('seq', 'vocab'), forward))  28.3 us
    ppermute x7, waiting for transfers between devices, shards(): came_behind.append(lax.ppermute(behind, ('seq', 'vocab'), backward))  19.8 us
    ppermute x7, starting transfers between devices, shards(): came_ahead.append(lax.ppermute(ahead, ('seq', 'vocab'), forward))  13.4 us
    pallas_call x14, Pallas kernels, ready(): pl.pallas_call(functools.partial(ready_kernel, chain, step), out_shape=pl...  12 us
    ppermute x1, starting transfers between devices, shards(): came_behind = [lax.ppermute(behind, ('seq', 'vocab'), backward)]  11.4 us
    all_to_all x1, waiting for transfers between devices, shards(): lax.all_to_all(sent, 'vocab', split_axis=0, concat_axis=0, tiled=True)  10.1 us
    pallas_call x14, Pallas kernels, passed(): pl.pallas_call(functools.partial(pass_kernel, chain, step, home), out_sha...  8.15 us
  transfers between devices with their start and end apart: 20, of which 17 were waited for; matrix products, arithmetic and copies ran while one was open for 2% of the time, Pallas kernels for 13%

profile of v8, /device:TPU:6, one launch (start us, length us, event | category | flops | bytes accessed | tf_op | source)
XLA Modules:
  0.0 202.5 jit_solution(10049287684147848391)
XLA Ops:
  7.7 1.9 collective-permute-start
  9.7 3.6 %collective-permute-start.1 = (bf16[2,16,4736]{2,1,0:T(8,128)(2,1)S(1)}, bf16[2,16,4736]{2,1,0:T(8,128)(2,1)S(1)}, u32[]{:S(2)}, u32[]{:S(2)}) collective-permute-start(bf16[2,16,4736]{2,1,0:T(8,128)(2,1)S(1)} %get-tuple-element.155), channel_id=1, source_target_pairs={{16,0},{32,16},{48,32},{64,48},{80,64},{96,80},{112,96},{17,1},{33... | collective-permute-start | bytes 909320 | tf_op jit(solution)/shard_map/halo/ppermute | solution.py:24
  19.3 11.4 %collective-permute-start.3 = (bf16[12,104,128]{2,1,0:T(8,128)(2,1)S(1)}, bf16[12,104,128]{2,1,0:T(8,128)(2,1)S(1)}, u32[]{:S(2)}, u32[]{:S(2)}) collective-permute-start(bf16[12,104,128]{2,1,0:T(8,128)(2,1)S(1)} %get-tuple-element.94), channel_id=1, source_target_pairs={{0,15},{1,0},{2,1},{3,2},{4,3},{5,4},{6,5},{7,6},{8,7},{9,8},{10,9... | collective-permute-start | bytes 958472 | tf_op jit(solution)/shard_map/ring/ppermute | solution.py:627
  30.8 1.9 collective-permute-start.2
  32.7 4.0 %plan.1 = (s32[8,256]{1,0:T(8,128)S(1)}, s32[8,128]{1,0:T(8,128)S(1)}, s32[8,128]{1,0:T(8,128)S(1)}) custom-call(s32[2]{0:T(128)S(1)} %pad_add_fusion.place_ref, s32[16,64]{1,0:T(8,128)S(1)} %reshape.252.listed_ref, s32[8,128]{1,0:T(8,128)S(1)} %get-tuple-element.88.after_ref), custom_call_target="tpu_custom_call" | custom-call | tf_op jit(solution)/shard_map/plan/pallas_call | solution.py:598
  39.0 5.6 %collective-permute-start.5 = (bf16[23,104,128]{2,1,0:T(8,128)(2,1)S(1)}, bf16[23,104,128]{2,1,0:T(8,128)(2,1)S(1)}, u32[]{:S(2)}, u32[]{:S(2)}) collective-permute-start(bf16[23,104,128]{2,1,0:T(8,128)(2,1)S(1)} %ring.29.after_ref), channel_id=1, source_target_pairs={{0,15},{1,0},{2,1},{3,2},{4,3},{5,4},{6,5},{7,6},{8,7},{9,8},{10,9... | collective-permute-start | bytes 1837064 | tf_op jit(solution)/shard_map/ring/ppermute | solution.py:632
  44.9 2.5 %collective-permute-done.2.newest_ref.refs_0_.refs_1_ = bf16[21,104,128]{2,1,0:T(8,128)(2,1)S(1)} collective-permute-done((bf16[21,104,128]{2,1,0:T(8,128)(2,1)S(1)}, bf16[21,104,128]{2,1,0:T(8,128)(2,1)S(1)}, u32[]{:S(2)}, u32[]{:S(2)}) %collective-permute-start.2) | collective-permute-done | bytes 559136 | tf_op jit(solution)/shard_map/ring/ppermute | solution.py:628
  47.6 1.9 collective-permute-start.4
  50.0 7.4 %collective-permute-done.5.newest_ref.refs_1_.refs_9_ = bf16[23,104,128]{2,1,0:T(8,128)(2,1)S(1)} collective-permute-done((bf16[23,104,128]{2,1,0:T(8,128)(2,1)S(1)}, bf16[23,104,128]{2,1,0:T(8,128)(2,1)S(1)}, u32[]{:S(2)}, u32[]{:S(2)}) %collective-permute-start.5) | collective-permute-done | bytes 612384 | tf_op jit(solution)/shard_map/ring/ppermute | solution.py:632
  58.5 5.6 %collective-permute-start.7 = (bf16[23,104,128]{2,1,0:T(8,128)(2,1)}, bf16[23,104,128]{2,1,0:T(8,128)(2,1)S(1)}, u32[]{:S(2)}, u32[]{:S(2)}) collective-permute-start(bf16[23,104,128]{2,1,0:T(8,128)(2,1)} %ring.33.after_ref), channel_id=1, source_target_pairs={{0,15},{1,0},{2,1},{3,2},{4,3},{5,4},{6,5},{7,6},{8,7},{9,8},{10,9... | collective-permute-start | bytes 1837064 | tf_op jit(solution)/shard_map/ring/ppermute | solution.py:632
  65.6 1.9 collective-permute-start.6
  69.0 6.7 %collective-permute-done.7.newest_ref.refs_2_.refs_10_ = bf16[23,104,128]{2,1,0:T(8,128)(2,1)S(1)} collective-permute-done((bf16[23,104,128]{2,1,0:T(8,128)(2,1)}, bf16[23,104,128]{2,1,0:T(8,128)(2,1)S(1)}, u32[]{:S(2)}, u32[]{:S(2)}) %collective-permute-start.7) | collective-permute-done | bytes 612384 | tf_op jit(solution)/shard_map/ring/ppermute | solution.py:632
  76.0 5.5 %collective-permute-start.9 = (bf16[23,104,128]{2,1,0:T(8,128)(2,1)S(1)}, bf16[23,104,128]{2,1,0:T(8,128)(2,1)S(1)}, u32[]{:S(2)}, u32[]{:S(2)}) collective-permute-start(bf16[23,104,128]{2,1,0:T(8,128)(2,1)S(1)} %ring.37.after_ref), channel_id=1, source_target_pairs={{0,15},{1,0},{2,1},{3,2},{4,3},{5,4},{6,5},{7,6},{8,7},{9,8},{10,9... | collective-permute-start | bytes 1837064 | tf_op jit(solution)/shard_map/ring/ppermute | solution.py:632
  81.9 2.5 %collective-permute-done.6.newest_ref.refs_2_.refs_3_ = bf16[21,104,128]{2,1,0:T(8,128)(2,1)} collective-permute-done((bf16[21,104,128]{2,1,0:T(8,128)(2,1)}, bf16[21,104,128]{2,1,0:T(8,128)(2,1)}, u32[]{:S(2)}, u32[]{:S(2)}) %collective-permute-start.6) | collective-permute-done | bytes 559136 | tf_op jit(solution)/shard_map/ring/ppermute | solution.py:635
  85.7 1.9 collective-permute-start.8
  88.3 4.1 %collective-permute-done.9.newest_ref.refs_3_.refs_11_ = bf16[23,104,128]{2,1,0:T(8,128)(2,1)S(1)} collective-permute-done((bf16[23,104,128]{2,1,0:T(8,128)(2,1)S(1)}, bf16[23,104,128]{2,1,0:T(8,128)(2,1)S(1)}, u32[]{:S(2)}, u32[]{:S(2)}) %collective-permute-start.9) | collective-permute-done | bytes 612384 | tf_op jit(solution)/shard_map/ring/ppermute | solution.py:632
  92.6 5.6 %collective-permute-start.11 = (bf16[22,104,128]{2,1,0:T(8,128)(2,1)S(1)}, bf16[22,104,128]{2,1,0:T(8,128)(2,1)S(1)}, u32[]{:S(2)}, u32[]{:S(2)}) collective-permute-start(bf16[22,104,128]{2,1,0:T(8,128)(2,1)S(1)} %ring.41.after_ref), channel_id=1, source_target_pairs={{0,15},{1,0},{2,1},{3,2},{4,3},{5,4},{6,5},{7,6},{8,7},{9,8},{10,9... | collective-permute-start | bytes 1757192 | tf_op jit(solution)/shard_map/ring/ppermute | solution.py:632
  99.9 3.2 %collective-permute-done.8.newest_ref.refs_3_.refs_4_ = bf16[21,104,128]{2,1,0:T(8,128)(2,1)S(1)} collective-permute-done((bf16[21,104,128]{2,1,0:T(8,128)(2,1)S(1)}, bf16[21,104,128]{2,1,0:T(8,128)(2,1)S(1)}, u32[]{:S(2)}, u32[]{:S(2)}) %collective-permute-start.8) | collective-permute-done | bytes 559136 | tf_op jit(solution)/shard_map/ring/ppermute | solution.py:635
  103.3 1.9 collective-permute-start.10
  107.7 5.6 %collective-permute-start.13 = (bf16[22,104,128]{2,1,0:T(8,128)(2,1)S(1)}, bf16[22,104,128]{2,1,0:T(8,128)(2,1)S(1)}, u32[]{:S(2)}, u32[]{:S(2)}) collective-permute-start(bf16[22,104,128]{2,1,0:T(8,128)(2,1)S(1)} %ring.45.after_ref), channel_id=1, source_target_pairs={{0,15},{1,0},{2,1},{3,2},{4,3},{5,4},{6,5},{7,6},{8,7},{9,8},{10,9... | collective-permute-start | bytes 1757192 | tf_op jit(solution)/shard_map/ring/ppermute | solution.py:632
  115.0 5.2 %collective-permute-done.10.newest_ref.refs_4_.refs_5_ = bf16[21,104,128]{2,1,0:T(8,128)(2,1)S(1)} collective-permute-done((bf16[21,104,128]{2,1,0:T(8,128)(2,1)S(1)}, bf16[21,104,128]{2,1,0:T(8,128)(2,1)S(1)}, u32[]{:S(2)}, u32[]{:S(2)}) %collective-permute-start.10) | collective-permute-done | bytes 559136 | tf_op jit(solution)/shard_map/ring/ppermute | solution.py:635
  120.5 1.9 collective-permute-start.12
  123.6 5.6 %collective-permute-start.15 = (bf16[22,104,128]{2,1,0:T(8,128)(2,1)S(1)}, bf16[22,104,128]{2,1,0:T(8,128)(2,1)S(1)}, u32[]{:S(2)}, u32[]{:S(2)}) collective-permute-start(bf16[22,104,128]{2,1,0:T(8,128)(2,1)S(1)} %ring.49.after_ref), channel_id=1, source_target_pairs={{0,15},{1,0},{2,1},{3,2},{4,3},{5,4},{6,5},{7,6},{8,7},{9,8},{10,9... | collective-permute-start | bytes 1757192 | tf_op jit(solution)/shard_map/ring/ppermute | solution.py:632
  130.9 5.8 %collective-permute-done.12.newest_ref.refs_6_.refs_5_ = bf16[21,104,128]{2,1,0:T(8,128)(2,1)S(1)} collective-permute-done((bf16[21,104,128]{2,1,0:T(8,128)(2,1)S(1)}, bf16[21,104,128]{2,1,0:T(8,128)(2,1)S(1)}, u32[]{:S(2)}, u32[]{:S(2)}) %collective-permute-start.12) | collective-permute-done | bytes 559136 | tf_op jit(solution)/shard_map/ring/ppermute | solution.py:635
  136.9 1.9 collective-permute-start.14
  140.9 5.6 %collective-permute-start.17 = (bf16[22,104,128]{2,1,0:T(8,128)(2,1)}, bf16[22,104,128]{2,1,0:T(8,128)(2,1)}, u32[]{:S(2)}, u32[]{:S(2)}) collective-permute-start(bf16[22,104,128]{2,1,0:T(8,128)(2,1)} %ring.53.after_ref), channel_id=1, source_target_pairs={{0,15},{1,0},{2,1},{3,2},{4,3},{5,4},{6,5},{7,6},{8,7},{9,8},{10,9... | collective-permute-start | bytes 1757192 | tf_op jit(solution)/shard_map/ring/ppermute | solution.py:632
  148.3 5.2 %collective-permute-done.14.refs_7_.newest_ref = bf16[21,104,128]{2,1,0:T(8,128)(2,1)S(1)} collective-permute-done((bf16[21,104,128]{2,1,0:T(8,128)(2,1)S(1)}, bf16[21,104,128]{2,1,0:T(8,128)(2,1)S(1)}, u32[]{:S(2)}, u32[]{:S(2)}) %collective-permute-start.14) | collective-permute-done | bytes 559136 | tf_op jit(solution)/shard_map/ring/ppermute | solution.py:635
  157.4 2.4 %stage.1.held_ref = bf16[96,104,128]{2,1,0:T(8,128)(2,1)S(1)} custom-call(s32[8,128]{1,0:T(8,128)S(1)} %get-tuple-element.90.item_ref, bf16[38,104,128]{2,1,0:T(8,128)(2,1)S(1)} %get-tuple-element.91.home_ref.refs_0_, bf16[21,104,128]{2,1,0:T(8,128)(2,1)S(1)} %collective-permute-done.2.newest_ref.refs_0_.refs_1_, ...), custom_call_target="tpu_custom_call" | custom-call | tf_op jit(solution)/shard_map/stage/pallas_call | solution.py:648
  161.2 6.4 %collective-permute-done.16.ahead_ref = bf16[21,104,128]{2,1,0:T(8,128)(2,1)} collective-permute-done((bf16[21,104,128]{2,1,0:T(8,128)(2,1)}, bf16[21,104,128]{2,1,0:T(8,128)(2,1)}, u32[]{:S(2)}, u32[]{:S(2)}) %collective-permute-start.16) | collective-permute-done | bytes 559136 | tf_op jit(solution)/shard_map/ring/ppermute | solution.py:635
  169.3 5.6 %map.1 = f32[8,128]{1,0:T(8,128)S(1)} custom-call(s32[8,128]{1,0:T(8,128)S(1)} %get-tuple-element.90.item_ref, bf16[96,104,128]{2,1,0:T(8,128)(2,1)S(1)} %copy-done.4, bf16[21,104,128]{2,1,0:T(8,128)(2,1)} %collective-permute-done.16.ahead_ref, bf16[22,104,128]{2,1,0:T(8,128)(2,1)} %collective-permute-done.17.behind_ref, ...), custom_call_target="tpu_custom_call" | custom-call | tf_op jit(solution)/shard_map/map/pallas_call | solution.py:657
  175.6 6.6 %all-to-all-start.1 = ((f32[16,4,128]{2,1,0:T(4,128)}), f32[16,4,128]{2,1,0:T(4,128)S(1)}, u32[]{:S(2)}, u32[]{:S(2)}) async-start(f32[16,4,128]{2,1,0:T(4,128)} %broadcast_in_dim.55), calls=%async_computation.1 | async-start | bytes 65536 | tf_op jit(solution)/shard_map/finish/all_to_all | solution.py:671
  184.7 10.1 %all-to-all-done.1 = f32[16,4,128]{2,1,0:T(4,128)S(1)} async-done(((f32[16,4,128]{2,1,0:T(4,128)}), f32[16,4,128]{2,1,0:T(4,128)S(1)}, u32[]{:S(2)}, u32[]{:S(2)}) %all-to-all-start.1) | async-done | bytes 32800 | tf_op jit(solution)/shard_map/finish/all_to_all | solution.py:671
  (94 shorter events, 40.4 us)
Async XLA Ops:
  6.5 11.2 %copy-start.8 = (bf16[2,64,4736]{2,1,0:T(8,128)(2,1)S(1)}, bf16[2,64,4736]{2,1,0:T(8,128)(2,1)}, u32[]{:S(2)}) copy-start(bf16[2,64,4736]{2,1,0:T(8,128)(2,1)} %own_ref.1) | copy-start | bytes 3637252
  6.5 154.7 %all-gather.2.cloned.1.call-start = ((), (), s32[]{:S(2)}) async-start(), calls=%async_computation.2 | async-start | bytes 2621440 | tf_op jit(solution)/shard_map/weights/all_gather | solution.py:556
  7.7 8.1 %collective-permute-start = (bf16[2,16,4736]{2,1,0:T(8,128)(2,1)S(1)}, bf16[2,16,4736]{2,1,0:T(8,128)(2,1)S(1)}, u32[]{:S(2)}, u32[]{:S(2)}) collective-permute-start(bf16[2,16,4736]{2,1,0:T(8,128)(2,1)S(1)} %get-tuple-element.156), channel_id=1, source_target_pairs={{0,16},{16,32},{32,48},{48,64},{64,80},{80,96},{96,112},{1,17},{17... | collective-permute-start | bytes 909320 | tf_op jit(solution)/shard_map/halo/ppermute | solution.py:23
  9.7 8.0 %collective-permute-start.1 = (bf16[2,16,4736]{2,1,0:T(8,128)(2,1)S(1)}, bf16[2,16,4736]{2,1,0:T(8,128)(2,1)S(1)}, u32[]{:S(2)}, u32[]{:S(2)}) collective-permute-start(bf16[2,16,4736]{2,1,0:T(8,128)(2,1)S(1)} %get-tuple-element.155), channel_id=1, source_target_pairs={{16,0},{32,16},{48,32},{64,48},{80,64},{96,80},{112,96},{17,1},{33... | collective-permute-start | bytes 909320 | tf_op jit(solution)/shard_map/halo/ppermute | solution.py:24
  15.9 14.9 %copy-start.9 = (bf16[2,16,4736]{2,1,0:T(8,128)(2,1)}, bf16[2,16,4736]{2,1,0:T(8,128)(2,1)S(1)}, u32[]{:S(2)}) copy-start(bf16[2,16,4736]{2,1,0:T(8,128)(2,1)S(1)} %collective-permute-done.low_ref) | copy-start | bytes 909316
  17.6 21.4 %copy-start.11 = (bf16[2,16,4736]{2,1,0:T(8,128)(2,1)}, bf16[2,16,4736]{2,1,0:T(8,128)(2,1)S(1)}, u32[]{:S(2)}) copy-start(bf16[2,16,4736]{2,1,0:T(8,128)(2,1)S(1)} %collective-permute-done.1.high_ref) | copy-start | bytes 909316
  19.3 19.4 %collective-permute-start.3 = (bf16[12,104,128]{2,1,0:T(8,128)(2,1)S(1)}, bf16[12,104,128]{2,1,0:T(8,128)(2,1)S(1)}, u32[]{:S(2)}, u32[]{:S(2)}) collective-permute-start(bf16[12,104,128]{2,1,0:T(8,128)(2,1)S(1)} %get-tuple-element.94), channel_id=1, source_target_pairs={{0,15},{1,0},{2,1},{3,2},{4,3},{5,4},{6,5},{7,6},{8,7},{9,8},{10,9... | collective-permute-start | bytes 958472 | tf_op jit(solution)/shard_map/ring/ppermute | solution.py:627
  30.8 16.6 %collective-permute-start.2 = (bf16[21,104,128]{2,1,0:T(8,128)(2,1)S(1)}, bf16[21,104,128]{2,1,0:T(8,128)(2,1)S(1)}, u32[]{:S(2)}, u32[]{:S(2)}) collective-permute-start(bf16[21,104,128]{2,1,0:T(8,128)(2,1)S(1)} %get-tuple-element.92.after_ref), channel_id=1, source_target_pairs={{0,1},{1,2},{2,3},{3,4},{4,5},{5,6},{6,7},{7,8},{8,9},{9,10},{10,1... | collective-permute-start | bytes 1677320 | tf_op jit(solution)/shard_map/ring/ppermute | solution.py:628
  38.7 10.8 %copy-start = (bf16[12,104,128]{2,1,0:T(8,128)(2,1)}, bf16[12,104,128]{2,1,0:T(8,128)(2,1)S(1)}, u32[]{:S(2)}) copy-start(bf16[12,104,128]{2,1,0:T(8,128)(2,1)S(1)} %collective-permute-done.3.newest_ref.refs_0_.refs_8_) | copy-start | bytes 958468
  39.0 18.3 %collective-permute-start.5 = (bf16[23,104,128]{2,1,0:T(8,128)(2,1)S(1)}, bf16[23,104,128]{2,1,0:T(8,128)(2,1)S(1)}, u32[]{:S(2)}, u32[]{:S(2)}) collective-permute-start(bf16[23,104,128]{2,1,0:T(8,128)(2,1)S(1)} %ring.29.after_ref), channel_id=1, source_target_pairs={{0,15},{1,0},{2,1},{3,2},{4,3},{5,4},{6,5},{7,6},{8,7},{9,8},{10,9... | collective-permute-start | bytes 1837064 | tf_op jit(solution)/shard_map/ring/ppermute | solution.py:632
  47.6 16.9 %collective-permute-start.4 = (bf16[21,104,128]{2,1,0:T(8,128)(2,1)S(1)}, bf16[21,104,128]{2,1,0:T(8,128)(2,1)S(1)}, u32[]{:S(2)}, u32[]{:S(2)}) collective-permute-start(bf16[21,104,128]{2,1,0:T(8,128)(2,1)S(1)} %ring.31.after_ref), channel_id=1, source_target_pairs={{0,1},{1,2},{2,3},{3,4},{4,5},{5,6},{6,7},{7,8},{8,9},{9,10},{10,1... | collective-permute-start | bytes 1677320 | tf_op jit(solution)/shard_map/ring/ppermute | solution.py:635
  58.5 17.2 %collective-permute-start.7 = (bf16[23,104,128]{2,1,0:T(8,128)(2,1)}, bf16[23,104,128]{2,1,0:T(8,128)(2,1)S(1)}, u32[]{:S(2)}, u32[]{:S(2)}) collective-permute-start(bf16[23,104,128]{2,1,0:T(8,128)(2,1)} %ring.33.after_ref), channel_id=1, source_target_pairs={{0,15},{1,0},{2,1},{3,2},{4,3},{5,4},{6,5},{7,6},{8,7},{9,8},{10,9... | collective-permute-start | bytes 1837064 | tf_op jit(solution)/shard_map/ring/ppermute | solution.py:632
  65.6 18.8 %collective-permute-start.6 = (bf16[21,104,128]{2,1,0:T(8,128)(2,1)}, bf16[21,104,128]{2,1,0:T(8,128)(2,1)}, u32[]{:S(2)}, u32[]{:S(2)}) collective-permute-start(bf16[21,104,128]{2,1,0:T(8,128)(2,1)} %ring.35.after_ref), channel_id=1, source_target_pairs={{0,1},{1,2},{2,3},{3,4},{4,5},{5,6},{6,7},{7,8},{8,9},{9,10},{10,1... | collective-permute-start | bytes 1677320 | tf_op jit(solution)/shard_map/ring/ppermute | solution.py:635
  67.5 1.0 copy-start.1
  76.0 16.4 %collective-permute-start.9 = (bf16[23,104,128]{2,1,0:T(8,128)(2,1)S(1)}, bf16[23,104,128]{2,1,0:T(8,128)(2,1)S(1)}, u32[]{:S(2)}, u32[]{:S(2)}) collective-permute-start(bf16[23,104,128]{2,1,0:T(8,128)(2,1)S(1)} %ring.37.after_ref), channel_id=1, source_target_pairs={{0,15},{1,0},{2,1},{3,2},{4,3},{5,4},{6,5},{7,6},{8,7},{9,8},{10,9... | collective-permute-start | bytes 1837064 | tf_op jit(solution)/shard_map/ring/ppermute | solution.py:632
  85.7 17.4 %collective-permute-start.8 = (bf16[21,104,128]{2,1,0:T(8,128)(2,1)S(1)}, bf16[21,104,128]{2,1,0:T(8,128)(2,1)S(1)}, u32[]{:S(2)}, u32[]{:S(2)}) collective-permute-start(bf16[21,104,128]{2,1,0:T(8,128)(2,1)S(1)} %ring.39.after_ref), channel_id=1, source_target_pairs={{0,1},{1,2},{2,3},{3,4},{4,5},{5,6},{6,7},{7,8},{8,9},{9,10},{10,1... | collective-permute-start | bytes 1677320 | tf_op jit(solution)/shard_map/ring/ppermute | solution.py:635
  92.6 14.8 %collective-permute-start.11 = (bf16[22,104,128]{2,1,0:T(8,128)(2,1)S(1)}, bf16[22,104,128]{2,1,0:T(8,128)(2,1)S(1)}, u32[]{:S(2)}, u32[]{:S(2)}) collective-permute-start(bf16[22,104,128]{2,1,0:T(8,128)(2,1)S(1)} %ring.41.after_ref), channel_id=1, source_target_pairs={{0,15},{1,0},{2,1},{3,2},{4,3},{5,4},{6,5},{7,6},{8,7},{9,8},{10,9... | collective-permute-start | bytes 1757192 | tf_op jit(solution)/shard_map/ring/ppermute | solution.py:632
  103.3 16.8 %collective-permute-start.10 = (bf16[21,104,128]{2,1,0:T(8,128)(2,1)S(1)}, bf16[21,104,128]{2,1,0:T(8,128)(2,1)S(1)}, u32[]{:S(2)}, u32[]{:S(2)}) collective-permute-start(bf16[21,104,128]{2,1,0:T(8,128)(2,1)S(1)} %ring.43.after_ref), channel_id=1, source_target_pairs={{0,1},{1,2},{2,3},{3,4},{4,5},{5,6},{6,7},{7,8},{8,9},{9,10},{10,1... | collective-permute-start | bytes 1677320 | tf_op jit(solution)/shard_map/ring/ppermute | solution.py:635
  107.7 15.6 %collective-permute-start.13 = (bf16[22,104,128]{2,1,0:T(8,128)(2,1)S(1)}, bf16[22,104,128]{2,1,0:T(8,128)(2,1)S(1)}, u32[]{:S(2)}, u32[]{:S(2)}) collective-permute-start(bf16[22,104,128]{2,1,0:T(8,128)(2,1)S(1)} %ring.45.after_ref), channel_id=1, source_target_pairs={{0,15},{1,0},{2,1},{3,2},{4,3},{5,4},{6,5},{7,6},{8,7},{9,8},{10,9... | collective-permute-start | bytes 1757192 | tf_op jit(solution)/shard_map/ring/ppermute | solution.py:632
  120.5 16.2 %collective-permute-start.12 = (bf16[21,104,128]{2,1,0:T(8,128)(2,1)S(1)}, bf16[21,104,128]{2,1,0:T(8,128)(2,1)S(1)}, u32[]{:S(2)}, u32[]{:S(2)}) collective-permute-start(bf16[21,104,128]{2,1,0:T(8,128)(2,1)S(1)} %ring.47.after_ref), channel_id=1, source_target_pairs={{0,1},{1,2},{2,3},{3,4},{4,5},{5,6},{6,7},{7,8},{8,9},{9,10},{10,1... | collective-permute-start | bytes 1677320 | tf_op jit(solution)/shard_map/ring/ppermute | solution.py:635
  123.6 16.2 %collective-permute-start.15 = (bf16[22,104,128]{2,1,0:T(8,128)(2,1)S(1)}, bf16[22,104,128]{2,1,0:T(8,128)(2,1)S(1)}, u32[]{:S(2)}, u32[]{:S(2)}) collective-permute-start(bf16[22,104,128]{2,1,0:T(8,128)(2,1)S(1)} %ring.49.after_ref), channel_id=1, source_target_pairs={{0,15},{1,0},{2,1},{3,2},{4,3},{5,4},{6,5},{7,6},{8,7},{9,8},{10,9... | collective-permute-start | bytes 1757192 | tf_op jit(solution)/shard_map/ring/ppermute | solution.py:632
  136.9 16.6 %collective-permute-start.14 = (bf16[21,104,128]{2,1,0:T(8,128)(2,1)S(1)}, bf16[21,104,128]{2,1,0:T(8,128)(2,1)S(1)}, u32[]{:S(2)}, u32[]{:S(2)}) collective-permute-start(bf16[21,104,128]{2,1,0:T(8,128)(2,1)S(1)} %ring.51.after_ref), channel_id=1, source_target_pairs={{0,1},{1,2},{2,3},{3,4},{4,5},{5,6},{6,7},{7,8},{8,9},{9,10},{10,1... | collective-permute-start | bytes 1677320 | tf_op jit(solution)/shard_map/ring/ppermute | solution.py:635
  140.9 26.7 %collective-permute-start.17 = (bf16[22,104,128]{2,1,0:T(8,128)(2,1)}, bf16[22,104,128]{2,1,0:T(8,128)(2,1)}, u32[]{:S(2)}, u32[]{:S(2)}) collective-permute-start(bf16[22,104,128]{2,1,0:T(8,128)(2,1)} %ring.53.after_ref), channel_id=1, source_target_pairs={{0,15},{1,0},{2,1},{3,2},{4,3},{5,4},{6,5},{7,6},{8,7},{9,8},{10,9... | collective-permute-start | bytes 1757192 | tf_op jit(solution)/shard_map/ring/ppermute | solution.py:632
  148.3 8.2 %copy-start.5 = (bf16[2,64,4096]{2,1,0:T(8,128)(2,1)S(1)}, bf16[2,64,4096]{2,1,0:T(8,128)(2,1)}, u32[]{:S(2)}) copy-start(bf16[2,64,4096]{2,1,0:T(8,128)(2,1)} %student_ref.3) | copy-start | bytes 3145732
  148.3 9.0 %copy-start.2 = (bf16[12,104,128]{2,1,0:T(8,128)(2,1)S(1)}, bf16[12,104,128]{2,1,0:T(8,128)(2,1)}, u32[]{:S(2)}) copy-start(bf16[12,104,128]{2,1,0:T(8,128)(2,1)} %copy-done) | copy-start | bytes 958468
  154.6 13.0 %collective-permute-start.16 = (bf16[21,104,128]{2,1,0:T(8,128)(2,1)}, bf16[21,104,128]{2,1,0:T(8,128)(2,1)}, u32[]{:S(2)}, u32[]{:S(2)}) collective-permute-start(bf16[21,104,128]{2,1,0:T(8,128)(2,1)} %ring.55), channel_id=1, source_target_pairs={{0,1},{1,2},{2,3},{3,4},{4,5},{5,6},{6,7},{7,8},{8,9},{9,10},{10,1... | collective-permute-start | bytes 1677320 | tf_op jit(solution)/shard_map/ring/ppermute | solution.py:635
  159.7 1.5 copy-start.3
  167.6 1.7 copy-start.4
  169.3 15.3 %copy-start.6 = (bf16[2,64,4096]{2,1,0:T(8,128)(2,1)S(1)}, bf16[2,64,4096]{2,1,0:T(8,128)(2,1)}, u32[]{:S(2)}) copy-start(bf16[2,64,4096]{2,1,0:T(8,128)(2,1)} %student_ref.3) | copy-start | bytes 3145732
  169.3 15.3 %copy-start.10 = (bf16[2,16,4736]{2,1,0:T(8,128)(2,1)S(1)}, bf16[2,16,4736]{2,1,0:T(8,128)(2,1)}, u32[]{:S(2)}) copy-start(bf16[2,16,4736]{2,1,0:T(8,128)(2,1)} %copy-done.9) | copy-start | bytes 909316
  169.3 15.3 %copy-start.13 = (s32[512,2]{0,1:T(2,128)S(1)}, s32[512,2]{0,1:T(2,128)}, u32[]{:S(2)}) copy-start(s32[512,2]{0,1:T(2,128)} %param.12) | copy-start | bytes 12292
  175.6 19.2 %all-to-all-start.1 = ((f32[16,4,128]{2,1,0:T(4,128)}), f32[16,4,128]{2,1,0:T(4,128)S(1)}, u32[]{:S(2)}, u32[]{:S(2)}) async-start(f32[16,4,128]{2,1,0:T(4,128)} %broadcast_in_dim.55), calls=%async_computation.1 | async-start | bytes 65536 | tf_op jit(solution)/shard_map/finish/all_to_all | solution.py:671
  (1 other events, 0.6 us)
Sparse Core Ops, SparseCore 0:
  67.7 35.6 all-gather.1

commit v9 on v8

--- a/solution.py
+++ b/solution.py
@@ -18,7 +18,7 @@
 
 def halo(block, width):
     count = lax.axis_size("seq")
-    forward = [(i, i + 1) for i in range(count - 1)]
+    forward = [(i, (i + 1) % count) for i in range(count)]
     backward = [(target, source) for source, target in forward]
     low = lax.ppermute(block[:, block.shape[1] - width :], "seq", forward)
     high = lax.ppermute(block[:, :width], "seq", backward)
@@ -572,8 +572,7 @@
     vmem = pl.BlockSpec(memory_space=pltpu.VMEM)
     smem = pl.BlockSpec(memory_space=pltpu.SMEM)
     anywhere = pl.BlockSpec(memory_space=pl.ANY)
-    def room(mib):
-        return pltpu.CompilerParams(vmem_limit_bytes=mib * 1024 * 1024)
+    room = pltpu.CompilerParams(vmem_limit_bytes=20 * 1024 * 1024)
 
     def planes(count):
         return jax.ShapeDtypeStruct((count, ROWS, BLK), jnp.bfloat16)
@@ -590,7 +589,7 @@
                 pltpu.VMEM((doc_count * span, teacher_cols), jnp.bfloat16),
                 pltpu.VMEM((teacher_blocks, ROWS, BLK), jnp.bfloat16),
             ],
-            compiler_params=room(16),
+            compiler_params=room,
         )(jnp.broadcast_to(place[:, None], (2, BLK)), listed, teacher_logits, low, high, pick)
 
     with jax.named_scope("plan"):
@@ -601,7 +600,7 @@
             in_specs=[smem, vmem, vmem],
             out_specs=(vmem,) * 3,
             scratch_shapes=[pltpu.VMEM((6 * steps, vocab_count, BLK), jnp.float32)],
-            compiler_params=room(8),
+            compiler_params=room,
         )(place, listed, packed)
 
     def ready(chain, step, after, frames):
@@ -610,7 +609,7 @@
             out_shape=planes(SIZES[chain][step]),
             in_specs=[anywhere] + [vmem] * (2 + len(frames)),
             out_specs=vmem,
-            compiler_params=room(8),
+            compiler_params=room,
         )(after, send, own, *frames)
 
     def passed(chain, step, part, newest):
@@ -619,7 +618,7 @@
             out_shape=planes(SIZES[chain][step]),
             in_specs=[vmem] * 3,
             out_specs=vmem,
-            compiler_params=room(4),
+            compiler_params=room,
         )(send, part, newest)
 
     with jax.named_scope("ring"):
@@ -640,7 +639,7 @@
             out_shape=(jax.ShapeDtypeStruct((row_count, BLK), jnp.float32),) * 2,
             in_specs=[vmem],
             out_specs=(vmem,) * 2,
-            compiler_params=room(8),
+            compiler_params=room,
         )(student_logits)
 
     with jax.named_scope("stage"):
@@ -650,7 +649,7 @@
             out_shape=planes(pair_count + 2 * vocab_count),
             in_specs=[smem] + [vmem] * len(early),
             out_specs=vmem,
-            compiler_params=room(16),
+            compiler_params=room,
         )(items, *early)
 
     with jax.named_scope("map"):
@@ -663,7 +662,7 @@
                 pltpu.VMEM((pair_count + 2 * vocab_count, ROWS, BLK), jnp.bfloat16),
                 pltpu.VMEM((3 * steps, row_count, BLK), jnp.float32),
             ],
-            compiler_params=room(20),
+            compiler_params=room,
         )(items, held, came_ahead[-1], came_behind[-1], spread, weights, student_logits, top, total)
 
     with jax.named_scope("finish"):

time: 204 us -> 199 us (0.975)
  starting transfers between devices: 78 us -> 71.6 us
    ppermute x7, waiting for transfers between devices: 19.8 us -> 45.4 us  [shards(): came_behind.append(lax.ppermute(behind, ('seq', 'vocab'), backward))]
    ppermute x7, waiting for transfers between devices: 28.3 us -> 6.43 us  [shards(): came_ahead.append(lax.ppermute(ahead, ('seq', 'vocab'), forward))]
  transfers between devices with their start and end apart: 20 -> 20, of which waited for: 17 -> 11; matrix products, arithmetic and copies ran while one was open for 2% -> 2% of each run, Pallas kernels for 13% -> 14%
where the time goes in v9:
time: 199 us; the launch traced here: 197 us
  starting transfers between devices  71.6 us (36%)
  waiting for transfers between devices  65.9 us (33%)
  Pallas kernels  34.4 us (17%)
  between operations  15.2 us (8%)
  local copies, waits for them, and re-layouts  8.35 us (4%)
  other arithmetic  2.02 us (1%)
    ppermute x7, waiting for transfers between devices, shards(): came_behind.append(lax.ppermute(behind, ('seq', 'vocab'), backward))  45.4 us
    ppermute x7, starting transfers between devices, shards(): came_behind.append(lax.ppermute(behind, ('seq', 'vocab'), backward))  38.7 us
    ppermute x7, starting transfers between devices, shards(): came_ahead.append(lax.ppermute(ahead, ('seq', 'vocab'), forward))  13.4 us
    pallas_call x14, Pallas kernels, ready(): pl.pallas_call(functools.partial(ready_kernel, chain, step), out_shape=pl...  12 us
    ppermute x1, starting transfers between devices, shards(): came_behind = [lax.ppermute(behind, ('seq', 'vocab'), backward)]  10.6 us
    all_to_all x1, waiting for transfers between devices, shards(): lax.all_to_all(sent, 'vocab', split_axis=0, concat_axis=0, tiled=True)  10.1 us
    pallas_call x14, Pallas kernels, passed(): pl.pallas_call(functools.partial(pass_kernel, chain, step, home), out_sha...  8.18 us
    ppermute x7, waiting for transfers between devices, shards(): came_ahead.append(lax.ppermute(ahead, ('seq', 'vocab'), forward))  6.43 us
  transfers between devices with their start and end apart: 20, of which 11 were waited for; matrix products, arithmetic and copies ran while one was open for 2% of the time, Pallas kernels for 14%

profile of v9, /device:TPU:6, one launch (start us, length us, event | category | flops | bytes accessed | tf_op | source)
XLA Modules:
  0.0 197.5 jit_solution(12903981187210827381)
XLA Ops:
  7.8 1.7 collective-permute-start.1
  11.7 2.3 %collective-permute-done.low_ref = bf16[2,16,4736]{2,1,0:T(8,128)(2,1)S(1)} collective-permute-done((bf16[2,16,4736]{2,1,0:T(8,128)(2,1)S(1)}, bf16[2,16,4736]{2,1,0:T(8,128)(2,1)S(1)}, u32[]{:S(2)}, u32[]{:S(2)}) %collective-permute-start) | collective-permute-done | bytes 303136 | tf_op jit(solution)/shard_map/halo/ppermute | solution.py:23
  16.5 10.6 %collective-permute-start.3 = (bf16[12,104,128]{2,1,0:T(8,128)(2,1)S(1)}, bf16[12,104,128]{2,1,0:T(8,128)(2,1)S(1)}, u32[]{:S(2)}, u32[]{:S(2)}) collective-permute-start(bf16[12,104,128]{2,1,0:T(8,128)(2,1)S(1)} %get-tuple-element.94), channel_id=1, source_target_pairs={{0,15},{1,0},{2,1},{3,2},{4,3},{5,4},{6,5},{7,6},{8,7},{9,8},{10,9... | collective-permute-start | bytes 958472 | tf_op jit(solution)/shard_map/ring/ppermute | solution.py:626
  27.1 1.9 collective-permute-start.2
  29.0 4.0 %plan.1 = (s32[8,256]{1,0:T(8,128)S(1)}, s32[8,128]{1,0:T(8,128)S(1)}, s32[8,128]{1,0:T(8,128)S(1)}) custom-call(s32[2]{0:T(128)S(1)} %pad_add_fusion.place_ref, s32[16,64]{1,0:T(8,128)S(1)} %reshape.252.listed_ref, s32[8,128]{1,0:T(8,128)S(1)} %get-tuple-element.88.after_ref), custom_call_target="tpu_custom_call" | custom-call | tf_op jit(solution)/shard_map/plan/pallas_call | solution.py:597
  33.6 5.1 %collective-permute-start.5 = (bf16[23,104,128]{2,1,0:T(8,128)(2,1)S(1)}, bf16[23,104,128]{2,1,0:T(8,128)(2,1)S(1)}, u32[]{:S(2)}, u32[]{:S(2)}) collective-permute-start(bf16[23,104,128]{2,1,0:T(8,128)(2,1)S(1)} %ring.29.after_ref), channel_id=1, source_target_pairs={{0,15},{1,0},{2,1},{3,2},{4,3},{5,4},{6,5},{7,6},{8,7},{9,8},{10,9... | collective-permute-start | bytes 1837064 | tf_op jit(solution)/shard_map/ring/ppermute | solution.py:631
  40.0 1.9 collective-permute-start.4
  42.4 6.9 %collective-permute-done.5.newest_ref.refs_1_.refs_9_ = bf16[23,104,128]{2,1,0:T(8,128)(2,1)S(1)} collective-permute-done((bf16[23,104,128]{2,1,0:T(8,128)(2,1)S(1)}, bf16[23,104,128]{2,1,0:T(8,128)(2,1)S(1)}, u32[]{:S(2)}, u32[]{:S(2)}) %collective-permute-start.5) | collective-permute-done | bytes 612384 | tf_op jit(solution)/shard_map/ring/ppermute | solution.py:631
  50.5 5.6 %collective-permute-start.7 = (bf16[23,104,128]{2,1,0:T(8,128)(2,1)}, bf16[23,104,128]{2,1,0:T(8,128)(2,1)S(1)}, u32[]{:S(2)}, u32[]{:S(2)}) collective-permute-start(bf16[23,104,128]{2,1,0:T(8,128)(2,1)} %ring.33.after_ref), channel_id=1, source_target_pairs={{0,15},{1,0},{2,1},{3,2},{4,3},{5,4},{6,5},{7,6},{8,7},{9,8},{10,9... | collective-permute-start | bytes 1837064 | tf_op jit(solution)/shard_map/ring/ppermute | solution.py:631
  57.6 1.9 collective-permute-start.6
  61.0 7.6 %collective-permute-done.7.newest_ref.refs_2_.refs_10_ = bf16[23,104,128]{2,1,0:T(8,128)(2,1)S(1)} collective-permute-done((bf16[23,104,128]{2,1,0:T(8,128)(2,1)}, bf16[23,104,128]{2,1,0:T(8,128)(2,1)S(1)}, u32[]{:S(2)}, u32[]{:S(2)}) %collective-permute-start.7) | collective-permute-done | bytes 612384 | tf_op jit(solution)/shard_map/ring/ppermute | solution.py:631
  68.9 5.6 %collective-permute-start.9 = (bf16[23,104,128]{2,1,0:T(8,128)(2,1)S(1)}, bf16[23,104,128]{2,1,0:T(8,128)(2,1)S(1)}, u32[]{:S(2)}, u32[]{:S(2)}) collective-permute-start(bf16[23,104,128]{2,1,0:T(8,128)(2,1)S(1)} %ring.37.after_ref), channel_id=1, source_target_pairs={{0,15},{1,0},{2,1},{3,2},{4,3},{5,4},{6,5},{7,6},{8,7},{9,8},{10,9... | collective-permute-start | bytes 1837064 | tf_op jit(solution)/shard_map/ring/ppermute | solution.py:631
  76.4 1.9 collective-permute-start.8
  78.9 8.5 %collective-permute-done.9.newest_ref.refs_3_.refs_11_ = bf16[23,104,128]{2,1,0:T(8,128)(2,1)S(1)} collective-permute-done((bf16[23,104,128]{2,1,0:T(8,128)(2,1)S(1)}, bf16[23,104,128]{2,1,0:T(8,128)(2,1)S(1)}, u32[]{:S(2)}, u32[]{:S(2)}) %collective-permute-start.9) | collective-permute-done | bytes 612384 | tf_op jit(solution)/shard_map/ring/ppermute | solution.py:631
  87.7 5.6 %collective-permute-start.11 = (bf16[22,104,128]{2,1,0:T(8,128)(2,1)S(1)}, bf16[22,104,128]{2,1,0:T(8,128)(2,1)S(1)}, u32[]{:S(2)}, u32[]{:S(2)}) collective-permute-start(bf16[22,104,128]{2,1,0:T(8,128)(2,1)S(1)} %ring.41.after_ref), channel_id=1, source_target_pairs={{0,15},{1,0},{2,1},{3,2},{4,3},{5,4},{6,5},{7,6},{8,7},{9,8},{10,9... | collective-permute-start | bytes 1757192 | tf_op jit(solution)/shard_map/ring/ppermute | solution.py:631
  95.3 1.9 collective-permute-start.10
  98.0 8.6 %collective-permute-done.11.newest_ref.refs_4_.refs_12_ = bf16[22,104,128]{2,1,0:T(8,128)(2,1)S(1)} collective-permute-done((bf16[22,104,128]{2,1,0:T(8,128)(2,1)S(1)}, bf16[22,104,128]{2,1,0:T(8,128)(2,1)S(1)}, u32[]{:S(2)}, u32[]{:S(2)}) %collective-permute-start.11) | collective-permute-done | bytes 585760 | tf_op jit(solution)/shard_map/ring/ppermute | solution.py:631
  106.9 5.6 %collective-permute-start.13 = (bf16[22,104,128]{2,1,0:T(8,128)(2,1)S(1)}, bf16[22,104,128]{2,1,0:T(8,128)(2,1)S(1)}, u32[]{:S(2)}, u32[]{:S(2)}) collective-permute-start(bf16[22,104,128]{2,1,0:T(8,128)(2,1)S(1)} %ring.45.after_ref), channel_id=1, source_target_pairs={{0,15},{1,0},{2,1},{3,2},{4,3},{5,4},{6,5},{7,6},{8,7},{9,8},{10,9... | collective-permute-start | bytes 1757192 | tf_op jit(solution)/shard_map/ring/ppermute | solution.py:631
  114.5 1.9 collective-permute-start.12
  117.1 7.6 %collective-permute-done.13.newest_ref.refs_13_.refs_5_ = bf16[22,104,128]{2,1,0:T(8,128)(2,1)S(1)} collective-permute-done((bf16[22,104,128]{2,1,0:T(8,128)(2,1)S(1)}, bf16[22,104,128]{2,1,0:T(8,128)(2,1)S(1)}, u32[]{:S(2)}, u32[]{:S(2)}) %collective-permute-start.13) | collective-permute-done | bytes 585760 | tf_op jit(solution)/shard_map/ring/ppermute | solution.py:631
  124.9 5.6 %collective-permute-start.15 = (bf16[22,104,128]{2,1,0:T(8,128)(2,1)S(1)}, bf16[22,104,128]{2,1,0:T(8,128)(2,1)S(1)}, u32[]{:S(2)}, u32[]{:S(2)}) collective-permute-start(bf16[22,104,128]{2,1,0:T(8,128)(2,1)S(1)} %ring.49.after_ref), channel_id=1, source_target_pairs={{0,15},{1,0},{2,1},{3,2},{4,3},{5,4},{6,5},{7,6},{8,7},{9,8},{10,9... | collective-permute-start | bytes 1757192 | tf_op jit(solution)/shard_map/ring/ppermute | solution.py:631
  132.5 1.9 collective-permute-start.14
  135.2 6.2 %collective-permute-done.15.refs_14_.newest_ref = bf16[22,104,128]{2,1,0:T(8,128)(2,1)S(1)} collective-permute-done((bf16[22,104,128]{2,1,0:T(8,128)(2,1)S(1)}, bf16[22,104,128]{2,1,0:T(8,128)(2,1)S(1)}, u32[]{:S(2)}, u32[]{:S(2)}) %collective-permute-start.15) | collective-permute-done | bytes 585760 | tf_op jit(solution)/shard_map/ring/ppermute | solution.py:631
  142.5 5.6 %collective-permute-start.17 = (bf16[22,104,128]{2,1,0:T(8,128)(2,1)}, bf16[22,104,128]{2,1,0:T(8,128)(2,1)}, u32[]{:S(2)}, u32[]{:S(2)}) collective-permute-start(bf16[22,104,128]{2,1,0:T(8,128)(2,1)} %ring.53.after_ref), channel_id=1, source_target_pairs={{0,15},{1,0},{2,1},{3,2},{4,3},{5,4},{6,5},{7,6},{8,7},{9,8},{10,9... | collective-permute-start | bytes 1757192 | tf_op jit(solution)/shard_map/ring/ppermute | solution.py:631
  148.1 1.8 ring.54.part_ref
  151.1 1.9 collective-permute-start.16
  153.8 2.4 %stage.1.held_ref = bf16[96,104,128]{2,1,0:T(8,128)(2,1)S(1)} custom-call(s32[8,128]{1,0:T(8,128)S(1)} %get-tuple-element.90.item_ref, bf16[38,104,128]{2,1,0:T(8,128)(2,1)S(1)} %get-tuple-element.91.home_ref.refs_0_, bf16[21,104,128]{2,1,0:T(8,128)(2,1)S(1)} %collective-permute-done.2.newest_ref.refs_0_.refs_1_, ...), custom_call_target="tpu_custom_call" | custom-call | tf_op jit(solution)/shard_map/stage/pallas_call | solution.py:647
  157.6 6.4 %collective-permute-done.16.ahead_ref = bf16[21,104,128]{2,1,0:T(8,128)(2,1)} collective-permute-done((bf16[21,104,128]{2,1,0:T(8,128)(2,1)}, bf16[21,104,128]{2,1,0:T(8,128)(2,1)}, u32[]{:S(2)}, u32[]{:S(2)}) %collective-permute-start.16) | collective-permute-done | bytes 559136 | tf_op jit(solution)/shard_map/ring/ppermute | solution.py:634
  164.0 1.7 copy-done.4
  165.8 5.6 %map.1 = f32[8,128]{1,0:T(8,128)S(1)} custom-call(s32[8,128]{1,0:T(8,128)S(1)} %get-tuple-element.90.item_ref, bf16[96,104,128]{2,1,0:T(8,128)(2,1)S(1)} %copy-done.4, bf16[21,104,128]{2,1,0:T(8,128)(2,1)} %collective-permute-done.16.ahead_ref, bf16[22,104,128]{2,1,0:T(8,128)(2,1)} %collective-permute-done.17.behind_ref, ...), custom_call_target="tpu_custom_call" | custom-call | tf_op jit(solution)/shard_map/map/pallas_call | solution.py:656
  172.0 5.2 %all-to-all-start.1 = ((f32[16,4,128]{2,1,0:T(4,128)}), f32[16,4,128]{2,1,0:T(4,128)S(1)}, u32[]{:S(2)}, u32[]{:S(2)}) async-start(f32[16,4,128]{2,1,0:T(4,128)} %broadcast_in_dim.55), calls=%async_computation.1 | async-start | bytes 65536 | tf_op jit(solution)/shard_map/finish/all_to_all | solution.py:670
  179.7 10.1 %all-to-all-done.1 = f32[16,4,128]{2,1,0:T(4,128)S(1)} async-done(((f32[16,4,128]{2,1,0:T(4,128)}), f32[16,4,128]{2,1,0:T(4,128)S(1)}, u32[]{:S(2)}, u32[]{:S(2)}) %all-to-all-start.1) | async-done | bytes 32800 | tf_op jit(solution)/shard_map/finish/all_to_all | solution.py:670
  (94 shorter events, 31.0 us)
Async XLA Ops:
  6.5 8.3 %copy-start.8 = (bf16[2,64,4736]{2,1,0:T(8,128)(2,1)S(1)}, bf16[2,64,4736]{2,1,0:T(8,128)(2,1)}, u32[]{:S(2)}) copy-start(bf16[2,64,4736]{2,1,0:T(8,128)(2,1)} %own_ref.1) | copy-start | bytes 3637252
  6.5 151.1 %all-gather.2.cloned.1.call-start = ((), (), s32[]{:S(2)}) async-start(), calls=%async_computation.2 | async-start | bytes 2621440 | tf_op jit(solution)/shard_map/weights/all_gather | solution.py:556
  7.7 6.2 %collective-permute-start = (bf16[2,16,4736]{2,1,0:T(8,128)(2,1)S(1)}, bf16[2,16,4736]{2,1,0:T(8,128)(2,1)S(1)}, u32[]{:S(2)}, u32[]{:S(2)}) collective-permute-start(bf16[2,16,4736]{2,1,0:T(8,128)(2,1)S(1)} %get-tuple-element.156), channel_id=1, source_target_pairs={{0,16},{16,32},{32,48},{48,64},{64,80},{80,96},{96,112},{112,0},{1... | collective-permute-start | bytes 909320 | tf_op jit(solution)/shard_map/halo/ppermute | solution.py:23
  7.8 7.0 %collective-permute-start.1 = (bf16[2,16,4736]{2,1,0:T(8,128)(2,1)S(1)}, bf16[2,16,4736]{2,1,0:T(8,128)(2,1)S(1)}, u32[]{:S(2)}, u32[]{:S(2)}) collective-permute-start(bf16[2,16,4736]{2,1,0:T(8,128)(2,1)S(1)} %get-tuple-element.155), channel_id=1, source_target_pairs={{16,0},{32,16},{48,32},{64,48},{80,64},{96,80},{112,96},{0,112},{1... | collective-permute-start | bytes 909320 | tf_op jit(solution)/shard_map/halo/ppermute | solution.py:24
  14.0 13.1 %copy-start.9 = (bf16[2,16,4736]{2,1,0:T(8,128)(2,1)}, bf16[2,16,4736]{2,1,0:T(8,128)(2,1)S(1)}, u32[]{:S(2)}) copy-start(bf16[2,16,4736]{2,1,0:T(8,128)(2,1)S(1)} %collective-permute-done.low_ref) | copy-start | bytes 909316
  14.8 18.8 %copy-start.11 = (bf16[2,16,4736]{2,1,0:T(8,128)(2,1)}, bf16[2,16,4736]{2,1,0:T(8,128)(2,1)S(1)}, u32[]{:S(2)}) copy-start(bf16[2,16,4736]{2,1,0:T(8,128)(2,1)S(1)} %collective-permute-done.1.high_ref) | copy-start | bytes 909316
  16.5 16.8 %collective-permute-start.3 = (bf16[12,104,128]{2,1,0:T(8,128)(2,1)S(1)}, bf16[12,104,128]{2,1,0:T(8,128)(2,1)S(1)}, u32[]{:S(2)}, u32[]{:S(2)}) collective-permute-start(bf16[12,104,128]{2,1,0:T(8,128)(2,1)S(1)} %get-tuple-element.94), channel_id=1, source_target_pairs={{0,15},{1,0},{2,1},{3,2},{4,3},{5,4},{6,5},{7,6},{8,7},{9,8},{10,9... | collective-permute-start | bytes 958472 | tf_op jit(solution)/shard_map/ring/ppermute | solution.py:626
  27.1 12.7 %collective-permute-start.2 = (bf16[21,104,128]{2,1,0:T(8,128)(2,1)S(1)}, bf16[21,104,128]{2,1,0:T(8,128)(2,1)S(1)}, u32[]{:S(2)}, u32[]{:S(2)}) collective-permute-start(bf16[21,104,128]{2,1,0:T(8,128)(2,1)S(1)} %get-tuple-element.92.after_ref), channel_id=1, source_target_pairs={{0,1},{1,2},{2,3},{3,4},{4,5},{5,6},{6,7},{7,8},{8,9},{9,10},{10,1... | collective-permute-start | bytes 1677320 | tf_op jit(solution)/shard_map/ring/ppermute | solution.py:627
  33.3 8.6 %copy-start = (bf16[12,104,128]{2,1,0:T(8,128)(2,1)}, bf16[12,104,128]{2,1,0:T(8,128)(2,1)S(1)}, u32[]{:S(2)}) copy-start(bf16[12,104,128]{2,1,0:T(8,128)(2,1)S(1)} %collective-permute-done.3.newest_ref.refs_0_.refs_8_) | copy-start | bytes 958468
  33.6 15.7 %collective-permute-start.5 = (bf16[23,104,128]{2,1,0:T(8,128)(2,1)S(1)}, bf16[23,104,128]{2,1,0:T(8,128)(2,1)S(1)}, u32[]{:S(2)}, u32[]{:S(2)}) collective-permute-start(bf16[23,104,128]{2,1,0:T(8,128)(2,1)S(1)} %ring.29.after_ref), channel_id=1, source_target_pairs={{0,15},{1,0},{2,1},{3,2},{4,3},{5,4},{6,5},{7,6},{8,7},{9,8},{10,9... | collective-permute-start | bytes 1837064 | tf_op jit(solution)/shard_map/ring/ppermute | solution.py:631
  40.0 16.4 %collective-permute-start.4 = (bf16[21,104,128]{2,1,0:T(8,128)(2,1)S(1)}, bf16[21,104,128]{2,1,0:T(8,128)(2,1)S(1)}, u32[]{:S(2)}, u32[]{:S(2)}) collective-permute-start(bf16[21,104,128]{2,1,0:T(8,128)(2,1)S(1)} %ring.31.after_ref), channel_id=1, source_target_pairs={{0,1},{1,2},{2,3},{3,4},{4,5},{5,6},{6,7},{7,8},{8,9},{9,10},{10,1... | collective-permute-start | bytes 1677320 | tf_op jit(solution)/shard_map/ring/ppermute | solution.py:634
  50.5 18.1 %collective-permute-start.7 = (bf16[23,104,128]{2,1,0:T(8,128)(2,1)}, bf16[23,104,128]{2,1,0:T(8,128)(2,1)S(1)}, u32[]{:S(2)}, u32[]{:S(2)}) collective-permute-start(bf16[23,104,128]{2,1,0:T(8,128)(2,1)} %ring.33.after_ref), channel_id=1, source_target_pairs={{0,15},{1,0},{2,1},{3,2},{4,3},{5,4},{6,5},{7,6},{8,7},{9,8},{10,9... | collective-permute-start | bytes 1837064 | tf_op jit(solution)/shard_map/ring/ppermute | solution.py:631
  57.6 17.4 %collective-permute-start.6 = (bf16[21,104,128]{2,1,0:T(8,128)(2,1)}, bf16[21,104,128]{2,1,0:T(8,128)(2,1)}, u32[]{:S(2)}, u32[]{:S(2)}) collective-permute-start(bf16[21,104,128]{2,1,0:T(8,128)(2,1)} %ring.35.after_ref), channel_id=1, source_target_pairs={{0,1},{1,2},{2,3},{3,4},{4,5},{5,6},{6,7},{7,8},{8,9},{9,10},{10,1... | collective-permute-start | bytes 1677320 | tf_op jit(solution)/shard_map/ring/ppermute | solution.py:634
  59.5 1.0 copy-start.1
  68.9 9.4 %copy-start.2 = (bf16[12,104,128]{2,1,0:T(8,128)(2,1)S(1)}, bf16[12,104,128]{2,1,0:T(8,128)(2,1)}, u32[]{:S(2)}) copy-start(bf16[12,104,128]{2,1,0:T(8,128)(2,1)} %copy-done) | copy-start | bytes 958468
  68.9 18.6 %collective-permute-start.9 = (bf16[23,104,128]{2,1,0:T(8,128)(2,1)S(1)}, bf16[23,104,128]{2,1,0:T(8,128)(2,1)S(1)}, u32[]{:S(2)}, u32[]{:S(2)}) collective-permute-start(bf16[23,104,128]{2,1,0:T(8,128)(2,1)S(1)} %ring.37.after_ref), channel_id=1, source_target_pairs={{0,15},{1,0},{2,1},{3,2},{4,3},{5,4},{6,5},{7,6},{8,7},{9,8},{10,9... | collective-permute-start | bytes 1837064 | tf_op jit(solution)/shard_map/ring/ppermute | solution.py:631
  76.4 18.6 %collective-permute-start.8 = (bf16[21,104,128]{2,1,0:T(8,128)(2,1)S(1)}, bf16[21,104,128]{2,1,0:T(8,128)(2,1)S(1)}, u32[]{:S(2)}, u32[]{:S(2)}) collective-permute-start(bf16[21,104,128]{2,1,0:T(8,128)(2,1)S(1)} %ring.39.after_ref), channel_id=1, source_target_pairs={{0,1},{1,2},{2,3},{3,4},{4,5},{5,6},{6,7},{7,8},{8,9},{9,10},{10,1... | collective-permute-start | bytes 1677320 | tf_op jit(solution)/shard_map/ring/ppermute | solution.py:634
  87.7 18.9 %collective-permute-start.11 = (bf16[22,104,128]{2,1,0:T(8,128)(2,1)S(1)}, bf16[22,104,128]{2,1,0:T(8,128)(2,1)S(1)}, u32[]{:S(2)}, u32[]{:S(2)}) collective-permute-start(bf16[22,104,128]{2,1,0:T(8,128)(2,1)S(1)} %ring.41.after_ref), channel_id=1, source_target_pairs={{0,15},{1,0},{2,1},{3,2},{4,3},{5,4},{6,5},{7,6},{8,7},{9,8},{10,9... | collective-permute-start | bytes 1757192 | tf_op jit(solution)/shard_map/ring/ppermute | solution.py:631
  95.3 18.9 %collective-permute-start.10 = (bf16[21,104,128]{2,1,0:T(8,128)(2,1)S(1)}, bf16[21,104,128]{2,1,0:T(8,128)(2,1)S(1)}, u32[]{:S(2)}, u32[]{:S(2)}) collective-permute-start(bf16[21,104,128]{2,1,0:T(8,128)(2,1)S(1)} %ring.43.after_ref), channel_id=1, source_target_pairs={{0,1},{1,2},{2,3},{3,4},{4,5},{5,6},{6,7},{7,8},{8,9},{9,10},{10,1... | collective-permute-start | bytes 1677320 | tf_op jit(solution)/shard_map/ring/ppermute | solution.py:634
  106.9 17.7 %collective-permute-start.13 = (bf16[22,104,128]{2,1,0:T(8,128)(2,1)S(1)}, bf16[22,104,128]{2,1,0:T(8,128)(2,1)S(1)}, u32[]{:S(2)}, u32[]{:S(2)}) collective-permute-start(bf16[22,104,128]{2,1,0:T(8,128)(2,1)S(1)} %ring.45.after_ref), channel_id=1, source_target_pairs={{0,15},{1,0},{2,1},{3,2},{4,3},{5,4},{6,5},{7,6},{8,7},{9,8},{10,9... | collective-permute-start | bytes 1757192 | tf_op jit(solution)/shard_map/ring/ppermute | solution.py:631
  114.5 17.7 %collective-permute-start.12 = (bf16[21,104,128]{2,1,0:T(8,128)(2,1)S(1)}, bf16[21,104,128]{2,1,0:T(8,128)(2,1)S(1)}, u32[]{:S(2)}, u32[]{:S(2)}) collective-permute-start(bf16[21,104,128]{2,1,0:T(8,128)(2,1)S(1)} %ring.47.after_ref), channel_id=1, source_target_pairs={{0,1},{1,2},{2,3},{3,4},{4,5},{5,6},{6,7},{7,8},{8,9},{9,10},{10,1... | collective-permute-start | bytes 1677320 | tf_op jit(solution)/shard_map/ring/ppermute | solution.py:634
  124.9 16.5 %collective-permute-start.15 = (bf16[22,104,128]{2,1,0:T(8,128)(2,1)S(1)}, bf16[22,104,128]{2,1,0:T(8,128)(2,1)S(1)}, u32[]{:S(2)}, u32[]{:S(2)}) collective-permute-start(bf16[22,104,128]{2,1,0:T(8,128)(2,1)S(1)} %ring.49.after_ref), channel_id=1, source_target_pairs={{0,15},{1,0},{2,1},{3,2},{4,3},{5,4},{6,5},{7,6},{8,7},{9,8},{10,9... | collective-permute-start | bytes 1757192 | tf_op jit(solution)/shard_map/ring/ppermute | solution.py:631
  132.5 17.5 %collective-permute-start.14 = (bf16[21,104,128]{2,1,0:T(8,128)(2,1)S(1)}, bf16[21,104,128]{2,1,0:T(8,128)(2,1)S(1)}, u32[]{:S(2)}, u32[]{:S(2)}) collective-permute-start(bf16[21,104,128]{2,1,0:T(8,128)(2,1)S(1)} %ring.51.after_ref), channel_id=1, source_target_pairs={{0,1},{1,2},{2,3},{3,4},{4,5},{5,6},{6,7},{7,8},{8,9},{9,10},{10,1... | collective-permute-start | bytes 1677320 | tf_op jit(solution)/shard_map/ring/ppermute | solution.py:634
  142.5 21.5 %collective-permute-start.17 = (bf16[22,104,128]{2,1,0:T(8,128)(2,1)}, bf16[22,104,128]{2,1,0:T(8,128)(2,1)}, u32[]{:S(2)}, u32[]{:S(2)}) collective-permute-start(bf16[22,104,128]{2,1,0:T(8,128)(2,1)} %ring.53.after_ref), channel_id=1, source_target_pairs={{0,15},{1,0},{2,1},{3,2},{4,3},{5,4},{6,5},{7,6},{8,7},{9,8},{10,9... | collective-permute-start | bytes 1757192 | tf_op jit(solution)/shard_map/ring/ppermute | solution.py:631
  149.9 3.0 %copy-start.5 = (bf16[2,64,4096]{2,1,0:T(8,128)(2,1)S(1)}, bf16[2,64,4096]{2,1,0:T(8,128)(2,1)}, u32[]{:S(2)}) copy-start(bf16[2,64,4096]{2,1,0:T(8,128)(2,1)} %student_ref.3) | copy-start | bytes 3145732
  151.1 13.0 %collective-permute-start.16 = (bf16[21,104,128]{2,1,0:T(8,128)(2,1)}, bf16[21,104,128]{2,1,0:T(8,128)(2,1)}, u32[]{:S(2)}, u32[]{:S(2)}) collective-permute-start(bf16[21,104,128]{2,1,0:T(8,128)(2,1)} %ring.55), channel_id=1, source_target_pairs={{0,1},{1,2},{2,3},{3,4},{4,5},{5,6},{6,7},{7,8},{8,9},{9,10},{10,1... | collective-permute-start | bytes 1677320 | tf_op jit(solution)/shard_map/ring/ppermute | solution.py:634
  156.1 1.5 copy-start.3
  164.0 1.7 copy-start.4
  165.8 13.9 %copy-start.6 = (bf16[2,64,4096]{2,1,0:T(8,128)(2,1)S(1)}, bf16[2,64,4096]{2,1,0:T(8,128)(2,1)}, u32[]{:S(2)}) copy-start(bf16[2,64,4096]{2,1,0:T(8,128)(2,1)} %student_ref.3) | copy-start | bytes 3145732
  165.8 13.9 %copy-start.10 = (bf16[2,16,4736]{2,1,0:T(8,128)(2,1)S(1)}, bf16[2,16,4736]{2,1,0:T(8,128)(2,1)}, u32[]{:S(2)}) copy-start(bf16[2,16,4736]{2,1,0:T(8,128)(2,1)} %copy-done.9) | copy-start | bytes 909316
  165.8 13.9 %copy-start.13 = (s32[512,2]{0,1:T(2,128)S(1)}, s32[512,2]{0,1:T(2,128)}, u32[]{:S(2)}) copy-start(s32[512,2]{0,1:T(2,128)} %param.12) | copy-start | bytes 12292
  172.0 17.8 %all-to-all-start.1 = ((f32[16,4,128]{2,1,0:T(4,128)}), f32[16,4,128]{2,1,0:T(4,128)S(1)}, u32[]{:S(2)}, u32[]{:S(2)}) async-start(f32[16,4,128]{2,1,0:T(4,128)} %broadcast_in_dim.55), calls=%async_computation.1 | async-start | bytes 65536 | tf_op jit(solution)/shard_map/finish/all_to_all | solution.py:670
  (1 other events, 0.6 us)
Sparse Core Ops, SparseCore 0:
  59.7 35.3 all-gather.1

commit v10 on v9

--- a/solution.py
+++ b/solution.py
@@ -11,7 +11,7 @@
 K = 2
 W = 16
 ROWS = 104
-SIZES = ((21,) * 8, (12, 23, 23, 23, 22, 22, 22, 22))
+SIZES = ((30, 21, 20, 20, 20, 20, 20, 20), (12, 23, 23, 23, 22, 22, 22, 22))
 STARTS = tuple(tuple(sum(sizes[:f]) for f in range(len(sizes))) for sizes in SIZES)
 TINY = 1.2e-38
 

time: 199 us -> 204 us (1.025)
  starting transfers between devices: 71.6 us -> 81.1 us
  waiting for transfers between devices: 65.9 us -> 58.1 us
  Pallas kernels: 34.4 us -> 39 us
    ppermute x7, waiting for transfers between devices: 45.4 us -> 36.1 us  [shards(): came_behind.append(lax.ppermute(behind, ('seq', 'vocab'), backward))]
    all_to_all x1, starting transfers between devices: 5.17 us -> 12.8 us  [shards(): lax.all_to_all(sent, 'vocab', split_axis=0, concat_axis=0, tiled=True)]
    ppermute x7, starting transfers between devices: 13.4 us -> 18.6 us  [shards(): came_ahead.append(lax.ppermute(ahead, ('seq', 'vocab'), forward))]
    pallas_call x14, Pallas kernels: 12 us -> 15.8 us  [ready(): pl.pallas_call(functools.partial(ready_kernel, chain, step), out_shape=pl...]
    ppermute x1, waiting for transfers between devices: 0.01 us -> 3.61 us  [shards(): came_behind = [lax.ppermute(behind, ('seq', 'vocab'), backward)]]
    ppermute x7, starting transfers between devices: 38.7 us -> 35.5 us  [shards(): came_behind.append(lax.ppermute(behind, ('seq', 'vocab'), backward))]
    unnamed x27 -> x21, local copies, waits for them, and re-layouts: 5.58 us -> 4.61 us
  transfers between devices with their start and end apart: 20 -> 20, of which waited for: 11 -> 12; matrix products, arithmetic and copies ran while one was open for 2% -> 2% of each run, Pallas kernels for 14% -> 16%
where the time goes in v10:
time: 204 us; the launch traced here: 203 us
  starting transfers between devices  81.1 us (40%)
  waiting for transfers between devices  58.1 us (28%)
  Pallas kernels  39 us (19%)
  between operations  15.2 us (7%)
  local copies, waits for them, and re-layouts  7.38 us (4%)
    ppermute x7, waiting for transfers between devices, shards(): came_behind.append(lax.ppermute(behind, ('seq', 'vocab'), backward))  36.1 us
    ppermute x7, starting transfers between devices, shards(): came_behind.append(lax.ppermute(behind, ('seq', 'vocab'), backward))  35.5 us
    ppermute x7, starting transfers between devices, shards(): came_ahead.append(lax.ppermute(ahead, ('seq', 'vocab'), forward))  18.6 us
    pallas_call x14, Pallas kernels, ready(): pl.pallas_call(functools.partial(ready_kernel, chain, step), out_shape=pl...  15.8 us
    all_to_all x1, starting transfers between devices, shards(): lax.all_to_all(sent, 'vocab', split_axis=0, concat_axis=0, tiled=True)  12.8 us
    all_to_all x1, waiting for transfers between devices, shards(): lax.all_to_all(sent, 'vocab', split_axis=0, concat_axis=0, tiled=True)  10.1 us
    ppermute x1, starting transfers between devices, shards(): came_behind = [lax.ppermute(behind, ('seq', 'vocab'), backward)]  9.5 us
    pallas_call x14, Pallas kernels, passed(): pl.pallas_call(functools.partial(pass_kernel, chain, step, home), out_sha...  9.13 us
  transfers between devices with their start and end apart: 20, of which 12 were waited for; matrix products, arithmetic and copies ran while one was open for 2% of the time, Pallas kernels for 16%

profile of v10, /device:TPU:6, one launch (start us, length us, event | category | flops | bytes accessed | tf_op | source)
XLA Modules:
  0.0 202.9 jit_solution(10841059320901652803)
XLA Ops:
  11.7 2.3 %collective-permute-done.low_ref = bf16[2,16,4736]{2,1,0:T(8,128)(2,1)S(1)} collective-permute-done((bf16[2,16,4736]{2,1,0:T(8,128)(2,1)S(1)}, bf16[2,16,4736]{2,1,0:T(8,128)(2,1)S(1)}, u32[]{:S(2)}, u32[]{:S(2)}) %collective-permute-start) | collective-permute-done | bytes 303136 | tf_op jit(solution)/shard_map/halo/ppermute | solution.py:23
  16.5 3.0 %collective-permute-start.2 = (bf16[30,104,128]{2,1,0:T(8,128)(2,1)S(1)}, bf16[30,104,128]{2,1,0:T(8,128)(2,1)S(1)}, u32[]{:S(2)}, u32[]{:S(2)}) collective-permute-start(bf16[30,104,128]{2,1,0:T(8,128)(2,1)S(1)} %get-tuple-element.92.after_ref), channel_id=1, source_target_pairs={{0,1},{1,2},{2,3},{3,4},{4,5},{5,6},{6,7},{7,8},{8,9},{9,10},{10,1... | collective-permute-start | bytes 2396168 | tf_op jit(solution)/shard_map/ring/ppermute | solution.py:627
  19.5 9.5 %collective-permute-start.3 = (bf16[12,104,128]{2,1,0:T(8,128)(2,1)S(1)}, bf16[12,104,128]{2,1,0:T(8,128)(2,1)S(1)}, u32[]{:S(2)}, u32[]{:S(2)}) collective-permute-start(bf16[12,104,128]{2,1,0:T(8,128)(2,1)S(1)} %get-tuple-element.94), channel_id=1, source_target_pairs={{0,15},{1,0},{2,1},{3,2},{4,3},{5,4},{6,5},{7,6},{8,7},{9,8},{10,9... | collective-permute-start | bytes 958472 | tf_op jit(solution)/shard_map/ring/ppermute | solution.py:626
  29.0 4.0 %plan.1 = (s32[8,256]{1,0:T(8,128)S(1)}, s32[8,128]{1,0:T(8,128)S(1)}, s32[8,128]{1,0:T(8,128)S(1)}) custom-call(s32[2]{0:T(128)S(1)} %pad_add_fusion.place_ref, s32[16,64]{1,0:T(8,128)S(1)} %reshape.252.listed_ref, s32[8,128]{1,0:T(8,128)S(1)} %get-tuple-element.88.after_ref), custom_call_target="tpu_custom_call" | custom-call | tf_op jit(solution)/shard_map/plan/pallas_call | solution.py:597
  33.3 3.6 %collective-permute-done.3.newest_ref.refs_0_.refs_8_ = bf16[12,104,128]{2,1,0:T(8,128)(2,1)S(1)} collective-permute-done((bf16[12,104,128]{2,1,0:T(8,128)(2,1)S(1)}, bf16[12,104,128]{2,1,0:T(8,128)(2,1)S(1)}, u32[]{:S(2)}, u32[]{:S(2)}) %collective-permute-start.3) | collective-permute-done | bytes 319520 | tf_op jit(solution)/shard_map/ring/ppermute | solution.py:626
  37.2 5.6 %collective-permute-start.5 = (bf16[23,104,128]{2,1,0:T(8,128)(2,1)S(1)}, bf16[23,104,128]{2,1,0:T(8,128)(2,1)S(1)}, u32[]{:S(2)}, u32[]{:S(2)}) collective-permute-start(bf16[23,104,128]{2,1,0:T(8,128)(2,1)S(1)} %ring.29.after_ref), channel_id=1, source_target_pairs={{0,15},{1,0},{2,1},{3,2},{4,3},{5,4},{6,5},{7,6},{8,7},{9,8},{10,9... | collective-permute-start | bytes 1837064 | tf_op jit(solution)/shard_map/ring/ppermute | solution.py:631
  43.4 1.9 collective-permute-start.4
  45.7 7.0 %collective-permute-done.5.newest_ref.refs_1_.refs_9_ = bf16[23,104,128]{2,1,0:T(8,128)(2,1)S(1)} collective-permute-done((bf16[23,104,128]{2,1,0:T(8,128)(2,1)S(1)}, bf16[23,104,128]{2,1,0:T(8,128)(2,1)S(1)}, u32[]{:S(2)}, u32[]{:S(2)}) %collective-permute-start.5) | collective-permute-done | bytes 612384 | tf_op jit(solution)/shard_map/ring/ppermute | solution.py:631
  53.8 5.6 %collective-permute-start.7 = (bf16[23,104,128]{2,1,0:T(8,128)(2,1)}, bf16[23,104,128]{2,1,0:T(8,128)(2,1)}, u32[]{:S(2)}, u32[]{:S(2)}) collective-permute-start(bf16[23,104,128]{2,1,0:T(8,128)(2,1)} %ring.33.after_ref), channel_id=1, source_target_pairs={{0,15},{1,0},{2,1},{3,2},{4,3},{5,4},{6,5},{7,6},{8,7},{9,8},{10,9... | collective-permute-start | bytes 1837064 | tf_op jit(solution)/shard_map/ring/ppermute | solution.py:631
  60.9 1.9 collective-permute-start.6
  63.3 5.7 %collective-permute-done.7.newest_ref.refs_2_.refs_10_ = bf16[23,104,128]{2,1,0:T(8,128)(2,1)} collective-permute-done((bf16[23,104,128]{2,1,0:T(8,128)(2,1)}, bf16[23,104,128]{2,1,0:T(8,128)(2,1)}, u32[]{:S(2)}, u32[]{:S(2)}) %collective-permute-start.7) | collective-permute-done | bytes 612384 | tf_op jit(solution)/shard_map/ring/ppermute | solution.py:631
  70.3 5.6 %collective-permute-start.9 = (bf16[23,104,128]{2,1,0:T(8,128)(2,1)S(1)}, bf16[23,104,128]{2,1,0:T(8,128)(2,1)S(1)}, u32[]{:S(2)}, u32[]{:S(2)}) collective-permute-start(bf16[23,104,128]{2,1,0:T(8,128)(2,1)S(1)} %ring.37.after_ref), channel_id=1, source_target_pairs={{0,15},{1,0},{2,1},{3,2},{4,3},{5,4},{6,5},{7,6},{8,7},{9,8},{10,9... | collective-permute-start | bytes 1837064 | tf_op jit(solution)/shard_map/ring/ppermute | solution.py:631
  77.6 1.9 collective-permute-start.8
  81.3 4.3 %collective-permute-done.9.newest_ref.refs_3_.refs_11_ = bf16[23,104,128]{2,1,0:T(8,128)(2,1)S(1)} collective-permute-done((bf16[23,104,128]{2,1,0:T(8,128)(2,1)S(1)}, bf16[23,104,128]{2,1,0:T(8,128)(2,1)S(1)}, u32[]{:S(2)}, u32[]{:S(2)}) %collective-permute-start.9) | collective-permute-done | bytes 612384 | tf_op jit(solution)/shard_map/ring/ppermute | solution.py:631
  85.9 5.6 %collective-permute-start.11 = (bf16[22,104,128]{2,1,0:T(8,128)(2,1)S(1)}, bf16[22,104,128]{2,1,0:T(8,128)(2,1)S(1)}, u32[]{:S(2)}, u32[]{:S(2)}) collective-permute-start(bf16[22,104,128]{2,1,0:T(8,128)(2,1)S(1)} %ring.41.after_ref), channel_id=1, source_target_pairs={{0,15},{1,0},{2,1},{3,2},{4,3},{5,4},{6,5},{7,6},{8,7},{9,8},{10,9... | collective-permute-start | bytes 1757192 | tf_op jit(solution)/shard_map/ring/ppermute | solution.py:631
  93.3 4.7 %collective-permute-start.10 = (bf16[20,104,128]{2,1,0:T(8,128)(2,1)S(1)}, bf16[20,104,128]{2,1,0:T(8,128)(2,1)S(1)}, u32[]{:S(2)}, u32[]{:S(2)}) collective-permute-start(bf16[20,104,128]{2,1,0:T(8,128)(2,1)S(1)} %ring.43.after_ref), channel_id=1, source_target_pairs={{0,1},{1,2},{2,3},{3,4},{4,5},{5,6},{6,7},{7,8},{8,9},{9,10},{10,1... | collective-permute-start | bytes 1597448 | tf_op jit(solution)/shard_map/ring/ppermute | solution.py:634
  99.8 7.2 %collective-permute-done.11.newest_ref.refs_4_.refs_12_ = bf16[22,104,128]{2,1,0:T(8,128)(2,1)S(1)} collective-permute-done((bf16[22,104,128]{2,1,0:T(8,128)(2,1)S(1)}, bf16[22,104,128]{2,1,0:T(8,128)(2,1)S(1)}, u32[]{:S(2)}, u32[]{:S(2)}) %collective-permute-start.11) | collective-permute-done | bytes 585760 | tf_op jit(solution)/shard_map/ring/ppermute | solution.py:631
  107.2 2.1 %collective-permute-start.13 = (bf16[22,104,128]{2,1,0:T(8,128)(2,1)S(1)}, bf16[22,104,128]{2,1,0:T(8,128)(2,1)S(1)}, u32[]{:S(2)}, u32[]{:S(2)}) collective-permute-start(bf16[22,104,128]{2,1,0:T(8,128)(2,1)S(1)} %ring.45.after_ref), channel_id=1, source_target_pairs={{0,15},{1,0},{2,1},{3,2},{4,3},{5,4},{6,5},{7,6},{8,7},{9,8},{10,9... | collective-permute-start | bytes 1757192 | tf_op jit(solution)/shard_map/ring/ppermute | solution.py:631
  111.2 3.9 %collective-permute-start.12 = (bf16[20,104,128]{2,1,0:T(8,128)(2,1)S(1)}, bf16[20,104,128]{2,1,0:T(8,128)(2,1)S(1)}, u32[]{:S(2)}, u32[]{:S(2)}) collective-permute-start(bf16[20,104,128]{2,1,0:T(8,128)(2,1)S(1)} %ring.47.after_ref), channel_id=1, source_target_pairs={{0,1},{1,2},{2,3},{3,4},{4,5},{5,6},{6,7},{7,8},{8,9},{9,10},{10,1... | collective-permute-start | bytes 1597448 | tf_op jit(solution)/shard_map/ring/ppermute | solution.py:634
  116.9 5.5 %collective-permute-done.13.newest_ref.refs_13_.refs_5_ = bf16[22,104,128]{2,1,0:T(8,128)(2,1)S(1)} collective-permute-done((bf16[22,104,128]{2,1,0:T(8,128)(2,1)S(1)}, bf16[22,104,128]{2,1,0:T(8,128)(2,1)S(1)}, u32[]{:S(2)}, u32[]{:S(2)}) %collective-permute-start.13) | collective-permute-done | bytes 585760 | tf_op jit(solution)/shard_map/ring/ppermute | solution.py:631
  122.6 5.4 %collective-permute-start.15 = (bf16[22,104,128]{2,1,0:T(8,128)(2,1)S(1)}, bf16[22,104,128]{2,1,0:T(8,128)(2,1)S(1)}, u32[]{:S(2)}, u32[]{:S(2)}) collective-permute-start(bf16[22,104,128]{2,1,0:T(8,128)(2,1)S(1)} %ring.49.after_ref), channel_id=1, source_target_pairs={{0,15},{1,0},{2,1},{3,2},{4,3},{5,4},{6,5},{7,6},{8,7},{9,8},{10,9... | collective-permute-start | bytes 1757192 | tf_op jit(solution)/shard_map/ring/ppermute | solution.py:631
  129.9 2.3 %collective-permute-start.14 = (bf16[20,104,128]{2,1,0:T(8,128)(2,1)S(1)}, bf16[20,104,128]{2,1,0:T(8,128)(2,1)S(1)}, u32[]{:S(2)}, u32[]{:S(2)}) collective-permute-start(bf16[20,104,128]{2,1,0:T(8,128)(2,1)S(1)} %ring.51.after_ref), channel_id=1, source_target_pairs={{0,1},{1,2},{2,3},{3,4},{4,5},{5,6},{6,7},{7,8},{8,9},{9,10},{10,1... | collective-permute-start | bytes 1597448 | tf_op jit(solution)/shard_map/ring/ppermute | solution.py:634
  132.2 1.9 ring.52.part_ref
  134.1 5.6 %collective-permute-done.15.refs_14_.newest_ref = bf16[22,104,128]{2,1,0:T(8,128)(2,1)S(1)} collective-permute-done((bf16[22,104,128]{2,1,0:T(8,128)(2,1)S(1)}, bf16[22,104,128]{2,1,0:T(8,128)(2,1)S(1)}, u32[]{:S(2)}, u32[]{:S(2)}) %collective-permute-start.15) | collective-permute-done | bytes 585760 | tf_op jit(solution)/shard_map/ring/ppermute | solution.py:631
  140.8 5.6 %collective-permute-start.17 = (bf16[22,104,128]{2,1,0:T(8,128)(2,1)}, bf16[22,104,128]{2,1,0:T(8,128)(2,1)}, u32[]{:S(2)}, u32[]{:S(2)}) collective-permute-start(bf16[22,104,128]{2,1,0:T(8,128)(2,1)} %ring.53.after_ref), channel_id=1, source_target_pairs={{0,15},{1,0},{2,1},{3,2},{4,3},{5,4},{6,5},{7,6},{8,7},{9,8},{10,9... | collective-permute-start | bytes 1757192 | tf_op jit(solution)/shard_map/ring/ppermute | solution.py:631
  146.4 1.8 ring.54.part_ref
  149.3 1.9 collective-permute-start.16
  152.0 2.5 %stage.1.held_ref = bf16[96,104,128]{2,1,0:T(8,128)(2,1)S(1)} custom-call(s32[8,128]{1,0:T(8,128)S(1)} %get-tuple-element.90.item_ref, bf16[38,104,128]{2,1,0:T(8,128)(2,1)S(1)} %get-tuple-element.91.home_ref.refs_0_, bf16[30,104,128]{2,1,0:T(8,128)(2,1)S(1)} %collective-permute-done.2.newest_ref.refs_0_.refs_1_, ...), custom_call_target="tpu_custom_call" | custom-call | tf_op jit(solution)/shard_map/stage/pallas_call | solution.py:647
  156.9 5.1 %collective-permute-done.16.ahead_ref = bf16[20,104,128]{2,1,0:T(8,128)(2,1)} collective-permute-done((bf16[20,104,128]{2,1,0:T(8,128)(2,1)}, bf16[20,104,128]{2,1,0:T(8,128)(2,1)}, u32[]{:S(2)}, u32[]{:S(2)}) %collective-permute-start.16) | collective-permute-done | bytes 532512 | tf_op jit(solution)/shard_map/ring/ppermute | solution.py:634
  163.7 5.4 %map.1 = f32[8,128]{1,0:T(8,128)S(1)} custom-call(s32[8,128]{1,0:T(8,128)S(1)} %get-tuple-element.90.item_ref, bf16[96,104,128]{2,1,0:T(8,128)(2,1)S(1)} %copy-done.1, bf16[20,104,128]{2,1,0:T(8,128)(2,1)} %collective-permute-done.16.ahead_ref, bf16[22,104,128]{2,1,0:T(8,128)(2,1)} %collective-permute-done.17.behind_ref, ...), custom_call_target="tpu_custom_call" | custom-call | tf_op jit(solution)/shard_map/map/pallas_call | solution.py:656
  169.8 12.8 %all-to-all-start.1 = ((f32[16,4,128]{2,1,0:T(4,128)}), f32[16,4,128]{2,1,0:T(4,128)S(1)}, u32[]{:S(2)}, u32[]{:S(2)}) async-start(f32[16,4,128]{2,1,0:T(4,128)} %broadcast_in_dim.55), calls=%async_computation.1 | async-start | bytes 65536 | tf_op jit(solution)/shard_map/finish/all_to_all | solution.py:670
  185.1 10.1 %all-to-all-done.1 = f32[16,4,128]{2,1,0:T(4,128)S(1)} async-done(((f32[16,4,128]{2,1,0:T(4,128)}), f32[16,4,128]{2,1,0:T(4,128)S(1)}, u32[]{:S(2)}, u32[]{:S(2)}) %all-to-all-start.1) | async-done | bytes 32800 | tf_op jit(solution)/shard_map/finish/all_to_all | solution.py:670
  (88 shorter events, 36.6 us)
Async XLA Ops:
  6.5 8.3 %copy-start.6 = (bf16[2,64,4736]{2,1,0:T(8,128)(2,1)S(1)}, bf16[2,64,4736]{2,1,0:T(8,128)(2,1)}, u32[]{:S(2)}) copy-start(bf16[2,64,4736]{2,1,0:T(8,128)(2,1)} %own_ref.1) | copy-start | bytes 3637252
  6.5 149.5 %all-gather.2.cloned.1.call-start = ((), (), s32[]{:S(2)}) async-start(), calls=%async_computation.2 | async-start | bytes 2621440 | tf_op jit(solution)/shard_map/weights/all_gather | solution.py:556
  7.7 6.2 %collective-permute-start = (bf16[2,16,4736]{2,1,0:T(8,128)(2,1)S(1)}, bf16[2,16,4736]{2,1,0:T(8,128)(2,1)S(1)}, u32[]{:S(2)}, u32[]{:S(2)}) collective-permute-start(bf16[2,16,4736]{2,1,0:T(8,128)(2,1)S(1)} %get-tuple-element.156), channel_id=1, source_target_pairs={{0,16},{16,32},{32,48},{48,64},{64,80},{80,96},{96,112},{112,0},{1... | collective-permute-start | bytes 909320 | tf_op jit(solution)/shard_map/halo/ppermute | solution.py:23
  7.8 7.0 %collective-permute-start.1 = (bf16[2,16,4736]{2,1,0:T(8,128)(2,1)S(1)}, bf16[2,16,4736]{2,1,0:T(8,128)(2,1)S(1)}, u32[]{:S(2)}, u32[]{:S(2)}) collective-permute-start(bf16[2,16,4736]{2,1,0:T(8,128)(2,1)S(1)} %get-tuple-element.155), channel_id=1, source_target_pairs={{16,0},{32,16},{48,32},{64,48},{80,64},{96,80},{112,96},{0,112},{1... | collective-permute-start | bytes 909320 | tf_op jit(solution)/shard_map/halo/ppermute | solution.py:24
  14.0 19.3 %copy-start.7 = (bf16[2,16,4736]{2,1,0:T(8,128)(2,1)}, bf16[2,16,4736]{2,1,0:T(8,128)(2,1)S(1)}, u32[]{:S(2)}) copy-start(bf16[2,16,4736]{2,1,0:T(8,128)(2,1)S(1)} %collective-permute-done.low_ref) | copy-start | bytes 909316
  14.8 18.5 %copy-start.9 = (bf16[2,16,4736]{2,1,0:T(8,128)(2,1)}, bf16[2,16,4736]{2,1,0:T(8,128)(2,1)S(1)}, u32[]{:S(2)}) copy-start(bf16[2,16,4736]{2,1,0:T(8,128)(2,1)S(1)} %collective-permute-done.1.high_ref) | copy-start | bytes 909316
  16.5 26.6 %collective-permute-start.2 = (bf16[30,104,128]{2,1,0:T(8,128)(2,1)S(1)}, bf16[30,104,128]{2,1,0:T(8,128)(2,1)S(1)}, u32[]{:S(2)}, u32[]{:S(2)}) collective-permute-start(bf16[30,104,128]{2,1,0:T(8,128)(2,1)S(1)} %get-tuple-element.92.after_ref), channel_id=1, source_target_pairs={{0,1},{1,2},{2,3},{3,4},{4,5},{5,6},{6,7},{7,8},{8,9},{9,10},{10,1... | collective-permute-start | bytes 2396168 | tf_op jit(solution)/shard_map/ring/ppermute | solution.py:627
  19.5 17.4 %collective-permute-start.3 = (bf16[12,104,128]{2,1,0:T(8,128)(2,1)S(1)}, bf16[12,104,128]{2,1,0:T(8,128)(2,1)S(1)}, u32[]{:S(2)}, u32[]{:S(2)}) collective-permute-start(bf16[12,104,128]{2,1,0:T(8,128)(2,1)S(1)} %get-tuple-element.94), channel_id=1, source_target_pairs={{0,15},{1,0},{2,1},{3,2},{4,3},{5,4},{6,5},{7,6},{8,7},{9,8},{10,9... | collective-permute-start | bytes 958472 | tf_op jit(solution)/shard_map/ring/ppermute | solution.py:626
  37.2 15.5 %collective-permute-start.5 = (bf16[23,104,128]{2,1,0:T(8,128)(2,1)S(1)}, bf16[23,104,128]{2,1,0:T(8,128)(2,1)S(1)}, u32[]{:S(2)}, u32[]{:S(2)}) collective-permute-start(bf16[23,104,128]{2,1,0:T(8,128)(2,1)S(1)} %ring.29.after_ref), channel_id=1, source_target_pairs={{0,15},{1,0},{2,1},{3,2},{4,3},{5,4},{6,5},{7,6},{8,7},{9,8},{10,9... | collective-permute-start | bytes 1837064 | tf_op jit(solution)/shard_map/ring/ppermute | solution.py:631
  43.4 16.4 %collective-permute-start.4 = (bf16[21,104,128]{2,1,0:T(8,128)(2,1)S(1)}, bf16[21,104,128]{2,1,0:T(8,128)(2,1)S(1)}, u32[]{:S(2)}, u32[]{:S(2)}) collective-permute-start(bf16[21,104,128]{2,1,0:T(8,128)(2,1)S(1)} %ring.31.after_ref), channel_id=1, source_target_pairs={{0,1},{1,2},{2,3},{3,4},{4,5},{5,6},{6,7},{7,8},{8,9},{9,10},{10,1... | collective-permute-start | bytes 1677320 | tf_op jit(solution)/shard_map/ring/ppermute | solution.py:634
  53.8 15.1 %collective-permute-start.7 = (bf16[23,104,128]{2,1,0:T(8,128)(2,1)}, bf16[23,104,128]{2,1,0:T(8,128)(2,1)}, u32[]{:S(2)}, u32[]{:S(2)}) collective-permute-start(bf16[23,104,128]{2,1,0:T(8,128)(2,1)} %ring.33.after_ref), channel_id=1, source_target_pairs={{0,15},{1,0},{2,1},{3,2},{4,3},{5,4},{6,5},{7,6},{8,7},{9,8},{10,9... | collective-permute-start | bytes 1837064 | tf_op jit(solution)/shard_map/ring/ppermute | solution.py:631
  60.9 15.4 %collective-permute-start.6 = (bf16[20,104,128]{2,1,0:T(8,128)(2,1)}, bf16[20,104,128]{2,1,0:T(8,128)(2,1)}, u32[]{:S(2)}, u32[]{:S(2)}) collective-permute-start(bf16[20,104,128]{2,1,0:T(8,128)(2,1)} %ring.35.after_ref), channel_id=1, source_target_pairs={{0,1},{1,2},{2,3},{3,4},{4,5},{5,6},{6,7},{7,8},{8,9},{9,10},{10,1... | collective-permute-start | bytes 1597448 | tf_op jit(solution)/shard_map/ring/ppermute | solution.py:634
  70.3 15.3 %collective-permute-start.9 = (bf16[23,104,128]{2,1,0:T(8,128)(2,1)S(1)}, bf16[23,104,128]{2,1,0:T(8,128)(2,1)S(1)}, u32[]{:S(2)}, u32[]{:S(2)}) collective-permute-start(bf16[23,104,128]{2,1,0:T(8,128)(2,1)S(1)} %ring.37.after_ref), channel_id=1, source_target_pairs={{0,15},{1,0},{2,1},{3,2},{4,3},{5,4},{6,5},{7,6},{8,7},{9,8},{10,9... | collective-permute-start | bytes 1837064 | tf_op jit(solution)/shard_map/ring/ppermute | solution.py:631
  77.6 15.4 %collective-permute-start.8 = (bf16[20,104,128]{2,1,0:T(8,128)(2,1)S(1)}, bf16[20,104,128]{2,1,0:T(8,128)(2,1)S(1)}, u32[]{:S(2)}, u32[]{:S(2)}) collective-permute-start(bf16[20,104,128]{2,1,0:T(8,128)(2,1)S(1)} %ring.39.after_ref), channel_id=1, source_target_pairs={{0,1},{1,2},{2,3},{3,4},{4,5},{5,6},{6,7},{7,8},{8,9},{9,10},{10,1... | collective-permute-start | bytes 1597448 | tf_op jit(solution)/shard_map/ring/ppermute | solution.py:634
  85.9 21.1 %collective-permute-start.11 = (bf16[22,104,128]{2,1,0:T(8,128)(2,1)S(1)}, bf16[22,104,128]{2,1,0:T(8,128)(2,1)S(1)}, u32[]{:S(2)}, u32[]{:S(2)}) collective-permute-start(bf16[22,104,128]{2,1,0:T(8,128)(2,1)S(1)} %ring.41.after_ref), channel_id=1, source_target_pairs={{0,15},{1,0},{2,1},{3,2},{4,3},{5,4},{6,5},{7,6},{8,7},{9,8},{10,9... | collective-permute-start | bytes 1757192 | tf_op jit(solution)/shard_map/ring/ppermute | solution.py:631
  93.3 17.6 %collective-permute-start.10 = (bf16[20,104,128]{2,1,0:T(8,128)(2,1)S(1)}, bf16[20,104,128]{2,1,0:T(8,128)(2,1)S(1)}, u32[]{:S(2)}, u32[]{:S(2)}) collective-permute-start(bf16[20,104,128]{2,1,0:T(8,128)(2,1)S(1)} %ring.43.after_ref), channel_id=1, source_target_pairs={{0,1},{1,2},{2,3},{3,4},{4,5},{5,6},{6,7},{7,8},{8,9},{9,10},{10,1... | collective-permute-start | bytes 1597448 | tf_op jit(solution)/shard_map/ring/ppermute | solution.py:634
  107.2 15.2 %collective-permute-start.13 = (bf16[22,104,128]{2,1,0:T(8,128)(2,1)S(1)}, bf16[22,104,128]{2,1,0:T(8,128)(2,1)S(1)}, u32[]{:S(2)}, u32[]{:S(2)}) collective-permute-start(bf16[22,104,128]{2,1,0:T(8,128)(2,1)S(1)} %ring.45.after_ref), channel_id=1, source_target_pairs={{0,15},{1,0},{2,1},{3,2},{4,3},{5,4},{6,5},{7,6},{8,7},{9,8},{10,9... | collective-permute-start | bytes 1757192 | tf_op jit(solution)/shard_map/ring/ppermute | solution.py:631
  111.2 18.5 %collective-permute-start.12 = (bf16[20,104,128]{2,1,0:T(8,128)(2,1)S(1)}, bf16[20,104,128]{2,1,0:T(8,128)(2,1)S(1)}, u32[]{:S(2)}, u32[]{:S(2)}) collective-permute-start(bf16[20,104,128]{2,1,0:T(8,128)(2,1)S(1)} %ring.47.after_ref), channel_id=1, source_target_pairs={{0,1},{1,2},{2,3},{3,4},{4,5},{5,6},{6,7},{7,8},{8,9},{9,10},{10,1... | collective-permute-start | bytes 1597448 | tf_op jit(solution)/shard_map/ring/ppermute | solution.py:634
  122.6 17.1 %collective-permute-start.15 = (bf16[22,104,128]{2,1,0:T(8,128)(2,1)S(1)}, bf16[22,104,128]{2,1,0:T(8,128)(2,1)S(1)}, u32[]{:S(2)}, u32[]{:S(2)}) collective-permute-start(bf16[22,104,128]{2,1,0:T(8,128)(2,1)S(1)} %ring.49.after_ref), channel_id=1, source_target_pairs={{0,15},{1,0},{2,1},{3,2},{4,3},{5,4},{6,5},{7,6},{8,7},{9,8},{10,9... | collective-permute-start | bytes 1757192 | tf_op jit(solution)/shard_map/ring/ppermute | solution.py:631
  129.9 18.3 %collective-permute-start.14 = (bf16[20,104,128]{2,1,0:T(8,128)(2,1)S(1)}, bf16[20,104,128]{2,1,0:T(8,128)(2,1)S(1)}, u32[]{:S(2)}, u32[]{:S(2)}) collective-permute-start(bf16[20,104,128]{2,1,0:T(8,128)(2,1)S(1)} %ring.51.after_ref), channel_id=1, source_target_pairs={{0,1},{1,2},{2,3},{3,4},{4,5},{5,6},{6,7},{7,8},{8,9},{9,10},{10,1... | collective-permute-start | bytes 1597448 | tf_op jit(solution)/shard_map/ring/ppermute | solution.py:634
  140.8 16.1 %collective-permute-start.17 = (bf16[22,104,128]{2,1,0:T(8,128)(2,1)}, bf16[22,104,128]{2,1,0:T(8,128)(2,1)}, u32[]{:S(2)}, u32[]{:S(2)}) collective-permute-start(bf16[22,104,128]{2,1,0:T(8,128)(2,1)} %ring.53.after_ref), channel_id=1, source_target_pairs={{0,15},{1,0},{2,1},{3,2},{4,3},{5,4},{6,5},{7,6},{8,7},{9,8},{10,9... | collective-permute-start | bytes 1757192 | tf_op jit(solution)/shard_map/ring/ppermute | solution.py:631
  148.2 3.0 %copy-start.2 = (bf16[2,64,4096]{2,1,0:T(8,128)(2,1)S(1)}, bf16[2,64,4096]{2,1,0:T(8,128)(2,1)}, u32[]{:S(2)}) copy-start(bf16[2,64,4096]{2,1,0:T(8,128)(2,1)} %student_ref.3) | copy-start | bytes 3145732
  149.3 12.7 %collective-permute-start.16 = (bf16[20,104,128]{2,1,0:T(8,128)(2,1)}, bf16[20,104,128]{2,1,0:T(8,128)(2,1)}, u32[]{:S(2)}, u32[]{:S(2)}) collective-permute-start(bf16[20,104,128]{2,1,0:T(8,128)(2,1)} %ring.55), channel_id=1, source_target_pairs={{0,1},{1,2},{2,3},{3,4},{4,5},{5,6},{6,7},{7,8},{8,9},{9,10},{10,1... | collective-permute-start | bytes 1597448 | tf_op jit(solution)/shard_map/ring/ppermute | solution.py:634
  154.5 1.5 copy-start
  162.0 1.7 copy-start.1
  163.7 21.3 %copy-start.3 = (bf16[2,64,4096]{2,1,0:T(8,128)(2,1)S(1)}, bf16[2,64,4096]{2,1,0:T(8,128)(2,1)}, u32[]{:S(2)}) copy-start(bf16[2,64,4096]{2,1,0:T(8,128)(2,1)} %student_ref.3) | copy-start | bytes 3145732
  163.7 21.4 %copy-start.8 = (bf16[2,16,4736]{2,1,0:T(8,128)(2,1)S(1)}, bf16[2,16,4736]{2,1,0:T(8,128)(2,1)}, u32[]{:S(2)}) copy-start(bf16[2,16,4736]{2,1,0:T(8,128)(2,1)} %copy-done.7) | copy-start | bytes 909316
  163.7 21.4 %copy-start.11 = (s32[512,2]{0,1:T(2,128)S(1)}, s32[512,2]{0,1:T(2,128)}, u32[]{:S(2)}) copy-start(s32[512,2]{0,1:T(2,128)} %param.12) | copy-start | bytes 12292
  169.8 25.4 %all-to-all-start.1 = ((f32[16,4,128]{2,1,0:T(4,128)}), f32[16,4,128]{2,1,0:T(4,128)S(1)}, u32[]{:S(2)}, u32[]{:S(2)}) async-start(f32[16,4,128]{2,1,0:T(4,128)} %broadcast_in_dim.55), calls=%async_computation.1 | async-start | bytes 65536 | tf_op jit(solution)/shard_map/finish/all_to_all | solution.py:670
  195.5 0.6 copy-start.12
Sparse Core Ops, SparseCore 0:
  62.9 39.8 all-gather.1

commit v11 on v10

--- a/solution.py
+++ b/solution.py
@@ -11,7 +11,7 @@
 K = 2
 W = 16
 ROWS = 104
-SIZES = ((30, 21, 20, 20, 20, 20, 20, 20), (12, 23, 23, 23, 22, 22, 22, 22))
+SIZES = ((24, 21, 21, 21, 20, 20, 20, 20), (14, 22, 22, 22, 22, 22, 22, 22))
 STARTS = tuple(tuple(sum(sizes[:f]) for f in range(len(sizes))) for sizes in SIZES)
 TINY = 1.2e-38
 
@@ -477,7 +477,9 @@
     table = jnp.where(
         lane == 0, mass, jnp.where(lane == 1, cross, jnp.where(lane == 2, student_top, total_ref[...]))
     )
-    out_ref[...] = table.T[:8]
+    parts = table.T[:4]
+    for v in range(out_ref.shape[0]):
+        out_ref[v] = parts
 
 
 def whole(padded_parts, cand, src_block, weights, student_logits):
@@ -655,7 +657,7 @@
     with jax.named_scope("map"):
         sums = pl.pallas_call(
             functools.partial(map_kernel, steps),
-            out_shape=jax.ShapeDtypeStruct((8, row_count), jnp.float32),
+            out_shape=jax.ShapeDtypeStruct((vocab_count, 4, row_count), jnp.float32),
             in_specs=[smem] + [vmem] * 8,
             out_specs=vmem,
             scratch_shapes=[
@@ -666,8 +668,7 @@
         )(items, held, came_ahead[-1], came_behind[-1], spread, weights, student_logits, top, total)
 
     with jax.named_scope("finish"):
-        sent = jnp.broadcast_to(sums[None, :4], (vocab_count, 4, row_count))
-        parts = lax.all_to_all(sent, "vocab", split_axis=0, concat_axis=0, tiled=True)
+        parts = lax.all_to_all(sums, "vocab", split_axis=0, concat_axis=0, tiled=True)
         mass_part, cross_part, top_part, total_part = (parts[:, i] for i in range(4))
         student_top = jnp.max(top_part, axis=0)
         log_total = student_top + jnp.log(jnp.sum(jnp.exp(top_part - student_top) * total_part, axis=0))

time: 204 us -> 199 us (0.975)
  the two profiles are of different devices: /device:TPU:6 before, /device:TPU:24 now
where the time goes in v11:
time: 199 us; the launch traced here: 198 us
  starting transfers between devices  72.6 us (36%)
  waiting for transfers between devices  61.8 us (31%)
  Pallas kernels  39.6 us (20%)
  between operations  15.1 us (8%)
  local copies, waits for them, and re-layouts  6.74 us (3%)
  other arithmetic  2.02 us (1%)
    ppermute x7, starting transfers between devices, shards(): came_behind.append(lax.ppermute(behind, ('seq', 'vocab'), backward))  39.4 us
    ppermute x7, waiting for transfers between devices, shards(): came_behind.append(lax.ppermute(behind, ('seq', 'vocab'), backward))  37.8 us
    pallas_call x14, Pallas kernels, ready(): pl.pallas_call(functools.partial(ready_kernel, chain, step), out_shape=pl...  15.7 us
    ppermute x7, starting transfers between devices, shards(): came_ahead.append(lax.ppermute(ahead, ('seq', 'vocab'), forward))  13.4 us
    ppermute x1, starting transfers between devices, shards(): came_behind = [lax.ppermute(behind, ('seq', 'vocab'), backward)]  11.4 us
    all_to_all x1, waiting for transfers between devices, shards(): lax.all_to_all(sums, 'vocab', split_axis=0, concat_axis=0, tiled=True)  10.1 us
    ppermute x7, waiting for transfers between devices, shards(): came_ahead.append(lax.ppermute(ahead, ('seq', 'vocab'), forward))  9.3 us
    pallas_call x14, Pallas kernels, passed(): pl.pallas_call(functools.partial(pass_kernel, chain, step, home), out_sha...  9.12 us
  transfers between devices with their start and end apart: 20, of which 13 were waited for; matrix products, arithmetic and copies ran while one was open for 2% of the time, Pallas kernels for 16%

profile of v11, /device:TPU:24, one launch (start us, length us, event | category | flops | bytes accessed | tf_op | source)
XLA Modules:
  0.0 197.8 jit_solution(7602721387957845098)
XLA Ops:
  7.8 2.9 %collective-permute-start.1 = (bf16[2,16,4736]{2,1,0:T(8,128)(2,1)S(1)}, bf16[2,16,4736]{2,1,0:T(8,128)(2,1)S(1)}, u32[]{:S(2)}, u32[]{:S(2)}) collective-permute-start(bf16[2,16,4736]{2,1,0:T(8,128)(2,1)S(1)} %get-tuple-element.155), channel_id=1, source_target_pairs={{16,0},{32,16},{48,32},{64,48},{80,64},{96,80},{112,96},{0,112},{1... | collective-permute-start | bytes 909320 | tf_op jit(solution)/shard_map/halo/ppermute | solution.py:24
  12.9 2.3 %collective-permute-done.low_ref = bf16[2,16,4736]{2,1,0:T(8,128)(2,1)S(1)} collective-permute-done((bf16[2,16,4736]{2,1,0:T(8,128)(2,1)S(1)}, bf16[2,16,4736]{2,1,0:T(8,128)(2,1)S(1)}, u32[]{:S(2)}, u32[]{:S(2)}) %collective-permute-start) | collective-permute-done | bytes 303136 | tf_op jit(solution)/shard_map/halo/ppermute | solution.py:23
  16.9 11.4 %collective-permute-start.3 = (bf16[14,104,128]{2,1,0:T(8,128)(2,1)S(1)}, bf16[14,104,128]{2,1,0:T(8,128)(2,1)S(1)}, u32[]{:S(2)}, u32[]{:S(2)}) collective-permute-start(bf16[14,104,128]{2,1,0:T(8,128)(2,1)S(1)} %get-tuple-element.94), channel_id=1, source_target_pairs={{0,15},{1,0},{2,1},{3,2},{4,3},{5,4},{6,5},{7,6},{8,7},{9,8},{10,9... | collective-permute-start | bytes 1118216 | tf_op jit(solution)/shard_map/ring/ppermute | solution.py:628
  28.3 1.9 collective-permute-start.2
  30.2 4.0 %plan.1 = (s32[8,256]{1,0:T(8,128)S(1)}, s32[8,128]{1,0:T(8,128)S(1)}, s32[8,128]{1,0:T(8,128)S(1)}) custom-call(s32[2]{0:T(128)S(1)} %pad_add_fusion.place_ref, s32[16,64]{1,0:T(8,128)S(1)} %reshape.251.listed_ref, s32[8,128]{1,0:T(8,128)S(1)} %get-tuple-element.88.after_ref), custom_call_target="tpu_custom_call" | custom-call | tf_op jit(solution)/shard_map/plan/pallas_call | solution.py:599
  36.2 5.6 %collective-permute-start.5 = (bf16[22,104,128]{2,1,0:T(8,128)(2,1)S(1)}, bf16[22,104,128]{2,1,0:T(8,128)(2,1)S(1)}, u32[]{:S(2)}, u32[]{:S(2)}) collective-permute-start(bf16[22,104,128]{2,1,0:T(8,128)(2,1)S(1)} %ring.29.after_ref), channel_id=1, source_target_pairs={{0,15},{1,0},{2,1},{3,2},{4,3},{5,4},{6,5},{7,6},{8,7},{9,8},{10,9... | collective-permute-start | bytes 1757192 | tf_op jit(solution)/shard_map/ring/ppermute | solution.py:633
  43.2 1.9 collective-permute-start.4
  45.6 6.7 %collective-permute-done.5.newest_ref.refs_1_.refs_9_ = bf16[22,104,128]{2,1,0:T(8,128)(2,1)S(1)} collective-permute-done((bf16[22,104,128]{2,1,0:T(8,128)(2,1)S(1)}, bf16[22,104,128]{2,1,0:T(8,128)(2,1)S(1)}, u32[]{:S(2)}, u32[]{:S(2)}) %collective-permute-start.5) | collective-permute-done | bytes 585760 | tf_op jit(solution)/shard_map/ring/ppermute | solution.py:633
  53.4 5.6 %collective-permute-start.7 = (bf16[22,104,128]{2,1,0:T(8,128)(2,1)}, bf16[22,104,128]{2,1,0:T(8,128)(2,1)}, u32[]{:S(2)}, u32[]{:S(2)}) collective-permute-start(bf16[22,104,128]{2,1,0:T(8,128)(2,1)} %ring.33.after_ref), channel_id=1, source_target_pairs={{0,15},{1,0},{2,1},{3,2},{4,3},{5,4},{6,5},{7,6},{8,7},{9,8},{10,9... | collective-permute-start | bytes 1757192 | tf_op jit(solution)/shard_map/ring/ppermute | solution.py:633
  60.5 1.9 collective-permute-start.6
  62.9 8.3 %collective-permute-done.7.newest_ref.refs_2_.refs_10_ = bf16[22,104,128]{2,1,0:T(8,128)(2,1)} collective-permute-done((bf16[22,104,128]{2,1,0:T(8,128)(2,1)}, bf16[22,104,128]{2,1,0:T(8,128)(2,1)}, u32[]{:S(2)}, u32[]{:S(2)}) %collective-permute-start.7) | collective-permute-done | bytes 585760 | tf_op jit(solution)/shard_map/ring/ppermute | solution.py:633
  72.5 5.6 %collective-permute-start.9 = (bf16[22,104,128]{2,1,0:T(8,128)(2,1)S(1)}, bf16[22,104,128]{2,1,0:T(8,128)(2,1)S(1)}, u32[]{:S(2)}, u32[]{:S(2)}) collective-permute-start(bf16[22,104,128]{2,1,0:T(8,128)(2,1)S(1)} %ring.37.after_ref), channel_id=1, source_target_pairs={{0,15},{1,0},{2,1},{3,2},{4,3},{5,4},{6,5},{7,6},{8,7},{9,8},{10,9... | collective-permute-start | bytes 1757192 | tf_op jit(solution)/shard_map/ring/ppermute | solution.py:633
  79.8 1.9 collective-permute-start.8
  83.5 8.0 %collective-permute-done.9.newest_ref.refs_3_.refs_11_ = bf16[22,104,128]{2,1,0:T(8,128)(2,1)S(1)} collective-permute-done((bf16[22,104,128]{2,1,0:T(8,128)(2,1)S(1)}, bf16[22,104,128]{2,1,0:T(8,128)(2,1)S(1)}, u32[]{:S(2)}, u32[]{:S(2)}) %collective-permute-start.9) | collective-permute-done | bytes 585760 | tf_op jit(solution)/shard_map/ring/ppermute | solution.py:633
  91.7 5.6 %collective-permute-start.11 = (bf16[22,104,128]{2,1,0:T(8,128)(2,1)S(1)}, bf16[22,104,128]{2,1,0:T(8,128)(2,1)S(1)}, u32[]{:S(2)}, u32[]{:S(2)}) collective-permute-start(bf16[22,104,128]{2,1,0:T(8,128)(2,1)S(1)} %ring.41.after_ref), channel_id=1, source_target_pairs={{0,15},{1,0},{2,1},{3,2},{4,3},{5,4},{6,5},{7,6},{8,7},{9,8},{10,9... | collective-permute-start | bytes 1757192 | tf_op jit(solution)/shard_map/ring/ppermute | solution.py:633
  99.2 1.9 collective-permute-start.10
  102.8 6.7 %collective-permute-done.11.newest_ref.refs_4_.refs_12_ = bf16[22,104,128]{2,1,0:T(8,128)(2,1)S(1)} collective-permute-done((bf16[22,104,128]{2,1,0:T(8,128)(2,1)S(1)}, bf16[22,104,128]{2,1,0:T(8,128)(2,1)S(1)}, u32[]{:S(2)}, u32[]{:S(2)}) %collective-permute-start.11) | collective-permute-done | bytes 585760 | tf_op jit(solution)/shard_map/ring/ppermute | solution.py:633
  109.8 5.8 %collective-permute-start.13 = (bf16[22,104,128]{2,1,0:T(8,128)(2,1)S(1)}, bf16[22,104,128]{2,1,0:T(8,128)(2,1)S(1)}, u32[]{:S(2)}, u32[]{:S(2)}) collective-permute-start(bf16[22,104,128]{2,1,0:T(8,128)(2,1)S(1)} %ring.45.after_ref), channel_id=1, source_target_pairs={{0,15},{1,0},{2,1},{3,2},{4,3},{5,4},{6,5},{7,6},{8,7},{9,8},{10,9... | collective-permute-start | bytes 1757192 | tf_op jit(solution)/shard_map/ring/ppermute | solution.py:633
  117.5 1.9 collective-permute-start.12
  121.1 5.2 %collective-permute-done.13.newest_ref.refs_13_.refs_5_ = bf16[22,104,128]{2,1,0:T(8,128)(2,1)S(1)} collective-permute-done((bf16[22,104,128]{2,1,0:T(8,128)(2,1)S(1)}, bf16[22,104,128]{2,1,0:T(8,128)(2,1)S(1)}, u32[]{:S(2)}, u32[]{:S(2)}) %collective-permute-start.13) | collective-permute-done | bytes 585760 | tf_op jit(solution)/shard_map/ring/ppermute | solution.py:633
  126.6 5.6 %collective-permute-start.15 = (bf16[22,104,128]{2,1,0:T(8,128)(2,1)S(1)}, bf16[22,104,128]{2,1,0:T(8,128)(2,1)S(1)}, u32[]{:S(2)}, u32[]{:S(2)}) collective-permute-start(bf16[22,104,128]{2,1,0:T(8,128)(2,1)S(1)} %ring.49.after_ref), channel_id=1, source_target_pairs={{0,15},{1,0},{2,1},{3,2},{4,3},{5,4},{6,5},{7,6},{8,7},{9,8},{10,9... | collective-permute-start | bytes 1757192 | tf_op jit(solution)/shard_map/ring/ppermute | solution.py:633
  134.8 1.9 collective-permute-start.14
  136.8 1.9 ring.52.part_ref
  138.7 2.9 %collective-permute-done.15.refs_14_.newest_ref = bf16[22,104,128]{2,1,0:T(8,128)(2,1)S(1)} collective-permute-done((bf16[22,104,128]{2,1,0:T(8,128)(2,1)S(1)}, bf16[22,104,128]{2,1,0:T(8,128)(2,1)S(1)}, u32[]{:S(2)}, u32[]{:S(2)}) %collective-permute-start.15) | collective-permute-done | bytes 585760 | tf_op jit(solution)/shard_map/ring/ppermute | solution.py:633
  142.6 5.6 %collective-permute-start.17 = (bf16[22,104,128]{2,1,0:T(8,128)(2,1)}, bf16[22,104,128]{2,1,0:T(8,128)(2,1)}, u32[]{:S(2)}, u32[]{:S(2)}) collective-permute-start(bf16[22,104,128]{2,1,0:T(8,128)(2,1)} %ring.53.after_ref), channel_id=1, source_target_pairs={{0,15},{1,0},{2,1},{3,2},{4,3},{5,4},{6,5},{7,6},{8,7},{9,8},{10,9... | collective-permute-start | bytes 1757192 | tf_op jit(solution)/shard_map/ring/ppermute | solution.py:633
  150.1 2.5 %collective-permute-done.14.refs_7_.newest_ref = bf16[20,104,128]{2,1,0:T(8,128)(2,1)S(1)} collective-permute-done((bf16[20,104,128]{2,1,0:T(8,128)(2,1)S(1)}, bf16[20,104,128]{2,1,0:T(8,128)(2,1)S(1)}, u32[]{:S(2)}, u32[]{:S(2)}) %collective-permute-start.14) | collective-permute-done | bytes 532512 | tf_op jit(solution)/shard_map/ring/ppermute | solution.py:636
  153.7 1.9 collective-permute-start.16
  156.4 2.5 %stage.1.held_ref = bf16[96,104,128]{2,1,0:T(8,128)(2,1)S(1)} custom-call(s32[8,128]{1,0:T(8,128)S(1)} %get-tuple-element.90.item_ref, bf16[38,104,128]{2,1,0:T(8,128)(2,1)S(1)} %get-tuple-element.91.home_ref.refs_0_, bf16[24,104,128]{2,1,0:T(8,128)(2,1)S(1)} %collective-permute-done.2.newest_ref.refs_0_.refs_1_, ...), custom_call_target="tpu_custom_call" | custom-call | tf_op jit(solution)/shard_map/stage/pallas_call | solution.py:649
  160.3 6.0 %collective-permute-done.16.ahead_ref = bf16[20,104,128]{2,1,0:T(8,128)(2,1)} collective-permute-done((bf16[20,104,128]{2,1,0:T(8,128)(2,1)}, bf16[20,104,128]{2,1,0:T(8,128)(2,1)}, u32[]{:S(2)}, u32[]{:S(2)}) %collective-permute-start.16) | collective-permute-done | bytes 532512 | tf_op jit(solution)/shard_map/ring/ppermute | solution.py:636
  168.1 6.1 %map.1 = f32[16,4,128]{2,1,0:T(4,128)} custom-call(s32[8,128]{1,0:T(8,128)S(1)} %get-tuple-element.90.item_ref, bf16[96,104,128]{2,1,0:T(8,128)(2,1)S(1)} %copy-done.1, bf16[20,104,128]{2,1,0:T(8,128)(2,1)} %collective-permute-done.16.ahead_ref, bf16[22,104,128]{2,1,0:T(8,128)(2,1)} %collective-permute-done.17.behind_ref, ...), custom_call_target="tpu_custom_call" | custom-call | tf_op jit(solution)/shard_map/map/pallas_call | solution.py:658
  174.1 3.5 %all-to-all-start.1 = ((f32[16,4,128]{2,1,0:T(4,128)}), f32[16,4,128]{2,1,0:T(4,128)S(1)}, u32[]{:S(2)}, u32[]{:S(2)}) async-start(f32[16,4,128]{2,1,0:T(4,128)} %map.1), calls=%async_computation.1 | async-start | bytes 65536 | tf_op jit(solution)/shard_map/finish/all_to_all | solution.py:671
  180.1 10.1 %all-to-all-done.1 = f32[16,4,128]{2,1,0:T(4,128)S(1)} async-done(((f32[16,4,128]{2,1,0:T(4,128)}), f32[16,4,128]{2,1,0:T(4,128)S(1)}, u32[]{:S(2)}, u32[]{:S(2)}) %all-to-all-start.1) | async-done | bytes 32800 | tf_op jit(solution)/shard_map/finish/all_to_all | solution.py:671
  (86 shorter events, 37.3 us)
Async XLA Ops:
  6.5 8.7 %copy-start.6 = (bf16[2,64,4736]{2,1,0:T(8,128)(2,1)S(1)}, bf16[2,64,4736]{2,1,0:T(8,128)(2,1)}, u32[]{:S(2)}) copy-start(bf16[2,64,4736]{2,1,0:T(8,128)(2,1)} %own_ref.1) | copy-start | bytes 3637252
  6.5 153.8 %all-gather.2.cloned.1.call-start = ((), (), s32[]{:S(2)}) async-start(), calls=%async_computation.2 | async-start | bytes 2621440 | tf_op jit(solution)/shard_map/weights/all_gather | solution.py:558
  7.7 7.5 %collective-permute-start = (bf16[2,16,4736]{2,1,0:T(8,128)(2,1)S(1)}, bf16[2,16,4736]{2,1,0:T(8,128)(2,1)S(1)}, u32[]{:S(2)}, u32[]{:S(2)}) collective-permute-start(bf16[2,16,4736]{2,1,0:T(8,128)(2,1)S(1)} %get-tuple-element.156), channel_id=1, source_target_pairs={{0,16},{16,32},{32,48},{48,64},{64,80},{80,96},{96,112},{112,0},{1... | collective-permute-start | bytes 909320 | tf_op jit(solution)/shard_map/halo/ppermute | solution.py:23
  7.8 7.4 %collective-permute-start.1 = (bf16[2,16,4736]{2,1,0:T(8,128)(2,1)S(1)}, bf16[2,16,4736]{2,1,0:T(8,128)(2,1)S(1)}, u32[]{:S(2)}, u32[]{:S(2)}) collective-permute-start(bf16[2,16,4736]{2,1,0:T(8,128)(2,1)S(1)} %get-tuple-element.155), channel_id=1, source_target_pairs={{16,0},{32,16},{48,32},{64,48},{80,64},{96,80},{112,96},{0,112},{1... | collective-permute-start | bytes 909320 | tf_op jit(solution)/shard_map/halo/ppermute | solution.py:24
  15.2 20.8 %copy-start.7 = (bf16[2,16,4736]{2,1,0:T(8,128)(2,1)}, bf16[2,16,4736]{2,1,0:T(8,128)(2,1)S(1)}, u32[]{:S(2)}) copy-start(bf16[2,16,4736]{2,1,0:T(8,128)(2,1)S(1)} %collective-permute-done.low_ref) | copy-start | bytes 909316
  15.2 20.8 %copy-start.9 = (bf16[2,16,4736]{2,1,0:T(8,128)(2,1)}, bf16[2,16,4736]{2,1,0:T(8,128)(2,1)S(1)}, u32[]{:S(2)}) copy-start(bf16[2,16,4736]{2,1,0:T(8,128)(2,1)S(1)} %collective-permute-done.1.high_ref) | copy-start | bytes 909316
  16.9 19.1 %collective-permute-start.3 = (bf16[14,104,128]{2,1,0:T(8,128)(2,1)S(1)}, bf16[14,104,128]{2,1,0:T(8,128)(2,1)S(1)}, u32[]{:S(2)}, u32[]{:S(2)}) collective-permute-start(bf16[14,104,128]{2,1,0:T(8,128)(2,1)S(1)} %get-tuple-element.94), channel_id=1, source_target_pairs={{0,15},{1,0},{2,1},{3,2},{4,3},{5,4},{6,5},{7,6},{8,7},{9,8},{10,9... | collective-permute-start | bytes 1118216 | tf_op jit(solution)/shard_map/ring/ppermute | solution.py:628
  28.3 14.7 %collective-permute-start.2 = (bf16[24,104,128]{2,1,0:T(8,128)(2,1)S(1)}, bf16[24,104,128]{2,1,0:T(8,128)(2,1)S(1)}, u32[]{:S(2)}, u32[]{:S(2)}) collective-permute-start(bf16[24,104,128]{2,1,0:T(8,128)(2,1)S(1)} %get-tuple-element.92.after_ref), channel_id=1, source_target_pairs={{0,1},{1,2},{2,3},{3,4},{4,5},{5,6},{6,7},{7,8},{8,9},{9,10},{10,1... | collective-permute-start | bytes 1916936 | tf_op jit(solution)/shard_map/ring/ppermute | solution.py:629
  36.2 16.1 %collective-permute-start.5 = (bf16[22,104,128]{2,1,0:T(8,128)(2,1)S(1)}, bf16[22,104,128]{2,1,0:T(8,128)(2,1)S(1)}, u32[]{:S(2)}, u32[]{:S(2)}) collective-permute-start(bf16[22,104,128]{2,1,0:T(8,128)(2,1)S(1)} %ring.29.after_ref), channel_id=1, source_target_pairs={{0,15},{1,0},{2,1},{3,2},{4,3},{5,4},{6,5},{7,6},{8,7},{9,8},{10,9... | collective-permute-start | bytes 1757192 | tf_op jit(solution)/shard_map/ring/ppermute | solution.py:633
  43.2 16.2 %collective-permute-start.4 = (bf16[21,104,128]{2,1,0:T(8,128)(2,1)S(1)}, bf16[21,104,128]{2,1,0:T(8,128)(2,1)S(1)}, u32[]{:S(2)}, u32[]{:S(2)}) collective-permute-start(bf16[21,104,128]{2,1,0:T(8,128)(2,1)S(1)} %ring.31.after_ref), channel_id=1, source_target_pairs={{0,1},{1,2},{2,3},{3,4},{4,5},{5,6},{6,7},{7,8},{8,9},{9,10},{10,1... | collective-permute-start | bytes 1677320 | tf_op jit(solution)/shard_map/ring/ppermute | solution.py:636
  53.4 17.7 %collective-permute-start.7 = (bf16[22,104,128]{2,1,0:T(8,128)(2,1)}, bf16[22,104,128]{2,1,0:T(8,128)(2,1)}, u32[]{:S(2)}, u32[]{:S(2)}) collective-permute-start(bf16[22,104,128]{2,1,0:T(8,128)(2,1)} %ring.33.after_ref), channel_id=1, source_target_pairs={{0,15},{1,0},{2,1},{3,2},{4,3},{5,4},{6,5},{7,6},{8,7},{9,8},{10,9... | collective-permute-start | bytes 1757192 | tf_op jit(solution)/shard_map/ring/ppermute | solution.py:633
  60.5 18.0 %collective-permute-start.6 = (bf16[21,104,128]{2,1,0:T(8,128)(2,1)}, bf16[21,104,128]{2,1,0:T(8,128)(2,1)}, u32[]{:S(2)}, u32[]{:S(2)}) collective-permute-start(bf16[21,104,128]{2,1,0:T(8,128)(2,1)} %ring.35.after_ref), channel_id=1, source_target_pairs={{0,1},{1,2},{2,3},{3,4},{4,5},{5,6},{6,7},{7,8},{8,9},{9,10},{10,1... | collective-permute-start | bytes 1677320 | tf_op jit(solution)/shard_map/ring/ppermute | solution.py:636
  72.5 18.9 %collective-permute-start.9 = (bf16[22,104,128]{2,1,0:T(8,128)(2,1)S(1)}, bf16[22,104,128]{2,1,0:T(8,128)(2,1)S(1)}, u32[]{:S(2)}, u32[]{:S(2)}) collective-permute-start(bf16[22,104,128]{2,1,0:T(8,128)(2,1)S(1)} %ring.37.after_ref), channel_id=1, source_target_pairs={{0,15},{1,0},{2,1},{3,2},{4,3},{5,4},{6,5},{7,6},{8,7},{9,8},{10,9... | collective-permute-start | bytes 1757192 | tf_op jit(solution)/shard_map/ring/ppermute | solution.py:633
  79.8 19.0 %collective-permute-start.8 = (bf16[21,104,128]{2,1,0:T(8,128)(2,1)S(1)}, bf16[21,104,128]{2,1,0:T(8,128)(2,1)S(1)}, u32[]{:S(2)}, u32[]{:S(2)}) collective-permute-start(bf16[21,104,128]{2,1,0:T(8,128)(2,1)S(1)} %ring.39.after_ref), channel_id=1, source_target_pairs={{0,1},{1,2},{2,3},{3,4},{4,5},{5,6},{6,7},{7,8},{8,9},{9,10},{10,1... | collective-permute-start | bytes 1677320 | tf_op jit(solution)/shard_map/ring/ppermute | solution.py:636
  91.7 17.9 %collective-permute-start.11 = (bf16[22,104,128]{2,1,0:T(8,128)(2,1)S(1)}, bf16[22,104,128]{2,1,0:T(8,128)(2,1)S(1)}, u32[]{:S(2)}, u32[]{:S(2)}) collective-permute-start(bf16[22,104,128]{2,1,0:T(8,128)(2,1)S(1)} %ring.41.after_ref), channel_id=1, source_target_pairs={{0,15},{1,0},{2,1},{3,2},{4,3},{5,4},{6,5},{7,6},{8,7},{9,8},{10,9... | collective-permute-start | bytes 1757192 | tf_op jit(solution)/shard_map/ring/ppermute | solution.py:633
  99.2 18.1 %collective-permute-start.10 = (bf16[20,104,128]{2,1,0:T(8,128)(2,1)S(1)}, bf16[20,104,128]{2,1,0:T(8,128)(2,1)S(1)}, u32[]{:S(2)}, u32[]{:S(2)}) collective-permute-start(bf16[20,104,128]{2,1,0:T(8,128)(2,1)S(1)} %ring.43.after_ref), channel_id=1, source_target_pairs={{0,1},{1,2},{2,3},{3,4},{4,5},{5,6},{6,7},{7,8},{8,9},{9,10},{10,1... | collective-permute-start | bytes 1597448 | tf_op jit(solution)/shard_map/ring/ppermute | solution.py:636
  109.8 16.5 %collective-permute-start.13 = (bf16[22,104,128]{2,1,0:T(8,128)(2,1)S(1)}, bf16[22,104,128]{2,1,0:T(8,128)(2,1)S(1)}, u32[]{:S(2)}, u32[]{:S(2)}) collective-permute-start(bf16[22,104,128]{2,1,0:T(8,128)(2,1)S(1)} %ring.45.after_ref), channel_id=1, source_target_pairs={{0,15},{1,0},{2,1},{3,2},{4,3},{5,4},{6,5},{7,6},{8,7},{9,8},{10,9... | collective-permute-start | bytes 1757192 | tf_op jit(solution)/shard_map/ring/ppermute | solution.py:633
  117.5 17.1 %collective-permute-start.12 = (bf16[20,104,128]{2,1,0:T(8,128)(2,1)S(1)}, bf16[20,104,128]{2,1,0:T(8,128)(2,1)S(1)}, u32[]{:S(2)}, u32[]{:S(2)}) collective-permute-start(bf16[20,104,128]{2,1,0:T(8,128)(2,1)S(1)} %ring.47.after_ref), channel_id=1, source_target_pairs={{0,1},{1,2},{2,3},{3,4},{4,5},{5,6},{6,7},{7,8},{8,9},{9,10},{10,1... | collective-permute-start | bytes 1597448 | tf_op jit(solution)/shard_map/ring/ppermute | solution.py:636
  126.6 15.0 %collective-permute-start.15 = (bf16[22,104,128]{2,1,0:T(8,128)(2,1)S(1)}, bf16[22,104,128]{2,1,0:T(8,128)(2,1)S(1)}, u32[]{:S(2)}, u32[]{:S(2)}) collective-permute-start(bf16[22,104,128]{2,1,0:T(8,128)(2,1)S(1)} %ring.49.after_ref), channel_id=1, source_target_pairs={{0,15},{1,0},{2,1},{3,2},{4,3},{5,4},{6,5},{7,6},{8,7},{9,8},{10,9... | collective-permute-start | bytes 1757192 | tf_op jit(solution)/shard_map/ring/ppermute | solution.py:633
  134.8 17.7 %collective-permute-start.14 = (bf16[20,104,128]{2,1,0:T(8,128)(2,1)S(1)}, bf16[20,104,128]{2,1,0:T(8,128)(2,1)S(1)}, u32[]{:S(2)}, u32[]{:S(2)}) collective-permute-start(bf16[20,104,128]{2,1,0:T(8,128)(2,1)S(1)} %ring.51.after_ref), channel_id=1, source_target_pairs={{0,1},{1,2},{2,3},{3,4},{4,5},{5,6},{6,7},{7,8},{8,9},{9,10},{10,1... | collective-permute-start | bytes 1597448 | tf_op jit(solution)/shard_map/ring/ppermute | solution.py:636
  142.6 23.7 %collective-permute-start.17 = (bf16[22,104,128]{2,1,0:T(8,128)(2,1)}, bf16[22,104,128]{2,1,0:T(8,128)(2,1)}, u32[]{:S(2)}, u32[]{:S(2)}) collective-permute-start(bf16[22,104,128]{2,1,0:T(8,128)(2,1)} %ring.53.after_ref), channel_id=1, source_target_pairs={{0,15},{1,0},{2,1},{3,2},{4,3},{5,4},{6,5},{7,6},{8,7},{9,8},{10,9... | collective-permute-start | bytes 1757192 | tf_op jit(solution)/shard_map/ring/ppermute | solution.py:633
  150.0 5.5 %copy-start.2 = (bf16[2,64,4096]{2,1,0:T(8,128)(2,1)S(1)}, bf16[2,64,4096]{2,1,0:T(8,128)(2,1)}, u32[]{:S(2)}) copy-start(bf16[2,64,4096]{2,1,0:T(8,128)(2,1)} %student_ref.3) | copy-start | bytes 3145732
  153.7 12.7 %collective-permute-start.16 = (bf16[20,104,128]{2,1,0:T(8,128)(2,1)}, bf16[20,104,128]{2,1,0:T(8,128)(2,1)}, u32[]{:S(2)}, u32[]{:S(2)}) collective-permute-start(bf16[20,104,128]{2,1,0:T(8,128)(2,1)} %ring.55), channel_id=1, source_target_pairs={{0,1},{1,2},{2,3},{3,4},{4,5},{5,6},{6,7},{7,8},{8,9},{9,10},{10,1... | collective-permute-start | bytes 1597448 | tf_op jit(solution)/shard_map/ring/ppermute | solution.py:636
  158.8 1.5 copy-start
  166.3 1.7 copy-start.1
  168.1 12.0 %copy-start.3 = (bf16[2,64,4096]{2,1,0:T(8,128)(2,1)S(1)}, bf16[2,64,4096]{2,1,0:T(8,128)(2,1)}, u32[]{:S(2)}) copy-start(bf16[2,64,4096]{2,1,0:T(8,128)(2,1)} %student_ref.3) | copy-start | bytes 3145732
  168.1 12.0 %copy-start.8 = (bf16[2,16,4736]{2,1,0:T(8,128)(2,1)S(1)}, bf16[2,16,4736]{2,1,0:T(8,128)(2,1)}, u32[]{:S(2)}) copy-start(bf16[2,16,4736]{2,1,0:T(8,128)(2,1)} %copy-done.7) | copy-start | bytes 909316
  168.1 12.0 %copy-start.11 = (s32[512,2]{0,1:T(2,128)S(1)}, s32[512,2]{0,1:T(2,128)}, u32[]{:S(2)}) copy-start(s32[512,2]{0,1:T(2,128)} %param.12) | copy-start | bytes 12292
  174.1 16.1 %all-to-all-start.1 = ((f32[16,4,128]{2,1,0:T(4,128)}), f32[16,4,128]{2,1,0:T(4,128)S(1)}, u32[]{:S(2)}, u32[]{:S(2)}) async-start(f32[16,4,128]{2,1,0:T(4,128)} %map.1), calls=%async_computation.1 | async-start | bytes 65536 | tf_op jit(solution)/shard_map/finish/all_to_all | solution.py:671
  190.4 0.6 copy-start.12
Sparse Core Ops, SparseCore 0:
  62.6 30.5 all-gather.1

commit v12 on v11

--- a/solution.py
+++ b/solution.py
@@ -11,7 +11,7 @@
 K = 2
 W = 16
 ROWS = 104
-SIZES = ((24, 21, 21, 21, 20, 20, 20, 20), (14, 22, 22, 22, 22, 22, 22, 22))
+SIZES = ((24, 21, 21, 21, 20, 20, 20, 20), (10, 23, 23, 23, 23, 22, 22, 22))
 STARTS = tuple(tuple(sum(sizes[:f]) for f in range(len(sizes))) for sizes in SIZES)
 TINY = 1.2e-38
 
@@ -356,7 +356,7 @@
     third = total - first - second
     lane = lax.broadcasted_iota(jnp.int32, (rows, BLK), 1)
     home_ref[blocks] = jnp.where(
-        lane == 0, top, jnp.where(lane == 1, first, jnp.where(lane == 2, second, jnp.where(lane == 3, third, 0.0)))
+        lane < 32, top, jnp.where(lane < 64, first, jnp.where(lane < 96, second, third))
     ).astype(jnp.bfloat16)
     for out_ref, choice in zip((first_ref, second_ref), first_choice(blocks, place_ref, listed_ref)):
         for j, at in enumerate(choice):
@@ -447,16 +447,18 @@
     bring(item_ref, steps, ahead_ref, stage_ref)
     bring(item_ref, 2 * steps, behind_ref, stage_ref)
     holders = [h for h in range(steps + 1)] + [2 * steps + h for h in range(1, steps)]
-    peaks, sums = [], []
-    for h in holders:
-        stats = jnp.dot(spread, stage_ref[K * blocks + h], preferred_element_type=jnp.float32)
-        peaks.append(stats[:, 0:1])
-        sums.append(stats[:, 1:2] + stats[:, 2:3] + stats[:, 3:4])
-    peak = functools.reduce(jnp.maximum, peaks)
-    powers = [jnp.exp(p - peak) for p in peaks]
-    norm = sum(p * t for p, t in zip(powers, sums))
-    for h, power in zip(holders, powers):
-        scale_ref[h] = jnp.broadcast_to(power / norm, (rows, BLK))
+    lane = lax.broadcasted_iota(jnp.int32, (spread.shape[1], BLK), 1)
+    stats = jnp.zeros((spread.shape[1], BLK), jnp.float32)
+    for i, h in enumerate(holders):
+        stats = jnp.where((lane & 31) == i, stage_ref[K * blocks + h].astype(jnp.float32), stats)
+    stats = jnp.dot(spread, stats.astype(jnp.bfloat16), preferred_element_type=jnp.float32)
+    held = lax.broadcasted_iota(jnp.int32, (rows, BLK), 1) < len(holders)
+    peak = jnp.max(jnp.where(held, stats, -jnp.inf), axis=1, keepdims=True)
+    power = jnp.where(held, jnp.exp(jnp.where(held, stats, peak) - peak), 0.0)
+    sums = pltpu.roll(stats, 96, 1) + pltpu.roll(stats, 64, 1) + pltpu.roll(stats, 32, 1)
+    scale = power / jnp.sum(power * sums, axis=1, keepdims=True)
+    for i, h in enumerate(holders):
+        scale_ref[h] = jnp.broadcast_to(scale[:, i : i + 1], (rows, BLK))
     student_top = top_ref[...]
     mass = jnp.zeros((rows, BLK), jnp.float32)
     cross = jnp.zeros((rows, BLK), jnp.float32)

time: 199 us -> 198 us (level)
  the two profiles are of different devices: /device:TPU:24 before, /device:TPU:6 now
where the time goes in v12:
time: 198 us; the launch traced here: 194 us
  starting transfers between devices  69.9 us (35%)
  waiting for transfers between devices  63.3 us (32%)
  Pallas kernels  33.9 us (17%)
  between operations  15.2 us (8%)
  local copies, waits for them, and re-layouts  9.19 us (5%)
  other arithmetic  2.58 us (1%)
    ppermute x7, waiting for transfers between devices, shards(): came_behind.append(lax.ppermute(behind, ('seq', 'vocab'), backward))  42.3 us
    ppermute x7, starting transfers between devices, shards(): came_behind.append(lax.ppermute(behind, ('seq', 'vocab'), backward))  38.7 us
    ppermute x7, starting transfers between devices, shards(): came_ahead.append(lax.ppermute(ahead, ('seq', 'vocab'), forward))  13.4 us
    pallas_call x14, Pallas kernels, ready(): pl.pallas_call(functools.partial(ready_kernel, chain, step), out_shape=pl...  11.9 us
    ppermute x1, starting transfers between devices, shards(): came_behind = [lax.ppermute(behind, ('seq', 'vocab'), backward)]  10.6 us
    all_to_all x1, waiting for transfers between devices, shards(): lax.all_to_all(sums, 'vocab', split_axis=0, concat_axis=0, tiled=True)  10.1 us
    pallas_call x14, Pallas kernels, passed(): pl.pallas_call(functools.partial(pass_kernel, chain, step, home), out_sha...  8.18 us
    unnamed x37, local copies, waits for them, and re-layouts  7.05 us
  transfers between devices with their start and end apart: 20, of which 13 were waited for; matrix products, arithmetic and copies ran while one was open for 2% of the time, Pallas kernels for 14%

profile of v12, /device:TPU:6, one launch (start us, length us, event | category | flops | bytes accessed | tf_op | source)
XLA Modules:
  0.0 194.0 jit_solution(16265737698021109303)
XLA Ops:
  7.8 1.7 collective-permute-start.1
  12.2 1.8 collective-permute-done.low_ref
  16.5 10.6 %collective-permute-start.3 = (bf16[10,104,128]{2,1,0:T(8,128)(2,1)S(1)}, bf16[10,104,128]{2,1,0:T(8,128)(2,1)S(1)}, u32[]{:S(2)}, u32[]{:S(2)}) collective-permute-start(bf16[10,104,128]{2,1,0:T(8,128)(2,1)S(1)} %get-tuple-element.94), channel_id=1, source_target_pairs={{0,15},{1,0},{2,1},{3,2},{4,3},{5,4},{6,5},{7,6},{8,7},{9,8},{10,9... | collective-permute-start | bytes 798728 | tf_op jit(solution)/shard_map/ring/ppermute | solution.py:630
  27.2 1.9 collective-permute-start.2
  29.1 4.0 %plan.1 = (s32[8,256]{1,0:T(8,128)S(1)}, s32[8,128]{1,0:T(8,128)S(1)}, s32[8,128]{1,0:T(8,128)S(1)}) custom-call(s32[2]{0:T(128)S(1)} %pad_add_fusion.place_ref, s32[16,64]{1,0:T(8,128)S(1)} %reshape.251.listed_ref, s32[8,128]{1,0:T(8,128)S(1)} %get-tuple-element.88.after_ref), custom_call_target="tpu_custom_call" | custom-call | tf_op jit(solution)/shard_map/plan/pallas_call | solution.py:601
  33.7 5.1 %collective-permute-start.5 = (bf16[23,104,128]{2,1,0:T(8,128)(2,1)S(1)}, bf16[23,104,128]{2,1,0:T(8,128)(2,1)S(1)}, u32[]{:S(2)}, u32[]{:S(2)}) collective-permute-start(bf16[23,104,128]{2,1,0:T(8,128)(2,1)S(1)} %ring.29.after_ref), channel_id=1, source_target_pairs={{0,15},{1,0},{2,1},{3,2},{4,3},{5,4},{6,5},{7,6},{8,7},{9,8},{10,9... | collective-permute-start | bytes 1837064 | tf_op jit(solution)/shard_map/ring/ppermute | solution.py:635
  40.9 1.9 collective-permute-start.4
  43.3 5.8 %collective-permute-done.5.newest_ref.refs_1_.refs_9_ = bf16[23,104,128]{2,1,0:T(8,128)(2,1)S(1)} collective-permute-done((bf16[23,104,128]{2,1,0:T(8,128)(2,1)S(1)}, bf16[23,104,128]{2,1,0:T(8,128)(2,1)S(1)}, u32[]{:S(2)}, u32[]{:S(2)}) %collective-permute-start.5) | collective-permute-done | bytes 612384 | tf_op jit(solution)/shard_map/ring/ppermute | solution.py:635
  50.2 5.6 %collective-permute-start.7 = (bf16[23,104,128]{2,1,0:T(8,128)(2,1)}, bf16[23,104,128]{2,1,0:T(8,128)(2,1)S(1)}, u32[]{:S(2)}, u32[]{:S(2)}) collective-permute-start(bf16[23,104,128]{2,1,0:T(8,128)(2,1)} %ring.33.after_ref), channel_id=1, source_target_pairs={{0,15},{1,0},{2,1},{3,2},{4,3},{5,4},{6,5},{7,6},{8,7},{9,8},{10,9... | collective-permute-start | bytes 1837064 | tf_op jit(solution)/shard_map/ring/ppermute | solution.py:635
  57.4 1.9 collective-permute-start.6
  60.7 7.4 %collective-permute-done.7.newest_ref.refs_2_.refs_10_ = bf16[23,104,128]{2,1,0:T(8,128)(2,1)S(1)} collective-permute-done((bf16[23,104,128]{2,1,0:T(8,128)(2,1)}, bf16[23,104,128]{2,1,0:T(8,128)(2,1)S(1)}, u32[]{:S(2)}, u32[]{:S(2)}) %collective-permute-start.7) | collective-permute-done | bytes 612384 | tf_op jit(solution)/shard_map/ring/ppermute | solution.py:635
  68.4 5.6 %collective-permute-start.9 = (bf16[23,104,128]{2,1,0:T(8,128)(2,1)S(1)}, bf16[23,104,128]{2,1,0:T(8,128)(2,1)S(1)}, u32[]{:S(2)}, u32[]{:S(2)}) collective-permute-start(bf16[23,104,128]{2,1,0:T(8,128)(2,1)S(1)} %ring.37.after_ref), channel_id=1, source_target_pairs={{0,15},{1,0},{2,1},{3,2},{4,3},{5,4},{6,5},{7,6},{8,7},{9,8},{10,9... | collective-permute-start | bytes 1837064 | tf_op jit(solution)/shard_map/ring/ppermute | solution.py:635
  75.9 1.9 collective-permute-start.8
  78.5 8.2 %collective-permute-done.9.newest_ref.refs_3_.refs_11_ = bf16[23,104,128]{2,1,0:T(8,128)(2,1)S(1)} collective-permute-done((bf16[23,104,128]{2,1,0:T(8,128)(2,1)S(1)}, bf16[23,104,128]{2,1,0:T(8,128)(2,1)S(1)}, u32[]{:S(2)}, u32[]{:S(2)}) %collective-permute-start.9) | collective-permute-done | bytes 612384 | tf_op jit(solution)/shard_map/ring/ppermute | solution.py:635
  86.9 5.6 %collective-permute-start.11 = (bf16[23,104,128]{2,1,0:T(8,128)(2,1)S(1)}, bf16[23,104,128]{2,1,0:T(8,128)(2,1)S(1)}, u32[]{:S(2)}, u32[]{:S(2)}) collective-permute-start(bf16[23,104,128]{2,1,0:T(8,128)(2,1)S(1)} %ring.41.after_ref), channel_id=1, source_target_pairs={{0,15},{1,0},{2,1},{3,2},{4,3},{5,4},{6,5},{7,6},{8,7},{9,8},{10,9... | collective-permute-start | bytes 1837064 | tf_op jit(solution)/shard_map/ring/ppermute | solution.py:635
  94.6 1.9 collective-permute-start.10
  97.3 8.6 %collective-permute-done.11.newest_ref.refs_4_.refs_12_ = bf16[23,104,128]{2,1,0:T(8,128)(2,1)S(1)} collective-permute-done((bf16[23,104,128]{2,1,0:T(8,128)(2,1)S(1)}, bf16[23,104,128]{2,1,0:T(8,128)(2,1)S(1)}, u32[]{:S(2)}, u32[]{:S(2)}) %collective-permute-start.11) | collective-permute-done | bytes 612384 | tf_op jit(solution)/shard_map/ring/ppermute | solution.py:635
  106.2 5.6 %collective-permute-start.13 = (bf16[22,104,128]{2,1,0:T(8,128)(2,1)S(1)}, bf16[22,104,128]{2,1,0:T(8,128)(2,1)S(1)}, u32[]{:S(2)}, u32[]{:S(2)}) collective-permute-start(bf16[22,104,128]{2,1,0:T(8,128)(2,1)S(1)} %ring.45.after_ref), channel_id=1, source_target_pairs={{0,15},{1,0},{2,1},{3,2},{4,3},{5,4},{6,5},{7,6},{8,7},{9,8},{10,9... | collective-permute-start | bytes 1757192 | tf_op jit(solution)/shard_map/ring/ppermute | solution.py:635
  113.7 1.9 collective-permute-start.12
  116.3 7.1 %collective-permute-done.13.newest_ref.refs_13_.refs_5_ = bf16[22,104,128]{2,1,0:T(8,128)(2,1)S(1)} collective-permute-done((bf16[22,104,128]{2,1,0:T(8,128)(2,1)S(1)}, bf16[22,104,128]{2,1,0:T(8,128)(2,1)S(1)}, u32[]{:S(2)}, u32[]{:S(2)}) %collective-permute-start.13) | collective-permute-done | bytes 585760 | tf_op jit(solution)/shard_map/ring/ppermute | solution.py:635
  123.6 5.6 %collective-permute-start.15 = (bf16[22,104,128]{2,1,0:T(8,128)(2,1)S(1)}, bf16[22,104,128]{2,1,0:T(8,128)(2,1)S(1)}, u32[]{:S(2)}, u32[]{:S(2)}) collective-permute-start(bf16[22,104,128]{2,1,0:T(8,128)(2,1)S(1)} %ring.49.after_ref), channel_id=1, source_target_pairs={{0,15},{1,0},{2,1},{3,2},{4,3},{5,4},{6,5},{7,6},{8,7},{9,8},{10,9... | collective-permute-start | bytes 1757192 | tf_op jit(solution)/shard_map/ring/ppermute | solution.py:635
  131.1 1.9 collective-permute-start.14
  133.9 5.4 %collective-permute-done.15.refs_14_.newest_ref = bf16[22,104,128]{2,1,0:T(8,128)(2,1)S(1)} collective-permute-done((bf16[22,104,128]{2,1,0:T(8,128)(2,1)S(1)}, bf16[22,104,128]{2,1,0:T(8,128)(2,1)S(1)}, u32[]{:S(2)}, u32[]{:S(2)}) %collective-permute-start.15) | collective-permute-done | bytes 585760 | tf_op jit(solution)/shard_map/ring/ppermute | solution.py:635
  140.3 5.6 %collective-permute-start.17 = (bf16[22,104,128]{2,1,0:T(8,128)(2,1)}, bf16[22,104,128]{2,1,0:T(8,128)(2,1)}, u32[]{:S(2)}, u32[]{:S(2)}) collective-permute-start(bf16[22,104,128]{2,1,0:T(8,128)(2,1)} %ring.53.after_ref), channel_id=1, source_target_pairs={{0,15},{1,0},{2,1},{3,2},{4,3},{5,4},{6,5},{7,6},{8,7},{9,8},{10,9... | collective-permute-start | bytes 1757192 | tf_op jit(solution)/shard_map/ring/ppermute | solution.py:635
  145.9 1.8 ring.54.part_ref
  149.8 1.9 collective-permute-start.16
  153.1 2.3 %stage.1.held_ref = bf16[96,104,128]{2,1,0:T(8,128)(2,1)S(1)} custom-call(s32[8,128]{1,0:T(8,128)S(1)} %get-tuple-element.90.item_ref, bf16[38,104,128]{2,1,0:T(8,128)(2,1)S(1)} %get-tuple-element.91.home_ref.refs_0_, bf16[24,104,128]{2,1,0:T(8,128)(2,1)S(1)} %collective-permute-done.2.newest_ref.refs_0_.refs_1_, ...), custom_call_target="tpu_custom_call" | custom-call | tf_op jit(solution)/shard_map/stage/pallas_call | solution.py:651
  156.9 5.5 %collective-permute-done.16.ahead_ref = bf16[20,104,128]{2,1,0:T(8,128)(2,1)} collective-permute-done((bf16[20,104,128]{2,1,0:T(8,128)(2,1)}, bf16[20,104,128]{2,1,0:T(8,128)(2,1)}, u32[]{:S(2)}, u32[]{:S(2)}) %collective-permute-start.16) | collective-permute-done | bytes 532512 | tf_op jit(solution)/shard_map/ring/ppermute | solution.py:638
  162.4 1.7 copy-done.4
  165.0 5.3 %map.1 = f32[16,4,128]{2,1,0:T(4,128)} custom-call(s32[8,128]{1,0:T(8,128)S(1)} %get-tuple-element.90.item_ref, bf16[96,104,128]{2,1,0:T(8,128)(2,1)S(1)} %copy-done.4, bf16[20,104,128]{2,1,0:T(8,128)(2,1)} %collective-permute-done.16.ahead_ref, bf16[22,104,128]{2,1,0:T(8,128)(2,1)} %collective-permute-done.17.behind_ref, ...), custom_call_target="tpu_custom_call" | custom-call | tf_op jit(solution)/shard_map/map/pallas_call | solution.py:660
  170.3 3.5 %all-to-all-start.1 = ((f32[16,4,128]{2,1,0:T(4,128)}), f32[16,4,128]{2,1,0:T(4,128)S(1)}, u32[]{:S(2)}, u32[]{:S(2)}) async-start(f32[16,4,128]{2,1,0:T(4,128)} %map.1), calls=%async_computation.1 | async-start | bytes 65536 | tf_op jit(solution)/shard_map/finish/all_to_all | solution.py:673
  176.3 10.1 %all-to-all-done.1 = f32[16,4,128]{2,1,0:T(4,128)S(1)} async-done(((f32[16,4,128]{2,1,0:T(4,128)}), f32[16,4,128]{2,1,0:T(4,128)S(1)}, u32[]{:S(2)}, u32[]{:S(2)}) %all-to-all-start.1) | async-done | bytes 32800 | tf_op jit(solution)/shard_map/finish/all_to_all | solution.py:673
  (102 shorter events, 34.3 us)
Async XLA Ops:
  6.5 8.3 %copy-start.10 = (bf16[2,64,4736]{2,1,0:T(8,128)(2,1)S(1)}, bf16[2,64,4736]{2,1,0:T(8,128)(2,1)}, u32[]{:S(2)}) copy-start(bf16[2,64,4736]{2,1,0:T(8,128)(2,1)} %own_ref.1) | copy-start | bytes 3637252
  6.5 150.3 %all-gather.2.cloned.1.call-start = ((), (), s32[]{:S(2)}) async-start(), calls=%async_computation.2 | async-start | bytes 2621440 | tf_op jit(solution)/shard_map/weights/all_gather | solution.py:560
  7.7 6.2 %collective-permute-start = (bf16[2,16,4736]{2,1,0:T(8,128)(2,1)S(1)}, bf16[2,16,4736]{2,1,0:T(8,128)(2,1)S(1)}, u32[]{:S(2)}, u32[]{:S(2)}) collective-permute-start(bf16[2,16,4736]{2,1,0:T(8,128)(2,1)S(1)} %get-tuple-element.156), channel_id=1, source_target_pairs={{0,16},{16,32},{32,48},{48,64},{64,80},{80,96},{96,112},{112,0},{1... | collective-permute-start | bytes 909320 | tf_op jit(solution)/shard_map/halo/ppermute | solution.py:23
  7.8 7.0 %collective-permute-start.1 = (bf16[2,16,4736]{2,1,0:T(8,128)(2,1)S(1)}, bf16[2,16,4736]{2,1,0:T(8,128)(2,1)S(1)}, u32[]{:S(2)}, u32[]{:S(2)}) collective-permute-start(bf16[2,16,4736]{2,1,0:T(8,128)(2,1)S(1)} %get-tuple-element.155), channel_id=1, source_target_pairs={{16,0},{32,16},{48,32},{64,48},{80,64},{96,80},{112,96},{0,112},{1... | collective-permute-start | bytes 909320 | tf_op jit(solution)/shard_map/halo/ppermute | solution.py:24
  11.0 141.3 %copy-start.18 = (pred[192]{0:T(512)(128)(4,1)}, pred[192]{0:T(512)(128)(4,1)S(1)}, u32[]{:S(2)}) copy-start(pred[192]{0:T(512)(128)(4,1)S(1)} %fusion.20) | copy-start | bytes 580
  14.0 13.2 %copy-start.11 = (bf16[2,16,4736]{2,1,0:T(8,128)(2,1)}, bf16[2,16,4736]{2,1,0:T(8,128)(2,1)S(1)}, u32[]{:S(2)}) copy-start(bf16[2,16,4736]{2,1,0:T(8,128)(2,1)S(1)} %collective-permute-done.low_ref) | copy-start | bytes 909316
  14.8 12.4 %copy-start.13 = (bf16[2,16,4736]{2,1,0:T(8,128)(2,1)}, bf16[2,16,4736]{2,1,0:T(8,128)(2,1)S(1)}, u32[]{:S(2)}) copy-start(bf16[2,16,4736]{2,1,0:T(8,128)(2,1)S(1)} %collective-permute-done.1.high_ref) | copy-start | bytes 909316
  16.5 16.8 %collective-permute-start.3 = (bf16[10,104,128]{2,1,0:T(8,128)(2,1)S(1)}, bf16[10,104,128]{2,1,0:T(8,128)(2,1)S(1)}, u32[]{:S(2)}, u32[]{:S(2)}) collective-permute-start(bf16[10,104,128]{2,1,0:T(8,128)(2,1)S(1)} %get-tuple-element.94), channel_id=1, source_target_pairs={{0,15},{1,0},{2,1},{3,2},{4,3},{5,4},{6,5},{7,6},{8,7},{9,8},{10,9... | collective-permute-start | bytes 798728 | tf_op jit(solution)/shard_map/ring/ppermute | solution.py:630
  27.2 13.5 %collective-permute-start.2 = (bf16[24,104,128]{2,1,0:T(8,128)(2,1)S(1)}, bf16[24,104,128]{2,1,0:T(8,128)(2,1)S(1)}, u32[]{:S(2)}, u32[]{:S(2)}) collective-permute-start(bf16[24,104,128]{2,1,0:T(8,128)(2,1)S(1)} %get-tuple-element.92.after_ref), channel_id=1, source_target_pairs={{0,1},{1,2},{2,3},{3,4},{4,5},{5,6},{6,7},{7,8},{8,9},{9,10},{10,1... | collective-permute-start | bytes 1916936 | tf_op jit(solution)/shard_map/ring/ppermute | solution.py:631
  33.4 9.5 %copy-start = (bf16[10,104,128]{2,1,0:T(8,128)(2,1)}, bf16[10,104,128]{2,1,0:T(8,128)(2,1)S(1)}, u32[]{:S(2)}) copy-start(bf16[10,104,128]{2,1,0:T(8,128)(2,1)S(1)} %collective-permute-done.3.newest_ref.refs_0_.refs_8_) | copy-start | bytes 798724
  33.7 15.5 %collective-permute-start.5 = (bf16[23,104,128]{2,1,0:T(8,128)(2,1)S(1)}, bf16[23,104,128]{2,1,0:T(8,128)(2,1)S(1)}, u32[]{:S(2)}, u32[]{:S(2)}) collective-permute-start(bf16[23,104,128]{2,1,0:T(8,128)(2,1)S(1)} %ring.29.after_ref), channel_id=1, source_target_pairs={{0,15},{1,0},{2,1},{3,2},{4,3},{5,4},{6,5},{7,6},{8,7},{9,8},{10,9... | collective-permute-start | bytes 1837064 | tf_op jit(solution)/shard_map/ring/ppermute | solution.py:635
  40.9 15.3 %collective-permute-start.4 = (bf16[21,104,128]{2,1,0:T(8,128)(2,1)S(1)}, bf16[21,104,128]{2,1,0:T(8,128)(2,1)S(1)}, u32[]{:S(2)}, u32[]{:S(2)}) collective-permute-start(bf16[21,104,128]{2,1,0:T(8,128)(2,1)S(1)} %ring.31.after_ref), channel_id=1, source_target_pairs={{0,1},{1,2},{2,3},{3,4},{4,5},{5,6},{6,7},{7,8},{8,9},{9,10},{10,1... | collective-permute-start | bytes 1677320 | tf_op jit(solution)/shard_map/ring/ppermute | solution.py:638
  50.2 17.9 %collective-permute-start.7 = (bf16[23,104,128]{2,1,0:T(8,128)(2,1)}, bf16[23,104,128]{2,1,0:T(8,128)(2,1)S(1)}, u32[]{:S(2)}, u32[]{:S(2)}) collective-permute-start(bf16[23,104,128]{2,1,0:T(8,128)(2,1)} %ring.33.after_ref), channel_id=1, source_target_pairs={{0,15},{1,0},{2,1},{3,2},{4,3},{5,4},{6,5},{7,6},{8,7},{9,8},{10,9... | collective-permute-start | bytes 1837064 | tf_op jit(solution)/shard_map/ring/ppermute | solution.py:635
  57.4 17.2 %collective-permute-start.6 = (bf16[21,104,128]{2,1,0:T(8,128)(2,1)}, bf16[21,104,128]{2,1,0:T(8,128)(2,1)}, u32[]{:S(2)}, u32[]{:S(2)}) collective-permute-start(bf16[21,104,128]{2,1,0:T(8,128)(2,1)} %ring.35.after_ref), channel_id=1, source_target_pairs={{0,1},{1,2},{2,3},{3,4},{4,5},{5,6},{6,7},{7,8},{8,9},{9,10},{10,1... | collective-permute-start | bytes 1677320 | tf_op jit(solution)/shard_map/ring/ppermute | solution.py:638
  68.4 9.4 %copy-start.2 = (bf16[10,104,128]{2,1,0:T(8,128)(2,1)S(1)}, bf16[10,104,128]{2,1,0:T(8,128)(2,1)}, u32[]{:S(2)}) copy-start(bf16[10,104,128]{2,1,0:T(8,128)(2,1)} %copy-done) | copy-start | bytes 798724
  68.4 18.2 %collective-permute-start.9 = (bf16[23,104,128]{2,1,0:T(8,128)(2,1)S(1)}, bf16[23,104,128]{2,1,0:T(8,128)(2,1)S(1)}, u32[]{:S(2)}, u32[]{:S(2)}) collective-permute-start(bf16[23,104,128]{2,1,0:T(8,128)(2,1)S(1)} %ring.37.after_ref), channel_id=1, source_target_pairs={{0,15},{1,0},{2,1},{3,2},{4,3},{5,4},{6,5},{7,6},{8,7},{9,8},{10,9... | collective-permute-start | bytes 1837064 | tf_op jit(solution)/shard_map/ring/ppermute | solution.py:635
  75.9 18.4 %collective-permute-start.8 = (bf16[21,104,128]{2,1,0:T(8,128)(2,1)S(1)}, bf16[21,104,128]{2,1,0:T(8,128)(2,1)S(1)}, u32[]{:S(2)}, u32[]{:S(2)}) collective-permute-start(bf16[21,104,128]{2,1,0:T(8,128)(2,1)S(1)} %ring.39.after_ref), channel_id=1, source_target_pairs={{0,1},{1,2},{2,3},{3,4},{4,5},{5,6},{6,7},{7,8},{8,9},{9,10},{10,1... | collective-permute-start | bytes 1677320 | tf_op jit(solution)/shard_map/ring/ppermute | solution.py:638
  86.9 18.9 %collective-permute-start.11 = (bf16[23,104,128]{2,1,0:T(8,128)(2,1)S(1)}, bf16[23,104,128]{2,1,0:T(8,128)(2,1)S(1)}, u32[]{:S(2)}, u32[]{:S(2)}) collective-permute-start(bf16[23,104,128]{2,1,0:T(8,128)(2,1)S(1)} %ring.41.after_ref), channel_id=1, source_target_pairs={{0,15},{1,0},{2,1},{3,2},{4,3},{5,4},{6,5},{7,6},{8,7},{9,8},{10,9... | collective-permute-start | bytes 1837064 | tf_op jit(solution)/shard_map/ring/ppermute | solution.py:635
  94.6 18.8 %collective-permute-start.10 = (bf16[20,104,128]{2,1,0:T(8,128)(2,1)S(1)}, bf16[20,104,128]{2,1,0:T(8,128)(2,1)S(1)}, u32[]{:S(2)}, u32[]{:S(2)}) collective-permute-start(bf16[20,104,128]{2,1,0:T(8,128)(2,1)S(1)} %ring.43.after_ref), channel_id=1, source_target_pairs={{0,1},{1,2},{2,3},{3,4},{4,5},{5,6},{6,7},{7,8},{8,9},{9,10},{10,1... | collective-permute-start | bytes 1597448 | tf_op jit(solution)/shard_map/ring/ppermute | solution.py:638
  106.2 17.2 %collective-permute-start.13 = (bf16[22,104,128]{2,1,0:T(8,128)(2,1)S(1)}, bf16[22,104,128]{2,1,0:T(8,128)(2,1)S(1)}, u32[]{:S(2)}, u32[]{:S(2)}) collective-permute-start(bf16[22,104,128]{2,1,0:T(8,128)(2,1)S(1)} %ring.45.after_ref), channel_id=1, source_target_pairs={{0,15},{1,0},{2,1},{3,2},{4,3},{5,4},{6,5},{7,6},{8,7},{9,8},{10,9... | collective-permute-start | bytes 1757192 | tf_op jit(solution)/shard_map/ring/ppermute | solution.py:635
  113.7 17.2 %collective-permute-start.12 = (bf16[20,104,128]{2,1,0:T(8,128)(2,1)S(1)}, bf16[20,104,128]{2,1,0:T(8,128)(2,1)S(1)}, u32[]{:S(2)}, u32[]{:S(2)}) collective-permute-start(bf16[20,104,128]{2,1,0:T(8,128)(2,1)S(1)} %ring.47.after_ref), channel_id=1, source_target_pairs={{0,1},{1,2},{2,3},{3,4},{4,5},{5,6},{6,7},{7,8},{8,9},{9,10},{10,1... | collective-permute-start | bytes 1597448 | tf_op jit(solution)/shard_map/ring/ppermute | solution.py:638
  123.6 15.6 %collective-permute-start.15 = (bf16[22,104,128]{2,1,0:T(8,128)(2,1)S(1)}, bf16[22,104,128]{2,1,0:T(8,128)(2,1)S(1)}, u32[]{:S(2)}, u32[]{:S(2)}) collective-permute-start(bf16[22,104,128]{2,1,0:T(8,128)(2,1)S(1)} %ring.49.after_ref), channel_id=1, source_target_pairs={{0,15},{1,0},{2,1},{3,2},{4,3},{5,4},{6,5},{7,6},{8,7},{9,8},{10,9... | collective-permute-start | bytes 1757192 | tf_op jit(solution)/shard_map/ring/ppermute | solution.py:635
  131.1 17.6 %collective-permute-start.14 = (bf16[20,104,128]{2,1,0:T(8,128)(2,1)S(1)}, bf16[20,104,128]{2,1,0:T(8,128)(2,1)S(1)}, u32[]{:S(2)}, u32[]{:S(2)}) collective-permute-start(bf16[20,104,128]{2,1,0:T(8,128)(2,1)S(1)} %ring.51.after_ref), channel_id=1, source_target_pairs={{0,1},{1,2},{2,3},{3,4},{4,5},{5,6},{6,7},{7,8},{8,9},{9,10},{10,1... | collective-permute-start | bytes 1597448 | tf_op jit(solution)/shard_map/ring/ppermute | solution.py:638
  140.3 22.1 %collective-permute-start.17 = (bf16[22,104,128]{2,1,0:T(8,128)(2,1)}, bf16[22,104,128]{2,1,0:T(8,128)(2,1)}, u32[]{:S(2)}, u32[]{:S(2)}) collective-permute-start(bf16[22,104,128]{2,1,0:T(8,128)(2,1)} %ring.53.after_ref), channel_id=1, source_target_pairs={{0,15},{1,0},{2,1},{3,2},{4,3},{5,4},{6,5},{7,6},{8,7},{9,8},{10,9... | collective-permute-start | bytes 1757192 | tf_op jit(solution)/shard_map/ring/ppermute | solution.py:635
  147.7 4.0 %copy-start.7 = (bf16[2,64,4096]{2,1,0:T(8,128)(2,1)S(1)}, bf16[2,64,4096]{2,1,0:T(8,128)(2,1)}, u32[]{:S(2)}) copy-start(bf16[2,64,4096]{2,1,0:T(8,128)(2,1)} %student_ref.3) | copy-start | bytes 3145732
  149.8 12.7 %collective-permute-start.16 = (bf16[20,104,128]{2,1,0:T(8,128)(2,1)}, bf16[20,104,128]{2,1,0:T(8,128)(2,1)}, u32[]{:S(2)}, u32[]{:S(2)}) collective-permute-start(bf16[20,104,128]{2,1,0:T(8,128)(2,1)} %ring.55), channel_id=1, source_target_pairs={{0,1},{1,2},{2,3},{3,4},{4,5},{5,6},{6,7},{7,8},{8,9},{9,10},{10,1... | collective-permute-start | bytes 1597448 | tf_op jit(solution)/shard_map/ring/ppermute | solution.py:638
  165.0 8.8 %copy-start.19 = (pred[192]{0:T(512)(128)(4,1)S(1)}, pred[192]{0:T(512)(128)(4,1)}, u32[]{:S(2)}) copy-start(pred[192]{0:T(512)(128)(4,1)} %copy-done.18) | copy-start | bytes 580
  165.0 11.2 %copy-start.8 = (bf16[2,64,4096]{2,1,0:T(8,128)(2,1)S(1)}, bf16[2,64,4096]{2,1,0:T(8,128)(2,1)}, u32[]{:S(2)}) copy-start(bf16[2,64,4096]{2,1,0:T(8,128)(2,1)} %student_ref.3) | copy-start | bytes 3145732
  165.0 11.3 %copy-start.12 = (bf16[2,16,4736]{2,1,0:T(8,128)(2,1)S(1)}, bf16[2,16,4736]{2,1,0:T(8,128)(2,1)}, u32[]{:S(2)}) copy-start(bf16[2,16,4736]{2,1,0:T(8,128)(2,1)} %copy-done.11) | copy-start | bytes 909316
  165.0 11.3 %copy-start.15 = (s32[512,2]{0,1:T(2,128)S(1)}, s32[512,2]{0,1:T(2,128)}, u32[]{:S(2)}) copy-start(s32[512,2]{0,1:T(2,128)} %param.12) | copy-start | bytes 12292
  165.0 11.3 %copy-start.16 = (s32[2,64]{1,0:T(2,128)S(1)}, s32[2,64]{1,0:T(2,128)}, u32[]{:S(2)}) copy-start(s32[2,64]{1,0:T(2,128)} %get-tuple-element.146) | copy-start | bytes 1540
  170.3 16.1 %all-to-all-start.1 = ((f32[16,4,128]{2,1,0:T(4,128)}), f32[16,4,128]{2,1,0:T(4,128)S(1)}, u32[]{:S(2)}, u32[]{:S(2)}) async-start(f32[16,4,128]{2,1,0:T(4,128)} %map.1), calls=%async_computation.1 | async-start | bytes 65536 | tf_op jit(solution)/shard_map/finish/all_to_all | solution.py:673
  (6 other events, 6.2 us)
Sparse Core Ops, SparseCore 0:
  59.4 35.1 all-gather.1

commit v13 on v12

--- a/solution.py
+++ b/solution.py
@@ -219,7 +219,6 @@
     share = turn(jnp.broadcast_to(share, shape))[:1]
     share = jnp.sum(jnp.where(pair_lane == holder, share, 0), axis=1, keepdims=True)
     hops = ways(distance, inner, share, vocab_count)
-    scale = jnp.where(distance <= half, distance, 2 * vocab_count - distance)
     points = jnp.zeros((pair_count, 1), f32)
     for way in range(2):
         found = lax.dot_general(
@@ -234,15 +233,14 @@
     points = jnp.where(distance == 0, inner.astype(f32), points)
     by_stats = [jnp.sum(jnp.where(lane == blocks, p, 0.0), axis=1, keepdims=True) for p in pointer]
     hop = lax.broadcasted_iota(i32, (vocab_count, 1), 0)
-    stat_ok = [hop <= half, (hop >= 1) & (hop < half)]
-    points = jnp.concatenate(
-        [points] + [jnp.where(ok, p, 0.0) for ok, p in zip(stat_ok, by_stats)], axis=0
-    ).astype(i32)
-    other = jnp.concatenate(
-        [(hops[1] > 0).astype(i32), jnp.zeros((vocab_count, 1), i32), jnp.ones((vocab_count, 1), i32)], axis=0
-    )
+    mirror = ones(lax.broadcasted_iota(i32, small, 0) + lax.broadcasted_iota(i32, small, 1) == vocab_count)
+    mirrored = jnp.dot(
+        mirror, jnp.broadcast_to(by_stats[1], shape).astype(jnp.bfloat16), preferred_element_type=f32
+    )[:, :1]
+    points = jnp.concatenate([points, jnp.where(hop <= half, by_stats[0], mirrored)], axis=0).astype(i32)
+    other = jnp.concatenate([(hops[1] > 0).astype(i32), (hop > half).astype(i32)], axis=0)
     other = jnp.where(straight, other, 1 - other)
-    scale = jnp.concatenate([scale, jnp.zeros((2 * vocab_count, 1), i32)], axis=0)
+    scale = jnp.concatenate([distance, jnp.zeros((vocab_count, 1), i32)], axis=0)
     frame = jnp.zeros(points.shape, i32)
     base = jnp.full(points.shape, home, i32)
     limit = jnp.where(other == 1, SIZES[1][0], SIZES[0][0])
@@ -446,7 +444,7 @@
         stage_ref[i] = held_ref[i]
     bring(item_ref, steps, ahead_ref, stage_ref)
     bring(item_ref, 2 * steps, behind_ref, stage_ref)
-    holders = [h for h in range(steps + 1)] + [2 * steps + h for h in range(1, steps)]
+    holders = range(2 * steps)
     lane = lax.broadcasted_iota(jnp.int32, (spread.shape[1], BLK), 1)
     stats = jnp.zeros((spread.shape[1], BLK), jnp.float32)
     for i, h in enumerate(holders):
@@ -650,7 +648,7 @@
         early = (own, *came_ahead[:-1], *came_behind[:-1])
         held = pl.pallas_call(
             functools.partial(stage_kernel, steps),
-            out_shape=planes(pair_count + 2 * vocab_count),
+            out_shape=planes(pair_count + vocab_count),
             in_specs=[smem] + [vmem] * len(early),
             out_specs=vmem,
             compiler_params=room,
@@ -663,8 +661,8 @@
             in_specs=[smem] + [vmem] * 8,
             out_specs=vmem,
             scratch_shapes=[
-                pltpu.VMEM((pair_count + 2 * vocab_count, ROWS, BLK), jnp.bfloat16),
-                pltpu.VMEM((3 * steps, row_count, BLK), jnp.float32),
+                pltpu.VMEM((pair_count + vocab_count, ROWS, BLK), jnp.bfloat16),
+                pltpu.VMEM((vocab_count, row_count, BLK), jnp.float32),
             ],
             compiler_params=room,
         )(items, held, came_ahead[-1], came_behind[-1], spread, weights, student_logits, top, total)

time: 198 us -> 198 us (level)
    unnamed x37 -> x33, local copies, waits for them, and re-layouts: 7.05 us -> 6.79 us
  transfers between devices with their start and end apart: 20 -> 20, of which waited for: 13 -> 12; matrix products, arithmetic and copies ran while one was open for 2% -> 2% of each run, Pallas kernels for 14% -> 14%
where the time goes in v13:
time: 198 us; the launch traced here: 194 us
  starting transfers between devices  70.2 us (35%)
  waiting for transfers between devices  63.3 us (32%)
  Pallas kernels  33.8 us (17%)
  between operations  15.3 us (8%)
  local copies, waits for them, and re-layouts  9 us (5%)
  other arithmetic  2.65 us (1%)
    ppermute x7, waiting for transfers between devices, shards(): came_behind.append(lax.ppermute(behind, ('seq', 'vocab'), backward))  42.7 us
    ppermute x7, starting transfers between devices, shards(): came_behind.append(lax.ppermute(behind, ('seq', 'vocab'), backward))  38.7 us
    ppermute x7, starting transfers between devices, shards(): came_ahead.append(lax.ppermute(ahead, ('seq', 'vocab'), forward))  13.4 us
    pallas_call x14, Pallas kernels, ready(): pl.pallas_call(functools.partial(ready_kernel, chain, step), out_shape=pl...  11.9 us
    ppermute x1, starting transfers between devices, shards(): came_behind = [lax.ppermute(behind, ('seq', 'vocab'), backward)]  10.6 us
    all_to_all x1, waiting for transfers between devices, shards(): lax.all_to_all(sums, 'vocab', split_axis=0, concat_axis=0, tiled=True)  9.89 us
    pallas_call x14, Pallas kernels, passed(): pl.pallas_call(functools.partial(pass_kernel, chain, step, home), out_sha...  8.16 us
    unnamed x33, local copies, waits for them, and re-layouts  6.79 us
  transfers between devices with their start and end apart: 20, of which 12 were waited for; matrix products, arithmetic and copies ran while one was open for 2% of the time, Pallas kernels for 14%

profile of v13, /device:TPU:6, one launch (start us, length us, event | category | flops | bytes accessed | tf_op | source)
XLA Modules:
  0.0 194.3 jit_solution(5838141144000211181)
XLA Ops:
  7.8 1.7 collective-permute-start.1
  12.2 1.8 collective-permute-done.low_ref
  16.5 10.6 %collective-permute-start.3 = (bf16[10,104,128]{2,1,0:T(8,128)(2,1)S(1)}, bf16[10,104,128]{2,1,0:T(8,128)(2,1)S(1)}, u32[]{:S(2)}, u32[]{:S(2)}) collective-permute-start(bf16[10,104,128]{2,1,0:T(8,128)(2,1)S(1)} %get-tuple-element.94), channel_id=1, source_target_pairs={{0,15},{1,0},{2,1},{3,2},{4,3},{5,4},{6,5},{7,6},{8,7},{9,8},{10,9... | collective-permute-start | bytes 798728 | tf_op jit(solution)/shard_map/ring/ppermute | solution.py:628
  27.2 1.9 collective-permute-start.2
  29.1 4.1 %plan.1 = (s32[8,256]{1,0:T(8,128)S(1)}, s32[8,128]{1,0:T(8,128)S(1)}, s32[8,128]{1,0:T(8,128)S(1)}) custom-call(s32[2]{0:T(128)S(1)} %pad_add_fusion.place_ref, s32[16,64]{1,0:T(8,128)S(1)} %reshape.251.listed_ref, s32[8,128]{1,0:T(8,128)S(1)} %get-tuple-element.88.after_ref), custom_call_target="tpu_custom_call" | custom-call | tf_op jit(solution)/shard_map/plan/pallas_call | solution.py:599
  33.8 5.1 %collective-permute-start.5 = (bf16[23,104,128]{2,1,0:T(8,128)(2,1)S(1)}, bf16[23,104,128]{2,1,0:T(8,128)(2,1)S(1)}, u32[]{:S(2)}, u32[]{:S(2)}) collective-permute-start(bf16[23,104,128]{2,1,0:T(8,128)(2,1)S(1)} %ring.29.after_ref), channel_id=1, source_target_pairs={{0,15},{1,0},{2,1},{3,2},{4,3},{5,4},{6,5},{7,6},{8,7},{9,8},{10,9... | collective-permute-start | bytes 1837064 | tf_op jit(solution)/shard_map/ring/ppermute | solution.py:633
  40.9 1.9 collective-permute-start.4
  43.3 6.1 %collective-permute-done.5.newest_ref.refs_1_.refs_9_ = bf16[23,104,128]{2,1,0:T(8,128)(2,1)S(1)} collective-permute-done((bf16[23,104,128]{2,1,0:T(8,128)(2,1)S(1)}, bf16[23,104,128]{2,1,0:T(8,128)(2,1)S(1)}, u32[]{:S(2)}, u32[]{:S(2)}) %collective-permute-start.5) | collective-permute-done | bytes 612384 | tf_op jit(solution)/shard_map/ring/ppermute | solution.py:633
  50.5 5.6 %collective-permute-start.7 = (bf16[23,104,128]{2,1,0:T(8,128)(2,1)}, bf16[23,104,128]{2,1,0:T(8,128)(2,1)S(1)}, u32[]{:S(2)}, u32[]{:S(2)}) collective-permute-start(bf16[23,104,128]{2,1,0:T(8,128)(2,1)} %ring.33.after_ref), channel_id=1, source_target_pairs={{0,15},{1,0},{2,1},{3,2},{4,3},{5,4},{6,5},{7,6},{8,7},{9,8},{10,9... | collective-permute-start | bytes 1837064 | tf_op jit(solution)/shard_map/ring/ppermute | solution.py:633
  57.6 1.9 collective-permute-start.6
  61.0 7.5 %collective-permute-done.7.newest_ref.refs_2_.refs_10_ = bf16[23,104,128]{2,1,0:T(8,128)(2,1)S(1)} collective-permute-done((bf16[23,104,128]{2,1,0:T(8,128)(2,1)}, bf16[23,104,128]{2,1,0:T(8,128)(2,1)S(1)}, u32[]{:S(2)}, u32[]{:S(2)}) %collective-permute-start.7) | collective-permute-done | bytes 612384 | tf_op jit(solution)/shard_map/ring/ppermute | solution.py:633
  68.8 5.6 %collective-permute-start.9 = (bf16[23,104,128]{2,1,0:T(8,128)(2,1)S(1)}, bf16[23,104,128]{2,1,0:T(8,128)(2,1)S(1)}, u32[]{:S(2)}, u32[]{:S(2)}) collective-permute-start(bf16[23,104,128]{2,1,0:T(8,128)(2,1)S(1)} %ring.37.after_ref), channel_id=1, source_target_pairs={{0,15},{1,0},{2,1},{3,2},{4,3},{5,4},{6,5},{7,6},{8,7},{9,8},{10,9... | collective-permute-start | bytes 1837064 | tf_op jit(solution)/shard_map/ring/ppermute | solution.py:633
  76.2 1.9 collective-permute-start.8
  78.8 8.3 %collective-permute-done.9.newest_ref.refs_3_.refs_11_ = bf16[23,104,128]{2,1,0:T(8,128)(2,1)S(1)} collective-permute-done((bf16[23,104,128]{2,1,0:T(8,128)(2,1)S(1)}, bf16[23,104,128]{2,1,0:T(8,128)(2,1)S(1)}, u32[]{:S(2)}, u32[]{:S(2)}) %collective-permute-start.9) | collective-permute-done | bytes 612384 | tf_op jit(solution)/shard_map/ring/ppermute | solution.py:633
  87.5 5.6 %collective-permute-start.11 = (bf16[23,104,128]{2,1,0:T(8,128)(2,1)S(1)}, bf16[23,104,128]{2,1,0:T(8,128)(2,1)S(1)}, u32[]{:S(2)}, u32[]{:S(2)}) collective-permute-start(bf16[23,104,128]{2,1,0:T(8,128)(2,1)S(1)} %ring.41.after_ref), channel_id=1, source_target_pairs={{0,15},{1,0},{2,1},{3,2},{4,3},{5,4},{6,5},{7,6},{8,7},{9,8},{10,9... | collective-permute-start | bytes 1837064 | tf_op jit(solution)/shard_map/ring/ppermute | solution.py:633
  94.9 1.9 collective-permute-start.10
  97.7 8.7 %collective-permute-done.11.newest_ref.refs_4_.refs_12_ = bf16[23,104,128]{2,1,0:T(8,128)(2,1)S(1)} collective-permute-done((bf16[23,104,128]{2,1,0:T(8,128)(2,1)S(1)}, bf16[23,104,128]{2,1,0:T(8,128)(2,1)S(1)}, u32[]{:S(2)}, u32[]{:S(2)}) %collective-permute-start.11) | collective-permute-done | bytes 612384 | tf_op jit(solution)/shard_map/ring/ppermute | solution.py:633
  106.7 5.6 %collective-permute-start.13 = (bf16[22,104,128]{2,1,0:T(8,128)(2,1)S(1)}, bf16[22,104,128]{2,1,0:T(8,128)(2,1)S(1)}, u32[]{:S(2)}, u32[]{:S(2)}) collective-permute-start(bf16[22,104,128]{2,1,0:T(8,128)(2,1)S(1)} %ring.45.after_ref), channel_id=1, source_target_pairs={{0,15},{1,0},{2,1},{3,2},{4,3},{5,4},{6,5},{7,6},{8,7},{9,8},{10,9... | collective-permute-start | bytes 1757192 | tf_op jit(solution)/shard_map/ring/ppermute | solution.py:633
  114.2 1.9 collective-permute-start.12
  116.8 6.9 %collective-permute-done.13.newest_ref.refs_13_.refs_5_ = bf16[22,104,128]{2,1,0:T(8,128)(2,1)S(1)} collective-permute-done((bf16[22,104,128]{2,1,0:T(8,128)(2,1)S(1)}, bf16[22,104,128]{2,1,0:T(8,128)(2,1)S(1)}, u32[]{:S(2)}, u32[]{:S(2)}) %collective-permute-start.13) | collective-permute-done | bytes 585760 | tf_op jit(solution)/shard_map/ring/ppermute | solution.py:633
  124.0 5.6 %collective-permute-start.15 = (bf16[22,104,128]{2,1,0:T(8,128)(2,1)S(1)}, bf16[22,104,128]{2,1,0:T(8,128)(2,1)S(1)}, u32[]{:S(2)}, u32[]{:S(2)}) collective-permute-start(bf16[22,104,128]{2,1,0:T(8,128)(2,1)S(1)} %ring.49.after_ref), channel_id=1, source_target_pairs={{0,15},{1,0},{2,1},{3,2},{4,3},{5,4},{6,5},{7,6},{8,7},{9,8},{10,9... | collective-permute-start | bytes 1757192 | tf_op jit(solution)/shard_map/ring/ppermute | solution.py:633
  129.6 1.7 ring.50.part_ref
  131.6 1.9 collective-permute-start.14
  134.4 5.1 %collective-permute-done.15.refs_14_.newest_ref = bf16[22,104,128]{2,1,0:T(8,128)(2,1)S(1)} collective-permute-done((bf16[22,104,128]{2,1,0:T(8,128)(2,1)S(1)}, bf16[22,104,128]{2,1,0:T(8,128)(2,1)S(1)}, u32[]{:S(2)}, u32[]{:S(2)}) %collective-permute-start.15) | collective-permute-done | bytes 585760 | tf_op jit(solution)/shard_map/ring/ppermute | solution.py:633
  140.6 5.6 %collective-permute-start.17 = (bf16[22,104,128]{2,1,0:T(8,128)(2,1)}, bf16[22,104,128]{2,1,0:T(8,128)(2,1)}, u32[]{:S(2)}, u32[]{:S(2)}) collective-permute-start(bf16[22,104,128]{2,1,0:T(8,128)(2,1)} %ring.53.after_ref), channel_id=1, source_target_pairs={{0,15},{1,0},{2,1},{3,2},{4,3},{5,4},{6,5},{7,6},{8,7},{9,8},{10,9... | collective-permute-start | bytes 1757192 | tf_op jit(solution)/shard_map/ring/ppermute | solution.py:633
  146.2 1.8 ring.54.part_ref
  149.9 1.9 collective-permute-start.16
  153.2 2.1 %stage.1.held_ref = bf16[80,104,128]{2,1,0:T(8,128)(2,1)S(1)} custom-call(s32[8,128]{1,0:T(8,128)S(1)} %get-tuple-element.90.item_ref, bf16[38,104,128]{2,1,0:T(8,128)(2,1)S(1)} %get-tuple-element.91.home_ref.refs_0_, bf16[24,104,128]{2,1,0:T(8,128)(2,1)S(1)} %collective-permute-done.2.newest_ref.refs_0_.refs_1_, ...), custom_call_target="tpu_custom_call" | custom-call | tf_op jit(solution)/shard_map/stage/pallas_call | solution.py:649
  156.6 5.9 %collective-permute-done.16.ahead_ref = bf16[20,104,128]{2,1,0:T(8,128)(2,1)} collective-permute-done((bf16[20,104,128]{2,1,0:T(8,128)(2,1)}, bf16[20,104,128]{2,1,0:T(8,128)(2,1)}, u32[]{:S(2)}, u32[]{:S(2)}) %collective-permute-start.16) | collective-permute-done | bytes 532512 | tf_op jit(solution)/shard_map/ring/ppermute | solution.py:636
  165.0 5.2 %map.1 = f32[16,4,128]{2,1,0:T(4,128)} custom-call(s32[8,128]{1,0:T(8,128)S(1)} %get-tuple-element.90.item_ref, bf16[80,104,128]{2,1,0:T(8,128)(2,1)S(1)} %copy-done.4, bf16[20,104,128]{2,1,0:T(8,128)(2,1)} %collective-permute-done.16.ahead_ref, bf16[22,104,128]{2,1,0:T(8,128)(2,1)} %collective-permute-done.17.behind_ref, ...), custom_call_target="tpu_custom_call" | custom-call | tf_op jit(solution)/shard_map/map/pallas_call | solution.py:658
  170.2 3.8 %all-to-all-start.1 = ((f32[16,4,128]{2,1,0:T(4,128)}), f32[16,4,128]{2,1,0:T(4,128)S(1)}, u32[]{:S(2)}, u32[]{:S(2)}) async-start(f32[16,4,128]{2,1,0:T(4,128)} %map.1), calls=%async_computation.1 | async-start | bytes 65536 | tf_op jit(solution)/shard_map/finish/all_to_all | solution.py:671
  176.7 9.9 %all-to-all-done.1 = f32[16,4,128]{2,1,0:T(4,128)S(1)} async-done(((f32[16,4,128]{2,1,0:T(4,128)}), f32[16,4,128]{2,1,0:T(4,128)S(1)}, u32[]{:S(2)}, u32[]{:S(2)}) %all-to-all-start.1) | async-done | bytes 32800 | tf_op jit(solution)/shard_map/finish/all_to_all | solution.py:671
  (98 shorter events, 33.8 us)
Async XLA Ops:
  6.5 8.3 %copy-start.10 = (bf16[2,64,4736]{2,1,0:T(8,128)(2,1)S(1)}, bf16[2,64,4736]{2,1,0:T(8,128)(2,1)}, u32[]{:S(2)}) copy-start(bf16[2,64,4736]{2,1,0:T(8,128)(2,1)} %own_ref.1) | copy-start | bytes 3637252
  6.5 150.1 %all-gather.2.cloned.1.call-start = ((), (), s32[]{:S(2)}) async-start(), calls=%async_computation.2 | async-start | bytes 2621440 | tf_op jit(solution)/shard_map/weights/all_gather | solution.py:558
  7.7 6.2 %collective-permute-start = (bf16[2,16,4736]{2,1,0:T(8,128)(2,1)S(1)}, bf16[2,16,4736]{2,1,0:T(8,128)(2,1)S(1)}, u32[]{:S(2)}, u32[]{:S(2)}) collective-permute-start(bf16[2,16,4736]{2,1,0:T(8,128)(2,1)S(1)} %get-tuple-element.156), channel_id=1, source_target_pairs={{0,16},{16,32},{32,48},{48,64},{64,80},{80,96},{96,112},{112,0},{1... | collective-permute-start | bytes 909320 | tf_op jit(solution)/shard_map/halo/ppermute | solution.py:23
  7.8 7.0 %collective-permute-start.1 = (bf16[2,16,4736]{2,1,0:T(8,128)(2,1)S(1)}, bf16[2,16,4736]{2,1,0:T(8,128)(2,1)S(1)}, u32[]{:S(2)}, u32[]{:S(2)}) collective-permute-start(bf16[2,16,4736]{2,1,0:T(8,128)(2,1)S(1)} %get-tuple-element.155), channel_id=1, source_target_pairs={{16,0},{32,16},{48,32},{64,48},{80,64},{96,80},{112,96},{0,112},{1... | collective-permute-start | bytes 909320 | tf_op jit(solution)/shard_map/halo/ppermute | solution.py:24
  11.0 141.4 %copy-start.18 = (pred[192]{0:T(512)(128)(4,1)}, pred[192]{0:T(512)(128)(4,1)S(1)}, u32[]{:S(2)}) copy-start(pred[192]{0:T(512)(128)(4,1)S(1)} %fusion.20) | copy-start | bytes 580
  14.0 13.2 %copy-start.12 = (bf16[2,16,4736]{2,1,0:T(8,128)(2,1)}, bf16[2,16,4736]{2,1,0:T(8,128)(2,1)S(1)}, u32[]{:S(2)}) copy-start(bf16[2,16,4736]{2,1,0:T(8,128)(2,1)S(1)} %collective-permute-done.low_ref) | copy-start | bytes 909316
  14.8 12.4 %copy-start.14 = (bf16[2,16,4736]{2,1,0:T(8,128)(2,1)}, bf16[2,16,4736]{2,1,0:T(8,128)(2,1)S(1)}, u32[]{:S(2)}) copy-start(bf16[2,16,4736]{2,1,0:T(8,128)(2,1)S(1)} %collective-permute-done.1.high_ref) | copy-start | bytes 909316
  16.5 17.0 %collective-permute-start.3 = (bf16[10,104,128]{2,1,0:T(8,128)(2,1)S(1)}, bf16[10,104,128]{2,1,0:T(8,128)(2,1)S(1)}, u32[]{:S(2)}, u32[]{:S(2)}) collective-permute-start(bf16[10,104,128]{2,1,0:T(8,128)(2,1)S(1)} %get-tuple-element.94), channel_id=1, source_target_pairs={{0,15},{1,0},{2,1},{3,2},{4,3},{5,4},{6,5},{7,6},{8,7},{9,8},{10,9... | collective-permute-start | bytes 798728 | tf_op jit(solution)/shard_map/ring/ppermute | solution.py:628
  27.2 13.5 %collective-permute-start.2 = (bf16[24,104,128]{2,1,0:T(8,128)(2,1)S(1)}, bf16[24,104,128]{2,1,0:T(8,128)(2,1)S(1)}, u32[]{:S(2)}, u32[]{:S(2)}) collective-permute-start(bf16[24,104,128]{2,1,0:T(8,128)(2,1)S(1)} %get-tuple-element.92.after_ref), channel_id=1, source_target_pairs={{0,1},{1,2},{2,3},{3,4},{4,5},{5,6},{6,7},{7,8},{8,9},{9,10},{10,1... | collective-permute-start | bytes 1916936 | tf_op jit(solution)/shard_map/ring/ppermute | solution.py:629
  33.5 9.4 %copy-start = (bf16[10,104,128]{2,1,0:T(8,128)(2,1)}, bf16[10,104,128]{2,1,0:T(8,128)(2,1)S(1)}, u32[]{:S(2)}) copy-start(bf16[10,104,128]{2,1,0:T(8,128)(2,1)S(1)} %collective-permute-done.3.newest_ref.refs_0_.refs_8_) | copy-start | bytes 798724
  33.8 15.6 %collective-permute-start.5 = (bf16[23,104,128]{2,1,0:T(8,128)(2,1)S(1)}, bf16[23,104,128]{2,1,0:T(8,128)(2,1)S(1)}, u32[]{:S(2)}, u32[]{:S(2)}) collective-permute-start(bf16[23,104,128]{2,1,0:T(8,128)(2,1)S(1)} %ring.29.after_ref), channel_id=1, source_target_pairs={{0,15},{1,0},{2,1},{3,2},{4,3},{5,4},{6,5},{7,6},{8,7},{9,8},{10,9... | collective-permute-start | bytes 1837064 | tf_op jit(solution)/shard_map/ring/ppermute | solution.py:633
  40.9 15.6 %collective-permute-start.4 = (bf16[21,104,128]{2,1,0:T(8,128)(2,1)S(1)}, bf16[21,104,128]{2,1,0:T(8,128)(2,1)S(1)}, u32[]{:S(2)}, u32[]{:S(2)}) collective-permute-start(bf16[21,104,128]{2,1,0:T(8,128)(2,1)S(1)} %ring.31.after_ref), channel_id=1, source_target_pairs={{0,1},{1,2},{2,3},{3,4},{4,5},{5,6},{6,7},{7,8},{8,9},{9,10},{10,1... | collective-permute-start | bytes 1677320 | tf_op jit(solution)/shard_map/ring/ppermute | solution.py:636
  50.5 18.0 %collective-permute-start.7 = (bf16[23,104,128]{2,1,0:T(8,128)(2,1)}, bf16[23,104,128]{2,1,0:T(8,128)(2,1)S(1)}, u32[]{:S(2)}, u32[]{:S(2)}) collective-permute-start(bf16[23,104,128]{2,1,0:T(8,128)(2,1)} %ring.33.after_ref), channel_id=1, source_target_pairs={{0,15},{1,0},{2,1},{3,2},{4,3},{5,4},{6,5},{7,6},{8,7},{9,8},{10,9... | collective-permute-start | bytes 1837064 | tf_op jit(solution)/shard_map/ring/ppermute | solution.py:633
  57.6 17.2 %collective-permute-start.6 = (bf16[21,104,128]{2,1,0:T(8,128)(2,1)}, bf16[21,104,128]{2,1,0:T(8,128)(2,1)}, u32[]{:S(2)}, u32[]{:S(2)}) collective-permute-start(bf16[21,104,128]{2,1,0:T(8,128)(2,1)} %ring.35.after_ref), channel_id=1, source_target_pairs={{0,1},{1,2},{2,3},{3,4},{4,5},{5,6},{6,7},{7,8},{8,9},{9,10},{10,1... | collective-permute-start | bytes 1677320 | tf_op jit(solution)/shard_map/ring/ppermute | solution.py:636
  68.8 9.4 %copy-start.2 = (bf16[10,104,128]{2,1,0:T(8,128)(2,1)S(1)}, bf16[10,104,128]{2,1,0:T(8,128)(2,1)}, u32[]{:S(2)}) copy-start(bf16[10,104,128]{2,1,0:T(8,128)(2,1)} %copy-done) | copy-start | bytes 798724
  68.8 18.4 %collective-permute-start.9 = (bf16[23,104,128]{2,1,0:T(8,128)(2,1)S(1)}, bf16[23,104,128]{2,1,0:T(8,128)(2,1)S(1)}, u32[]{:S(2)}, u32[]{:S(2)}) collective-permute-start(bf16[23,104,128]{2,1,0:T(8,128)(2,1)S(1)} %ring.37.after_ref), channel_id=1, source_target_pairs={{0,15},{1,0},{2,1},{3,2},{4,3},{5,4},{6,5},{7,6},{8,7},{9,8},{10,9... | collective-permute-start | bytes 1837064 | tf_op jit(solution)/shard_map/ring/ppermute | solution.py:633
  76.2 18.4 %collective-permute-start.8 = (bf16[21,104,128]{2,1,0:T(8,128)(2,1)S(1)}, bf16[21,104,128]{2,1,0:T(8,128)(2,1)S(1)}, u32[]{:S(2)}, u32[]{:S(2)}) collective-permute-start(bf16[21,104,128]{2,1,0:T(8,128)(2,1)S(1)} %ring.39.after_ref), channel_id=1, source_target_pairs={{0,1},{1,2},{2,3},{3,4},{4,5},{5,6},{6,7},{7,8},{8,9},{9,10},{10,1... | collective-permute-start | bytes 1677320 | tf_op jit(solution)/shard_map/ring/ppermute | solution.py:636
  87.5 18.9 %collective-permute-start.11 = (bf16[23,104,128]{2,1,0:T(8,128)(2,1)S(1)}, bf16[23,104,128]{2,1,0:T(8,128)(2,1)S(1)}, u32[]{:S(2)}, u32[]{:S(2)}) collective-permute-start(bf16[23,104,128]{2,1,0:T(8,128)(2,1)S(1)} %ring.41.after_ref), channel_id=1, source_target_pairs={{0,15},{1,0},{2,1},{3,2},{4,3},{5,4},{6,5},{7,6},{8,7},{9,8},{10,9... | collective-permute-start | bytes 1837064 | tf_op jit(solution)/shard_map/ring/ppermute | solution.py:633
  94.9 19.0 %collective-permute-start.10 = (bf16[20,104,128]{2,1,0:T(8,128)(2,1)S(1)}, bf16[20,104,128]{2,1,0:T(8,128)(2,1)S(1)}, u32[]{:S(2)}, u32[]{:S(2)}) collective-permute-start(bf16[20,104,128]{2,1,0:T(8,128)(2,1)S(1)} %ring.43.after_ref), channel_id=1, source_target_pairs={{0,1},{1,2},{2,3},{3,4},{4,5},{5,6},{6,7},{7,8},{8,9},{9,10},{10,1... | collective-permute-start | bytes 1597448 | tf_op jit(solution)/shard_map/ring/ppermute | solution.py:636
  106.7 17.0 %collective-permute-start.13 = (bf16[22,104,128]{2,1,0:T(8,128)(2,1)S(1)}, bf16[22,104,128]{2,1,0:T(8,128)(2,1)S(1)}, u32[]{:S(2)}, u32[]{:S(2)}) collective-permute-start(bf16[22,104,128]{2,1,0:T(8,128)(2,1)S(1)} %ring.45.after_ref), channel_id=1, source_target_pairs={{0,15},{1,0},{2,1},{3,2},{4,3},{5,4},{6,5},{7,6},{8,7},{9,8},{10,9... | collective-permute-start | bytes 1757192 | tf_op jit(solution)/shard_map/ring/ppermute | solution.py:633
  114.2 17.1 %collective-permute-start.12 = (bf16[20,104,128]{2,1,0:T(8,128)(2,1)S(1)}, bf16[20,104,128]{2,1,0:T(8,128)(2,1)S(1)}, u32[]{:S(2)}, u32[]{:S(2)}) collective-permute-start(bf16[20,104,128]{2,1,0:T(8,128)(2,1)S(1)} %ring.47.after_ref), channel_id=1, source_target_pairs={{0,1},{1,2},{2,3},{3,4},{4,5},{5,6},{6,7},{7,8},{8,9},{9,10},{10,1... | collective-permute-start | bytes 1597448 | tf_op jit(solution)/shard_map/ring/ppermute | solution.py:636
  124.0 15.5 %collective-permute-start.15 = (bf16[22,104,128]{2,1,0:T(8,128)(2,1)S(1)}, bf16[22,104,128]{2,1,0:T(8,128)(2,1)S(1)}, u32[]{:S(2)}, u32[]{:S(2)}) collective-permute-start(bf16[22,104,128]{2,1,0:T(8,128)(2,1)S(1)} %ring.49.after_ref), channel_id=1, source_target_pairs={{0,15},{1,0},{2,1},{3,2},{4,3},{5,4},{6,5},{7,6},{8,7},{9,8},{10,9... | collective-permute-start | bytes 1757192 | tf_op jit(solution)/shard_map/ring/ppermute | solution.py:633
  131.6 17.2 %collective-permute-start.14 = (bf16[20,104,128]{2,1,0:T(8,128)(2,1)S(1)}, bf16[20,104,128]{2,1,0:T(8,128)(2,1)S(1)}, u32[]{:S(2)}, u32[]{:S(2)}) collective-permute-start(bf16[20,104,128]{2,1,0:T(8,128)(2,1)S(1)} %ring.51.after_ref), channel_id=1, source_target_pairs={{0,1},{1,2},{2,3},{3,4},{4,5},{5,6},{6,7},{7,8},{8,9},{9,10},{10,1... | collective-permute-start | bytes 1597448 | tf_op jit(solution)/shard_map/ring/ppermute | solution.py:636
  140.6 22.0 %collective-permute-start.17 = (bf16[22,104,128]{2,1,0:T(8,128)(2,1)}, bf16[22,104,128]{2,1,0:T(8,128)(2,1)}, u32[]{:S(2)}, u32[]{:S(2)}) collective-permute-start(bf16[22,104,128]{2,1,0:T(8,128)(2,1)} %ring.53.after_ref), channel_id=1, source_target_pairs={{0,15},{1,0},{2,1},{3,2},{4,3},{5,4},{6,5},{7,6},{8,7},{9,8},{10,9... | collective-permute-start | bytes 1757192 | tf_op jit(solution)/shard_map/ring/ppermute | solution.py:633
  148.0 3.8 %copy-start.7 = (bf16[2,64,4096]{2,1,0:T(8,128)(2,1)S(1)}, bf16[2,64,4096]{2,1,0:T(8,128)(2,1)}, u32[]{:S(2)}) copy-start(bf16[2,64,4096]{2,1,0:T(8,128)(2,1)} %student_ref.3) | copy-start | bytes 3145732
  149.9 12.7 %collective-permute-start.16 = (bf16[20,104,128]{2,1,0:T(8,128)(2,1)}, bf16[20,104,128]{2,1,0:T(8,128)(2,1)}, u32[]{:S(2)}, u32[]{:S(2)}) collective-permute-start(bf16[20,104,128]{2,1,0:T(8,128)(2,1)} %ring.55), channel_id=1, source_target_pairs={{0,1},{1,2},{2,3},{3,4},{4,5},{5,6},{6,7},{7,8},{8,9},{9,10},{10,1... | collective-permute-start | bytes 1597448 | tf_op jit(solution)/shard_map/ring/ppermute | solution.py:636
  155.3 1.4 copy-start.3
  162.5 1.6 copy-start.4
  165.0 9.0 %copy-start.19 = (pred[192]{0:T(512)(128)(4,1)S(1)}, pred[192]{0:T(512)(128)(4,1)}, u32[]{:S(2)}) copy-start(pred[192]{0:T(512)(128)(4,1)} %copy-done.18) | copy-start | bytes 580
  165.0 11.7 %copy-start.15 = (s32[512,2]{0,1:T(2,128)S(1)}, s32[512,2]{0,1:T(2,128)}, u32[]{:S(2)}) copy-start(s32[512,2]{0,1:T(2,128)} %param.12) | copy-start | bytes 12292
  165.0 11.7 %copy-start.16 = (s32[2,64]{1,0:T(2,128)S(1)}, s32[2,64]{1,0:T(2,128)}, u32[]{:S(2)}) copy-start(s32[2,64]{1,0:T(2,128)} %get-tuple-element.146) | copy-start | bytes 1540
  170.2 16.4 %all-to-all-start.1 = ((f32[16,4,128]{2,1,0:T(4,128)}), f32[16,4,128]{2,1,0:T(4,128)S(1)}, u32[]{:S(2)}, u32[]{:S(2)}) async-start(f32[16,4,128]{2,1,0:T(4,128)} %map.1), calls=%async_computation.1 | async-start | bytes 65536 | tf_op jit(solution)/shard_map/finish/all_to_all | solution.py:671
  (4 other events, 3.0 us)
Sparse Core Ops, SparseCore 0:
  59.7 35.1 all-gather.1
